TPU v7x, 32 devices: a whole 2x2x4 slice. The times are simulated.
32 devices in a mesh: rep: 2 (over y), own: 4 (over z), tp: 2 (over x), sub: 2 (over core).
Axes of the slice: x: 2, y: 2, z: 4, core: 2. Of those that a mesh axis runs over, the one named last changes fastest.
Arguments:
- tokens: bfloat16 [8192, 5120], P(('rep', 'own', 'sub'), 'tp'), parts along dimension 0, may hold values from -6 to 6
- grad_output: bfloat16 [8192, 1024], P(('rep', 'own', 'sub'), 'tp'), parts along dimension 0, may hold values from -6 to 6
- frozen_value: bfloat16 [5120, 1024], P('tp', 'sub'), may hold values from -0.078125 to 0.078125
- shared_down: bfloat16 [5120, 64], P('tp'), may hold values from -0.078125 to 0.078125
- head_up: bfloat16 [64, 64, 1024], P('own', None, 'tp'), may hold values from -0.1875 to 0.1875
- adapter_ids: int32 [16], P('rep'), parts along dimension 0, may hold values from 0 to 63
- lengths: int32 [16], P(('rep', 'own', 'sub')), parts along dimension 0, may hold values from 1 to 512, 3072 in all
Outputs:
- input_gradient: bfloat16 [8192, 5120], P(('rep', 'own', 'sub'), 'tp'), parts along dimension 0
- shared_down_gradient: float32 [10240, 64], P(('rep', 'tp')), parts along dimension 0
- grad_heads: float32 [128, 64, 1024], P(('rep', 'own'), None, 'tp'), parts along dimension 0
There are 2 independent parts, one for each index of `rep`. A program takes and returns all parts, laid end to end along the dimension named above; an argument that names none is the same for every part. Nothing has to cross between parts.
All inputs are finite; a program needn't handle non-finite values. No bound on the sum of `lengths` on one device may be relied on, other than what follows from the above.
Results may differ from a plain program's by a relative error of at most 0.0034.
Values may be sent and summed in bfloat16 or wider, within the bound.
No kernel may reach another device: no remote copies, remote signals or barrier semaphores. Data moves between devices by JAX's collectives and lax.ppermute only.
A program may use at most 64 MiB of HBM per device.

v0:
```python
import jax
import jax.numpy as jnp
from jax import lax
from jax.sharding import PartitionSpec as P

adapter_scale = 2.0


def on_device(tokens, grad_output, frozen_value, shared_down, head_up, adapter_ids, lengths):
    count_of_rows = tokens.shape[0]
    own_count = lax.axis_size("own")
    sub_count = lax.axis_size("sub")
    own_at = lax.axis_index("own")
    sub_at = lax.axis_index("sub")
    pair_at = own_at * sub_count + sub_at
    my_adapter = lax.dynamic_index_in_dim(adapter_ids, pair_at, 0, keepdims=False)
    per_owner = head_up.shape[0]
    local_ids = own_at * per_owner + jnp.arange(per_owner, dtype=jnp.int32)
    positions = jnp.arange(count_of_rows, dtype=jnp.int32)
    kept_grad = jnp.where(
        (positions < lengths[0])[:, None], grad_output, jnp.zeros_like(grad_output)
    )
    pair_ids = jnp.arange(own_count, dtype=jnp.int32) * sub_count + sub_at
    wanted = jnp.take(adapter_ids, pair_ids)
    selector = (wanted[:, None] == local_ids[None, :]).astype(jnp.bfloat16)
    outgoing = jnp.einsum(
        "jk,krc->jrc", selector, head_up, preferred_element_type=jnp.float32
    ).astype(jnp.bfloat16)
    incoming = lax.all_to_all(outgoing, "own", split_axis=0, concat_axis=0, tiled=True)
    head_mine = lax.dynamic_index_in_dim(incoming, my_adapter // per_owner, 0, keepdims=False)
    low_part = jnp.dot(tokens, shared_down, preferred_element_type=jnp.float32)
    back_part = lax.dot_general(
        kept_grad, head_mine, (((1,), (1,)), ((), ())), preferred_element_type=jnp.float32
    )
    low_sum, back_sum = lax.psum((low_part, back_part), "tp")
    low_rank = low_sum.astype(jnp.bfloat16)
    rank_backward = back_sum.astype(jnp.bfloat16)
    whole_grad = lax.all_gather(kept_grad, "tp", axis=1, tiled=True)
    frozen_value_term = lax.dot_general(
        whole_grad,
        lax.all_gather(frozen_value, "sub", axis=1, tiled=True),
        (((1,), (1,)), ((), ())),
        preferred_element_type=jnp.float32,
    )
    adapter_side_term = lax.dot_general(
        rank_backward, shared_down, (((1,), (1,)), ((), ())), preferred_element_type=jnp.float32
    )
    input_gradient = (frozen_value_term + adapter_scale * adapter_side_term).astype(jnp.bfloat16)
    scale_factor = adapter_scale / count_of_rows
    shared_part = scale_factor * lax.dot_general(
        tokens, rank_backward, (((0,), (0,)), ((), ())), preferred_element_type=jnp.float32
    )
    head_part = scale_factor * lax.dot_general(
        low_rank, kept_grad, (((0,), (0,)), ((), ())), preferred_element_type=jnp.float32
    )
    dest_owner = jnp.arange(own_count * sub_count, dtype=jnp.int32) // sub_count
    slot_mask = (dest_owner == my_adapter // per_owner).astype(jnp.float32)
    sending = slot_mask[:, None, None] * head_part[None, :, :]
    arrived = lax.all_to_all(sending, ("own", "sub"), split_axis=0, concat_axis=0, tiled=True)
    belongs = (adapter_ids[None, :] == local_ids[:, None]).astype(jnp.float32)
    grad_heads = jnp.einsum("kj,jrc->krc", belongs, arrived, precision=lax.Precision.HIGHEST)
    shared_down_gradient = lax.psum(shared_part, ("own", "sub"))
    return (input_gradient, shared_down_gradient, grad_heads)


def solution(mesh):
    placed = (
        P(("rep", "own", "sub"), "tp"),
        P(("rep", "own", "sub"), "tp"),
        P("tp", "sub"),
        P("tp", None),
        P("own", None, "tp"),
        P("rep"),
        P(("rep", "own", "sub")),
    )
    return jax.shard_map(
        on_device,
        mesh=mesh,
        in_specs=placed,
        out_specs=(
            P(("rep", "own", "sub"), "tp"),
            P(("rep", "tp"), None),
            P(("rep", "own"), None, "tp"),
        ),
        check_vma=False,
    )
```

profile of v0, /device:TPU:0, one launch (start us, length us, event | category | flops | bytes accessed | tf_op | source)
XLA Modules:
  0.0 129.6 jit_solution(12388251907544690907)
XLA Ops:
  8.9 2.0 %broadcast_select_fusion = bf16[512,512]{1,0:T(8,128)(2,1)} fusion(bf16[512,512]{1,0:T(8,128)(2,1)} %param.8, pred[512]{0:T(512)(128)(4,1)S(1)} %iota_compare_fusion), kind=kLoop, calls=%fused_computation.10 | loop fusion | flops 262144 | bytes 1049088 | tf_op jit(solution)/shard_map/jit(_where)/select_n | solution.py:20
  10.9 0.0 all-gather.5.cloned.1.call-start
  10.9 0.7 all-gather.5.cloned.1.call-update
  11.7 0.6 gather_fusion
  12.3 1.9 %convolution_convert_fusion = bf16[4,64,512]{2,0,1:T(4,128)(2,1)S(1)} fusion(bf16[16,64,512]{2,1,0:T(8,128)(2,1)} %param.11, s32[16]{0:T(128)S(1)} %iota_add_fusion, s32[4]{0:T(128)S(1)} %and_select_fusion.1), kind=kOutput, calls=%fused_computation.4 | convolution fusion | flops 4325440 | bytes 1310800 | tf_op jit(solution)/shard_map/jk,krc->jrc/dot_general | solution.py:26
  14.3 0.7 copy.15
  15.0 6.5 %all-to-all-start = ((bf16[4,64,512]{2,1,0:T(8,128)(2,1)}), bf16[4,64,512]{2,1,0:T(8,128)(2,1)}, u32[]{:S(2)}, u32[]{:S(2)}) async-start(bf16[4,64,512]{2,1,0:T(8,128)(2,1)} %copy.15), calls=%async_computation | async-start | bytes 524288 | tf_op jit(solution)/shard_map/all_to_all | solution.py:29
  21.5 0.6 dynamic_slice.8
  24.7 1.6 %fusion.21 = f32[512,64]{0,1:T(8,128)} fusion(bf16[512,2560]{1,0:T(8,128)(2,1)S(1)} %copy-done, bf16[2560,64]{0,1:T(8,128)(2,1)S(1)} %copy-done.3), kind=kOutput, calls=%fused_computation.39 | convolution fusion | flops 167772160 | bytes 3080192 | tf_op jit(solution)/shard_map/dot_general | solution.py:31
  26.2 4.2 %all-to-all-done = bf16[4,64,512]{2,1,0:T(8,128)(2,1)} async-done(((bf16[4,64,512]{2,1,0:T(8,128)(2,1)}), bf16[4,64,512]{2,1,0:T(8,128)(2,1)}, u32[]{:S(2)}, u32[]{:S(2)}) %all-to-all-start) | async-done | bytes 262176 | tf_op jit(solution)/shard_map/all_to_all | solution.py:29
  30.5 1.8 %fusion.4 = f32[512,64]{0,1:T(8,128)} fusion(bf16[512,512]{1,0:T(8,128)(2,1)S(1)} %copy-done.2, bf16[4,64,512]{2,1,0:T(8,128)(2,1)} %all-to-all-done, s32[]{:T(128)S(6)} %select_n.60), kind=kOutput, calls=%fused_computation.11 | convolution fusion | flops 33554432 | bytes 720900 | tf_op jit(solution)/shard_map/dot_general | solution.py:32
  32.3 13.9 %all-reduce.5 = (bf16[512,64]{0,1:T(8,128)(2,1)S(1)}, bf16[512,64]{0,1:T(8,128)(2,1)}) all-reduce(f32[512,64]{0,1:T(8,128)} %fusion.4, f32[512,64]{0,1:T(8,128)} %fusion.21), channel_id=1, replica_groups=mesh['rep'=2,'own'=4,'tp'=2,'sub'=2] {'tp'}, use_global_device_ids=true, to_apply=%region_0.1 | all-reduce | flops 65536 | bytes 393216 | tf_op jit(solution)/shard_map/psum | solution.py:35
  46.1 1.1 convolution_multiply_fusion.1
  47.2 1.2 broadcast_multiply_fusion
  48.3 4.2 %all-to-all-start.1 = ((f32[8,64,512]{2,1,0:T(8,128)}), f32[8,64,512]{2,1,0:T(8,128)}, u32[]{:S(2)}, u32[]{:S(2)}) async-start(f32[8,64,512]{2,1,0:T(8,128)} %broadcast_multiply_fusion), calls=%async_computation.1 | async-start | bytes 2097152 | tf_op jit(solution)/shard_map/all_to_all | solution.py:59
  52.6 0.0 all-reduce.4.cloned.1.call-start
  52.6 1.4 %fusion = f32[2560,64]{0,1:T(8,128)} fusion(bf16[512,2560]{1,0:T(8,128)(2,1)S(1)} %copy-done, bf16[512,64]{0,1:T(8,128)(2,1)S(1)} %get-tuple-element.12), kind=kOutput, calls=%fused_computation.3 | convolution fusion | flops 167936000 | bytes 3342336 | tf_op jit(solution)/shard_map/dot_general | solution.py:50
  54.1 29.4 %all-to-all-done.1 = f32[8,64,512]{2,1,0:T(8,128)} async-done(((f32[8,64,512]{2,1,0:T(8,128)}), f32[8,64,512]{2,1,0:T(8,128)}, u32[]{:S(2)}, u32[]{:S(2)}) %all-to-all-start.1) | async-done | bytes 1048608 | tf_op jit(solution)/shard_map/all_to_all | solution.py:59
  83.5 2.7 %fusion.1 = f32[16,64,512]{2,0,1:T(8,128)S(1)} fusion(f32[8,64,512]{2,1,0:T(8,128)} %all-to-all-done.1, s32[16]{0:T(128)S(1)} %iota_add_fusion, s32[8]{0:T(128)S(1)} %copy-done.1), kind=kOutput, calls=%fused_computation.6 | convolution fusion | flops 50331776 | bytes 3145824 | tf_op jit(solution)/shard_map/kj,jrc->krc/dot_general | solution.py:61
  86.2 2.5 %copy.17 = f32[16,64,512]{2,1,0:T(8,128)} copy(f32[16,64,512]{2,0,1:T(8,128)S(1)} %fusion.1) | data formatting | bytes 4194304
  88.8 5.2 %fusion.20 = f32[512,2560]{1,0:T(8,128)S(1)} fusion(bf16[512,1024]{1,0:T(8,128)(2,1)} %all-gather.3.cloned.1.call-done, bf16[2560,1024]{1,0:T(8,128)(2,1)} %all-gather.5.cloned.1.call-done), kind=kOutput, calls=%fused_computation.38 | convolution fusion | flops 2684354560 | bytes 11534336 | tf_op jit(solution)/shard_map/dot_general | solution.py:39
  94.0 2.4 %add_convert_fusion = bf16[512,2560]{1,0:T(8,128)(2,1)} fusion(f32[512,2560]{1,0:T(8,128)S(1)} %fusion.20, bf16[2560,64]{0,1:T(8,128)(2,1)S(1)} %copy-done.3, bf16[512,64]{0,1:T(8,128)(2,1)S(1)} %get-tuple-element.12), kind=kOutput, calls=%fused_computation.1 | convolution fusion | flops 171704320 | bytes 8257536 | tf_op jit(solution)/shard_map/dot_general | solution.py:45
  96.3 23.9 %all-reduce.4.cloned.1.call-done = f32[2560,64]{0,1:T(8,128)} async-done(((f32[2560,64]{0,1:T(8,128)}), f32[2560,64]{0,1:T(8,128)}) %all-reduce.4.cloned.1.call-update) | async-done | bytes 655376 | tf_op jit(solution)/shard_map/psum | solution.py:62
  120.2 2.0 %copy.28 = f32[2560,64]{0,1:T(8,128)} copy(f32[2560,64]{0,1:T(8,128)} %all-reduce.4.cloned.1.call-done) | data formatting | bytes 1310720
  (19 shorter events, 0.1 us)
Async XLA Ops:
  8.0 16.7 %copy-start = (bf16[512,2560]{1,0:T(8,128)(2,1)S(1)}, bf16[512,2560]{1,0:T(8,128)(2,1)}, u32[]{:S(2)}) copy-start(bf16[512,2560]{1,0:T(8,128)(2,1)} %param.7) | copy-start | bytes 7864324
  8.0 3.7 %copy-start.1 = (s32[8]{0:T(128)S(1)}, s32[8]{0:T(128)}, u32[]{:S(2)}) copy-start(s32[8]{0:T(128)} %param.12) | copy-start | bytes 100
  8.0 80.7 %all-gather.3.cloned.1.call-start = ((), (), s32[]{:S(2)}) async-start(), calls=%async_computation.2 | async-start | bytes 1572864 | tf_op jit(solution)/shard_map/all_gather | solution.py:38
  10.9 13.8 %copy-start.3 = (bf16[2560,64]{0,1:T(8,128)(2,1)S(1)}, bf16[2560,64]{0,1:T(8,128)(2,1)}, u32[]{:S(2)}) copy-start(bf16[2560,64]{0,1:T(8,128)(2,1)} %param.10) | copy-start | bytes 983044
  10.9 77.9 %all-gather.5.cloned.1.call-start = ((), (), s32[]{:S(2)}) async-start(), calls=%async_computation.3 | async-start | bytes 7864320 | tf_op jit(solution)/shard_map/all_gather | solution.py:41
  15.0 15.5 %copy-start.2 = (bf16[512,512]{1,0:T(8,128)(2,1)S(1)}, bf16[512,512]{1,0:T(8,128)(2,1)}, u32[]{:S(2)}) copy-start(bf16[512,512]{1,0:T(8,128)(2,1)} %broadcast_select_fusion) | copy-start | bytes 1572868
  15.0 15.5 %all-to-all-start = ((bf16[4,64,512]{2,1,0:T(8,128)(2,1)}), bf16[4,64,512]{2,1,0:T(8,128)(2,1)}, u32[]{:S(2)}, u32[]{:S(2)}) async-start(bf16[4,64,512]{2,1,0:T(8,128)(2,1)} %copy.15), calls=%async_computation | async-start | bytes 524288 | tf_op jit(solution)/shard_map/all_to_all | solution.py:29
  48.3 35.2 %all-to-all-start.1 = ((f32[8,64,512]{2,1,0:T(8,128)}), f32[8,64,512]{2,1,0:T(8,128)}, u32[]{:S(2)}, u32[]{:S(2)}) async-start(f32[8,64,512]{2,1,0:T(8,128)} %broadcast_multiply_fusion), calls=%async_computation.1 | async-start | bytes 2097152 | tf_op jit(solution)/shard_map/all_to_all | solution.py:59
  52.6 67.6 %all-reduce.4.cloned.1.call-start = ((), (), s32[]{:S(2)}) async-start(), calls=%async_computation.4 | async-start | bytes 1310720 | tf_op jit(solution)/shard_map/psum | solution.py:62
Sparse Core Ops, SparseCore 0:
  11.0 23.9 all-gather.2
  36.6 15.5 all-gather.4
Sparse Core Ops, SparseCore 1:
  56.0 64.2 all-reduce.3
where the time goes:
time: 130 us
  waiting for transfers between devices  58.3 us (45%)
  between operations  19 us (15%)
  matrix products  18 us (14%)
  blocking collectives  13.9 us (11%)
  starting transfers between devices  10.8 us (8%)
  local copies, waits for them, and re-layouts  6.5 us (5%)
  other arithmetic  3.18 us (2%)
    all_to_all x1, waiting for transfers between devices, on_device(): lax.all_to_all(sending, ('own', 'sub'), split_axis=0, concat_axis=0, tile...  29.4 us
    psum x1, waiting for transfers between devices, on_device(): shared_down_gradient = lax.psum(shared_part, ('own', 'sub'))  23.9 us
    psum x1, blocking collectives, on_device(): low_sum, back_sum = lax.psum((low_part, back_part), 'tp')  13.9 us
    all_to_all x1, starting transfers between devices, on_device(): lax.all_to_all(outgoing, 'own', split_axis=0, concat_axis=0, tiled=True)  6.45 us
    dot_general x1, matrix products, on_device(): lax.dot_general(whole_grad, lax.all_gather(frozen_value, 'sub', axis=1, t...  5.2 us
    unnamed x10, local copies, waits for them, and re-layouts  4.53 us
    all_to_all x1, starting transfers between devices, on_device(): lax.all_to_all(sending, ('own', 'sub'), split_axis=0, concat_axis=0, tile...  4.24 us
    all_to_all x1, waiting for transfers between devices, on_device(): lax.all_to_all(outgoing, 'own', split_axis=0, concat_axis=0, tiled=True)  4.23 us
  transfers between devices with their start and end apart: 5, of which 3 were waited for; matrix products, arithmetic and copies ran while one was open for 18% of the time, Pallas kernels for 0%

commit v1 on v0

v1 whole, which is shorter than its diff:
```python
import functools

import jax
import jax.numpy as jnp
from jax import lax
from jax.experimental import pallas as pl
from jax.experimental.pallas import tpu as pltpu
from jax.sharding import PartitionSpec as P

adapter_scale = 2.0
f32 = jnp.float32
bf16 = jnp.bfloat16

OWN, SUB, TP, LENGTH, IDS = 0, 1, 2, 3, 4


def shift(x, axis, step):
    count = lax.axis_size(axis)
    return lax.ppermute(x, axis, [(i, (i + step) % count) for i in range(count)])


def width_of(whole):
    for width in (512, 256, 128):
        if whole % width == 0:
            return width
    return whole


def whole(shape):
    return pl.BlockSpec(shape, lambda i, info: (0,) * len(shape))


def call(body, info, operands, in_specs, out_specs, out_shape, grid, scratch=(), flops=0):
    moved = sum(x.size * x.dtype.itemsize for x in list(operands) + list(out_shape))
    return pl.pallas_call(
        body,
        out_shape=out_shape,
        grid_spec=pltpu.PrefetchScalarGridSpec(
            num_scalar_prefetch=1,
            grid=grid,
            in_specs=in_specs,
            out_specs=out_specs,
            scratch_shapes=scratch,
        ),
        compiler_params=pltpu.CompilerParams(vmem_limit_bytes=40 * 1024 * 1024),
        cost_estimate=pl.CostEstimate(flops=flops, bytes_accessed=moved, transcendentals=0),
    )(info, *operands)


def shape_of(dims, kind):
    return jax.ShapeDtypeStruct(dims, kind)


def pick_heads(info, head_up, own_count, sub_count):
    per_owner, rank, width = head_up.shape

    def place(step):
        def index(i, info):
            target = lax.rem(info[OWN] + step, own_count) * sub_count + info[SUB]
            local = info[IDS + target] - info[OWN] * per_owner
            return jnp.clip(local, 0, per_owner - 1), 0, 0

        return index

    def body(info, *refs):
        for source, target in zip(refs[:own_count], refs[own_count:]):
            target[...] = source[0]

    return call(
        body,
        info,
        [head_up] * own_count,
        [pl.BlockSpec((1, rank, width), place(step)) for step in range(own_count)],
        [whole((rank, width))] * own_count,
        [shape_of((rank, width), bf16)] * own_count,
        (1,),
    )


def project_low(info, tokens, down):
    rows, features = tokens.shape
    rank = down.shape[0]
    width = width_of(features)

    def body(info, tokens, down, low):
        part = lax.dot_general(
            down[...], tokens[...], (((1,), (1,)), ((), ())), preferred_element_type=f32
        )

        @pl.when(pl.program_id(0) == 0)
        def _():
            low[...] = part

        @pl.when(pl.program_id(0) > 0)
        def _():
            low[...] += part

    return call(
        body,
        info,
        [tokens, down],
        [
            pl.BlockSpec((rows, width), lambda i, info: (0, i)),
            pl.BlockSpec((rank, width), lambda i, info: (0, i)),
        ],
        [whole((rank, rows))],
        [shape_of((rank, rows), f32)],
        (features // width,),
        flops=2 * rows * rank * features,
    )[0]


def head_term(info, lows, grad, scale):
    rank, rows = lows[0].shape
    columns = grad.shape[1]

    def body(info, *refs):
        *lows, grad, term = refs
        total = lows[0][...]
        for low in lows[1:]:
            total = total + low[...]
        live = lax.broadcasted_iota(jnp.int32, total.shape, 1) < info[LENGTH]
        kept = jnp.where(live, total, 0.0).astype(bf16)
        term[...] = (scale * jnp.dot(kept, grad[...], preferred_element_type=f32)).astype(bf16)

    return call(
        body,
        info,
        list(lows) + [grad],
        [whole((rank, rows))] * len(lows) + [whole((rows, columns))],
        [whole((rank, columns))],
        [shape_of((rank, columns), bf16)],
        (1,),
        flops=2 * rows * rank * columns,
    )[0]


def back_and_shared(info, grads, heads, tokens, scale, sub_count):
    rows, features = tokens.shape
    rank, columns = heads[0].shape
    parts = len(grads)
    width = width_of(features)
    share = rank // sub_count

    def body(info, *refs):
        grads, heads = refs[:parts], refs[parts : 2 * parts]
        tokens, back, keep, send, total = refs[2 * parts :]

        @pl.when(pl.program_id(0) == 0)
        def _():
            both = None
            for grad, head in zip(grads, heads):
                part = lax.dot_general(
                    head[...], grad[...], (((1,), (1,)), ((), ())), preferred_element_type=f32
                )
                both = part if both is None else both + part
            live = lax.broadcasted_iota(jnp.int32, both.shape, 1) < info[LENGTH]
            back[...] = jnp.where(live, both, 0.0).astype(bf16)

        total[...] = scale * jnp.dot(back[...], tokens[...], preferred_element_type=f32)
        mine = pl.multiple_of(info[SUB] * share, share)
        other = pl.multiple_of((1 - info[SUB]) * share, share)
        keep[...] = total[pl.ds(mine, share), :]
        send[...] = total[pl.ds(other, share), :]

    return call(
        body,
        info,
        list(grads) + list(heads) + [tokens],
        [whole((rows, columns))] * parts
        + [whole((rank, columns))] * parts
        + [pl.BlockSpec((rows, width), lambda i, info: (0, i))],
        [whole((rank, rows))] + [pl.BlockSpec((share, width), lambda i, info: (0, i))] * 2,
        [shape_of((rank, rows), bf16)] + [shape_of((share, features), f32)] * 2,
        (features // width,),
        scratch=[pltpu.VMEM((rank, width), f32)],
        flops=2 * rows * rank * (features + parts * columns),
    )


def cut_shares(info, keep, arrived, own_count):
    share, features = keep.shape
    per = share // own_count

    def body(info, keep, arrived, mine, *rest):
        sends, total = rest[:-1], rest[-1]
        total[...] = keep[...] + arrived[...]
        for step in range(own_count):
            place = lax.rem(info[OWN] + step, own_count) * per
            if per % 8 == 0:
                place = pl.multiple_of(place, 8)
            piece = total[pl.ds(place, per), :]
            if step == 0:
                mine[...] = piece
            else:
                sends[step - 1][...] = piece.astype(bf16)

    return call(
        body,
        info,
        [keep, arrived],
        [whole((share, features))] * 2,
        [whole((per, features))] * own_count,
        [shape_of((per, features), f32)] + [shape_of((per, features), bf16)] * (own_count - 1),
        (1,),
        scratch=[pltpu.VMEM((share, features), f32)],
    )


def add_shares(info, mine, arrived):
    def body(info, mine, *refs):
        total = mine[...]
        for piece in refs[:-1]:
            total = total + piece[...].astype(f32)
        refs[-1][...] = total.astype(bf16)

    return call(
        body,
        info,
        [mine] + list(arrived),
        [whole(mine.shape)] * (1 + len(arrived)),
        [whole(mine.shape)],
        [shape_of(mine.shape, bf16)],
        (1,),
    )[0]


def join_shares(info, near, far, own_count):
    per, features = near[0].shape
    share = per * own_count

    def body(info, *refs):
        out = refs[-1]
        for step in range(own_count):
            owner = lax.rem(info[OWN] + own_count - step, own_count)
            for side, piece in ((info[SUB], refs[step]), (1 - info[SUB], refs[own_count + step])):
                place = side * share + owner * per
                if per % 8 == 0:
                    place = pl.multiple_of(place, 8)
                out[pl.ds(place, per), :] = piece[...].astype(f32)

    return call(
        body,
        info,
        list(near) + list(far),
        [whole((per, features))] * (2 * own_count),
        [whole((2 * share, features))],
        [shape_of((2 * share, features), f32)],
        (1,),
    )[0]


def place_terms(info, near, far, per_owner, own_count, sub_count):
    rank, columns = near[0].shape
    group = 4 if per_owner % 4 == 0 else 1

    def body(info, *refs):
        out = refs[-1]
        for at in range(group):
            tenant = info[OWN] * per_owner + pl.program_id(0) * group + at
            total = jnp.zeros((rank, columns), f32)
            for step in range(own_count):
                first = lax.rem(info[OWN] + own_count - step, own_count) * sub_count
                one = info[IDS + first + info[SUB]] == tenant
                two = info[IDS + first + 1 - info[SUB]] == tenant
                total = total + (
                    jnp.where(one, refs[step][...].astype(f32), 0.0)
                    + jnp.where(two, refs[own_count + step][...].astype(f32), 0.0)
                )
            out[at] = total

    return call(
        body,
        info,
        list(near) + list(far),
        [whole((rank, columns))] * (2 * own_count),
        [pl.BlockSpec((group, rank, columns), lambda i, info: (i, 0, 0))],
        [shape_of((per_owner, rank, columns), f32)],
        (per_owner // group,),
    )[0]


def input_side(info, grads, frozen, frozen_other, back, down):
    rows, columns = grads[0].shape
    features, half = frozen.shape
    rank = back.shape[0]
    parts = len(grads)
    width = width_of(features)

    def body(info, *refs):
        grads = refs[:parts]
        frozen, frozen_other, back, down, out, kept = refs[parts:]

        @pl.when(pl.program_id(0) == 0)
        def _():
            live = lax.broadcasted_iota(jnp.int32, (rows, columns), 0) < info[LENGTH]
            for step, grad in enumerate(grads):
                place = lax.rem(info[TP] + parts - step, parts) * columns
                kept[:, pl.ds(pl.multiple_of(place, 128), columns)] = jnp.where(
                    live, grad[...], jnp.zeros((rows, columns), bf16)
                )

        both = (((1,), (1,)), ((), ()))
        mine = pl.multiple_of(info[SUB] * half, 128)
        other = pl.multiple_of((1 - info[SUB]) * half, 128)
        total = lax.dot_general(
            kept[:, pl.ds(mine, half)], frozen[...], both, preferred_element_type=f32
        )
        total += lax.dot_general(
            kept[:, pl.ds(other, half)], frozen_other[...], both, preferred_element_type=f32
        )
        total += lax.dot_general(
            adapter_scale * back[...], down[...], (((0,), (0,)), ((), ())),
            preferred_element_type=f32,
        )
        out[...] = total.astype(bf16)

    return call(
        body,
        info,
        list(grads) + [frozen, frozen_other, back, down],
        [whole((rows, columns))] * parts
        + [pl.BlockSpec((width, half), lambda i, info: (i, 0))] * 2
        + [whole((rank, rows)), pl.BlockSpec((rank, width), lambda i, info: (0, i))],
        [pl.BlockSpec((rows, width), lambda i, info: (0, i))],
        [shape_of((rows, features), bf16)],
        (features // width,),
        scratch=[pltpu.VMEM((rows, parts * columns), bf16)],
        flops=2 * rows * features * (2 * half + rank),
    )[0]


def on_device(tokens, grad_output, frozen_value, shared_down, head_up, adapter_ids, lengths):
    rows = tokens.shape[0]
    own_count = lax.axis_size("own")
    sub_count = lax.axis_size("sub")
    tp_count = lax.axis_size("tp")
    per_owner = head_up.shape[0]
    scale = adapter_scale / rows

    frozen_other = shift(frozen_value, "sub", 1)
    grads = [grad_output] + [shift(grad_output, "tp", step) for step in range(1, tp_count)]

    own_at = lax.axis_index("own")
    place = jnp.stack([own_at, lax.axis_index("sub"), lax.axis_index("tp"), lengths[0]])
    info = jnp.concatenate([place.astype(jnp.int32), adapter_ids])
    down = shared_down.T

    picked = pick_heads(info, head_up, own_count, sub_count)
    offered = [picked[0]] + [shift(picked[step], "own", step) for step in range(1, own_count)]
    my_adapter = lax.dynamic_index_in_dim(
        adapter_ids, own_at * sub_count + lax.axis_index("sub"), 0, keepdims=False
    )
    away = lax.rem(own_at + own_count - my_adapter // per_owner, own_count)
    head = offered[0]
    for step in range(1, own_count):
        head = jnp.where(away == step, offered[step], head)
    heads = [head] + [shift(head, "tp", step) for step in range(1, tp_count)]

    low = project_low(info, tokens, down)
    lows = [low] + [shift(low, "tp", step) for step in range(1, tp_count)]
    term = head_term(info, lows, grad_output, scale)
    near = [term] + [shift(term, "own", step) for step in range(1, own_count)]
    far = [shift(piece, "sub", 1) for piece in near]

    back, keep, send = back_and_shared(info, grads, heads, tokens, scale, sub_count)
    arrived = shift(send, "sub", 1)
    mine, *sends = cut_shares(info, keep, arrived, own_count)
    pieces = [shift(piece, "own", step + 1) for step, piece in enumerate(sends)]
    share = add_shares(info, mine, pieces)
    near_shares = [share] + [shift(share, "own", step) for step in range(1, own_count)]
    far_shares = [shift(piece, "sub", 1) for piece in near_shares]

    input_gradient = input_side(info, grads, frozen_value, frozen_other, back, down)
    grad_heads = place_terms(info, near, far, per_owner, own_count, sub_count)
    shared_down_gradient = join_shares(info, near_shares, far_shares, own_count).T
    return (input_gradient, shared_down_gradient, grad_heads)


def solution(mesh):
    placed = (
        P(("rep", "own", "sub"), "tp"),
        P(("rep", "own", "sub"), "tp"),
        P("tp", "sub"),
        P("tp", None),
        P("own", None, "tp"),
        P("rep"),
        P(("rep", "own", "sub")),
    )
    return jax.shard_map(
        on_device,
        mesh=mesh,
        in_specs=placed,
        out_specs=(
            P(("rep", "own", "sub"), "tp"),
            P(("rep", "tp"), None),
            P(("rep", "own"), None, "tp"),
        ),
        check_vma=False,
    )
```

time: 130 us -> 72.6 us (0.56)
  waiting for transfers between devices: 58.3 us -> 18.4 us
  Pallas kernels: 0 us -> 21.5 us
  matrix products: 18 us -> 0 us
  between operations: 19 us -> 4.19 us
  blocking collectives: 13.9 us -> 0 us
  starting transfers between devices: 10.8 us -> 24.5 us
  local copies, waits for them, and re-layouts: 6.5 us -> 2.64 us
  other arithmetic: 3.18 us -> 0.86 us
    all_to_all x2 -> x0, waiting for transfers between devices: 33.6 us -> none  [the longest x1 29.4 us: on_device(): lax.all_to_all(sending, ('own', 'sub'), split_axis=0, concat_axis=0, tile...]
    ppermute x0 -> x25, starting transfers between devices: none -> 24.5 us  [shift(): lax.ppermute(x, axis, [(i, (i + step) % count) for i in range(count)])]
    psum x1 -> x0, waiting for transfers between devices: 23.9 us -> none  [on_device(): shared_down_gradient = lax.psum(shared_part, ('own', 'sub'))]
    pallas_call x0 -> x9, Pallas kernels: none -> 21.5 us  [call(): pl.pallas_call(body, out_shape=out_shape, grid_spec=pltpu.PrefetchScalarG...]
    ppermute x0 -> x25, waiting for transfers between devices: none -> 18.4 us  [shift(): lax.ppermute(x, axis, [(i, (i + step) % count) for i in range(count)])]
    dot_general x8 -> x0, matrix products: 18 us -> none  [the longest x1 5.2 us: on_device(): lax.dot_general(whole_grad, lax.all_gather(frozen_value, 'sub', axis=1, t...]
    psum x1 -> x0, blocking collectives: 13.9 us -> none  [on_device(): low_sum, back_sum = lax.psum((low_part, back_part), 'tp')]
    all_to_all x2 -> x0, starting transfers between devices: 10.7 us -> none  [the longest x1 6.45 us: on_device(): lax.all_to_all(outgoing, 'own', split_axis=0, concat_axis=0, tiled=True)]
  transfers between devices with their start and end apart: 5 -> 25, of which waited for: 3 -> 8; matrix products, arithmetic and copies ran while one was open for 18% -> 3% of each run, Pallas kernels for 0% -> 19%
where the time goes in v1:
time: 72.6 us; the launch traced here: 72.1 us
  starting transfers between devices  24.5 us (34%)
  Pallas kernels  21.5 us (30%)
  waiting for transfers between devices  18.4 us (25%)
  between operations  4.19 us (6%)
  local copies, waits for them, and re-layouts  2.64 us (4%)
  other arithmetic  0.86 us (1%)
    ppermute x25, starting transfers between devices, shift(): lax.ppermute(x, axis, [(i, (i + step) % count) for i in range(count)])  24.5 us
    pallas_call x9, Pallas kernels, call(): pl.pallas_call(body, out_shape=out_shape, grid_spec=pltpu.PrefetchScalarG...  21.5 us
    ppermute x25, waiting for transfers between devices, shift(): lax.ppermute(x, axis, [(i, (i + step) % count) for i in range(count)])  18.4 us
  transfers between devices with their start and end apart: 25, of which 8 were waited for; matrix products, arithmetic and copies ran while one was open for 3% of the time, Pallas kernels for 19%

profile of v1, /device:TPU:0, one launch (start us, length us, event | category | flops | bytes accessed | tf_op | source)
XLA Modules:
  0.0 72.1 jit_solution(16416567650960055512)
XLA Ops:
  1.2 2.6 %collective-permute-start = (bf16[512,512]{1,0:T(8,128)(2,1)}, bf16[512,512]{1,0:T(8,128)(2,1)}, u32[]{:S(2)}, u32[]{:S(2)}) collective-permute-start(bf16[512,512]{1,0:T(8,128)(2,1)} %refs_2_.5), channel_id=1, source_target_pairs={{0,2},{2,0},{1,3},{3,1},{4,6},{6,4},{5,7},{7,5},{8,10},{10,8},{9,1... | collective-permute-start | bytes 1572872 | tf_op jit(solution)/shard_map/ppermute | solution.py:19
  5.1 1.2 %copy-done = bf16[16,64,512]{2,1,0:T(8,128)(2,1)S(1)} copy-done((bf16[16,64,512]{2,1,0:T(8,128)(2,1)S(1)}, bf16[16,64,512]{2,1,0:T(8,128)(2,1)}, u32[]{:S(2)}) %copy-start) | copy-done | bytes 1048600
  6.3 1.2 %shard_map.94 = (bf16[64,512]{1,0:T(8,128)(2,1)S(1)}, bf16[64,512]{1,0:T(8,128)(2,1)}, bf16[64,512]{1,0:T(8,128)(2,1)}, bf16[64,512]{1,0:T(8,128)(2,1)}) custom-call(s32[12]{0:T(128)S(1)} %concatenate.3.info, bf16[16,64,512]{2,1,0:T(8,128)(2,1)S(1)} %copy-done, bf16[16,64,512]{2,1,0:T(8,128)(2,1)S(1)} %copy-done, bf16[16,64,512]{2,1,0:T(8,128)(2,1)S(1)} %copy-done, ...), custom_call_target="tpu_custom_call" | custom-call | bytes 4456448 | tf_op jit(solution)/shard_map/pallas_call | solution.py:35
  7.6 3.6 %collective-permute-start.2 = (bf16[64,512]{1,0:T(8,128)(2,1)}, bf16[64,512]{1,0:T(8,128)(2,1)}, u32[]{:S(2)}, u32[]{:S(2)}) collective-permute-start(bf16[64,512]{1,0:T(8,128)(2,1)} %get-tuple-element.14), channel_id=1, source_target_pairs={{0,12},{4,0},{8,4},{12,8},{1,13},{5,1},{9,5},{13,9},{2,14},{6,2},{... | collective-permute-start | bytes 196616 | tf_op jit(solution)/shard_map/ppermute | solution.py:19
  11.2 1.0 %collective-permute-start.4 = (bf16[64,512]{1,0:T(8,128)(2,1)}, bf16[64,512]{1,0:T(8,128)(2,1)}, u32[]{:S(2)}, u32[]{:S(2)}) collective-permute-start(bf16[64,512]{1,0:T(8,128)(2,1)} %get-tuple-element.16), channel_id=1, source_target_pairs={{0,4},{4,8},{8,12},{12,0},{1,5},{5,9},{9,13},{13,1},{2,6},{6,10},{... | collective-permute-start | bytes 196616 | tf_op jit(solution)/shard_map/ppermute | solution.py:19
  15.6 2.7 %collective-permute-done.3 = bf16[64,512]{1,0:T(8,128)(2,1)} collective-permute-done((bf16[64,512]{1,0:T(8,128)(2,1)}, bf16[64,512]{1,0:T(8,128)(2,1)}, u32[]{:S(2)}, u32[]{:S(2)}) %collective-permute-start.3) | collective-permute-done | bytes 65568 | tf_op jit(solution)/shard_map/ppermute | solution.py:19
  18.3 0.9 %select_select_fusion.refs_2_ = bf16[64,512]{1,0:T(8,128)(2,1)S(1)} fusion(bf16[64,512]{1,0:T(8,128)(2,1)} %collective-permute-done.2, bf16[64,512]{1,0:T(8,128)(2,1)} %collective-permute-done.3, bf16[64,512]{1,0:T(8,128)(2,1)} %collective-permute-done.4, bf16[64,512]{1,0:T(8,128)(2,1)S(1)} %get-tuple-element.17, pred[]{:T(512)S(6)} %eq.11, pred[]{:T(512)S(6)} %eq.10, ...), kind=kLoop, calls=%fused_computation | loop fusion | flops 98304 | bytes 327683 | tf_op jit(solution)/shard_map/jit(_where)/select_n | solution.py:357
  19.8 3.7 %collective-permute-done.5.refs_3_ = bf16[64,512]{1,0:T(8,128)(2,1)S(1)} collective-permute-done((bf16[64,512]{1,0:T(8,128)(2,1)S(1)}, bf16[64,512]{1,0:T(8,128)(2,1)S(1)}, u32[]{:S(2)}, u32[]{:S(2)}) %collective-permute-start.5) | collective-permute-done | bytes 65568 | tf_op jit(solution)/shard_map/ppermute | solution.py:19
  23.5 3.4 %shard_map.95 = (bf16[64,512]{1,0:T(8,128)(2,1)S(1)}, f32[32,2560]{1,0:T(8,128)S(1)}, f32[32,2560]{1,0:T(8,128)S(1)}) custom-call(s32[12]{0:T(128)S(1)} %concatenate.3.info, bf16[512,512]{1,0:T(8,128)(2,1)S(1)} %copy-done.2, bf16[512,512]{1,0:T(8,128)(2,1)} %collective-permute-done.refs_1_, bf16[64,512]{1,0:T(8,128)(2,1)S(1)} %select_select_fusion.refs_2_, ...), custom_call_target="tpu_custom_call" | custom-call | flops 234881024 | bytes 4521984 | tf_op jit(solution)/shard_map/pallas_call | solution.py:35
  27.0 2.3 %shard_map.100.refs_0_ = f32[64,512]{1,0:T(8,128)S(1)} custom-call(s32[12]{0:T(128)S(1)} %concatenate.3.info, bf16[512,2560]{1,0:T(8,128)(2,1)S(1)} %copy-done.1, bf16[64,2560]{1,0:T(8,128)(2,1)S(1)} %bitcast.6), custom_call_target="tpu_custom_call" | custom-call | flops 167772160 | bytes 3080192 | tf_op jit(solution)/shard_map/pallas_call | solution.py:35
  29.9 5.3 %collective-permute-done.17.refs_1_ = f32[64,512]{1,0:T(8,128)S(1)} collective-permute-done((f32[64,512]{1,0:T(8,128)S(1)}, f32[64,512]{1,0:T(8,128)S(1)}, u32[]{:S(2)}, u32[]{:S(2)}) %collective-permute-start.17) | collective-permute-done | bytes 131104 | tf_op jit(solution)/shard_map/ppermute | solution.py:19
  35.3 0.7 %shard_map.101.refs_0_ = bf16[64,512]{1,0:T(8,128)(2,1)S(1)} custom-call(s32[12]{0:T(128)S(1)} %concatenate.3.info, f32[64,512]{1,0:T(8,128)S(1)} %shard_map.100.refs_0_, f32[64,512]{1,0:T(8,128)S(1)} %collective-permute-done.17.refs_1_, bf16[512,512]{1,0:T(8,128)(2,1)S(1)} %copy-done.2), custom_call_target="tpu_custom_call" | custom-call | flops 33554432 | bytes 851968 | tf_op jit(solution)/shard_map/pallas_call | solution.py:35
  36.1 2.4 %collective-permute-start.19 = (bf16[64,512]{1,0:T(8,128)(2,1)S(1)}, bf16[64,512]{1,0:T(8,128)(2,1)S(1)}, u32[]{:S(2)}, u32[]{:S(2)}) collective-permute-start(bf16[64,512]{1,0:T(8,128)(2,1)S(1)} %shard_map.101.refs_0_), channel_id=1, source_target_pairs={{0,8},{4,12},{8,0},{12,4},{1,9},{5,13},{9,1},{13,5},{2,10},{6,14},... | collective-permute-start | bytes 196616 | tf_op jit(solution)/shard_map/ppermute | solution.py:19
  38.5 2.3 %collective-permute-start.20 = (bf16[64,512]{1,0:T(8,128)(2,1)S(1)}, bf16[64,512]{1,0:T(8,128)(2,1)S(1)}, u32[]{:S(2)}, u32[]{:S(2)}) collective-permute-start(bf16[64,512]{1,0:T(8,128)(2,1)S(1)} %shard_map.101.refs_0_), channel_id=1, source_target_pairs={{0,12},{4,0},{8,4},{12,8},{1,13},{5,1},{9,5},{13,9},{2,14},{6,2},{... | collective-permute-start | bytes 196616 | tf_op jit(solution)/shard_map/ppermute | solution.py:19
  41.5 1.4 %collective-permute-done.18.refs_1_ = bf16[64,512]{1,0:T(8,128)(2,1)S(1)} collective-permute-done((bf16[64,512]{1,0:T(8,128)(2,1)S(1)}, bf16[64,512]{1,0:T(8,128)(2,1)S(1)}, u32[]{:S(2)}, u32[]{:S(2)}) %collective-permute-start.18) | collective-permute-done | bytes 65568 | tf_op jit(solution)/shard_map/ppermute | solution.py:19
  42.9 1.9 %collective-permute-start.8 = (bf16[8,2560]{1,0:T(8,128)(2,1)S(1)}, bf16[8,2560]{1,0:T(8,128)(2,1)S(1)}, u32[]{:S(2)}, u32[]{:S(2)}) collective-permute-start(bf16[8,2560]{1,0:T(8,128)(2,1)S(1)} %get-tuple-element.23), channel_id=1, source_target_pairs={{0,8},{4,12},{8,0},{12,4},{1,9},{5,13},{9,1},{13,5},{2,10},{6,14},... | collective-permute-start | bytes 122888 | tf_op jit(solution)/shard_map/ppermute | solution.py:19
  44.8 3.4 %collective-permute-start.9 = (bf16[8,2560]{1,0:T(8,128)(2,1)S(1)}, bf16[8,2560]{1,0:T(8,128)(2,1)S(1)}, u32[]{:S(2)}, u32[]{:S(2)}) collective-permute-start(bf16[8,2560]{1,0:T(8,128)(2,1)S(1)} %get-tuple-element.24), channel_id=1, source_target_pairs={{0,12},{4,0},{8,4},{12,8},{1,13},{5,1},{9,5},{13,9},{2,14},{6,2},{... | collective-permute-start | bytes 122888 | tf_op jit(solution)/shard_map/ppermute | solution.py:19
  48.9 1.1 %collective-permute-done.9.refs_2_ = bf16[8,2560]{1,0:T(8,128)(2,1)S(1)} collective-permute-done((bf16[8,2560]{1,0:T(8,128)(2,1)S(1)}, bf16[8,2560]{1,0:T(8,128)(2,1)S(1)}, u32[]{:S(2)}, u32[]{:S(2)}) %collective-permute-start.9) | collective-permute-done | bytes 40992 | tf_op jit(solution)/shard_map/ppermute | solution.py:19
  50.6 4.7 %collective-permute-start.11 = (bf16[8,2560]{1,0:T(8,128)(2,1)S(1)}, bf16[8,2560]{1,0:T(8,128)(2,1)S(1)}, u32[]{:S(2)}, u32[]{:S(2)}) collective-permute-start(bf16[8,2560]{1,0:T(8,128)(2,1)S(1)} %shard_map.98.refs_0_), channel_id=1, source_target_pairs={{0,8},{4,12},{8,0},{12,4},{1,9},{5,13},{9,1},{13,5},{2,10},{6,14},... | collective-permute-start | bytes 122888 | tf_op jit(solution)/shard_map/ppermute | solution.py:19
  55.4 1.8 %collective-permute-done.10.refs_1_ = bf16[8,2560]{1,0:T(8,128)(2,1)S(1)} collective-permute-done((bf16[8,2560]{1,0:T(8,128)(2,1)S(1)}, bf16[8,2560]{1,0:T(8,128)(2,1)S(1)}, u32[]{:S(2)}, u32[]{:S(2)}) %collective-permute-start.10) | collective-permute-done | bytes 40992 | tf_op jit(solution)/shard_map/ppermute | solution.py:19
  57.2 1.6 %collective-permute-done.11.refs_2_ = bf16[8,2560]{1,0:T(8,128)(2,1)S(1)} collective-permute-done((bf16[8,2560]{1,0:T(8,128)(2,1)S(1)}, bf16[8,2560]{1,0:T(8,128)(2,1)S(1)}, u32[]{:S(2)}, u32[]{:S(2)}) %collective-permute-start.11) | collective-permute-done | bytes 40992 | tf_op jit(solution)/shard_map/ppermute | solution.py:19
  59.5 3.4 %shard_map.102 = f32[16,64,512]{2,1,0:T(8,128)} custom-call(s32[12]{0:T(128)S(1)} %concatenate.3.info, bf16[64,512]{1,0:T(8,128)(2,1)S(1)} %shard_map.101.refs_0_, bf16[64,512]{1,0:T(8,128)(2,1)S(1)} %collective-permute-done.18.refs_1_, bf16[64,512]{1,0:T(8,128)(2,1)S(1)} %collective-permute-done.19.refs_2_, ...), custom_call_target="tpu_custom_call" | custom-call | bytes 2621440 | tf_op jit(solution)/shard_map/pallas_call | solution.py:35
  62.9 1.4 %shard_map.99 = f32[64,2560]{1,0:T(8,128)} custom-call(s32[12]{0:T(128)S(1)} %concatenate.3.info, bf16[8,2560]{1,0:T(8,128)(2,1)S(1)} %shard_map.98.refs_0_, bf16[8,2560]{1,0:T(8,128)(2,1)S(1)} %collective-permute-done.10.refs_1_, bf16[8,2560]{1,0:T(8,128)(2,1)S(1)} %collective-permute-done.11.refs_2_, bf16[8,2560]{1,0:T(8,128)(2,1)S(1)} %collective-permute-done.12.refs_3_, ...), custom_call_target="tpu_custom_call" | custom-call | bytes 983040 | tf_op jit(solution)/shard_map/pallas_call | solution.py:35
  64.4 7.8 %shard_map.96 = bf16[512,2560]{1,0:T(8,128)(2,1)} custom-call(s32[12]{0:T(128)S(1)} %concatenate.3.info, bf16[512,512]{1,0:T(8,128)(2,1)S(1)} %copy-done.2, bf16[512,512]{1,0:T(8,128)(2,1)} %collective-permute-done.refs_1_, bf16[2560,512]{1,0:T(8,128)(2,1)S(1)} %copy-done.4, bf16[2560,512]{1,0:T(8,128)(2,1)} %collective-permute-done.1.refs_3_, ...), custom_call_target="tpu_custom_call" | custom-call | flops 2852126720 | bytes 9306112 | tf_op jit(solution)/shard_map/pallas_call | solution.py:35
  (50 shorter events, 5.9 us)
Async XLA Ops:
  0.6 63.7 %collective-permute-start.1 = (bf16[2560,512]{1,0:T(8,128)(2,1)}, bf16[2560,512]{1,0:T(8,128)(2,1)}, u32[]{:S(2)}, u32[]{:S(2)}) collective-permute-start(bf16[2560,512]{1,0:T(8,128)(2,1)} %refs_2_.4), channel_id=1, source_target_pairs={{0,1},{1,0},{2,3},{3,2},{4,5},{5,4},{6,7},{7,6},{8,9},{9,8},{10,11... | collective-permute-start | bytes 7864328 | tf_op jit(solution)/shard_map/ppermute | solution.py:19
  1.2 22.3 %collective-permute-start = (bf16[512,512]{1,0:T(8,128)(2,1)}, bf16[512,512]{1,0:T(8,128)(2,1)}, u32[]{:S(2)}, u32[]{:S(2)}) collective-permute-start(bf16[512,512]{1,0:T(8,128)(2,1)} %refs_2_.5), channel_id=1, source_target_pairs={{0,2},{2,0},{1,3},{3,1},{4,6},{6,4},{5,7},{7,5},{8,10},{10,8},{9,1... | collective-permute-start | bytes 1572872 | tf_op jit(solution)/shard_map/ppermute | solution.py:19
  7.6 8.0 %collective-permute-start.2 = (bf16[64,512]{1,0:T(8,128)(2,1)}, bf16[64,512]{1,0:T(8,128)(2,1)}, u32[]{:S(2)}, u32[]{:S(2)}) collective-permute-start(bf16[64,512]{1,0:T(8,128)(2,1)} %get-tuple-element.14), channel_id=1, source_target_pairs={{0,12},{4,0},{8,4},{12,8},{1,13},{5,1},{9,5},{13,9},{2,14},{6,2},{... | collective-permute-start | bytes 196616 | tf_op jit(solution)/shard_map/ppermute | solution.py:19
  11.2 7.1 %collective-permute-start.3 = (bf16[64,512]{1,0:T(8,128)(2,1)}, bf16[64,512]{1,0:T(8,128)(2,1)}, u32[]{:S(2)}, u32[]{:S(2)}) collective-permute-start(bf16[64,512]{1,0:T(8,128)(2,1)} %get-tuple-element.15), channel_id=1, source_target_pairs={{0,8},{4,12},{8,0},{12,4},{1,9},{5,13},{9,1},{13,5},{2,10},{6,14},... | collective-permute-start | bytes 196616 | tf_op jit(solution)/shard_map/ppermute | solution.py:19
  11.2 7.1 %collective-permute-start.4 = (bf16[64,512]{1,0:T(8,128)(2,1)}, bf16[64,512]{1,0:T(8,128)(2,1)}, u32[]{:S(2)}, u32[]{:S(2)}) collective-permute-start(bf16[64,512]{1,0:T(8,128)(2,1)} %get-tuple-element.16), channel_id=1, source_target_pairs={{0,4},{4,8},{8,12},{12,0},{1,5},{5,9},{9,13},{13,1},{2,6},{6,10},{... | collective-permute-start | bytes 196616 | tf_op jit(solution)/shard_map/ppermute | solution.py:19
  19.2 4.3 %collective-permute-start.5 = (bf16[64,512]{1,0:T(8,128)(2,1)S(1)}, bf16[64,512]{1,0:T(8,128)(2,1)S(1)}, u32[]{:S(2)}, u32[]{:S(2)}) collective-permute-start(bf16[64,512]{1,0:T(8,128)(2,1)S(1)} %select_select_fusion.refs_2_), channel_id=1, source_target_pairs={{0,2},{2,0},{1,3},{3,1},{4,6},{6,4},{5,7},{7,5},{8,10},{10,8},{9,1... | collective-permute-start | bytes 196616 | tf_op jit(solution)/shard_map/ppermute | solution.py:19
  26.9 13.9 %collective-permute-start.6 = (f32[32,2560]{1,0:T(8,128)S(1)}, f32[32,2560]{1,0:T(8,128)S(1)}, u32[]{:S(2)}, u32[]{:S(2)}) collective-permute-start(f32[32,2560]{1,0:T(8,128)S(1)} %get-tuple-element.20), channel_id=1, source_target_pairs={{0,1},{1,0},{2,3},{3,2},{4,5},{5,4},{6,7},{7,6},{8,9},{9,8},{10,11... | collective-permute-start | bytes 983048 | tf_op jit(solution)/shard_map/ppermute | solution.py:19
  29.3 6.0 %collective-permute-start.17 = (f32[64,512]{1,0:T(8,128)S(1)}, f32[64,512]{1,0:T(8,128)S(1)}, u32[]{:S(2)}, u32[]{:S(2)}) collective-permute-start(f32[64,512]{1,0:T(8,128)S(1)} %shard_map.100.refs_0_), channel_id=1, source_target_pairs={{0,2},{2,0},{1,3},{3,1},{4,6},{6,4},{5,7},{7,5},{8,10},{10,8},{9,1... | collective-permute-start | bytes 393224 | tf_op jit(solution)/shard_map/ppermute | solution.py:19
  36.0 6.8 %collective-permute-start.18 = (bf16[64,512]{1,0:T(8,128)(2,1)S(1)}, bf16[64,512]{1,0:T(8,128)(2,1)S(1)}, u32[]{:S(2)}, u32[]{:S(2)}) collective-permute-start(bf16[64,512]{1,0:T(8,128)(2,1)S(1)} %shard_map.101.refs_0_), channel_id=1, source_target_pairs={{0,4},{4,8},{8,12},{12,0},{1,5},{5,9},{9,13},{13,1},{2,6},{6,10},{... | collective-permute-start | bytes 196616 | tf_op jit(solution)/shard_map/ppermute | solution.py:19
  36.1 8.7 %collective-permute-start.19 = (bf16[64,512]{1,0:T(8,128)(2,1)S(1)}, bf16[64,512]{1,0:T(8,128)(2,1)S(1)}, u32[]{:S(2)}, u32[]{:S(2)}) collective-permute-start(bf16[64,512]{1,0:T(8,128)(2,1)S(1)} %shard_map.101.refs_0_), channel_id=1, source_target_pairs={{0,8},{4,12},{8,0},{12,4},{1,9},{5,13},{9,1},{13,5},{2,10},{6,14},... | collective-permute-start | bytes 196616 | tf_op jit(solution)/shard_map/ppermute | solution.py:19
  38.5 9.7 %collective-permute-start.20 = (bf16[64,512]{1,0:T(8,128)(2,1)S(1)}, bf16[64,512]{1,0:T(8,128)(2,1)S(1)}, u32[]{:S(2)}, u32[]{:S(2)}) collective-permute-start(bf16[64,512]{1,0:T(8,128)(2,1)S(1)} %shard_map.101.refs_0_), channel_id=1, source_target_pairs={{0,12},{4,0},{8,4},{12,8},{1,13},{5,1},{9,5},{13,9},{2,14},{6,2},{... | collective-permute-start | bytes 196616 | tf_op jit(solution)/shard_map/ppermute | solution.py:19
  41.4 6.9 %collective-permute-start.7 = (bf16[8,2560]{1,0:T(8,128)(2,1)S(1)}, bf16[8,2560]{1,0:T(8,128)(2,1)S(1)}, u32[]{:S(2)}, u32[]{:S(2)}) collective-permute-start(bf16[8,2560]{1,0:T(8,128)(2,1)S(1)} %get-tuple-element.22), channel_id=1, source_target_pairs={{0,4},{4,8},{8,12},{12,0},{1,5},{5,9},{9,13},{13,1},{2,6},{6,10},{... | collective-permute-start | bytes 122888 | tf_op jit(solution)/shard_map/ppermute | solution.py:19
  42.9 5.9 %collective-permute-start.8 = (bf16[8,2560]{1,0:T(8,128)(2,1)S(1)}, bf16[8,2560]{1,0:T(8,128)(2,1)S(1)}, u32[]{:S(2)}, u32[]{:S(2)}) collective-permute-start(bf16[8,2560]{1,0:T(8,128)(2,1)S(1)} %get-tuple-element.23), channel_id=1, source_target_pairs={{0,8},{4,12},{8,0},{12,4},{1,9},{5,13},{9,1},{13,5},{2,10},{6,14},... | collective-permute-start | bytes 122888 | tf_op jit(solution)/shard_map/ppermute | solution.py:19
  44.8 5.1 %collective-permute-start.9 = (bf16[8,2560]{1,0:T(8,128)(2,1)S(1)}, bf16[8,2560]{1,0:T(8,128)(2,1)S(1)}, u32[]{:S(2)}, u32[]{:S(2)}) collective-permute-start(bf16[8,2560]{1,0:T(8,128)(2,1)S(1)} %get-tuple-element.24), channel_id=1, source_target_pairs={{0,12},{4,0},{8,4},{12,8},{1,13},{5,1},{9,5},{13,9},{2,14},{6,2},{... | collective-permute-start | bytes 122888 | tf_op jit(solution)/shard_map/ppermute | solution.py:19
  48.3 2.3 %collective-permute-start.22 = (bf16[64,512]{1,0:T(8,128)(2,1)S(1)}, bf16[64,512]{1,0:T(8,128)(2,1)S(1)}, u32[]{:S(2)}, u32[]{:S(2)}) collective-permute-start(bf16[64,512]{1,0:T(8,128)(2,1)S(1)} %collective-permute-done.18.refs_1_), channel_id=1, source_target_pairs={{0,1},{1,0},{2,3},{3,2},{4,5},{5,4},{6,7},{7,6},{8,9},{9,8},{10,11... | collective-permute-start | bytes 196616 | tf_op jit(solution)/shard_map/ppermute | solution.py:19
  48.8 6.5 %collective-permute-start.23 = (bf16[64,512]{1,0:T(8,128)(2,1)S(1)}, bf16[64,512]{1,0:T(8,128)(2,1)S(1)}, u32[]{:S(2)}, u32[]{:S(2)}) collective-permute-start(bf16[64,512]{1,0:T(8,128)(2,1)S(1)} %collective-permute-done.19.refs_2_), channel_id=1, source_target_pairs={{0,1},{1,0},{2,3},{3,2},{4,5},{5,4},{6,7},{7,6},{8,9},{9,8},{10,11... | collective-permute-start | bytes 196616 | tf_op jit(solution)/shard_map/ppermute | solution.py:19
  49.9 5.3 %collective-permute-start.24 = (bf16[64,512]{1,0:T(8,128)(2,1)S(1)}, bf16[64,512]{1,0:T(8,128)(2,1)S(1)}, u32[]{:S(2)}, u32[]{:S(2)}) collective-permute-start(bf16[64,512]{1,0:T(8,128)(2,1)S(1)} %collective-permute-done.20.refs_3_), channel_id=1, source_target_pairs={{0,1},{1,0},{2,3},{3,2},{4,5},{5,4},{6,7},{7,6},{8,9},{9,8},{10,11... | collective-permute-start | bytes 196616 | tf_op jit(solution)/shard_map/ppermute | solution.py:19
  50.5 6.7 %collective-permute-start.10 = (bf16[8,2560]{1,0:T(8,128)(2,1)S(1)}, bf16[8,2560]{1,0:T(8,128)(2,1)S(1)}, u32[]{:S(2)}, u32[]{:S(2)}) collective-permute-start(bf16[8,2560]{1,0:T(8,128)(2,1)S(1)} %shard_map.98.refs_0_), channel_id=1, source_target_pairs={{0,4},{4,8},{8,12},{12,0},{1,5},{5,9},{9,13},{13,1},{2,6},{6,10},{... | collective-permute-start | bytes 122888 | tf_op jit(solution)/shard_map/ppermute | solution.py:19
  50.6 8.2 %collective-permute-start.11 = (bf16[8,2560]{1,0:T(8,128)(2,1)S(1)}, bf16[8,2560]{1,0:T(8,128)(2,1)S(1)}, u32[]{:S(2)}, u32[]{:S(2)}) collective-permute-start(bf16[8,2560]{1,0:T(8,128)(2,1)S(1)} %shard_map.98.refs_0_), channel_id=1, source_target_pairs={{0,8},{4,12},{8,0},{12,4},{1,9},{5,13},{9,1},{13,5},{2,10},{6,14},... | collective-permute-start | bytes 122888 | tf_op jit(solution)/shard_map/ppermute | solution.py:19
  55.3 4.2 %collective-permute-start.12 = (bf16[8,2560]{1,0:T(8,128)(2,1)S(1)}, bf16[8,2560]{1,0:T(8,128)(2,1)S(1)}, u32[]{:S(2)}, u32[]{:S(2)}) collective-permute-start(bf16[8,2560]{1,0:T(8,128)(2,1)S(1)} %shard_map.98.refs_0_), channel_id=1, source_target_pairs={{0,12},{4,0},{8,4},{12,8},{1,13},{5,1},{9,5},{13,9},{2,14},{6,2},{... | collective-permute-start | bytes 122888 | tf_op jit(solution)/shard_map/ppermute | solution.py:19
  55.3 7.6 %collective-permute-start.13 = (bf16[8,2560]{1,0:T(8,128)(2,1)S(1)}, bf16[8,2560]{1,0:T(8,128)(2,1)S(1)}, u32[]{:S(2)}, u32[]{:S(2)}) collective-permute-start(bf16[8,2560]{1,0:T(8,128)(2,1)S(1)} %shard_map.98.refs_0_), channel_id=1, source_target_pairs={{0,1},{1,0},{2,3},{3,2},{4,5},{5,4},{6,7},{7,6},{8,9},{9,8},{10,11... | collective-permute-start | bytes 122888 | tf_op jit(solution)/shard_map/ppermute | solution.py:19
  57.2 5.7 %collective-permute-start.14 = (bf16[8,2560]{1,0:T(8,128)(2,1)S(1)}, bf16[8,2560]{1,0:T(8,128)(2,1)S(1)}, u32[]{:S(2)}, u32[]{:S(2)}) collective-permute-start(bf16[8,2560]{1,0:T(8,128)(2,1)S(1)} %collective-permute-done.10.refs_1_), channel_id=1, source_target_pairs={{0,1},{1,0},{2,3},{3,2},{4,5},{5,4},{6,7},{7,6},{8,9},{9,8},{10,11... | collective-permute-start | bytes 122888 | tf_op jit(solution)/shard_map/ppermute | solution.py:19
  58.8 4.1 %collective-permute-start.15 = (bf16[8,2560]{1,0:T(8,128)(2,1)S(1)}, bf16[8,2560]{1,0:T(8,128)(2,1)S(1)}, u32[]{:S(2)}, u32[]{:S(2)}) collective-permute-start(bf16[8,2560]{1,0:T(8,128)(2,1)S(1)} %collective-permute-done.11.refs_2_), channel_id=1, source_target_pairs={{0,1},{1,0},{2,3},{3,2},{4,5},{5,4},{6,7},{7,6},{8,9},{9,8},{10,11... | collective-permute-start | bytes 122888 | tf_op jit(solution)/shard_map/ppermute | solution.py:19
  59.5 3.4 %collective-permute-start.16 = (bf16[8,2560]{1,0:T(8,128)(2,1)S(1)}, bf16[8,2560]{1,0:T(8,128)(2,1)S(1)}, u32[]{:S(2)}, u32[]{:S(2)}) collective-permute-start(bf16[8,2560]{1,0:T(8,128)(2,1)S(1)} %collective-permute-done.12.refs_3_), channel_id=1, source_target_pairs={{0,1},{1,0},{2,3},{3,2},{4,5},{5,4},{6,7},{7,6},{8,9},{9,8},{10,11... | collective-permute-start | bytes 122888 | tf_op jit(solution)/shard_map/ppermute | solution.py:19
  (7 other events, 103.8 us)

commit v2 on v0

v2 whole, which is shorter than its diff:
```python
import jax
import jax.numpy as jnp
from jax import lax
from jax.experimental import pallas as pl
from jax.experimental.pallas import tpu as pltpu
from jax.sharding import PartitionSpec as P

adapter_scale = 2.0
f32 = jnp.float32
bf16 = jnp.bfloat16

anywhere = pl.BlockSpec(memory_space=pl.ANY)
in_vmem = pl.BlockSpec(memory_space=pltpu.VMEM)
in_smem = pl.BlockSpec(memory_space=pltpu.SMEM)


def shift(x, axis, step):
    count = lax.axis_size(axis)
    return lax.ppermute(x, axis, [(i, (i + step) % count) for i in range(count)])


def swap(x, own_bit, sub_bit):
    subs = lax.axis_size("sub")
    whole = lax.axis_size("own") * subs
    other = own_bit * subs + sub_bit
    return lax.ppermute(x, ("own", "sub"), [(i, i ^ other) for i in range(whole)])


def shape_of(dims, kind):
    return jax.ShapeDtypeStruct(dims, kind)


def call(body, operands, specs, outs, out_specs=None, after=(), flops=0, **more):
    count = len(operands)

    def kernel(*refs):
        body(*refs[:count], *refs[count + len(after) :])

    moved = sum(x.size * x.dtype.itemsize for x in list(operands) + list(outs))
    return pl.pallas_call(
        kernel,
        out_shape=outs,
        in_specs=list(specs) + [anywhere] * len(after),
        out_specs=[in_vmem] * len(outs) if out_specs is None else out_specs,
        compiler_params=pltpu.CompilerParams(vmem_limit_bytes=24 * 1024 * 1024),
        cost_estimate=pl.CostEstimate(flops=flops, bytes_accessed=moved, transcendentals=0),
        **more,
    )(*operands, *after)


def pick_heads(adapter_ids, head_up, grad):
    per_owner, rank, width = head_up.shape
    own_count, sub_count = lax.axis_size("own"), lax.axis_size("sub")
    first = grad.shape[0] // 2

    def body(ids, head_up, grad, *refs):
        outs, early, sems = refs[:own_count], refs[own_count], refs[own_count + 1]
        own, sub = lax.axis_index("own"), lax.axis_index("sub")
        copies = []
        for step in range(own_count):
            target = lax.rem(own + step, own_count) * sub_count + sub
            local = jnp.clip(ids[target] - own * per_owner, 0, per_owner - 1)
            copies.append(pltpu.make_async_copy(head_up.at[local], outs[step], sems.at[step]))
        copies.append(
            pltpu.make_async_copy(grad.at[pl.ds(0, first)], early, sems.at[own_count])
        )
        for copy in copies:
            copy.start()
        for copy in copies:
            copy.wait()

    *picked, early = call(
        body,
        [adapter_ids, head_up, grad],
        [in_smem, anywhere, anywhere],
        [shape_of((rank, width), bf16)] * own_count + [shape_of((first, grad.shape[1]), bf16)],
        scratch_shapes=[pltpu.SemaphoreType.DMA((own_count + 1,))],
    )
    return picked, early


def project_low(tokens, down, after):
    rows, features = tokens.shape
    rank = down.shape[0]

    def body(tokens, down, low):
        low[...] = lax.dot_general(
            down[...], tokens[...], (((1,), (1,)), ((), ())), preferred_element_type=f32
        )

    return call(
        body,
        [tokens, down],
        [in_vmem] * 2,
        [shape_of((rank, rows), f32)],
        after=after,
        flops=2 * rows * rank * features,
    )[0]


def project_back(adapter_ids, offered, grad, per_owner, after):
    rank, columns = offered[0].shape
    rows = grad.shape[0]
    own_count, sub_count = lax.axis_size("own"), lax.axis_size("sub")
    first = rows // 2

    def body(ids, *refs):
        offered, grad, part, late, head = refs[:own_count], *refs[own_count:]
        own, sub = lax.axis_index("own"), lax.axis_index("sub")
        owner = lax.div(ids[own * sub_count + sub], per_owner)
        away = lax.rem(own + own_count - owner, own_count)
        for step in range(own_count):

            @pl.when(away == step)
            def _():
                head[...] = offered[step][...]

        part[...] = lax.dot_general(
            head[...], grad[...], (((1,), (1,)), ((), ())), preferred_element_type=f32
        )
        late[...] = grad[first:, :]

    return call(
        body,
        [adapter_ids, *offered, grad],
        [in_smem] + [in_vmem] * (own_count + 1),
        [shape_of((rank, rows), f32), shape_of((rows - first, columns), bf16)],
        after=after,
        scratch_shapes=[pltpu.VMEM((rank, columns), bf16)],
        flops=2 * rows * rank * columns,
    )


def head_term(lengths, lows, grad, scale, after):
    rank, rows = lows[0].shape
    columns = grad.shape[1]

    def body(lengths, *refs):
        *lows, grad, term = refs
        total = lows[0][...]
        for low in lows[1:]:
            total = total + low[...]
        live = lax.broadcasted_iota(jnp.int32, total.shape, 1) < lengths[0]
        kept = jnp.where(live, total, 0.0).astype(bf16)
        term[...] = (scale * jnp.dot(kept, grad[...], preferred_element_type=f32)).astype(bf16)

    return call(
        body,
        [lengths, *lows, grad],
        [in_smem] + [in_vmem] * (len(lows) + 1),
        [shape_of((rank, columns), bf16)],
        after=after,
        flops=2 * rows * rank * columns,
    )[0]


def share_of(own, sub):
    return sub * 2 + lax.rem(own, 2)


def shared_terms(lengths, parts, tokens, scale, after):
    rows, features = tokens.shape
    rank = parts[0].shape[0]
    share = rank // 4

    def body(lengths, *refs):
        parts, (tokens, back, mine, *sends, total) = refs[:count], refs[count:]
        own, sub = lax.axis_index("own"), lax.axis_index("sub")
        both = parts[0][...]
        for part in parts[1:]:
            both = both + part[...]
        live = lax.broadcasted_iota(jnp.int32, both.shape, 1) < lengths[0]
        back[...] = jnp.where(live, both, 0.0).astype(bf16)
        total[...] = scale * jnp.dot(back[...], tokens[...], preferred_element_type=f32)
        at = share_of(own, sub)

        def piece(flip):
            return total[pl.ds(pl.multiple_of((at ^ flip) * share, share), share), :]

        mine[...] = piece(0)
        for flip, send in zip((1, 2, 3), sends):
            send[...] = piece(flip).astype(bf16)

    count = len(parts)
    return call(
        body,
        [lengths, *parts, tokens],
        [in_smem] + [in_vmem] * (count + 1),
        [shape_of((rank, rows), bf16), shape_of((share, features), f32)]
        + [shape_of((share, features), bf16)] * 3,
        after=after,
        scratch_shapes=[pltpu.VMEM((rank, features), f32)],
        flops=2 * rows * rank * features,
    )


def add_up(pieces, after=()):
    def body(*refs):
        total = refs[0][...].astype(f32)
        for piece in refs[1:-1]:
            total = total + piece[...].astype(f32)
        refs[-1][...] = total.astype(bf16)

    return call(
        body,
        list(pieces),
        [in_vmem] * len(pieces),
        [shape_of(pieces[0].shape, bf16)],
        after=after,
    )[0]


def halve(pieces, bit):
    rows, features = pieces[0].shape
    half = rows // 2

    def body(*refs):
        total = refs[0][...].astype(f32)
        for piece in refs[1:-2]:
            total = total + piece[...].astype(f32)
        upper = lax.rem(lax.div(lax.axis_index("own"), bit), 2) == 1
        low, high = total[:half], total[half:]
        refs[-2][...] = jnp.where(upper, high, low)
        refs[-1][...] = jnp.where(upper, low, high).astype(bf16)

    return call(
        body,
        list(pieces),
        [in_vmem] * len(pieces),
        [shape_of((half, features), f32), shape_of((half, features), bf16)],
    )


def rejoin(mine, arrived, bit):
    rows, features = mine.shape

    def body(mine, arrived, out):
        upper = lax.rem(lax.div(lax.axis_index("own"), bit), 2) == 1
        one, two = mine[...].astype(f32), arrived[...].astype(f32)
        out[:rows] = jnp.where(upper, two, one).astype(bf16)
        out[rows:] = jnp.where(upper, one, two).astype(bf16)

    return call(
        body, [mine, arrived], [in_vmem] * 2, [shape_of((2 * rows, features), bf16)]
    )[0]


def join_shares(quarters, after):
    share, features = quarters[0].shape

    def body(*refs):
        out = refs[-1]
        at = share_of(lax.axis_index("own"), lax.axis_index("sub"))
        for flip in range(4):
            place = pl.multiple_of((at ^ flip) * share, share)
            out[pl.ds(place, share), :] = refs[flip][...].astype(f32)

    return call(
        body,
        quarters,
        [in_vmem] * 4,
        [shape_of((4 * share, features), f32)],
        after=after,
    )[0]


def pack_terms(near, after):
    def body(*refs):
        for at, piece in enumerate(refs[:-1]):
            refs[-1][at] = piece[...]

    return call(
        body,
        near,
        [in_vmem] * len(near),
        [shape_of((len(near),) + near[0].shape, bf16)],
        after=after,
    )[0]


def place_terms(adapter_ids, near, far, per_owner, after):
    own_count, rank, columns = near.shape
    sub_count = lax.axis_size("sub")
    group = 4 if per_owner % 4 == 0 else 1

    def body(ids, near, far, out):
        own, sub = lax.axis_index("own"), lax.axis_index("sub")
        for at in range(group):
            tenant = own * per_owner + pl.program_id(0) * group + at
            out[at] = jnp.zeros((rank, columns), f32)
            for step in range(own_count):
                first = lax.rem(own + own_count - step, own_count) * sub_count
                one = ids[first + sub] == tenant
                two = ids[first + 1 - sub] == tenant

                @pl.when(jnp.logical_or(one, two))
                def _():
                    out[at] += jnp.where(one, near[step].astype(f32), 0.0) + jnp.where(
                        two, far[step].astype(f32), 0.0
                    )

    every = pl.BlockSpec((own_count, rank, columns), lambda i: (0, 0, 0))
    return call(
        body,
        [adapter_ids, near, far],
        [in_smem, every, every],
        [shape_of((per_owner, rank, columns), f32)],
        out_specs=[pl.BlockSpec((group, rank, columns), lambda i: (i, 0, 0))],
        after=after,
        grid=(per_owner // group,),
    )[0]


def arrange(lengths, grad, others):
    rows, columns = grad.shape
    count = 1 + len(others) // 2
    first = rows // 2

    def body(lengths, grad, *refs):
        others, kept = refs[:-1], refs[-1]
        at = lax.axis_index("tp")
        live = lax.broadcasted_iota(jnp.int32, (rows, columns), 0) < lengths[0]
        zero = jnp.zeros((rows, columns), bf16)
        place = pl.multiple_of(at * columns, 128)
        kept[:, pl.ds(place, columns)] = jnp.where(live, grad[...], zero)
        for step in range(1, count):
            place = pl.multiple_of(lax.rem(at + count - step, count) * columns, 128)
            for base, piece in ((0, others[step - 1]), (first, others[count - 2 + step])):
                size = piece.shape[0]
                kept[base : base + size, pl.ds(place, columns)] = jnp.where(
                    live[base : base + size], piece[...], zero[base : base + size]
                )

    return call(
        body,
        [lengths, grad, *others],
        [in_smem] + [in_vmem] * (1 + len(others)),
        [shape_of((rows, count * columns), bf16)],
    )[0]


def input_side(kept, frozen, frozen_other, back, down, width, begin, count, before, after):
    rows, whole = kept.shape
    features, half = frozen.shape
    rank = back.shape[0]

    def body(*refs):
        kept, frozen, frozen_other, back, down = refs[:5]
        out = refs[-1]
        sub = lax.axis_index("sub")
        both = (((1,), (1,)), ((), ()))
        mine = pl.multiple_of(sub * half, 128)
        other = pl.multiple_of((1 - sub) * half, 128)
        total = lax.dot_general(
            kept[:, pl.ds(mine, half)], frozen[...], both, preferred_element_type=f32
        )
        total += lax.dot_general(
            kept[:, pl.ds(other, half)], frozen_other[...], both, preferred_element_type=f32
        )
        total += lax.dot_general(
            adapter_scale * back[...],
            down[...],
            (((0,), (0,)), ((), ())),
            preferred_element_type=f32,
        )
        out[...] = total.astype(bf16)

    held = [] if before is None else [before]
    return call(
        body,
        [kept, frozen, frozen_other, back, down] + held,
        [pl.BlockSpec((rows, whole), lambda i: (0, 0))]
        + [pl.BlockSpec((width, half), lambda i: (i + begin, 0))] * 2
        + [
            pl.BlockSpec((rank, rows), lambda i: (0, 0)),
            pl.BlockSpec((rank, width), lambda i: (0, i + begin)),
        ]
        + [anywhere] * len(held),
        [shape_of((rows, features), bf16)],
        out_specs=[pl.BlockSpec((rows, width), lambda i: (0, i + begin))],
        after=after,
        grid=(count,),
        input_output_aliases={5: 0} if held else {},
        flops=2 * rows * width * count * (2 * half + rank),
    )[0]


def on_device(tokens, grad_output, frozen_value, shared_down, head_up, adapter_ids, lengths):
    rows, features = tokens.shape
    own_count = lax.axis_size("own")
    tp_count = lax.axis_size("tp")
    per_owner = head_up.shape[0]
    scale = adapter_scale / rows
    down = shared_down.T
    tp_steps, own_steps = range(1, tp_count), range(1, own_count)

    frozen_other = shift(frozen_value, "sub", 1)
    picked, early = pick_heads(adapter_ids, head_up, grad_output)
    offered = [picked[0]] + [shift(picked[step], "own", step) for step in own_steps]
    early_grads = [shift(early, "tp", step) for step in tp_steps]

    low = project_low(tokens, down, [picked[0]])
    lows = [low] + [shift(low, "tp", step) for step in tp_steps]

    part, late = project_back(adapter_ids, offered, grad_output, per_owner, [low])
    parts = [part] + [shift(part, "tp", step) for step in tp_steps]
    late_grads = [shift(late, "tp", step) for step in tp_steps]

    term = head_term(lengths, lows, grad_output, scale, [part])
    near = [term] + [shift(term, "own", step) for step in own_steps]

    back, mine, *sends = shared_terms(lengths, parts, tokens, scale, [term])
    flips = ((1, 0), (0, 1), (1, 1))
    pieces = [mine] + [swap(send, *flip) for send, flip in zip(sends, flips)]

    near = pack_terms(near, [back])
    far = shift(near, "sub", 1)
    kept = arrange(lengths, grad_output, early_grads + late_grads)

    width = next(w for w in (512, 256, 128) if features % w == 0)
    blocks = features // width
    cut = max(1, blocks * 3 // 5)

    bits = [1 << i for i in range(1, own_count.bit_length() - 1)]
    for bit in bits[:-1]:
        stays, leaves = halve(pieces, bit)
        pieces = [stays, swap(leaves, bit, 0)]
    total = add_up(pieces, [near])
    input_gradient = input_side(
        kept, frozen_value, frozen_other, back, down, width, 0, cut, None, [total]
    )
    if bits:
        total = add_up([total, swap(total, bits[-1], 0)], [input_gradient])
    for bit in reversed(bits[:-1]):
        total = rejoin(total, swap(total, bit, 0), bit)
    quarters = [total] + [swap(total, *flip) for flip in flips]
    if cut < blocks:
        input_gradient = input_side(
            kept, frozen_value, frozen_other, back, down, width, cut, blocks - cut,
            input_gradient, [total],
        )
    grad_heads = place_terms(adapter_ids, near, far, per_owner, [total])
    shared_down_gradient = join_shares(quarters, [grad_heads]).T
    return (input_gradient, shared_down_gradient, grad_heads)


def solution(mesh):
    placed = (
        P(("rep", "own", "sub"), "tp"),
        P(("rep", "own", "sub"), "tp"),
        P("tp", "sub"),
        P("tp", None),
        P("own", None, "tp"),
        P("rep"),
        P(("rep", "own", "sub")),
    )
    return jax.shard_map(
        on_device,
        mesh=mesh,
        in_specs=placed,
        out_specs=(
            P(("rep", "own", "sub"), "tp"),
            P(("rep", "tp"), None),
            P(("rep", "own"), None, "tp"),
        ),
        check_vma=False,
    )
```

time: 130 us -> 56.7 us (0.44)
  waiting for transfers between devices: 58.3 us -> 16.3 us
  matrix products: 18 us -> 0 us
  between operations: 19 us -> 1.42 us
  blocking collectives: 13.9 us -> 0 us
  Pallas kernels: 0 us -> 13.5 us
  starting transfers between devices: 10.8 us -> 17.8 us
  other arithmetic: 3.18 us -> 0 us
    all_to_all x2 -> x0, waiting for transfers between devices: 33.6 us -> none  [the longest x1 29.4 us: on_device(): lax.all_to_all(sending, ('own', 'sub'), split_axis=0, concat_axis=0, tile...]
    psum x1 -> x0, waiting for transfers between devices: 23.9 us -> none  [on_device(): shared_down_gradient = lax.psum(shared_part, ('own', 'sub'))]
    dot_general x8 -> x0, matrix products: 18 us -> none  [the longest x1 5.2 us: on_device(): lax.dot_general(whole_grad, lax.all_gather(frozen_value, 'sub', axis=1, t...]
    ppermute x0 -> x19, starting transfers between devices: none -> 17.8 us  [the longest x12 12.3 us: shift(): lax.ppermute(x, axis, [(i, (i + step) % count) for i in range(count)])]
    ppermute x0 -> x19, waiting for transfers between devices: none -> 16.3 us  [the longest x12 8.78 us: shift(): lax.ppermute(x, axis, [(i, (i + step) % count) for i in range(count)])]
    psum x1 -> x0, blocking collectives: 13.9 us -> none  [on_device(): low_sum, back_sum = lax.psum((low_part, back_part), 'tp')]
    pallas_call x0 -> x13, Pallas kernels: none -> 13.5 us  [call(): pl.pallas_call(kernel, out_shape=outs, in_specs=list(specs) + [anywhere]...]
    all_to_all x2 -> x0, starting transfers between devices: 10.7 us -> none  [the longest x1 6.45 us: on_device(): lax.all_to_all(outgoing, 'own', split_axis=0, concat_axis=0, tiled=True)]
  transfers between devices with their start and end apart: 5 -> 19, of which waited for: 3 -> 7; matrix products, arithmetic and copies ran while one was open for 18% -> 0% of each run, Pallas kernels for 0% -> 22%
where the time goes in v2:
time: 56.7 us; the launch traced here: 56.4 us
  starting transfers between devices  17.8 us (31%)
  waiting for transfers between devices  16.3 us (29%)
  Pallas kernels  13.5 us (24%)
  local copies, waits for them, and re-layouts  7.39 us (13%)
  between operations  1.42 us (3%)
    pallas_call x13, Pallas kernels, call(): pl.pallas_call(kernel, out_shape=outs, in_specs=list(specs) + [anywhere]...  13.5 us
    ppermute x12, starting transfers between devices, shift(): lax.ppermute(x, axis, [(i, (i + step) % count) for i in range(count)])  12.3 us
    ppermute x12, waiting for transfers between devices, shift(): lax.ppermute(x, axis, [(i, (i + step) % count) for i in range(count)])  8.78 us
    ppermute x7, waiting for transfers between devices, swap(): lax.ppermute(x, ('own', 'sub'), [(i, i ^ other) for i in range(whole)])  7.5 us
    unnamed x24, local copies, waits for them, and re-layouts  7.39 us
    ppermute x7, starting transfers between devices, swap(): lax.ppermute(x, ('own', 'sub'), [(i, i ^ other) for i in range(whole)])  5.53 us
  transfers between devices with their start and end apart: 19, of which 7 were waited for; matrix products, arithmetic and copies ran while one was open for 0% of the time, Pallas kernels for 22%

profile of v2, /device:TPU:0, one launch (start us, length us, event | category | flops | bytes accessed | tf_op | source)
XLA Modules:
  0.0 56.4 jit_solution(6850660520431812424)
XLA Ops:
  1.2 1.0 %copy-done.4 = bf16[512,512]{1,0:T(8,128)(2,1)S(1)} copy-done((bf16[512,512]{1,0:T(8,128)(2,1)S(1)}, bf16[512,512]{1,0:T(8,128)(2,1)}, u32[]{:S(2)}) %copy-start.4) | copy-done | bytes 524312
  2.2 1.2 %copy-done.9 = bf16[16,64,512]{2,1,0:T(8,128)(2,1)S(1)} copy-done((bf16[16,64,512]{2,1,0:T(8,128)(2,1)S(1)}, bf16[16,64,512]{2,1,0:T(8,128)(2,1)}, u32[]{:S(2)}) %copy-start.9) | copy-done | bytes 1048600
  4.1 1.0 %shard_map.94 = (bf16[64,512]{1,0:T(8,128)(2,1)S(1)}, bf16[64,512]{1,0:T(8,128)(2,1)S(1)}, bf16[64,512]{1,0:T(8,128)(2,1)S(1)}, bf16[64,512]{1,0:T(8,128)(2,1)S(1)}, bf16[256,512]{1,0:T(8,128)(2,1)S(1)}) custom-call(s32[8]{0:T(128)S(1)} %copy-done.10, bf16[16,64,512]{2,1,0:T(8,128)(2,1)S(1)} %copy-done.9, bf16[512,512]{1,0:T(8,128)(2,1)S(1)} %copy-done.4), custom_call_target="tpu_custom_call" | custom-call | bytes 2097184 | tf_op jit(solution)/shard_map/pallas_call | solution.py:40
  5.1 2.6 %collective-permute-start.1 = (bf16[64,512]{1,0:T(8,128)(2,1)S(1)}, bf16[64,512]{1,0:T(8,128)(2,1)S(1)}, u32[]{:S(2)}, u32[]{:S(2)}) collective-permute-start(bf16[64,512]{1,0:T(8,128)(2,1)S(1)} %get-tuple-element.17), channel_id=1, source_target_pairs={{0,4},{4,8},{8,12},{12,0},{1,5},{5,9},{9,13},{13,1},{2,6},{6,10},{... | collective-permute-start | bytes 196616 | tf_op jit(solution)/shard_map/ppermute | solution.py:19
  7.7 2.6 %collective-permute-start.2 = (bf16[64,512]{1,0:T(8,128)(2,1)S(1)}, bf16[64,512]{1,0:T(8,128)(2,1)S(1)}, u32[]{:S(2)}, u32[]{:S(2)}) collective-permute-start(bf16[64,512]{1,0:T(8,128)(2,1)S(1)} %get-tuple-element.18), channel_id=1, source_target_pairs={{0,8},{4,12},{8,0},{12,4},{1,9},{5,13},{9,1},{13,5},{2,10},{6,14},... | collective-permute-start | bytes 196616 | tf_op jit(solution)/shard_map/ppermute | solution.py:19
  10.3 1.3 %collective-permute-start.3 = (bf16[64,512]{1,0:T(8,128)(2,1)S(1)}, bf16[64,512]{1,0:T(8,128)(2,1)S(1)}, u32[]{:S(2)}, u32[]{:S(2)}) collective-permute-start(bf16[64,512]{1,0:T(8,128)(2,1)S(1)} %get-tuple-element.19), channel_id=1, source_target_pairs={{0,12},{4,0},{8,4},{12,8},{1,13},{5,1},{9,5},{13,9},{2,14},{6,2},{... | collective-permute-start | bytes 196616 | tf_op jit(solution)/shard_map/ppermute | solution.py:19
  11.6 1.7 %copy-done.1 = bf16[512,2560]{1,0:T(8,128)(2,1)S(1)} copy-done((bf16[512,2560]{1,0:T(8,128)(2,1)S(1)}, bf16[512,2560]{1,0:T(8,128)(2,1)}, u32[]{:S(2)}) %copy-start.1) | copy-done | bytes 2621464
  13.4 1.0 %copy-done.7 = bf16[2560,64]{0,1:T(8,128)(2,1)S(1)} copy-done((bf16[2560,64]{0,1:T(8,128)(2,1)S(1)}, bf16[2560,64]{0,1:T(8,128)(2,1)}, u32[]{:S(2)}) %copy-start.7) | copy-done | bytes 327704
  14.4 0.9 %shard_map.95.refs_6_.refs_1_ = f32[64,512]{1,0:T(8,128)S(1)} custom-call(bf16[512,2560]{1,0:T(8,128)(2,1)S(1)} %copy-done.1, bf16[64,2560]{1,0:T(8,128)(2,1)S(1)} %bitcast.2, bf16[64,512]{1,0:T(8,128)(2,1)S(1)} %get-tuple-element.16.refs_2_.refs_1_), custom_call_target="tpu_custom_call" | custom-call | flops 167772160 | bytes 3080192 | tf_op jit(solution)/shard_map/pallas_call | solution.py:40
  15.3 1.6 %collective-permute-start.7 = (f32[64,512]{1,0:T(8,128)S(1)}, f32[64,512]{1,0:T(8,128)S(1)}, u32[]{:S(2)}, u32[]{:S(2)}) collective-permute-start(f32[64,512]{1,0:T(8,128)S(1)} %shard_map.95.refs_6_.refs_1_), channel_id=1, source_target_pairs={{0,2},{2,0},{1,3},{3,1},{4,6},{6,4},{5,7},{7,5},{8,10},{10,8},{9,1... | collective-permute-start | bytes 393224 | tf_op jit(solution)/shard_map/ppermute | solution.py:19
  18.9 2.1 %collective-permute-done.7.refs_2_ = f32[64,512]{1,0:T(8,128)S(1)} collective-permute-done((f32[64,512]{1,0:T(8,128)S(1)}, f32[64,512]{1,0:T(8,128)S(1)}, u32[]{:S(2)}, u32[]{:S(2)}) %collective-permute-start.7) | collective-permute-done | bytes 131104 | tf_op jit(solution)/shard_map/ppermute | solution.py:19
  21.5 2.0 %collective-permute-start = (bf16[256,512]{1,0:T(8,128)(2,1)S(1)}, bf16[256,512]{1,0:T(8,128)(2,1)S(1)}, u32[]{:S(2)}, u32[]{:S(2)}) collective-permute-start(bf16[256,512]{1,0:T(8,128)(2,1)S(1)} %get-tuple-element.15), channel_id=1, source_target_pairs={{0,2},{2,0},{1,3},{3,1},{4,6},{6,4},{5,7},{7,5},{8,10},{10,8},{9,1... | collective-permute-start | bytes 786440 | tf_op jit(solution)/shard_map/ppermute | solution.py:19
  24.3 3.6 %collective-permute-done.11.refs_1_ = bf16[64,512]{1,0:T(8,128)(2,1)S(1)} collective-permute-done((bf16[64,512]{1,0:T(8,128)(2,1)S(1)}, bf16[64,512]{1,0:T(8,128)(2,1)S(1)}, u32[]{:S(2)}, u32[]{:S(2)}) %collective-permute-start.11) | collective-permute-done | bytes 65568 | tf_op jit(solution)/shard_map/ppermute | solution.py:19
  28.5 1.5 %collective-permute-done.12.refs_2_ = bf16[64,512]{1,0:T(8,128)(2,1)S(1)} collective-permute-done((bf16[64,512]{1,0:T(8,128)(2,1)S(1)}, bf16[64,512]{1,0:T(8,128)(2,1)S(1)}, u32[]{:S(2)}, u32[]{:S(2)}) %collective-permute-start.12) | collective-permute-done | bytes 65568 | tf_op jit(solution)/shard_map/ppermute | solution.py:19
  30.6 1.6 %collective-permute-done.13.refs_3_ = bf16[64,512]{1,0:T(8,128)(2,1)S(1)} collective-permute-done((bf16[64,512]{1,0:T(8,128)(2,1)S(1)}, bf16[64,512]{1,0:T(8,128)(2,1)S(1)}, u32[]{:S(2)}, u32[]{:S(2)}) %collective-permute-start.13) | collective-permute-done | bytes 65568 | tf_op jit(solution)/shard_map/ppermute | solution.py:19
  32.2 2.3 %collective-permute-done.8.refs_1_ = bf16[16,2560]{1,0:T(8,128)(2,1)S(1)} collective-permute-done((bf16[16,2560]{1,0:T(8,128)(2,1)S(1)}, bf16[16,2560]{1,0:T(8,128)(2,1)S(1)}, u32[]{:S(2)}, u32[]{:S(2)}) %collective-permute-start.8) | collective-permute-done | bytes 81952 | tf_op jit(solution)/shard_map/ppermute | solution.py:26
  35.2 3.4 %collective-permute-done.10.refs_3_ = bf16[16,2560]{1,0:T(8,128)(2,1)S(1)} collective-permute-done((bf16[16,2560]{1,0:T(8,128)(2,1)S(1)}, bf16[16,2560]{1,0:T(8,128)(2,1)S(1)}, u32[]{:S(2)}, u32[]{:S(2)}) %collective-permute-start.10) | collective-permute-done | bytes 81952 | tf_op jit(solution)/shard_map/ppermute | solution.py:26
  38.6 2.0 %collective-permute-start.14 = (bf16[16,2560]{1,0:T(8,128)(2,1)S(1)}, bf16[16,2560]{1,0:T(8,128)(2,1)S(1)}, u32[]{:S(2)}, u32[]{:S(2)}) collective-permute-start(bf16[16,2560]{1,0:T(8,128)(2,1)S(1)} %shard_map.101.refs_5_.refs_0_), channel_id=1, source_target_pairs={{0,8},{1,9},{4,12},{5,13},{8,0},{9,1},{12,4},{13,5},{2,10},{3,11},... | collective-permute-start | bytes 245768 | tf_op jit(solution)/shard_map/ppermute | solution.py:26
  40.8 3.5 %shard_map.102.refs_2_.refs_5_ = bf16[512,2560]{1,0:T(8,128)(2,1)} custom-call(bf16[512,1024]{1,0:T(8,128)(2,1)S(1)} %shard_map.97.refs_0_, bf16[2560,512]{1,0:T(8,128)(2,1)S(1)} %copy-done.3, bf16[2560,512]{1,0:T(8,128)(2,1)S(1)} %collective-permute-done.5.refs_2_, bf16[64,512]{1,0:T(8,128)(2,1)S(1)} %get-tuple-element.22.refs_4_.refs_3_, ...), custom_call_target="tpu_custom_call" | custom-call | flops 1711276032 | bytes 9306112 | tf_op jit(solution)/shard_map/pallas_call | solution.py:40
  44.3 1.9 %collective-permute-done.14.refs_1_ = bf16[16,2560]{1,0:T(8,128)(2,1)S(1)} collective-permute-done((bf16[16,2560]{1,0:T(8,128)(2,1)S(1)}, bf16[16,2560]{1,0:T(8,128)(2,1)S(1)}, u32[]{:S(2)}, u32[]{:S(2)}) %collective-permute-start.14) | collective-permute-done | bytes 81952 | tf_op jit(solution)/shard_map/ppermute | solution.py:26
  46.1 1.7 %copy-done = bf16[512,2560]{1,0:T(8,128)(2,1)S(1)} copy-done((bf16[512,2560]{1,0:T(8,128)(2,1)S(1)}, bf16[512,2560]{1,0:T(8,128)(2,1)}, u32[]{:S(2)}) %copy-start) | copy-done | bytes 2621464
  48.0 2.0 %collective-permute-start.17 = (bf16[16,2560]{1,0:T(8,128)(2,1)S(1)}, bf16[16,2560]{1,0:T(8,128)(2,1)S(1)}, u32[]{:S(2)}, u32[]{:S(2)}) collective-permute-start(bf16[16,2560]{1,0:T(8,128)(2,1)S(1)} %shard_map.103.refs_6_.refs_3_.refs_0_), channel_id=1, source_target_pairs={{0,5},{1,4},{4,1},{5,0},{8,13},{9,12},{12,9},{13,8},{2,7},{3,6},{6... | collective-permute-start | bytes 245768 | tf_op jit(solution)/shard_map/ppermute | solution.py:26
  50.1 2.8 %shard_map.105.refs_4_ = f32[16,64,512]{2,1,0:T(8,128)} custom-call(s32[8]{0:T(128)S(1)} %copy-done.11, bf16[4,64,512]{2,1,0:T(8,128)(2,1)S(1)} %shard_map.100.refs_4_.refs_1_, bf16[4,64,512]{2,1,0:T(8,128)(2,1)S(1)} %collective-permute-done.18.refs_2_, bf16[16,2560]{1,0:T(8,128)(2,1)S(1)} %shard_map.103.refs_6_.refs_3_.refs_0_), custom_call_target="tpu_custom_call" | custom-call | bytes 2621472 | tf_op jit(solution)/shard_map/pallas_call | solution.py:40
  52.9 2.6 %shard_map.104 = bf16[512,2560]{1,0:T(8,128)(2,1)} custom-call(bf16[512,1024]{1,0:T(8,128)(2,1)S(1)} %shard_map.97.refs_0_, bf16[2560,512]{1,0:T(8,128)(2,1)S(1)} %copy-done.3, bf16[2560,512]{1,0:T(8,128)(2,1)S(1)} %collective-permute-done.5.refs_2_, bf16[64,512]{1,0:T(8,128)(2,1)S(1)} %get-tuple-element.22.refs_4_.refs_3_, ...), custom_call_target="tpu_custom_call", output_to_operand_aliasing={{}: (5, {})} | custom-call | flops 1140850688 | bytes 11927552 | tf_op jit(solution)/shard_map/pallas_call | solution.py:40
  (51 shorter events, 7.0 us)
Async XLA Ops:
  0.6 40.1 %collective-permute-start.5 = (bf16[2560,512]{1,0:T(8,128)(2,1)}, bf16[2560,512]{1,0:T(8,128)(2,1)S(1)}, u32[]{:S(2)}, u32[]{:S(2)}) collective-permute-start(bf16[2560,512]{1,0:T(8,128)(2,1)} %refs_1_.7), channel_id=1, source_target_pairs={{0,1},{1,0},{2,3},{3,2},{4,5},{5,4},{6,7},{7,6},{8,9},{9,8},{10,11... | collective-permute-start | bytes 7864328 | tf_op jit(solution)/shard_map/ppermute | solution.py:19
  4.1 12.8 %copy-start.5 = (bf16[512,512]{1,0:T(8,128)(2,1)S(1)}, bf16[512,512]{1,0:T(8,128)(2,1)}, u32[]{:S(2)}) copy-start(bf16[512,512]{1,0:T(8,128)(2,1)} %refs_3_.2) | copy-start | bytes 1572868
  5.1 11.8 %collective-permute-start.1 = (bf16[64,512]{1,0:T(8,128)(2,1)S(1)}, bf16[64,512]{1,0:T(8,128)(2,1)S(1)}, u32[]{:S(2)}, u32[]{:S(2)}) collective-permute-start(bf16[64,512]{1,0:T(8,128)(2,1)S(1)} %get-tuple-element.17), channel_id=1, source_target_pairs={{0,4},{4,8},{8,12},{12,0},{1,5},{5,9},{9,13},{13,1},{2,6},{6,10},{... | collective-permute-start | bytes 196616 | tf_op jit(solution)/shard_map/ppermute | solution.py:19
  7.7 9.1 %collective-permute-start.2 = (bf16[64,512]{1,0:T(8,128)(2,1)S(1)}, bf16[64,512]{1,0:T(8,128)(2,1)S(1)}, u32[]{:S(2)}, u32[]{:S(2)}) collective-permute-start(bf16[64,512]{1,0:T(8,128)(2,1)S(1)} %get-tuple-element.18), channel_id=1, source_target_pairs={{0,8},{4,12},{8,0},{12,4},{1,9},{5,13},{9,1},{13,5},{2,10},{6,14},... | collective-permute-start | bytes 196616 | tf_op jit(solution)/shard_map/ppermute | solution.py:19
  10.3 6.5 %collective-permute-start.3 = (bf16[64,512]{1,0:T(8,128)(2,1)S(1)}, bf16[64,512]{1,0:T(8,128)(2,1)S(1)}, u32[]{:S(2)}, u32[]{:S(2)}) collective-permute-start(bf16[64,512]{1,0:T(8,128)(2,1)S(1)} %get-tuple-element.19), channel_id=1, source_target_pairs={{0,12},{4,0},{8,4},{12,8},{1,13},{5,1},{9,5},{13,9},{2,14},{6,2},{... | collective-permute-start | bytes 196616 | tf_op jit(solution)/shard_map/ppermute | solution.py:19
  14.3 13.5 %copy-start.2 = (bf16[512,2560]{1,0:T(8,128)(2,1)S(1)}, bf16[512,2560]{1,0:T(8,128)(2,1)}, u32[]{:S(2)}) copy-start(bf16[512,2560]{1,0:T(8,128)(2,1)} %refs_3_.3) | copy-start | bytes 7864324
  15.3 5.8 %collective-permute-start.7 = (f32[64,512]{1,0:T(8,128)S(1)}, f32[64,512]{1,0:T(8,128)S(1)}, u32[]{:S(2)}, u32[]{:S(2)}) collective-permute-start(f32[64,512]{1,0:T(8,128)S(1)} %shard_map.95.refs_6_.refs_1_), channel_id=1, source_target_pairs={{0,2},{2,0},{1,3},{3,1},{4,6},{6,4},{5,7},{7,5},{8,10},{10,8},{9,1... | collective-permute-start | bytes 393224 | tf_op jit(solution)/shard_map/ppermute | solution.py:19
  17.7 6.0 %collective-permute-start.6 = (f32[64,512]{1,0:T(8,128)S(1)}, f32[64,512]{1,0:T(8,128)S(1)}, u32[]{:S(2)}, u32[]{:S(2)}) collective-permute-start(f32[64,512]{1,0:T(8,128)S(1)} %get-tuple-element.21.refs_4_.refs_1_), channel_id=1, source_target_pairs={{0,2},{2,0},{1,3},{3,1},{4,6},{6,4},{5,7},{7,5},{8,10},{10,8},{9,1... | collective-permute-start | bytes 393224 | tf_op jit(solution)/shard_map/ppermute | solution.py:19
  21.2 6.6 %collective-permute-start.11 = (bf16[64,512]{1,0:T(8,128)(2,1)S(1)}, bf16[64,512]{1,0:T(8,128)(2,1)S(1)}, u32[]{:S(2)}, u32[]{:S(2)}) collective-permute-start(bf16[64,512]{1,0:T(8,128)(2,1)S(1)} %shard_map.98.refs_4_.refs_0_), channel_id=1, source_target_pairs={{0,4},{4,8},{8,12},{12,0},{1,5},{5,9},{9,13},{13,1},{2,6},{6,10},{... | collective-permute-start | bytes 196616 | tf_op jit(solution)/shard_map/ppermute | solution.py:19
  21.5 19.1 %collective-permute-start = (bf16[256,512]{1,0:T(8,128)(2,1)S(1)}, bf16[256,512]{1,0:T(8,128)(2,1)S(1)}, u32[]{:S(2)}, u32[]{:S(2)}) collective-permute-start(bf16[256,512]{1,0:T(8,128)(2,1)S(1)} %get-tuple-element.15), channel_id=1, source_target_pairs={{0,2},{2,0},{1,3},{3,1},{4,6},{6,4},{5,7},{7,5},{8,10},{10,8},{9,1... | collective-permute-start | bytes 786440 | tf_op jit(solution)/shard_map/ppermute | solution.py:19
  23.6 17.2 %copy-start.3 = (bf16[2560,512]{1,0:T(8,128)(2,1)S(1)}, bf16[2560,512]{1,0:T(8,128)(2,1)}, u32[]{:S(2)}) copy-start(bf16[2560,512]{1,0:T(8,128)(2,1)} %refs_1_.7) | copy-start | bytes 7864324
  23.6 17.2 %copy-start.8 = (bf16[2560,64]{0,1:T(8,128)(2,1)S(1)}, bf16[2560,64]{0,1:T(8,128)(2,1)}, u32[]{:S(2)}) copy-start(bf16[2560,64]{0,1:T(8,128)(2,1)} %param.10) | copy-start | bytes 983044
  23.6 17.0 %collective-permute-start.4 = (bf16[256,512]{1,0:T(8,128)(2,1)S(1)}, bf16[256,512]{1,0:T(8,128)(2,1)S(1)}, u32[]{:S(2)}, u32[]{:S(2)}) collective-permute-start(bf16[256,512]{1,0:T(8,128)(2,1)S(1)} %get-tuple-element.20), channel_id=1, source_target_pairs={{0,2},{2,0},{1,3},{3,1},{4,6},{6,4},{5,7},{7,5},{8,10},{10,8},{9,1... | collective-permute-start | bytes 786440 | tf_op jit(solution)/shard_map/ppermute | solution.py:19
  23.7 6.3 %collective-permute-start.12 = (bf16[64,512]{1,0:T(8,128)(2,1)S(1)}, bf16[64,512]{1,0:T(8,128)(2,1)S(1)}, u32[]{:S(2)}, u32[]{:S(2)}) collective-permute-start(bf16[64,512]{1,0:T(8,128)(2,1)S(1)} %shard_map.98.refs_4_.refs_0_), channel_id=1, source_target_pairs={{0,8},{4,12},{8,0},{12,4},{1,9},{5,13},{9,1},{13,5},{2,10},{6,14},... | collective-permute-start | bytes 196616 | tf_op jit(solution)/shard_map/ppermute | solution.py:19
  27.9 4.3 %collective-permute-start.13 = (bf16[64,512]{1,0:T(8,128)(2,1)S(1)}, bf16[64,512]{1,0:T(8,128)(2,1)S(1)}, u32[]{:S(2)}, u32[]{:S(2)}) collective-permute-start(bf16[64,512]{1,0:T(8,128)(2,1)S(1)} %shard_map.98.refs_4_.refs_0_), channel_id=1, source_target_pairs={{0,12},{4,0},{8,4},{12,8},{1,13},{5,1},{9,5},{13,9},{2,14},{6,2},{... | collective-permute-start | bytes 196616 | tf_op jit(solution)/shard_map/ppermute | solution.py:19
  30.0 4.4 %collective-permute-start.8 = (bf16[16,2560]{1,0:T(8,128)(2,1)S(1)}, bf16[16,2560]{1,0:T(8,128)(2,1)S(1)}, u32[]{:S(2)}, u32[]{:S(2)}) collective-permute-start(bf16[16,2560]{1,0:T(8,128)(2,1)S(1)} %get-tuple-element.24), channel_id=1, source_target_pairs={{0,4},{1,5},{4,0},{5,1},{8,12},{9,13},{12,8},{13,9},{2,6},{3,7},{6... | collective-permute-start | bytes 245768 | tf_op jit(solution)/shard_map/ppermute | solution.py:26
  32.1 2.3 %collective-permute-start.9 = (bf16[16,2560]{1,0:T(8,128)(2,1)S(1)}, bf16[16,2560]{1,0:T(8,128)(2,1)S(1)}, u32[]{:S(2)}, u32[]{:S(2)}) collective-permute-start(bf16[16,2560]{1,0:T(8,128)(2,1)S(1)} %get-tuple-element.25), channel_id=1, source_target_pairs={{0,1},{1,0},{4,5},{5,4},{8,9},{9,8},{12,13},{13,12},{2,3},{3,2},{6... | collective-permute-start | bytes 245768 | tf_op jit(solution)/shard_map/ppermute | solution.py:26
  34.4 15.7 %collective-permute-start.18 = (bf16[4,64,512]{2,1,0:T(8,128)(2,1)S(1)}, bf16[4,64,512]{2,1,0:T(8,128)(2,1)S(1)}, u32[]{:S(2)}, u32[]{:S(2)}) collective-permute-start(bf16[4,64,512]{2,1,0:T(8,128)(2,1)S(1)} %shard_map.100.refs_4_.refs_1_), channel_id=1, source_target_pairs={{0,1},{1,0},{2,3},{3,2},{4,5},{5,4},{6,7},{7,6},{8,9},{9,8},{10,11... | collective-permute-start | bytes 786440 | tf_op jit(solution)/shard_map/ppermute | solution.py:19
  34.4 4.1 %collective-permute-start.10 = (bf16[16,2560]{1,0:T(8,128)(2,1)S(1)}, bf16[16,2560]{1,0:T(8,128)(2,1)S(1)}, u32[]{:S(2)}, u32[]{:S(2)}) collective-permute-start(bf16[16,2560]{1,0:T(8,128)(2,1)S(1)} %get-tuple-element.26), channel_id=1, source_target_pairs={{0,5},{1,4},{4,1},{5,0},{8,13},{9,12},{12,9},{13,8},{2,7},{3,6},{6... | collective-permute-start | bytes 245768 | tf_op jit(solution)/shard_map/ppermute | solution.py:26
  38.6 7.5 %collective-permute-start.14 = (bf16[16,2560]{1,0:T(8,128)(2,1)S(1)}, bf16[16,2560]{1,0:T(8,128)(2,1)S(1)}, u32[]{:S(2)}, u32[]{:S(2)}) collective-permute-start(bf16[16,2560]{1,0:T(8,128)(2,1)S(1)} %shard_map.101.refs_5_.refs_0_), channel_id=1, source_target_pairs={{0,8},{1,9},{4,12},{5,13},{8,0},{9,1},{12,4},{13,5},{2,10},{3,11},... | collective-permute-start | bytes 245768 | tf_op jit(solution)/shard_map/ppermute | solution.py:26
  47.9 7.6 %collective-permute-start.15 = (bf16[16,2560]{1,0:T(8,128)(2,1)S(1)}, bf16[16,2560]{1,0:T(8,128)(2,1)S(1)}, u32[]{:S(2)}, u32[]{:S(2)}) collective-permute-start(bf16[16,2560]{1,0:T(8,128)(2,1)S(1)} %shard_map.103.refs_6_.refs_3_.refs_0_), channel_id=1, source_target_pairs={{0,4},{1,5},{4,0},{5,1},{8,12},{9,13},{12,8},{13,9},{2,6},{3,7},{6... | collective-permute-start | bytes 245768 | tf_op jit(solution)/shard_map/ppermute | solution.py:26
  48.0 7.5 %collective-permute-start.16 = (bf16[16,2560]{1,0:T(8,128)(2,1)S(1)}, bf16[16,2560]{1,0:T(8,128)(2,1)S(1)}, u32[]{:S(2)}, u32[]{:S(2)}) collective-permute-start(bf16[16,2560]{1,0:T(8,128)(2,1)S(1)} %shard_map.103.refs_6_.refs_3_.refs_0_), channel_id=1, source_target_pairs={{0,1},{1,0},{4,5},{5,4},{8,9},{9,8},{12,13},{13,12},{2,3},{3,2},{6... | collective-permute-start | bytes 245768 | tf_op jit(solution)/shard_map/ppermute | solution.py:26
  48.0 7.4 %collective-permute-start.17 = (bf16[16,2560]{1,0:T(8,128)(2,1)S(1)}, bf16[16,2560]{1,0:T(8,128)(2,1)S(1)}, u32[]{:S(2)}, u32[]{:S(2)}) collective-permute-start(bf16[16,2560]{1,0:T(8,128)(2,1)S(1)} %shard_map.103.refs_6_.refs_3_.refs_0_), channel_id=1, source_target_pairs={{0,5},{1,4},{4,1},{5,0},{8,13},{9,12},{12,9},{13,8},{2,7},{3,6},{6... | collective-permute-start | bytes 245768 | tf_op jit(solution)/shard_map/ppermute | solution.py:26
  52.9 2.6 %copy-start.6 = (f32[16,64,512]{2,1,0:T(8,128)S(1)}, f32[16,64,512]{2,1,0:T(8,128)}, u32[]{:S(2)}) copy-start(f32[16,64,512]{2,1,0:T(8,128)} %shard_map.105.refs_4_) | copy-start | bytes 6291460
  (7 other events, 9.6 us)

commit v3 on v2

v3 whole, which is shorter than its diff:
```python
import jax
import jax.numpy as jnp
from jax import lax
from jax.experimental import pallas as pl
from jax.experimental.pallas import tpu as pltpu
from jax.sharding import PartitionSpec as P

adapter_scale = 2.0
f32 = jnp.float32
bf16 = jnp.bfloat16

anywhere = pl.BlockSpec(memory_space=pl.ANY)
in_hbm = pl.BlockSpec(memory_space=pltpu.HBM)
in_vmem = pl.BlockSpec(memory_space=pltpu.VMEM)
in_smem = pl.BlockSpec(memory_space=pltpu.SMEM)


def shift(x, axis, step):
    count = lax.axis_size(axis)
    return lax.ppermute(x, axis, [(i, (i + step) % count) for i in range(count)])


def swap(x, own_bit, sub_bit):
    subs = lax.axis_size("sub")
    whole = lax.axis_size("own") * subs
    other = own_bit * subs + sub_bit
    return lax.ppermute(x, ("own", "sub"), [(i, i ^ other) for i in range(whole)])


def width_of(features):
    return next(width for width in (512, 256, 128) if features % width == 0)


def stay(x):
    return pltpu.with_memory_space_constraint(x, pltpu.HBM)


def shape_of(dims, kind):
    return jax.ShapeDtypeStruct(dims, kind)


def call(body, operands, specs, outs, out_specs=None, after=(), flops=0, **more):
    count, idle = len(operands), len(after)

    def kernel(*refs):
        body(*refs[:count], *refs[count + idle :])

    moved = sum(x.size * x.dtype.itemsize for x in list(operands) + list(outs))
    return pl.pallas_call(
        kernel,
        out_shape=outs,
        in_specs=list(specs) + [anywhere] * len(after),
        out_specs=[in_vmem] * len(outs) if out_specs is None else out_specs,
        compiler_params=pltpu.CompilerParams(vmem_limit_bytes=24 * 1024 * 1024),
        cost_estimate=pl.CostEstimate(flops=flops, bytes_accessed=moved, transcendentals=0),
        **more,
    )(*operands, *after)


def pick_heads(adapter_ids, head_up):
    per_owner, rank, width = head_up.shape
    own_count, sub_count = lax.axis_size("own"), lax.axis_size("sub")

    def body(ids_far, head_up, *refs):
        outs, ids, sems = refs[:own_count], refs[own_count], refs[own_count + 1]
        own, sub = lax.axis_index("own"), lax.axis_index("sub")
        fetch = pltpu.make_async_copy(ids_far, ids, sems.at[own_count])
        fetch.start()
        fetch.wait()
        copies = []
        for step in range(own_count):
            target = (own ^ step) * sub_count + sub
            local = jnp.clip(ids[target] - own * per_owner, 0, per_owner - 1)
            copies.append(pltpu.make_async_copy(head_up.at[local], outs[step], sems.at[step]))
        for copy in copies:
            copy.start()
        for copy in copies:
            copy.wait()

    return call(
        body,
        [stay(adapter_ids), stay(head_up)],
        [in_hbm] * 2,
        [shape_of((rank, width), bf16)] * own_count,
        scratch_shapes=[
            pltpu.SMEM(adapter_ids.shape, jnp.int32),
            pltpu.SemaphoreType.DMA((own_count + 1,)),
        ],
    )


def project_low(tokens, down, after):
    rows, features = tokens.shape
    rank = down.shape[0]
    width = width_of(features)
    blocks = features // width

    def body(tokens, down, low, near_tokens, near_down, sems):
        copies = [pltpu.make_async_copy(down, near_down, sems.at[blocks])]
        for at in range(blocks):
            here = pl.ds(at * width, width)
            copies.append(
                pltpu.make_async_copy(tokens.at[:, here], near_tokens.at[:, here], sems.at[at])
            )
        for copy in copies:
            copy.start()
        copies[0].wait()
        total = None
        for at in range(blocks):
            copies[at + 1].wait()
            here = slice(at * width, (at + 1) * width)
            part = lax.dot_general(
                near_down[:, here], near_tokens[:, here], (((1,), (1,)), ((), ())),
                preferred_element_type=f32,
            )
            total = part if total is None else total + part
        low[...] = total

    return call(
        body,
        [stay(tokens), stay(down)],
        [in_hbm] * 2,
        [shape_of((rank, rows), f32), shape_of(tokens.shape, bf16), shape_of(down.shape, bf16)],
        after=after,
        flops=2 * rows * rank * features,
        scratch_shapes=[pltpu.SemaphoreType.DMA((blocks + 1,))],
    )


def project_back(adapter_ids, offered, grad, per_owner, after):
    rank, columns = offered[0].shape
    rows = grad.shape[0]
    own_count, sub_count = lax.axis_size("own"), lax.axis_size("sub")

    def body(ids, *refs):
        offered, grad, part, head = refs[:own_count], *refs[own_count:]
        own, sub = lax.axis_index("own"), lax.axis_index("sub")
        away = lax.div(ids[own * sub_count + sub], per_owner) ^ own
        for step in range(own_count):

            @pl.when(away == step)
            def _():
                head[...] = offered[step][...]

        part[...] = lax.dot_general(
            head[...], grad[...], (((1,), (1,)), ((), ())), preferred_element_type=f32
        )

    return call(
        body,
        [adapter_ids, *offered, grad],
        [in_smem] + [in_vmem] * (own_count + 1),
        [shape_of((rank, rows), f32)],
        after=after,
        scratch_shapes=[pltpu.VMEM((rank, columns), bf16)],
        flops=2 * rows * rank * columns,
    )[0]


def head_term(lengths, lows, grad, scale, after):
    rank, rows = lows[0].shape
    columns = grad.shape[1]

    def body(lengths, *refs):
        *lows, grad, term = refs
        total = lows[0][...]
        for low in lows[1:]:
            total = total + low[...]
        live = lax.broadcasted_iota(jnp.int32, total.shape, 1) < lengths[0]
        kept = jnp.where(live, total, 0.0).astype(bf16)
        term[0] = (scale * jnp.dot(kept, grad[...], preferred_element_type=f32)).astype(bf16)

    return call(
        body,
        [lengths, *lows, grad],
        [in_smem] + [in_vmem] * (len(lows) + 1),
        [shape_of((1, rank, columns), bf16)],
        after=after,
        flops=2 * rows * rank * columns,
    )[0]


def share_of(own, sub):
    return sub * 2 + lax.rem(own, 2)


def shared_terms(lengths, parts, tokens, grad, scale, after):
    rows, features = tokens.shape
    rank = parts[0].shape[0]
    share = rank // 4

    def body(lengths, *refs):
        parts, (tokens, grad, back, mine, *sends, again, total) = refs[:count], refs[count:]
        own, sub = lax.axis_index("own"), lax.axis_index("sub")
        both = parts[0][...]
        for part in parts[1:]:
            both = both + part[...]
        live = lax.broadcasted_iota(jnp.int32, both.shape, 1) < lengths[0]
        back[...] = jnp.where(live, both, 0.0).astype(bf16)
        total[...] = scale * jnp.dot(back[...], tokens[...], preferred_element_type=f32)
        at = share_of(own, sub)

        def piece(flip):
            return total[pl.ds(pl.multiple_of((at ^ flip) * share, share), share), :]

        mine[...] = piece(0)
        for flip, send in zip((1, 2, 3), sends):
            send[...] = piece(flip).astype(bf16)
        again[...] = grad[...]

    count = len(parts)
    return call(
        body,
        [lengths, *parts, tokens, grad],
        [in_smem] + [in_vmem] * (count + 2),
        [shape_of((rank, rows), bf16), shape_of((share, features), f32)]
        + [shape_of((share, features), bf16)] * 3
        + [shape_of(grad.shape, bf16)],
        after=after,
        scratch_shapes=[pltpu.VMEM((rank, features), f32)],
        flops=2 * rows * rank * features,
    )


def add_up(pieces, after=()):
    def body(*refs):
        total = refs[0][...].astype(f32)
        for piece in refs[1:-1]:
            total = total + piece[...].astype(f32)
        refs[-1][...] = total.astype(bf16)

    return call(
        body,
        list(pieces),
        [in_vmem] * len(pieces),
        [shape_of(pieces[0].shape, bf16)],
        after=after,
    )[0]


def halve(pieces, bit):
    rows, features = pieces[0].shape
    half = rows // 2

    def body(*refs):
        total = refs[0][...].astype(f32)
        for piece in refs[1:-2]:
            total = total + piece[...].astype(f32)
        upper = lax.rem(lax.div(lax.axis_index("own"), bit), 2) == 1
        low, high = total[:half], total[half:]
        refs[-2][...] = jnp.where(upper, high, low)
        refs[-1][...] = jnp.where(upper, low, high).astype(bf16)

    return call(
        body,
        list(pieces),
        [in_vmem] * len(pieces),
        [shape_of((half, features), f32), shape_of((half, features), bf16)],
    )


def rejoin(mine, arrived, bit):
    rows, features = mine.shape

    def body(mine, arrived, out):
        upper = lax.rem(lax.div(lax.axis_index("own"), bit), 2) == 1
        one, two = mine[...].astype(f32), arrived[...].astype(f32)
        out[:rows] = jnp.where(upper, two, one).astype(bf16)
        out[rows:] = jnp.where(upper, one, two).astype(bf16)

    return call(
        body, [mine, arrived], [in_vmem] * 2, [shape_of((2 * rows, features), bf16)]
    )[0]


def join_shares(quarters, after):
    share, features = quarters[0].shape

    def body(*refs):
        out = refs[-1]
        at = share_of(lax.axis_index("own"), lax.axis_index("sub"))
        for flip in range(4):
            place = pl.multiple_of((at ^ flip) * share, share)
            out[pl.ds(place, share), :] = refs[flip][...].astype(f32)

    return call(
        body,
        quarters,
        [in_vmem] * 4,
        [shape_of((4 * share, features), f32)],
        after=after,
    )[0]


def stack(pieces, after=()):
    depths = [piece.shape[0] for piece in pieces]

    def body(*refs):
        at = 0
        for depth, piece in zip(depths, refs[:-1]):
            refs[-1][at : at + depth] = piece[...]
            at += depth

    return call(
        body,
        list(pieces),
        [in_vmem] * len(pieces),
        [shape_of((sum(depths),) + pieces[0].shape[1:], bf16)],
        after=after,
    )[0]


def place_terms(adapter_ids, near, far, pattern, per_owner, after):
    _, rank, columns = near.shape
    sub_count = lax.axis_size("sub")

    def body(ids, near, far, out, mark, held, sem):
        own, sub = lax.axis_index("own"), lax.axis_index("sub")
        held[...] = jnp.zeros(held.shape, f32)
        mark[...] = jnp.zeros(mark.shape, f32)
        for at, step in enumerate(pattern):
            for side in range(sub_count):
                local = ids[(own ^ step) * sub_count + side] - own * per_owner

                @pl.when(jnp.logical_and(local >= 0, local < per_owner))
                def _():
                    term = jnp.where(sub == side, near[at], far[at])
                    held[pl.ds(local, 1)] += term.astype(f32)[None]

        copy = pltpu.make_async_copy(held, out, sem)
        copy.start()
        copy.wait()

    return call(
        body,
        [adapter_ids, near, far],
        [in_smem, in_vmem, in_vmem],
        [shape_of((per_owner, rank, columns), f32), shape_of((8, 128), f32)],
        out_specs=[in_hbm, in_vmem],
        after=after,
        scratch_shapes=[
            pltpu.VMEM((per_owner, rank, columns), f32),
            pltpu.SemaphoreType.DMA,
        ],
    )


def arrange(lengths, grads):
    rows, columns = grads[0].shape
    count = len(grads)

    def body(lengths, *refs):
        grads, kept = refs[:-1], refs[-1]
        at = lax.axis_index("tp")
        live = lax.broadcasted_iota(jnp.int32, (rows, columns), 0) < lengths[0]
        for step in range(count):
            place = pl.multiple_of(lax.rem(at + count - step, count) * columns, 128)
            kept[:, pl.ds(place, columns)] = jnp.where(
                live, grads[step][...], jnp.zeros((rows, columns), bf16)
            )

    return call(
        body,
        [lengths, *grads],
        [in_smem] + [in_vmem] * count,
        [shape_of((rows, count * columns), bf16)],
    )[0]


def input_side(kept, frozen, frozen_other, back, down, after):
    rows, whole = kept.shape
    features, half = frozen.shape
    rank = back.shape[0]
    width = width_of(features)
    blocks = features // width

    def body(kept, frozen, frozen_other, back, down, out, mark, held, sems):
        mark[...] = jnp.zeros(mark.shape, f32)
        sub = lax.axis_index("sub")
        both = (((1,), (1,)), ((), ()))
        mine = kept[:, pl.ds(pl.multiple_of(sub * half, 128), half)]
        other = kept[:, pl.ds(pl.multiple_of((1 - sub) * half, 128), half)]
        twice = adapter_scale * back[...]
        copies = []
        for at in range(blocks):
            here = slice(at * width, (at + 1) * width)
            total = lax.dot_general(mine, frozen[here, :], both, preferred_element_type=f32)
            total += lax.dot_general(other, frozen_other[here, :], both, preferred_element_type=f32)
            total += lax.dot_general(
                twice, down[:, here], (((0,), (0,)), ((), ())), preferred_element_type=f32
            )
            held[:, here] = total.astype(bf16)
            copies.append(
                pltpu.make_async_copy(held.at[:, here], out.at[:, here], sems.at[at])
            )
            copies[-1].start()
        for copy in copies:
            copy.wait()

    return call(
        body,
        [kept, frozen, frozen_other, back, down],
        [in_vmem] * 5,
        [shape_of((rows, features), bf16), shape_of((8, 128), f32)],
        out_specs=[in_hbm, in_vmem],
        after=after,
        scratch_shapes=[
            pltpu.VMEM((rows, features), bf16),
            pltpu.SemaphoreType.DMA((blocks,)),
        ],
        flops=2 * rows * features * (2 * half + rank),
    )


def on_device(tokens, grad_output, frozen_value, shared_down, head_up, adapter_ids, lengths):
    rows = tokens.shape[0]
    own_count = lax.axis_size("own")
    tp_count = lax.axis_size("tp")
    per_owner = head_up.shape[0]
    scale = adapter_scale / rows
    tp_steps, own_steps = range(1, tp_count), range(1, own_count)

    frozen_other = shift(frozen_value, "sub", 1)
    picked = pick_heads(adapter_ids, head_up)
    offered = [picked[0]] + [swap(picked[step], step, 0) for step in own_steps]

    low, tokens, down = project_low(tokens, shared_down.T, offered[1:2] or picked[:1])
    lows = [low] + [shift(low, "tp", step) for step in tp_steps]

    part = project_back(adapter_ids, offered, grad_output, per_owner, [low, frozen_other])
    parts = [part] + [shift(part, "tp", step) for step in tp_steps]

    near = head_term(lengths, lows, grad_output, scale, [part])
    far_bits = [1 << i for i in reversed(range(1, own_count.bit_length() - 1))]
    pattern = [0]
    for bit in far_bits[:1]:
        near_arrived = swap(near, bit, 0)

    back, mine, *sends, again = shared_terms(lengths, parts, tokens, grad_output, scale, [near])
    grads = [grad_output] + [shift(again, "tp", step) for step in tp_steps]
    flips = ((1, 0), (0, 1), (1, 1))
    pieces = [mine] + [swap(send, *flip) for send, flip in zip(sends, flips)]

    bits = far_bits[::-1]
    for bit in bits[:-1]:
        stays, leaves = halve(pieces, bit)
        pieces = [stays, swap(leaves, bit, 0)]
    total = add_up(pieces)

    for bit in far_bits + [1] * (own_count > 1):
        arrived = near_arrived if bit == far_bits[0] else swap(near, bit, 0)
        near = stack([near, arrived], [total])
        pattern = pattern + [step ^ bit for step in pattern]
    far = shift(near, "sub", 1)

    if bits:
        total = add_up([total, swap(total, bits[-1], 0)])
    for bit in reversed(bits[:-1]):
        total = rejoin(total, swap(total, bit, 0), bit)
    quarters = [total] + [swap(total, *flip) for flip in flips]
    kept = arrange(lengths, grads)
    input_gradient, mark = input_side(kept, frozen_value, frozen_other, back, down, [total])
    grad_heads, mark = place_terms(adapter_ids, near, far, pattern, per_owner, [mark])
    shared_down_gradient = join_shares(quarters, [mark]).T
    return (input_gradient, shared_down_gradient, grad_heads)


def solution(mesh):
    placed = (
        P(("rep", "own", "sub"), "tp"),
        P(("rep", "own", "sub"), "tp"),
        P("tp", "sub"),
        P("tp", None),
        P("own", None, "tp"),
        P("rep"),
        P(("rep", "own", "sub")),
    )
    return jax.shard_map(
        on_device,
        mesh=mesh,
        in_specs=placed,
        out_specs=(
            P(("rep", "own", "sub"), "tp"),
            P(("rep", "tp"), None),
            P(("rep", "own"), None, "tp"),
        ),
        check_vma=False,
    )
```

time: 56.7 us -> 48.7 us (0.86)
  local copies, waits for them, and re-layouts: 7.39 us -> 0.01 us
  waiting for transfers between devices: 16.3 us -> 12.6 us
  starting transfers between devices: 17.8 us -> 21 us
    ppermute x7 -> x12, starting transfers between devices: 5.53 us -> 15.6 us  [swap(): lax.ppermute(x, ('own', 'sub'), [(i, i ^ other) for i in range(whole)])]
    unnamed x24 -> x6, local copies, waits for them, and re-layouts: 7.39 us -> 0.01 us
    ppermute x12 -> x5, starting transfers between devices: 12.3 us -> 5.48 us  [shift(): lax.ppermute(x, axis, [(i, (i + step) % count) for i in range(count)])]
    ppermute x12 -> x5, waiting for transfers between devices: 8.78 us -> 2.6 us  [shift(): lax.ppermute(x, axis, [(i, (i + step) % count) for i in range(count)])]
    ppermute x7 -> x12, waiting for transfers between devices: 7.5 us -> 10 us  [swap(): lax.ppermute(x, ('own', 'sub'), [(i, i ^ other) for i in range(whole)])]
  transfers between devices with their start and end apart: 19 -> 17, of which waited for: 7 -> 7; matrix products, arithmetic and copies ran while one was open for 0% -> 0% of each run, Pallas kernels for 22% -> 24%
where the time goes in v3:
time: 48.7 us; the launch traced here: 48.4 us
  starting transfers between devices  21 us (43%)
  Pallas kernels  13.3 us (27%)
  waiting for transfers between devices  12.6 us (26%)
  between operations  1.45 us (3%)
    ppermute x12, starting transfers between devices, swap(): lax.ppermute(x, ('own', 'sub'), [(i, i ^ other) for i in range(whole)])  15.6 us
    pallas_call x13, Pallas kernels, call(): pl.pallas_call(kernel, out_shape=outs, in_specs=list(specs) + [anywhere]...  13.3 us
    ppermute x12, waiting for transfers between devices, swap(): lax.ppermute(x, ('own', 'sub'), [(i, i ^ other) for i in range(whole)])  10 us
    ppermute x5, starting transfers between devices, shift(): lax.ppermute(x, axis, [(i, (i + step) % count) for i in range(count)])  5.48 us
    ppermute x5, waiting for transfers between devices, shift(): lax.ppermute(x, axis, [(i, (i + step) % count) for i in range(count)])  2.6 us
  transfers between devices with their start and end apart: 17, of which 7 were waited for; matrix products, arithmetic and copies ran while one was open for 0% of the time, Pallas kernels for 24%

profile of v3, /device:TPU:0, one launch (start us, length us, event | category | flops | bytes accessed | tf_op | source)
XLA Modules:
  0.0 48.4 jit_solution(3357557458070842127)
XLA Ops:
  1.2 1.7 %shard_map.94 = (bf16[64,512]{1,0:T(8,128)(2,1)S(1)}, bf16[64,512]{1,0:T(8,128)(2,1)S(1)}, bf16[64,512]{1,0:T(8,128)(2,1)S(1)}, bf16[64,512]{1,0:T(8,128)(2,1)S(1)}) custom-call(s32[8]{0:T(128)} %refs_0_.10, bf16[16,64,512]{2,1,0:T(8,128)(2,1)} %refs_1_.3), custom_call_target="tpu_custom_call" | custom-call | bytes 1310752 | tf_op jit(solution)/shard_map/pallas_call | solution.py:49
  2.8 2.8 %collective-permute-start = (bf16[64,512]{1,0:T(8,128)(2,1)S(1)}, bf16[64,512]{1,0:T(8,128)(2,1)S(1)}, u32[]{:S(2)}, u32[]{:S(2)}) collective-permute-start(bf16[64,512]{1,0:T(8,128)(2,1)S(1)} %get-tuple-element.21), channel_id=1, source_target_pairs={{0,4},{1,5},{4,0},{5,1},{8,12},{9,13},{12,8},{13,9},{2,6},{3,7},{6... | collective-permute-start | bytes 196616 | tf_op jit(solution)/shard_map/ppermute | solution.py:27
  5.6 2.6 %collective-permute-start.1 = (bf16[64,512]{1,0:T(8,128)(2,1)S(1)}, bf16[64,512]{1,0:T(8,128)(2,1)S(1)}, u32[]{:S(2)}, u32[]{:S(2)}) collective-permute-start(bf16[64,512]{1,0:T(8,128)(2,1)S(1)} %get-tuple-element.22), channel_id=1, source_target_pairs={{0,8},{1,9},{4,12},{5,13},{8,0},{9,1},{12,4},{13,5},{2,10},{3,11},... | collective-permute-start | bytes 196616 | tf_op jit(solution)/shard_map/ppermute | solution.py:27
  8.3 2.3 %shard_map.95 = (f32[64,512]{1,0:T(8,128)S(1)}, bf16[512,2560]{1,0:T(8,128)(2,1)S(1)}, bf16[64,2560]{1,0:T(8,128)(2,1)S(1)}) custom-call(bf16[512,2560]{1,0:T(8,128)(2,1)} %refs_0_.8, bf16[64,2560]{1,0:T(8,128)(2,1)} %bitcast.3, bf16[64,512]{1,0:T(8,128)(2,1)S(1)} %collective-permute-done.refs_2_), custom_call_target="tpu_custom_call" | custom-call | flops 167772160 | bytes 6029312 | tf_op jit(solution)/shard_map/pallas_call | solution.py:49
  10.6 1.8 %collective-permute-start.5 = (f32[64,512]{1,0:T(8,128)S(1)}, f32[64,512]{1,0:T(8,128)S(1)}, u32[]{:S(2)}, u32[]{:S(2)}) collective-permute-start(f32[64,512]{1,0:T(8,128)S(1)} %get-tuple-element.24.refs_6_.refs_1_), channel_id=1, source_target_pairs={{0,2},{2,0},{1,3},{3,1},{4,6},{6,4},{5,7},{7,5},{8,10},{10,8},{9,1... | collective-permute-start | bytes 393224 | tf_op jit(solution)/shard_map/ppermute | solution.py:20
  12.4 0.9 %collective-permute-done.1.refs_3_ = bf16[64,512]{1,0:T(8,128)(2,1)S(1)} collective-permute-done((bf16[64,512]{1,0:T(8,128)(2,1)S(1)}, bf16[64,512]{1,0:T(8,128)(2,1)S(1)}, u32[]{:S(2)}, u32[]{:S(2)}) %collective-permute-start.1) | collective-permute-done | bytes 65568 | tf_op jit(solution)/shard_map/ppermute | solution.py:27
  13.3 1.1 %collective-permute-done.2.refs_4_ = bf16[64,512]{1,0:T(8,128)(2,1)S(1)} collective-permute-done((bf16[64,512]{1,0:T(8,128)(2,1)S(1)}, bf16[64,512]{1,0:T(8,128)(2,1)S(1)}, u32[]{:S(2)}, u32[]{:S(2)}) %collective-permute-start.2) | collective-permute-done | bytes 65568 | tf_op jit(solution)/shard_map/ppermute | solution.py:27
  14.4 0.9 %shard_map.96.refs_4_.refs_1_ = f32[64,512]{1,0:T(8,128)S(1)} custom-call(s32[8]{0:T(128)S(1)} %copy-done.1, bf16[64,512]{1,0:T(8,128)(2,1)S(1)} %get-tuple-element.20.refs_1_, bf16[64,512]{1,0:T(8,128)(2,1)S(1)} %collective-permute-done.refs_2_, bf16[64,512]{1,0:T(8,128)(2,1)S(1)} %collective-permute-done.1.refs_3_, ...), custom_call_target="tpu_custom_call" | custom-call | flops 33554432 | bytes 917536 | tf_op jit(solution)/shard_map/pallas_call | solution.py:49
  15.2 1.6 %collective-permute-start.4 = (f32[64,512]{1,0:T(8,128)S(1)}, f32[64,512]{1,0:T(8,128)S(1)}, u32[]{:S(2)}, u32[]{:S(2)}) collective-permute-start(f32[64,512]{1,0:T(8,128)S(1)} %shard_map.96.refs_4_.refs_1_), channel_id=1, source_target_pairs={{0,2},{2,0},{1,3},{3,1},{4,6},{6,4},{5,7},{7,5},{8,10},{10,8},{9,1... | collective-permute-start | bytes 393224 | tf_op jit(solution)/shard_map/ppermute | solution.py:20
  17.7 2.6 %collective-permute-done.4.refs_2_ = f32[64,512]{1,0:T(8,128)S(1)} collective-permute-done((f32[64,512]{1,0:T(8,128)S(1)}, f32[64,512]{1,0:T(8,128)S(1)}, u32[]{:S(2)}, u32[]{:S(2)}) %collective-permute-start.4) | collective-permute-done | bytes 131104 | tf_op jit(solution)/shard_map/ppermute | solution.py:20
  20.9 1.6 %collective-permute-start.6 = (bf16[512,512]{1,0:T(8,128)(2,1)S(1)}, bf16[512,512]{1,0:T(8,128)(2,1)S(1)}, u32[]{:S(2)}, u32[]{:S(2)}) collective-permute-start(bf16[512,512]{1,0:T(8,128)(2,1)S(1)} %get-tuple-element.26), channel_id=1, source_target_pairs={{0,2},{2,0},{1,3},{3,1},{4,6},{6,4},{5,7},{7,5},{8,10},{10,8},{9,1... | collective-permute-start | bytes 1572872 | tf_op jit(solution)/shard_map/ppermute | solution.py:20
  22.4 1.1 %collective-permute-start.7 = (bf16[16,2560]{1,0:T(8,128)(2,1)S(1)}, bf16[16,2560]{1,0:T(8,128)(2,1)S(1)}, u32[]{:S(2)}, u32[]{:S(2)}) collective-permute-start(bf16[16,2560]{1,0:T(8,128)(2,1)S(1)} %get-tuple-element.30), channel_id=1, source_target_pairs={{0,4},{1,5},{4,0},{5,1},{8,12},{9,13},{12,8},{13,9},{2,6},{3,7},{6... | collective-permute-start | bytes 245768 | tf_op jit(solution)/shard_map/ppermute | solution.py:27
  23.6 1.0 %collective-permute-start.9 = (bf16[16,2560]{1,0:T(8,128)(2,1)S(1)}, bf16[16,2560]{1,0:T(8,128)(2,1)S(1)}, u32[]{:S(2)}, u32[]{:S(2)}) collective-permute-start(bf16[16,2560]{1,0:T(8,128)(2,1)S(1)} %get-tuple-element.32), channel_id=1, source_target_pairs={{0,5},{1,4},{4,1},{5,0},{8,13},{9,12},{12,9},{13,8},{2,7},{3,6},{6... | collective-permute-start | bytes 245768 | tf_op jit(solution)/shard_map/ppermute | solution.py:27
  24.6 2.0 %collective-permute-start.14 = (bf16[1,64,512]{2,1,0:T(8,128)(2,1)S(1)}, bf16[1,64,512]{2,1,0:T(8,128)(2,1)S(1)}, u32[]{:S(2)}, u32[]{:S(2)}) collective-permute-start(bf16[1,64,512]{2,1,0:T(8,128)(2,1)S(1)} %shard_map.97.refs_5_.refs_0_), channel_id=1, source_target_pairs={{0,8},{1,9},{4,12},{5,13},{8,0},{9,1},{12,4},{13,5},{2,10},{3,11},... | collective-permute-start | bytes 196616 | tf_op jit(solution)/shard_map/ppermute | solution.py:27
  26.6 0.7 %collective-permute-done.7.refs_1_ = bf16[16,2560]{1,0:T(8,128)(2,1)S(1)} collective-permute-done((bf16[16,2560]{1,0:T(8,128)(2,1)S(1)}, bf16[16,2560]{1,0:T(8,128)(2,1)S(1)}, u32[]{:S(2)}, u32[]{:S(2)}) %collective-permute-start.7) | collective-permute-done | bytes 81952 | tf_op jit(solution)/shard_map/ppermute | solution.py:27
  27.3 1.6 %collective-permute-done.9.refs_3_ = bf16[16,2560]{1,0:T(8,128)(2,1)S(1)} collective-permute-done((bf16[16,2560]{1,0:T(8,128)(2,1)S(1)}, bf16[16,2560]{1,0:T(8,128)(2,1)S(1)}, u32[]{:S(2)}, u32[]{:S(2)}) %collective-permute-start.9) | collective-permute-done | bytes 81952 | tf_op jit(solution)/shard_map/ppermute | solution.py:27
  29.0 1.1 %collective-permute-done.14.refs_1_ = bf16[1,64,512]{2,1,0:T(8,128)(2,1)S(1)} collective-permute-done((bf16[1,64,512]{2,1,0:T(8,128)(2,1)S(1)}, bf16[1,64,512]{2,1,0:T(8,128)(2,1)S(1)}, u32[]{:S(2)}, u32[]{:S(2)}) %collective-permute-start.14) | collective-permute-done | bytes 65568 | tf_op jit(solution)/shard_map/ppermute | solution.py:27
  30.1 2.0 %collective-permute-start.15 = (bf16[2,64,512]{2,1,0:T(8,128)(2,1)S(1)}, bf16[2,64,512]{2,1,0:T(8,128)(2,1)S(1)}, u32[]{:S(2)}, u32[]{:S(2)}) collective-permute-start(bf16[2,64,512]{2,1,0:T(8,128)(2,1)S(1)} %shard_map.103.refs_0_), channel_id=1, source_target_pairs={{0,4},{1,5},{4,0},{5,1},{8,12},{9,13},{12,8},{13,9},{2,6},{3,7},{6... | collective-permute-start | bytes 393224 | tf_op jit(solution)/shard_map/ppermute | solution.py:27
  32.1 1.8 %collective-permute-start.10 = (bf16[16,2560]{1,0:T(8,128)(2,1)S(1)}, bf16[16,2560]{1,0:T(8,128)(2,1)S(1)}, u32[]{:S(2)}, u32[]{:S(2)}) collective-permute-start(bf16[16,2560]{1,0:T(8,128)(2,1)S(1)} %shard_map.100.refs_0_.refs_2_), channel_id=1, source_target_pairs={{0,8},{1,9},{4,12},{5,13},{8,0},{9,1},{12,4},{13,5},{2,10},{3,11},... | collective-permute-start | bytes 245768 | tf_op jit(solution)/shard_map/ppermute | solution.py:27
  33.9 4.6 %collective-permute-done.10.refs_1_ = bf16[16,2560]{1,0:T(8,128)(2,1)S(1)} collective-permute-done((bf16[16,2560]{1,0:T(8,128)(2,1)S(1)}, bf16[16,2560]{1,0:T(8,128)(2,1)S(1)}, u32[]{:S(2)}, u32[]{:S(2)}) %collective-permute-start.10) | collective-permute-done | bytes 81952 | tf_op jit(solution)/shard_map/ppermute | solution.py:27
  39.1 1.6 %collective-permute-start.13 = (bf16[16,2560]{1,0:T(8,128)(2,1)S(1)}, bf16[16,2560]{1,0:T(8,128)(2,1)S(1)}, u32[]{:S(2)}, u32[]{:S(2)}) collective-permute-start(bf16[16,2560]{1,0:T(8,128)(2,1)S(1)} %shard_map.101.refs_5_.refs_0_), channel_id=1, source_target_pairs={{0,5},{1,4},{4,1},{5,0},{8,13},{9,12},{12,9},{13,8},{2,7},{3,6},{6... | collective-permute-start | bytes 245768 | tf_op jit(solution)/shard_map/ppermute | solution.py:27
  40.9 4.4 %shard_map.102 = (bf16[512,2560]{1,0:T(8,128)(2,1)}, f32[8,128]{1,0:T(8,128)S(1)}) custom-call(bf16[512,1024]{1,0:T(8,128)(2,1)S(1)} %shard_map.99.refs_0_, bf16[2560,512]{1,0:T(8,128)(2,1)S(1)} %copy-done.2, bf16[2560,512]{1,0:T(8,128)(2,1)S(1)} %collective-permute-done.3.refs_7_.refs_2_, bf16[64,512]{1,0:T(8,128)(2,1)S(1)} %get-tuple-element.27.refs_3_, ...), custom_call_target="tpu_custom_call" | custom-call | flops 2852126720 | bytes 9310208 | tf_op jit(solution)/shard_map/pallas_call | solution.py:49
  45.4 2.1 %shard_map.105 = (f32[16,64,512]{2,1,0:T(8,128)}, f32[8,128]{1,0:T(8,128)S(1)}) custom-call(s32[8]{0:T(128)S(1)} %copy-done.1, bf16[4,64,512]{2,1,0:T(8,128)(2,1)S(1)} %shard_map.104.refs_1_, bf16[4,64,512]{2,1,0:T(8,128)(2,1)S(1)} %collective-permute-done.16.refs_2_, f32[8,128]{1,0:T(8,128)S(1)} %get-tuple-element.34.refs_3_), custom_call_target="tpu_custom_call" | custom-call | bytes 2625568 | tf_op jit(solution)/shard_map/pallas_call | solution.py:49
  47.5 0.9 %shard_map.106 = f32[64,2560]{1,0:T(8,128)} custom-call(bf16[16,2560]{1,0:T(8,128)(2,1)S(1)} %shard_map.101.refs_5_.refs_0_, bf16[16,2560]{1,0:T(8,128)(2,1)S(1)} %collective-permute-done.11.refs_1_, bf16[16,2560]{1,0:T(8,128)(2,1)S(1)} %collective-permute-done.12.refs_2_, bf16[16,2560]{1,0:T(8,128)(2,1)S(1)} %collective-permute-done.13.refs_3_, ...), custom_call_target="tpu_custom_call" | custom-call | bytes 983040 | tf_op jit(solution)/shard_map/pallas_call | solution.py:49
  (29 shorter events, 2.3 us)
Async XLA Ops:
  0.6 13.7 %copy-start.1 = (s32[8]{0:T(128)S(1)}, s32[8]{0:T(128)}, u32[]{:S(2)}) copy-start(s32[8]{0:T(128)} %refs_0_.10) | copy-start | bytes 100
  0.6 13.7 %copy-start = (bf16[512,512]{1,0:T(8,128)(2,1)S(1)}, bf16[512,512]{1,0:T(8,128)(2,1)}, u32[]{:S(2)}) copy-start(bf16[512,512]{1,0:T(8,128)(2,1)} %refs_1_.4) | copy-start | bytes 1572868
  0.7 13.7 %collective-permute-start.3 = (bf16[2560,512]{1,0:T(8,128)(2,1)}, bf16[2560,512]{1,0:T(8,128)(2,1)S(1)}, u32[]{:S(2)}, u32[]{:S(2)}) collective-permute-start(bf16[2560,512]{1,0:T(8,128)(2,1)} %refs_1_.5), channel_id=1, source_target_pairs={{0,1},{1,0},{2,3},{3,2},{4,5},{5,4},{6,7},{7,6},{8,9},{9,8},{10,11... | collective-permute-start | bytes 7864328 | tf_op jit(solution)/shard_map/ppermute | solution.py:20
  2.8 5.4 %collective-permute-start = (bf16[64,512]{1,0:T(8,128)(2,1)S(1)}, bf16[64,512]{1,0:T(8,128)(2,1)S(1)}, u32[]{:S(2)}, u32[]{:S(2)}) collective-permute-start(bf16[64,512]{1,0:T(8,128)(2,1)S(1)} %get-tuple-element.21), channel_id=1, source_target_pairs={{0,4},{1,5},{4,0},{5,1},{8,12},{9,13},{12,8},{13,9},{2,6},{3,7},{6... | collective-permute-start | bytes 196616 | tf_op jit(solution)/shard_map/ppermute | solution.py:27
  5.6 7.7 %collective-permute-start.1 = (bf16[64,512]{1,0:T(8,128)(2,1)S(1)}, bf16[64,512]{1,0:T(8,128)(2,1)S(1)}, u32[]{:S(2)}, u32[]{:S(2)}) collective-permute-start(bf16[64,512]{1,0:T(8,128)(2,1)S(1)} %get-tuple-element.22), channel_id=1, source_target_pairs={{0,8},{1,9},{4,12},{5,13},{8,0},{9,1},{12,4},{13,5},{2,10},{3,11},... | collective-permute-start | bytes 196616 | tf_op jit(solution)/shard_map/ppermute | solution.py:27
  8.3 6.1 %collective-permute-start.2 = (bf16[64,512]{1,0:T(8,128)(2,1)S(1)}, bf16[64,512]{1,0:T(8,128)(2,1)S(1)}, u32[]{:S(2)}, u32[]{:S(2)}) collective-permute-start(bf16[64,512]{1,0:T(8,128)(2,1)S(1)} %get-tuple-element.23), channel_id=1, source_target_pairs={{0,12},{1,13},{4,8},{5,9},{8,4},{9,5},{12,0},{13,1},{2,14},{3,15},... | collective-permute-start | bytes 196616 | tf_op jit(solution)/shard_map/ppermute | solution.py:27
  10.6 6.9 %collective-permute-start.5 = (f32[64,512]{1,0:T(8,128)S(1)}, f32[64,512]{1,0:T(8,128)S(1)}, u32[]{:S(2)}, u32[]{:S(2)}) collective-permute-start(f32[64,512]{1,0:T(8,128)S(1)} %get-tuple-element.24.refs_6_.refs_1_), channel_id=1, source_target_pairs={{0,2},{2,0},{1,3},{3,1},{4,6},{6,4},{5,7},{7,5},{8,10},{10,8},{9,1... | collective-permute-start | bytes 393224 | tf_op jit(solution)/shard_map/ppermute | solution.py:20
  15.2 5.0 %collective-permute-start.4 = (f32[64,512]{1,0:T(8,128)S(1)}, f32[64,512]{1,0:T(8,128)S(1)}, u32[]{:S(2)}, u32[]{:S(2)}) collective-permute-start(f32[64,512]{1,0:T(8,128)S(1)} %shard_map.96.refs_4_.refs_1_), channel_id=1, source_target_pairs={{0,2},{2,0},{1,3},{3,1},{4,6},{6,4},{5,7},{7,5},{8,10},{10,8},{9,1... | collective-permute-start | bytes 393224 | tf_op jit(solution)/shard_map/ppermute | solution.py:20
  20.9 20.1 %copy-start.2 = (bf16[2560,512]{1,0:T(8,128)(2,1)S(1)}, bf16[2560,512]{1,0:T(8,128)(2,1)}, u32[]{:S(2)}) copy-start(bf16[2560,512]{1,0:T(8,128)(2,1)} %refs_1_.5) | copy-start | bytes 7864324
  20.9 19.9 %collective-permute-start.6 = (bf16[512,512]{1,0:T(8,128)(2,1)S(1)}, bf16[512,512]{1,0:T(8,128)(2,1)S(1)}, u32[]{:S(2)}, u32[]{:S(2)}) collective-permute-start(bf16[512,512]{1,0:T(8,128)(2,1)S(1)} %get-tuple-element.26), channel_id=1, source_target_pairs={{0,2},{2,0},{1,3},{3,1},{4,6},{6,4},{5,7},{7,5},{8,10},{10,8},{9,1... | collective-permute-start | bytes 1572872 | tf_op jit(solution)/shard_map/ppermute | solution.py:20
  22.4 4.8 %collective-permute-start.7 = (bf16[16,2560]{1,0:T(8,128)(2,1)S(1)}, bf16[16,2560]{1,0:T(8,128)(2,1)S(1)}, u32[]{:S(2)}, u32[]{:S(2)}) collective-permute-start(bf16[16,2560]{1,0:T(8,128)(2,1)S(1)} %get-tuple-element.30), channel_id=1, source_target_pairs={{0,4},{1,5},{4,0},{5,1},{8,12},{9,13},{12,8},{13,9},{2,6},{3,7},{6... | collective-permute-start | bytes 245768 | tf_op jit(solution)/shard_map/ppermute | solution.py:27
  23.6 3.7 %collective-permute-start.8 = (bf16[16,2560]{1,0:T(8,128)(2,1)S(1)}, bf16[16,2560]{1,0:T(8,128)(2,1)S(1)}, u32[]{:S(2)}, u32[]{:S(2)}) collective-permute-start(bf16[16,2560]{1,0:T(8,128)(2,1)S(1)} %get-tuple-element.31), channel_id=1, source_target_pairs={{0,1},{1,0},{4,5},{5,4},{8,9},{9,8},{12,13},{13,12},{2,3},{3,2},{6... | collective-permute-start | bytes 245768 | tf_op jit(solution)/shard_map/ppermute | solution.py:27
  23.6 5.4 %collective-permute-start.9 = (bf16[16,2560]{1,0:T(8,128)(2,1)S(1)}, bf16[16,2560]{1,0:T(8,128)(2,1)S(1)}, u32[]{:S(2)}, u32[]{:S(2)}) collective-permute-start(bf16[16,2560]{1,0:T(8,128)(2,1)S(1)} %get-tuple-element.32), channel_id=1, source_target_pairs={{0,5},{1,4},{4,1},{5,0},{8,13},{9,12},{12,9},{13,8},{2,7},{3,6},{6... | collective-permute-start | bytes 245768 | tf_op jit(solution)/shard_map/ppermute | solution.py:27
  24.6 5.5 %collective-permute-start.14 = (bf16[1,64,512]{2,1,0:T(8,128)(2,1)S(1)}, bf16[1,64,512]{2,1,0:T(8,128)(2,1)S(1)}, u32[]{:S(2)}, u32[]{:S(2)}) collective-permute-start(bf16[1,64,512]{2,1,0:T(8,128)(2,1)S(1)} %shard_map.97.refs_5_.refs_0_), channel_id=1, source_target_pairs={{0,8},{1,9},{4,12},{5,13},{8,0},{9,1},{12,4},{13,5},{2,10},{3,11},... | collective-permute-start | bytes 196616 | tf_op jit(solution)/shard_map/ppermute | solution.py:27
  30.1 10.6 %collective-permute-start.15 = (bf16[2,64,512]{2,1,0:T(8,128)(2,1)S(1)}, bf16[2,64,512]{2,1,0:T(8,128)(2,1)S(1)}, u32[]{:S(2)}, u32[]{:S(2)}) collective-permute-start(bf16[2,64,512]{2,1,0:T(8,128)(2,1)S(1)} %shard_map.103.refs_0_), channel_id=1, source_target_pairs={{0,4},{1,5},{4,0},{5,1},{8,12},{9,13},{12,8},{13,9},{2,6},{3,7},{6... | collective-permute-start | bytes 393224 | tf_op jit(solution)/shard_map/ppermute | solution.py:27
  32.1 6.3 %collective-permute-start.10 = (bf16[16,2560]{1,0:T(8,128)(2,1)S(1)}, bf16[16,2560]{1,0:T(8,128)(2,1)S(1)}, u32[]{:S(2)}, u32[]{:S(2)}) collective-permute-start(bf16[16,2560]{1,0:T(8,128)(2,1)S(1)} %shard_map.100.refs_0_.refs_2_), channel_id=1, source_target_pairs={{0,8},{1,9},{4,12},{5,13},{8,0},{9,1},{12,4},{13,5},{2,10},{3,11},... | collective-permute-start | bytes 245768 | tf_op jit(solution)/shard_map/ppermute | solution.py:27
  38.5 9.0 %collective-permute-start.11 = (bf16[16,2560]{1,0:T(8,128)(2,1)S(1)}, bf16[16,2560]{1,0:T(8,128)(2,1)S(1)}, u32[]{:S(2)}, u32[]{:S(2)}) collective-permute-start(bf16[16,2560]{1,0:T(8,128)(2,1)S(1)} %shard_map.101.refs_5_.refs_0_), channel_id=1, source_target_pairs={{0,4},{1,5},{4,0},{5,1},{8,12},{9,13},{12,8},{13,9},{2,6},{3,7},{6... | collective-permute-start | bytes 245768 | tf_op jit(solution)/shard_map/ppermute | solution.py:27
  39.1 8.4 %collective-permute-start.12 = (bf16[16,2560]{1,0:T(8,128)(2,1)S(1)}, bf16[16,2560]{1,0:T(8,128)(2,1)S(1)}, u32[]{:S(2)}, u32[]{:S(2)}) collective-permute-start(bf16[16,2560]{1,0:T(8,128)(2,1)S(1)} %shard_map.101.refs_5_.refs_0_), channel_id=1, source_target_pairs={{0,1},{1,0},{4,5},{5,4},{8,9},{9,8},{12,13},{13,12},{2,3},{3,2},{6... | collective-permute-start | bytes 245768 | tf_op jit(solution)/shard_map/ppermute | solution.py:27
  39.1 8.4 %collective-permute-start.13 = (bf16[16,2560]{1,0:T(8,128)(2,1)S(1)}, bf16[16,2560]{1,0:T(8,128)(2,1)S(1)}, u32[]{:S(2)}, u32[]{:S(2)}) collective-permute-start(bf16[16,2560]{1,0:T(8,128)(2,1)S(1)} %shard_map.101.refs_5_.refs_0_), channel_id=1, source_target_pairs={{0,5},{1,4},{4,1},{5,0},{8,13},{9,12},{12,9},{13,8},{2,7},{3,6},{6... | collective-permute-start | bytes 245768 | tf_op jit(solution)/shard_map/ppermute | solution.py:27
  40.7 4.7 %collective-permute-start.16 = (bf16[4,64,512]{2,1,0:T(8,128)(2,1)S(1)}, bf16[4,64,512]{2,1,0:T(8,128)(2,1)S(1)}, u32[]{:S(2)}, u32[]{:S(2)}) collective-permute-start(bf16[4,64,512]{2,1,0:T(8,128)(2,1)S(1)} %shard_map.104.refs_1_), channel_id=1, source_target_pairs={{0,1},{1,0},{2,3},{3,2},{4,5},{5,4},{6,7},{7,6},{8,9},{9,8},{10,11... | collective-permute-start | bytes 786440 | tf_op jit(solution)/shard_map/ppermute | solution.py:20

commit v4 on v3

--- a/solution.py
+++ b/solution.py
@@ -57,36 +57,43 @@
     )(*operands, *after)
 
 
-def pick_heads(adapter_ids, head_up):
+def pick_heads(adapter_ids, head_up, grad):
     per_owner, rank, width = head_up.shape
     own_count, sub_count = lax.axis_size("own"), lax.axis_size("sub")
-
-    def body(ids_far, head_up, *refs):
-        outs, ids, sems = refs[:own_count], refs[own_count], refs[own_count + 1]
+    first = grad.shape[0] // 2
+
+    def body(ids_far, head_up, grad, *refs):
+        outs, early, away, ids, maps, sems = refs[:own_count], *refs[own_count:]
         own, sub = lax.axis_index("own"), lax.axis_index("sub")
-        fetch = pltpu.make_async_copy(ids_far, ids, sems.at[own_count])
-        fetch.start()
-        fetch.wait()
-        copies = []
-        for step in range(own_count):
-            target = (own ^ step) * sub_count + sub
-            local = jnp.clip(ids[target] - own * per_owner, 0, per_owner - 1)
-            copies.append(pltpu.make_async_copy(head_up.at[local], outs[step], sems.at[step]))
+        copies = [
+            pltpu.make_async_copy(ids_far, ids, sems.at[0]),
+            pltpu.make_async_copy(head_up, maps, sems.at[1]),
+            pltpu.make_async_copy(grad.at[pl.ds(0, first)], early, sems.at[2]),
+        ]
         for copy in copies:
             copy.start()
-        for copy in copies:
-            copy.wait()
-
-    return call(
-        body,
-        [stay(adapter_ids), stay(head_up)],
-        [in_hbm] * 2,
-        [shape_of((rank, width), bf16)] * own_count,
+        copies[0].wait()
+        copies[1].wait()
+        for step in range(own_count):
+            local = ids[(own ^ step) * sub_count + sub] - own * per_owner
+            outs[step][...] = maps[jnp.clip(local, 0, per_owner - 1)]
+        step = lax.div(ids[own * sub_count + sub], per_owner) ^ own
+        away[...] = jnp.full(away.shape, step, jnp.int32)
+        copies[2].wait()
+
+    *picked, early, away = call(
+        body,
+        [stay(adapter_ids), stay(head_up), stay(grad)],
+        [in_hbm] * 3,
+        [shape_of((rank, width), bf16)] * own_count
+        + [shape_of((first, grad.shape[1]), bf16), shape_of((8, 128), jnp.int32)],
         scratch_shapes=[
             pltpu.SMEM(adapter_ids.shape, jnp.int32),
-            pltpu.SemaphoreType.DMA((own_count + 1,)),
+            pltpu.VMEM(head_up.shape, bf16),
+            pltpu.SemaphoreType.DMA((3,)),
         ],
     )
+    return picked, early, away
 
 
 def project_low(tokens, down, after):
@@ -127,32 +134,26 @@
     )
 
 
-def project_back(adapter_ids, offered, grad, per_owner, after):
+def project_back(away, offered, grad, after):
     rank, columns = offered[0].shape
     rows = grad.shape[0]
-    own_count, sub_count = lax.axis_size("own"), lax.axis_size("sub")
-
-    def body(ids, *refs):
-        offered, grad, part, head = refs[:own_count], *refs[own_count:]
-        own, sub = lax.axis_index("own"), lax.axis_index("sub")
-        away = lax.div(ids[own * sub_count + sub], per_owner) ^ own
-        for step in range(own_count):
-
-            @pl.when(away == step)
-            def _():
-                head[...] = offered[step][...]
-
+
+    def body(away, *refs):
+        *offered, grad, part = refs
+        step = jnp.broadcast_to(away[:1, :1], (rank, columns))
+        head = offered[0][...].astype(f32)
+        for at in range(1, len(offered)):
+            head = jnp.where(step == at, offered[at][...].astype(f32), head)
         part[...] = lax.dot_general(
-            head[...], grad[...], (((1,), (1,)), ((), ())), preferred_element_type=f32
+            head.astype(bf16), grad[...], (((1,), (1,)), ((), ())), preferred_element_type=f32
         )
 
     return call(
         body,
-        [adapter_ids, *offered, grad],
-        [in_smem] + [in_vmem] * (own_count + 1),
+        [away, *offered, grad],
+        [in_vmem] * (len(offered) + 2),
         [shape_of((rank, rows), f32)],
         after=after,
-        scratch_shapes=[pltpu.VMEM((rank, columns), bf16)],
         flops=2 * rows * rank * columns,
     )[0]
 
@@ -160,62 +161,51 @@
 def head_term(lengths, lows, grad, scale, after):
     rank, rows = lows[0].shape
     columns = grad.shape[1]
+    first = rows // 2
 
     def body(lengths, *refs):
-        *lows, grad, term = refs
+        *lows, grad, term, late = refs
         total = lows[0][...]
         for low in lows[1:]:
             total = total + low[...]
         live = lax.broadcasted_iota(jnp.int32, total.shape, 1) < lengths[0]
         kept = jnp.where(live, total, 0.0).astype(bf16)
         term[0] = (scale * jnp.dot(kept, grad[...], preferred_element_type=f32)).astype(bf16)
+        late[...] = grad[first:, :]
 
     return call(
         body,
         [lengths, *lows, grad],
         [in_smem] + [in_vmem] * (len(lows) + 1),
-        [shape_of((1, rank, columns), bf16)],
+        [shape_of((1, rank, columns), bf16), shape_of((rows - first, columns), bf16)],
         after=after,
         flops=2 * rows * rank * columns,
-    )[0]
-
-
-def share_of(own, sub):
-    return sub * 2 + lax.rem(own, 2)
-
-
-def shared_terms(lengths, parts, tokens, grad, scale, after):
+    )
+
+
+def shared_terms(lengths, parts, tokens, scale, after):
     rows, features = tokens.shape
     rank = parts[0].shape[0]
-    share = rank // 4
+    share = rank // 2
 
     def body(lengths, *refs):
-        parts, (tokens, grad, back, mine, *sends, again, total) = refs[:count], refs[count:]
-        own, sub = lax.axis_index("own"), lax.axis_index("sub")
+        parts, (tokens, back, keep, send, total) = refs[:count], refs[count:]
+        sub = lax.axis_index("sub")
         both = parts[0][...]
         for part in parts[1:]:
             both = both + part[...]
         live = lax.broadcasted_iota(jnp.int32, both.shape, 1) < lengths[0]
         back[...] = jnp.where(live, both, 0.0).astype(bf16)
         total[...] = scale * jnp.dot(back[...], tokens[...], preferred_element_type=f32)
-        at = share_of(own, sub)
-
-        def piece(flip):
-            return total[pl.ds(pl.multiple_of((at ^ flip) * share, share), share), :]
-
-        mine[...] = piece(0)
-        for flip, send in zip((1, 2, 3), sends):
-            send[...] = piece(flip).astype(bf16)
-        again[...] = grad[...]
+        keep[...] = total[pl.ds(pl.multiple_of(sub * share, share), share), :]
+        send[...] = total[pl.ds(pl.multiple_of((1 - sub) * share, share), share), :]
 
     count = len(parts)
     return call(
         body,
-        [lengths, *parts, tokens, grad],
-        [in_smem] + [in_vmem] * (count + 2),
-        [shape_of((rank, rows), bf16), shape_of((share, features), f32)]
-        + [shape_of((share, features), bf16)] * 3
-        + [shape_of(grad.shape, bf16)],
+        [lengths, *parts, tokens],
+        [in_smem] + [in_vmem] * (count + 1),
+        [shape_of((rank, rows), bf16)] + [shape_of((share, features), f32)] * 2,
         after=after,
         scratch_shapes=[pltpu.VMEM((rank, features), f32)],
         flops=2 * rows * rank * features,
@@ -238,7 +228,7 @@
     )[0]
 
 
-def halve(pieces, bit):
+def halve(pieces, bit, after=()):
     rows, features = pieces[0].shape
     half = rows // 2
 
@@ -256,6 +246,7 @@
         list(pieces),
         [in_vmem] * len(pieces),
         [shape_of((half, features), f32), shape_of((half, features), bf16)],
+        after=after,
     )
 
 
@@ -273,21 +264,19 @@
     )[0]
 
 
-def join_shares(quarters, after):
-    share, features = quarters[0].shape
-
-    def body(*refs):
-        out = refs[-1]
-        at = share_of(lax.axis_index("own"), lax.axis_index("sub"))
-        for flip in range(4):
-            place = pl.multiple_of((at ^ flip) * share, share)
-            out[pl.ds(place, share), :] = refs[flip][...].astype(f32)
-
-    return call(
-        body,
-        quarters,
-        [in_vmem] * 4,
-        [shape_of((4 * share, features), f32)],
+def join_shares(mine, other, after):
+    share, features = mine.shape
+
+    def body(mine, other, out):
+        sub = lax.axis_index("sub")
+        for side, piece in ((sub, mine), (1 - sub, other)):
+            out[pl.ds(pl.multiple_of(side * share, share), share), :] = piece[...].astype(f32)
+
+    return call(
+        body,
+        [mine, other],
+        [in_vmem] * 2,
+        [shape_of((2 * share, features), f32)],
         after=after,
     )[0]
 
@@ -310,60 +299,108 @@
     )[0]
 
 
-def place_terms(adapter_ids, near, far, pattern, per_owner, after):
-    _, rank, columns = near.shape
-    sub_count = lax.axis_size("sub")
-
-    def body(ids, near, far, out, mark, held, sem):
-        own, sub = lax.axis_index("own"), lax.axis_index("sub")
+def clean(dims, after):
+    def body(out, mark, held, sem):
         held[...] = jnp.zeros(held.shape, f32)
         mark[...] = jnp.zeros(mark.shape, f32)
+        copies = [pltpu.make_async_copy(held, out.at[at], sem.at[at]) for at in range(dims[0])]
+        for copy in copies:
+            copy.start()
+        for copy in copies:
+            copy.wait()
+
+    return call(
+        body,
+        [],
+        [],
+        [shape_of(dims, f32), shape_of((8, 128), f32)],
+        out_specs=[in_hbm, in_vmem],
+        after=after,
+        scratch_shapes=[pltpu.VMEM(dims[1:], f32), pltpu.SemaphoreType.DMA((dims[0],))],
+    )
+
+
+def place_terms(adapter_ids, near, far, pattern, cleaned, after):
+    per_owner, rank, columns = cleaned.shape
+    sub_count = lax.axis_size("sub")
+
+    def body(ids_far, near, far, cleaned, out, mark, held, ids, counts, sems):
+        own, sub = lax.axis_index("own"), lax.axis_index("sub")
+        fetch = pltpu.make_async_copy(ids_far, ids, sems.at[per_owner])
+        fetch.start()
+        mark[...] = jnp.zeros(mark.shape, f32)
+        for local in range(per_owner):
+            counts[local] = 0
+        fetch.wait()
         for at, step in enumerate(pattern):
             for side in range(sub_count):
                 local = ids[(own ^ step) * sub_count + side] - own * per_owner
 
                 @pl.when(jnp.logical_and(local >= 0, local < per_owner))
                 def _():
-                    term = jnp.where(sub == side, near[at], far[at])
-                    held[pl.ds(local, 1)] += term.astype(f32)[None]
-
-        copy = pltpu.make_async_copy(held, out, sem)
-        copy.start()
-        copy.wait()
-
-    return call(
-        body,
-        [adapter_ids, near, far],
-        [in_smem, in_vmem, in_vmem],
-        [shape_of((per_owner, rank, columns), f32), shape_of((8, 128), f32)],
+                    term = jnp.where(sub == side, near[at], far[at]).astype(f32)
+
+                    @pl.when(counts[local] == 0)
+                    def _():
+                        held[local] = term
+
+                    @pl.when(counts[local] > 0)
+                    def _():
+                        held[local] += term
+
+                    counts[local] += 1
+
+        copies = [
+            pltpu.make_async_copy(held.at[local], out.at[local], sems.at[local])
+            for local in range(per_owner)
+        ]
+        for local, copy in enumerate(copies):
+            pl.when(counts[local] > 0)(copy.start)
+        for local, copy in enumerate(copies):
+            pl.when(counts[local] > 0)(copy.wait)
+
+    return call(
+        body,
+        [stay(adapter_ids), near, far, cleaned],
+        [in_hbm, in_vmem, in_vmem, in_hbm],
+        [shape_of(cleaned.shape, f32), shape_of((8, 128), f32)],
         out_specs=[in_hbm, in_vmem],
         after=after,
+        input_output_aliases={3: 0},
         scratch_shapes=[
-            pltpu.VMEM((per_owner, rank, columns), f32),
-            pltpu.SemaphoreType.DMA,
+            pltpu.VMEM(cleaned.shape, f32),
+            pltpu.SMEM(adapter_ids.shape, jnp.int32),
+            pltpu.SMEM((per_owner,), jnp.int32),
+            pltpu.SemaphoreType.DMA((per_owner + 1,)),
         ],
     )
 
 
-def arrange(lengths, grads):
-    rows, columns = grads[0].shape
-    count = len(grads)
-
-    def body(lengths, *refs):
-        grads, kept = refs[:-1], refs[-1]
+def arrange(lengths, grad, pieces, after):
+    rows, columns = grad.shape
+    count = 1 + len(pieces)
+    first = rows // 2
+
+    def body(lengths, grad, *refs):
+        pieces, kept = refs[:-1], refs[-1]
         at = lax.axis_index("tp")
         live = lax.broadcasted_iota(jnp.int32, (rows, columns), 0) < lengths[0]
-        for step in range(count):
+        zero = jnp.zeros((rows, columns), bf16)
+        place = pl.multiple_of(at * columns, 128)
+        kept[:, pl.ds(place, columns)] = jnp.where(live, grad[...], zero)
+        for step in range(1, count):
             place = pl.multiple_of(lax.rem(at + count - step, count) * columns, 128)
-            kept[:, pl.ds(place, columns)] = jnp.where(
-                live, grads[step][...], jnp.zeros((rows, columns), bf16)
-            )
-
-    return call(
-        body,
-        [lengths, *grads],
-        [in_smem] + [in_vmem] * count,
+            early, late = pieces[2 * step - 2 : 2 * step]
+            kept[:first, pl.ds(place, columns)] = jnp.where(live[:first], early[...], zero[:first])
+            kept[first:, pl.ds(place, columns)] = jnp.where(live[first:], late[...], zero[first:])
+
+    flat = [x for pair in pieces for x in pair]
+    return call(
+        body,
+        [lengths, grad, *flat],
+        [in_smem] + [in_vmem] * (1 + len(flat)),
         [shape_of((rows, count * columns), bf16)],
+        after=after,
     )[0]
 
 
@@ -421,47 +458,44 @@
     tp_steps, own_steps = range(1, tp_count), range(1, own_count)
 
     frozen_other = shift(frozen_value, "sub", 1)
-    picked = pick_heads(adapter_ids, head_up)
+    picked, early, away = pick_heads(adapter_ids, head_up, grad_output)
     offered = [picked[0]] + [swap(picked[step], step, 0) for step in own_steps]
+    early_grads = [shift(early, "tp", step) for step in tp_steps]
 
     low, tokens, down = project_low(tokens, shared_down.T, offered[1:2] or picked[:1])
     lows = [low] + [shift(low, "tp", step) for step in tp_steps]
 
-    part = project_back(adapter_ids, offered, grad_output, per_owner, [low, frozen_other])
+    part = project_back(away, offered, grad_output, [low, frozen_other, *early_grads])
     parts = [part] + [shift(part, "tp", step) for step in tp_steps]
 
-    near = head_term(lengths, lows, grad_output, scale, [part])
-    far_bits = [1 << i for i in reversed(range(1, own_count.bit_length() - 1))]
-    pattern = [0]
-    for bit in far_bits[:1]:
-        near_arrived = swap(near, bit, 0)
-
-    back, mine, *sends, again = shared_terms(lengths, parts, tokens, grad_output, scale, [near])
-    grads = [grad_output] + [shift(again, "tp", step) for step in tp_steps]
-    flips = ((1, 0), (0, 1), (1, 1))
-    pieces = [mine] + [swap(send, *flip) for send, flip in zip(sends, flips)]
-
-    bits = far_bits[::-1]
+    near, late = head_term(lengths, lows, grad_output, scale, [part])
+    late_grads = [shift(late, "tp", step) for step in tp_steps]
+    bits = [1 << i for i in range(own_count.bit_length() - 1)]
+    terms, pattern = [near], [0]
+    for bit in reversed(bits):
+        terms = terms + [swap(term, bit, 0) for term in terms]
+        pattern = pattern + [step ^ bit for step in pattern]
+
+    back, keep, send = shared_terms(lengths, parts, tokens, scale, [near])
+    pieces = [keep, shift(send, "sub", 1)]
+
+    mark = keep
     for bit in bits[:-1]:
         stays, leaves = halve(pieces, bit)
         pieces = [stays, swap(leaves, bit, 0)]
-    total = add_up(pieces)
-
-    for bit in far_bits + [1] * (own_count > 1):
-        arrived = near_arrived if bit == far_bits[0] else swap(near, bit, 0)
-        near = stack([near, arrived], [total])
-        pattern = pattern + [step ^ bit for step in pattern]
+        mark = leaves
+    cleaned, mark = clean((per_owner,) + near.shape[1:], [mark])
+    total = add_up(pieces, [mark])
+    kept = arrange(lengths, grad_output, list(zip(early_grads, late_grads)), [total])
+    input_gradient, mark = input_side(kept, frozen_value, frozen_other, back, down, [total])
+    near = stack(terms, [total])
     far = shift(near, "sub", 1)
-
     if bits:
-        total = add_up([total, swap(total, bits[-1], 0)])
+        total = add_up([total, swap(total, bits[-1], 0)], [mark])
+    grad_heads, mark = place_terms(adapter_ids, near, far, pattern, cleaned, [total])
     for bit in reversed(bits[:-1]):
         total = rejoin(total, swap(total, bit, 0), bit)
-    quarters = [total] + [swap(total, *flip) for flip in flips]
-    kept = arrange(lengths, grads)
-    input_gradient, mark = input_side(kept, frozen_value, frozen_other, back, down, [total])
-    grad_heads, mark = place_terms(adapter_ids, near, far, pattern, per_owner, [mark])
-    shared_down_gradient = join_shares(quarters, [mark]).T
+    shared_down_gradient = join_shares(total, shift(total, "sub", 1), [mark]).T
     return (input_gradient, shared_down_gradient, grad_heads)
 
 

time: 48.7 us -> 46.1 us (0.947)
  starting transfers between devices: 21 us -> 16.9 us
  waiting for transfers between devices: 12.6 us -> 14.1 us
    ppermute x12 -> x9, starting transfers between devices: 15.6 us -> 12 us  [swap(): lax.ppermute(x, ('own', 'sub'), [(i, i ^ other) for i in range(whole)])]
    ppermute x5 -> x8, waiting for transfers between devices: 2.6 us -> 3.57 us  [shift(): lax.ppermute(x, axis, [(i, (i + step) % count) for i in range(count)])]
    ppermute x5 -> x8, starting transfers between devices: 5.48 us -> 4.93 us  [shift(): lax.ppermute(x, axis, [(i, (i + step) % count) for i in range(count)])]
    ppermute x12 -> x9, waiting for transfers between devices: 10 us -> 10.5 us  [swap(): lax.ppermute(x, ('own', 'sub'), [(i, i ^ other) for i in range(whole)])]
    pallas_call x13 -> x15, Pallas kernels: 13.3 us -> 13.4 us  [call(): pl.pallas_call(kernel, out_shape=outs, in_specs=list(specs) + [anywhere]...]
  transfers between devices with their start and end apart: 17 -> 17, of which waited for: 7 -> 5; matrix products, arithmetic and copies ran while one was open for 0% -> 0% of each run, Pallas kernels for 24% -> 26%
where the time goes in v4:
time: 46.1 us; the launch traced here: 45.9 us
  starting transfers between devices  16.9 us (37%)
  waiting for transfers between devices  14.1 us (31%)
  Pallas kernels  13.4 us (29%)
  between operations  1.48 us (3%)
    pallas_call x15, Pallas kernels, call(): pl.pallas_call(kernel, out_shape=outs, in_specs=list(specs) + [anywhere]...  13.4 us
    ppermute x9, starting transfers between devices, swap(): lax.ppermute(x, ('own', 'sub'), [(i, i ^ other) for i in range(whole)])  12 us
    ppermute x9, waiting for transfers between devices, swap(): lax.ppermute(x, ('own', 'sub'), [(i, i ^ other) for i in range(whole)])  10.5 us
    ppermute x8, starting transfers between devices, shift(): lax.ppermute(x, axis, [(i, (i + step) % count) for i in range(count)])  4.93 us
    ppermute x8, waiting for transfers between devices, shift(): lax.ppermute(x, axis, [(i, (i + step) % count) for i in range(count)])  3.57 us
  transfers between devices with their start and end apart: 17, of which 5 were waited for; matrix products, arithmetic and copies ran while one was open for 0% of the time, Pallas kernels for 26%

profile of v4, /device:TPU:0, one launch (start us, length us, event | category | flops | bytes accessed | tf_op | source)
XLA Modules:
  0.0 45.9 jit_solution(1327630907495957847)
XLA Ops:
  0.6 0.5 %collective-permute-start.5 = (bf16[2560,512]{1,0:T(8,128)(2,1)}, bf16[2560,512]{1,0:T(8,128)(2,1)S(1)}, u32[]{:S(2)}, u32[]{:S(2)}) collective-permute-start(bf16[2560,512]{1,0:T(8,128)(2,1)} %refs_1_.5), channel_id=1, source_target_pairs={{0,1},{1,0},{2,3},{3,2},{4,5},{5,4},{6,7},{7,6},{8,9},{9,8},{10,11... | collective-permute-start | bytes 7864328 | tf_op jit(solution)/shard_map/ppermute | solution.py:20
  1.2 1.3 %shard_map.94 = (bf16[64,512]{1,0:T(8,128)(2,1)S(1)}, bf16[64,512]{1,0:T(8,128)(2,1)S(1)}, bf16[64,512]{1,0:T(8,128)(2,1)S(1)}, bf16[64,512]{1,0:T(8,128)(2,1)S(...) custom-call(s32[8]{0:T(128)} %refs_0_.8, bf16[16,64,512]{2,1,0:T(8,128)(2,1)} %refs_1_.3, bf16[512,512]{1,0:T(8,128)(2,1)} %refs_1_.4), custom_call_target="tpu_custom_call" | custom-call | bytes 2101280 | tf_op jit(solution)/shard_map/pallas_call | solution.py:49
  2.5 2.6 %collective-permute-start = (bf16[256,512]{1,0:T(8,128)(2,1)S(1)}, bf16[256,512]{1,0:T(8,128)(2,1)S(1)}, u32[]{:S(2)}, u32[]{:S(2)}) collective-permute-start(bf16[256,512]{1,0:T(8,128)(2,1)S(1)} %get-tuple-element.25), channel_id=1, source_target_pairs={{0,2},{2,0},{1,3},{3,1},{4,6},{6,4},{5,7},{7,5},{8,10},{10,8},{9,1... | collective-permute-start | bytes 786440 | tf_op jit(solution)/shard_map/ppermute | solution.py:20
  5.1 1.6 %collective-permute-start.1 = (bf16[64,512]{1,0:T(8,128)(2,1)S(1)}, bf16[64,512]{1,0:T(8,128)(2,1)S(1)}, u32[]{:S(2)}, u32[]{:S(2)}) collective-permute-start(bf16[64,512]{1,0:T(8,128)(2,1)S(1)} %get-tuple-element.26), channel_id=1, source_target_pairs={{0,4},{1,5},{4,0},{5,1},{8,12},{9,13},{12,8},{13,9},{2,6},{3,7},{6... | collective-permute-start | bytes 196616 | tf_op jit(solution)/shard_map/ppermute | solution.py:27
  6.7 2.6 %collective-permute-start.3 = (bf16[64,512]{1,0:T(8,128)(2,1)S(1)}, bf16[64,512]{1,0:T(8,128)(2,1)S(1)}, u32[]{:S(2)}, u32[]{:S(2)}) collective-permute-start(bf16[64,512]{1,0:T(8,128)(2,1)S(1)} %get-tuple-element.30), channel_id=1, source_target_pairs={{0,8},{1,9},{4,12},{5,13},{8,0},{9,1},{12,4},{13,5},{2,10},{3,11},... | collective-permute-start | bytes 196616 | tf_op jit(solution)/shard_map/ppermute | solution.py:27
  9.5 2.3 %shard_map.95 = (f32[64,512]{1,0:T(8,128)S(1)}, bf16[512,2560]{1,0:T(8,128)(2,1)S(1)}, bf16[64,2560]{1,0:T(8,128)(2,1)S(1)}) custom-call(bf16[512,2560]{1,0:T(8,128)(2,1)} %refs_0_.7, bf16[64,2560]{1,0:T(8,128)(2,1)} %bitcast.3, bf16[64,512]{1,0:T(8,128)(2,1)S(1)} %collective-permute-done.1.refs_2_), custom_call_target="tpu_custom_call" | custom-call | flops 167772160 | bytes 6029312 | tf_op jit(solution)/shard_map/pallas_call | solution.py:49
  11.8 0.4 collective-permute-start.2
  12.2 2.0 %collective-permute-done.3.refs_3_ = bf16[64,512]{1,0:T(8,128)(2,1)S(1)} collective-permute-done((bf16[64,512]{1,0:T(8,128)(2,1)S(1)}, bf16[64,512]{1,0:T(8,128)(2,1)S(1)}, u32[]{:S(2)}, u32[]{:S(2)}) %collective-permute-start.3) | collective-permute-done | bytes 65568 | tf_op jit(solution)/shard_map/ppermute | solution.py:27
  14.2 1.2 %collective-permute-done.4.refs_4_ = bf16[64,512]{1,0:T(8,128)(2,1)S(1)} collective-permute-done((bf16[64,512]{1,0:T(8,128)(2,1)S(1)}, bf16[64,512]{1,0:T(8,128)(2,1)S(1)}, u32[]{:S(2)}, u32[]{:S(2)}) %collective-permute-start.4) | collective-permute-done | bytes 65568 | tf_op jit(solution)/shard_map/ppermute | solution.py:27
  15.4 0.3 shard_map.96.refs_4_.refs_1_
  15.7 0.6 %collective-permute-start.7 = (f32[64,512]{1,0:T(8,128)S(1)}, f32[64,512]{1,0:T(8,128)S(1)}, u32[]{:S(2)}, u32[]{:S(2)}) collective-permute-start(f32[64,512]{1,0:T(8,128)S(1)} %shard_map.96.refs_4_.refs_1_), channel_id=1, source_target_pairs={{0,2},{2,0},{1,3},{3,1},{4,6},{6,4},{5,7},{7,5},{8,10},{10,8},{9,1... | collective-permute-start | bytes 393224 | tf_op jit(solution)/shard_map/ppermute | solution.py:20
  17.2 3.5 %collective-permute-done.7.refs_2_ = f32[64,512]{1,0:T(8,128)S(1)} collective-permute-done((f32[64,512]{1,0:T(8,128)S(1)}, f32[64,512]{1,0:T(8,128)S(1)}, u32[]{:S(2)}, u32[]{:S(2)}) %collective-permute-start.7) | collective-permute-done | bytes 131104 | tf_op jit(solution)/shard_map/ppermute | solution.py:20
  20.7 0.6 %shard_map.98 = (bf16[64,512]{1,0:T(8,128)(2,1)S(1)}, f32[32,2560]{1,0:T(8,128)S(1)}, f32[32,2560]{1,0:T(8,128)S(1)}) custom-call(s32[1]{0:T(128)S(6)} %copy.12.refs_0_, f32[64,512]{1,0:T(8,128)S(1)} %shard_map.96.refs_4_.refs_1_, f32[64,512]{1,0:T(8,128)S(1)} %collective-permute-done.7.refs_2_, bf16[512,2560]{1,0:T(8,128)(2,1)S(1)} %get-tuple-element.33.refs_3_, ...), custom_call_target="tpu_custom_call" | custom-call | flops 167772160 | bytes 3604484 | tf_op jit(solution)/shard_map/pallas_call | solution.py:49
  21.4 0.6 %collective-permute-start.6 = (bf16[256,512]{1,0:T(8,128)(2,1)S(1)}, bf16[256,512]{1,0:T(8,128)(2,1)S(1)}, u32[]{:S(2)}, u32[]{:S(2)}) collective-permute-start(bf16[256,512]{1,0:T(8,128)(2,1)S(1)} %get-tuple-element.32), channel_id=1, source_target_pairs={{0,2},{2,0},{1,3},{3,1},{4,6},{6,4},{5,7},{7,5},{8,10},{10,8},{9,1... | collective-permute-start | bytes 786440 | tf_op jit(solution)/shard_map/ppermute | solution.py:20
  22.0 2.0 %collective-permute-start.13 = (bf16[1,64,512]{2,1,0:T(8,128)(2,1)S(1)}, bf16[1,64,512]{2,1,0:T(8,128)(2,1)S(1)}, u32[]{:S(2)}, u32[]{:S(2)}) collective-permute-start(bf16[1,64,512]{2,1,0:T(8,128)(2,1)S(1)} %get-tuple-element.34.refs_4_.refs_0_), channel_id=1, source_target_pairs={{0,8},{1,9},{4,12},{5,13},{8,0},{9,1},{12,4},{13,5},{2,10},{3,11},... | collective-permute-start | bytes 196616 | tf_op jit(solution)/shard_map/ppermute | solution.py:27
  24.0 1.5 %collective-permute-start.9 = (bf16[16,2560]{1,0:T(8,128)(2,1)S(1)}, bf16[16,2560]{1,0:T(8,128)(2,1)S(1)}, u32[]{:S(2)}, u32[]{:S(2)}) collective-permute-start(bf16[16,2560]{1,0:T(8,128)(2,1)S(1)} %get-tuple-element.38.refs_0_), channel_id=1, source_target_pairs={{0,4},{1,5},{4,0},{5,1},{8,12},{9,13},{12,8},{13,9},{2,6},{3,7},{6... | collective-permute-start | bytes 245768 | tf_op jit(solution)/shard_map/ppermute | solution.py:27
  25.6 0.5 %collective-permute-start.14 = (bf16[1,64,512]{2,1,0:T(8,128)(2,1)S(1)}, bf16[1,64,512]{2,1,0:T(8,128)(2,1)S(1)}, u32[]{:S(2)}, u32[]{:S(2)}) collective-permute-start(bf16[1,64,512]{2,1,0:T(8,128)(2,1)S(1)} %get-tuple-element.34.refs_4_.refs_0_), channel_id=1, source_target_pairs={{0,4},{1,5},{4,0},{5,1},{8,12},{9,13},{12,8},{13,9},{2,6},{3,7},{6... | collective-permute-start | bytes 196616 | tf_op jit(solution)/shard_map/ppermute | solution.py:27
  26.1 2.4 %collective-permute-done.13.refs_1_ = bf16[1,64,512]{2,1,0:T(8,128)(2,1)S(1)} collective-permute-done((bf16[1,64,512]{2,1,0:T(8,128)(2,1)S(1)}, bf16[1,64,512]{2,1,0:T(8,128)(2,1)S(1)}, u32[]{:S(2)}, u32[]{:S(2)}) %collective-permute-start.13) | collective-permute-done | bytes 65568 | tf_op jit(solution)/shard_map/ppermute | solution.py:27
  28.6 1.4 %shard_map.100 = (f32[16,64,512]{2,1,0:T(8,128)}, f32[8,128]{1,0:T(8,128)S(1)}) custom-call(bf16[16,2560]{1,0:T(8,128)(2,1)S(1)} %get-tuple-element.38.refs_0_), custom_call_target="tpu_custom_call" | custom-call | bytes 2101248 | tf_op jit(solution)/shard_map/pallas_call | solution.py:49
  30.1 3.5 %collective-permute-start.10 = (bf16[16,2560]{1,0:T(8,128)(2,1)S(1)}, bf16[16,2560]{1,0:T(8,128)(2,1)S(1)}, u32[]{:S(2)}, u32[]{:S(2)}) collective-permute-start(bf16[16,2560]{1,0:T(8,128)(2,1)S(1)} %shard_map.101.refs_4_.refs_5_.refs_0_), channel_id=1, source_target_pairs={{0,8},{1,9},{4,12},{5,13},{8,0},{9,1},{12,4},{13,5},{2,10},{3,11},... | collective-permute-start | bytes 245768 | tf_op jit(solution)/shard_map/ppermute | solution.py:27
  33.8 4.4 %shard_map.103 = (bf16[512,2560]{1,0:T(8,128)(2,1)}, f32[8,128]{1,0:T(8,128)S(1)}) custom-call(bf16[512,1024]{1,0:T(8,128)(2,1)S(1)} %shard_map.102.refs_0_, bf16[2560,512]{1,0:T(8,128)(2,1)S(1)} %copy-done.1, bf16[2560,512]{1,0:T(8,128)(2,1)S(1)} %collective-permute-done.5.refs_7_.refs_2_, bf16[64,512]{1,0:T(8,128)(2,1)S(1)} %get-tuple-element.40.refs_3_, ...), custom_call_target="tpu_custom_call" | custom-call | flops 2852126720 | bytes 9310208 | tf_op jit(solution)/shard_map/pallas_call | solution.py:49
  38.3 4.8 %collective-permute-done.11.refs_1_ = bf16[16,2560]{1,0:T(8,128)(2,1)S(1)} collective-permute-done((bf16[16,2560]{1,0:T(8,128)(2,1)S(1)}, bf16[16,2560]{1,0:T(8,128)(2,1)S(1)}, u32[]{:S(2)}, u32[]{:S(2)}) %collective-permute-start.11) | collective-permute-done | bytes 81952 | tf_op jit(solution)/shard_map/ppermute | solution.py:27
  43.3 1.7 %shard_map.107 = (f32[16,64,512]{2,1,0:T(8,128)}, f32[8,128]{1,0:T(8,128)S(1)}) custom-call(s32[8]{0:T(128)} %refs_0_.8, bf16[4,64,512]{2,1,0:T(8,128)(2,1)S(1)} %shard_map.106.refs_1_, bf16[4,64,512]{2,1,0:T(8,128)(2,1)S(1)} %collective-permute-done.16.refs_2_, f32[16,64,512]{2,1,0:T(8,128)} %get-tuple-element.44.refs_3_, ...), custom_call_target="tpu_custom_call", output_to_operand_aliasing={{0}: (3, {})} | custom-call | bytes 4722720 | tf_op jit(solution)/shard_map/pallas_call | solution.py:49
  45.0 0.9 %shard_map.108 = f32[64,2560]{1,0:T(8,128)} custom-call(bf16[32,2560]{1,0:T(8,128)(2,1)S(1)} %shard_map.105.refs_0_, bf16[32,2560]{1,0:T(8,128)(2,1)S(1)} %collective-permute-done.12.refs_1_, f32[8,128]{1,0:T(8,128)S(1)} %get-tuple-element.45.refs_2_), custom_call_target="tpu_custom_call" | custom-call | bytes 983040 | tf_op jit(solution)/shard_map/pallas_call | solution.py:49
  (29 shorter events, 1.0 us)
Async XLA Ops:
  0.6 14.8 %copy-start = (bf16[512,512]{1,0:T(8,128)(2,1)S(1)}, bf16[512,512]{1,0:T(8,128)(2,1)}, u32[]{:S(2)}) copy-start(bf16[512,512]{1,0:T(8,128)(2,1)} %refs_1_.4) | copy-start | bytes 1572868
  0.6 14.8 %collective-permute-start.5 = (bf16[2560,512]{1,0:T(8,128)(2,1)}, bf16[2560,512]{1,0:T(8,128)(2,1)S(1)}, u32[]{:S(2)}, u32[]{:S(2)}) collective-permute-start(bf16[2560,512]{1,0:T(8,128)(2,1)} %refs_1_.5), channel_id=1, source_target_pairs={{0,1},{1,0},{2,3},{3,2},{4,5},{5,4},{6,7},{7,6},{8,9},{9,8},{10,11... | collective-permute-start | bytes 7864328 | tf_op jit(solution)/shard_map/ppermute | solution.py:20
  2.5 13.0 %collective-permute-start = (bf16[256,512]{1,0:T(8,128)(2,1)S(1)}, bf16[256,512]{1,0:T(8,128)(2,1)S(1)}, u32[]{:S(2)}, u32[]{:S(2)}) collective-permute-start(bf16[256,512]{1,0:T(8,128)(2,1)S(1)} %get-tuple-element.25), channel_id=1, source_target_pairs={{0,2},{2,0},{1,3},{3,1},{4,6},{6,4},{5,7},{7,5},{8,10},{10,8},{9,1... | collective-permute-start | bytes 786440 | tf_op jit(solution)/shard_map/ppermute | solution.py:20
  5.1 4.4 %collective-permute-start.1 = (bf16[64,512]{1,0:T(8,128)(2,1)S(1)}, bf16[64,512]{1,0:T(8,128)(2,1)S(1)}, u32[]{:S(2)}, u32[]{:S(2)}) collective-permute-start(bf16[64,512]{1,0:T(8,128)(2,1)S(1)} %get-tuple-element.26), channel_id=1, source_target_pairs={{0,4},{1,5},{4,0},{5,1},{8,12},{9,13},{12,8},{13,9},{2,6},{3,7},{6... | collective-permute-start | bytes 196616 | tf_op jit(solution)/shard_map/ppermute | solution.py:27
  6.7 7.5 %collective-permute-start.3 = (bf16[64,512]{1,0:T(8,128)(2,1)S(1)}, bf16[64,512]{1,0:T(8,128)(2,1)S(1)}, u32[]{:S(2)}, u32[]{:S(2)}) collective-permute-start(bf16[64,512]{1,0:T(8,128)(2,1)S(1)} %get-tuple-element.30), channel_id=1, source_target_pairs={{0,8},{1,9},{4,12},{5,13},{8,0},{9,1},{12,4},{13,5},{2,10},{3,11},... | collective-permute-start | bytes 196616 | tf_op jit(solution)/shard_map/ppermute | solution.py:27
  9.2 6.2 %collective-permute-start.4 = (bf16[64,512]{1,0:T(8,128)(2,1)S(1)}, bf16[64,512]{1,0:T(8,128)(2,1)S(1)}, u32[]{:S(2)}, u32[]{:S(2)}) collective-permute-start(bf16[64,512]{1,0:T(8,128)(2,1)S(1)} %get-tuple-element.31), channel_id=1, source_target_pairs={{0,12},{1,13},{4,8},{5,9},{8,4},{9,5},{12,0},{13,1},{2,14},{3,15},... | collective-permute-start | bytes 196616 | tf_op jit(solution)/shard_map/ppermute | solution.py:27
  11.8 5.2 %collective-permute-start.2 = (f32[64,512]{1,0:T(8,128)S(1)}, f32[64,512]{1,0:T(8,128)S(1)}, u32[]{:S(2)}, u32[]{:S(2)}) collective-permute-start(f32[64,512]{1,0:T(8,128)S(1)} %get-tuple-element.27.refs_6_.refs_1_), channel_id=1, source_target_pairs={{0,2},{2,0},{1,3},{3,1},{4,6},{6,4},{5,7},{7,5},{8,10},{10,8},{9,1... | collective-permute-start | bytes 393224 | tf_op jit(solution)/shard_map/ppermute | solution.py:20
  15.7 5.0 %collective-permute-start.7 = (f32[64,512]{1,0:T(8,128)S(1)}, f32[64,512]{1,0:T(8,128)S(1)}, u32[]{:S(2)}, u32[]{:S(2)}) collective-permute-start(f32[64,512]{1,0:T(8,128)S(1)} %shard_map.96.refs_4_.refs_1_), channel_id=1, source_target_pairs={{0,2},{2,0},{1,3},{3,1},{4,6},{6,4},{5,7},{7,5},{8,10},{10,8},{9,1... | collective-permute-start | bytes 393224 | tf_op jit(solution)/shard_map/ppermute | solution.py:20
  21.3 12.4 %copy-start.1 = (bf16[2560,512]{1,0:T(8,128)(2,1)S(1)}, bf16[2560,512]{1,0:T(8,128)(2,1)}, u32[]{:S(2)}) copy-start(bf16[2560,512]{1,0:T(8,128)(2,1)} %refs_1_.5) | copy-start | bytes 7864324
  21.4 2.6 %collective-permute-start.8 = (f32[32,2560]{1,0:T(8,128)S(1)}, f32[32,2560]{1,0:T(8,128)S(1)}, u32[]{:S(2)}, u32[]{:S(2)}) collective-permute-start(f32[32,2560]{1,0:T(8,128)S(1)} %get-tuple-element.36), channel_id=1, source_target_pairs={{0,1},{1,0},{2,3},{3,2},{4,5},{5,4},{6,7},{7,6},{8,9},{9,8},{10,11... | collective-permute-start | bytes 983048 | tf_op jit(solution)/shard_map/ppermute | solution.py:20
  21.4 12.2 %collective-permute-start.6 = (bf16[256,512]{1,0:T(8,128)(2,1)S(1)}, bf16[256,512]{1,0:T(8,128)(2,1)S(1)}, u32[]{:S(2)}, u32[]{:S(2)}) collective-permute-start(bf16[256,512]{1,0:T(8,128)(2,1)S(1)} %get-tuple-element.32), channel_id=1, source_target_pairs={{0,2},{2,0},{1,3},{3,1},{4,6},{6,4},{5,7},{7,5},{8,10},{10,8},{9,1... | collective-permute-start | bytes 786440 | tf_op jit(solution)/shard_map/ppermute | solution.py:20
  22.0 6.5 %collective-permute-start.13 = (bf16[1,64,512]{2,1,0:T(8,128)(2,1)S(1)}, bf16[1,64,512]{2,1,0:T(8,128)(2,1)S(1)}, u32[]{:S(2)}, u32[]{:S(2)}) collective-permute-start(bf16[1,64,512]{2,1,0:T(8,128)(2,1)S(1)} %get-tuple-element.34.refs_4_.refs_0_), channel_id=1, source_target_pairs={{0,8},{1,9},{4,12},{5,13},{8,0},{9,1},{12,4},{13,5},{2,10},{3,11},... | collective-permute-start | bytes 196616 | tf_op jit(solution)/shard_map/ppermute | solution.py:27
  24.0 6.0 %collective-permute-start.9 = (bf16[16,2560]{1,0:T(8,128)(2,1)S(1)}, bf16[16,2560]{1,0:T(8,128)(2,1)S(1)}, u32[]{:S(2)}, u32[]{:S(2)}) collective-permute-start(bf16[16,2560]{1,0:T(8,128)(2,1)S(1)} %get-tuple-element.38.refs_0_), channel_id=1, source_target_pairs={{0,4},{1,5},{4,0},{5,1},{8,12},{9,13},{12,8},{13,9},{2,6},{3,7},{6... | collective-permute-start | bytes 245768 | tf_op jit(solution)/shard_map/ppermute | solution.py:27
  25.6 8.0 %collective-permute-start.14 = (bf16[1,64,512]{2,1,0:T(8,128)(2,1)S(1)}, bf16[1,64,512]{2,1,0:T(8,128)(2,1)S(1)}, u32[]{:S(2)}, u32[]{:S(2)}) collective-permute-start(bf16[1,64,512]{2,1,0:T(8,128)(2,1)S(1)} %get-tuple-element.34.refs_4_.refs_0_), channel_id=1, source_target_pairs={{0,4},{1,5},{4,0},{5,1},{8,12},{9,13},{12,8},{13,9},{2,6},{3,7},{6... | collective-permute-start | bytes 196616 | tf_op jit(solution)/shard_map/ppermute | solution.py:27
  28.6 5.0 %collective-permute-start.15 = (bf16[1,64,512]{2,1,0:T(8,128)(2,1)S(1)}, bf16[1,64,512]{2,1,0:T(8,128)(2,1)S(1)}, u32[]{:S(2)}, u32[]{:S(2)}) collective-permute-start(bf16[1,64,512]{2,1,0:T(8,128)(2,1)S(1)} %collective-permute-done.13.refs_1_), channel_id=1, source_target_pairs={{0,4},{1,5},{4,0},{5,1},{8,12},{9,13},{12,8},{13,9},{2,6},{3,7},{6... | collective-permute-start | bytes 196616 | tf_op jit(solution)/shard_map/ppermute | solution.py:27
  30.1 8.2 %collective-permute-start.10 = (bf16[16,2560]{1,0:T(8,128)(2,1)S(1)}, bf16[16,2560]{1,0:T(8,128)(2,1)S(1)}, u32[]{:S(2)}, u32[]{:S(2)}) collective-permute-start(bf16[16,2560]{1,0:T(8,128)(2,1)S(1)} %shard_map.101.refs_4_.refs_5_.refs_0_), channel_id=1, source_target_pairs={{0,8},{1,9},{4,12},{5,13},{8,0},{9,1},{12,4},{13,5},{2,10},{3,11},... | collective-permute-start | bytes 245768 | tf_op jit(solution)/shard_map/ppermute | solution.py:27
  33.6 9.7 %collective-permute-start.16 = (bf16[4,64,512]{2,1,0:T(8,128)(2,1)S(1)}, bf16[4,64,512]{2,1,0:T(8,128)(2,1)S(1)}, u32[]{:S(2)}, u32[]{:S(2)}) collective-permute-start(bf16[4,64,512]{2,1,0:T(8,128)(2,1)S(1)} %shard_map.106.refs_1_), channel_id=1, source_target_pairs={{0,1},{1,0},{2,3},{3,2},{4,5},{5,4},{6,7},{7,6},{8,9},{9,8},{10,11... | collective-permute-start | bytes 786440 | tf_op jit(solution)/shard_map/ppermute | solution.py:20
  38.3 4.9 %collective-permute-start.11 = (bf16[16,2560]{1,0:T(8,128)(2,1)S(1)}, bf16[16,2560]{1,0:T(8,128)(2,1)S(1)}, u32[]{:S(2)}, u32[]{:S(2)}) collective-permute-start(bf16[16,2560]{1,0:T(8,128)(2,1)S(1)} %shard_map.104.refs_0_.refs_4_), channel_id=1, source_target_pairs={{0,4},{1,5},{4,0},{5,1},{8,12},{9,13},{12,8},{13,9},{2,6},{3,7},{6... | collective-permute-start | bytes 245768 | tf_op jit(solution)/shard_map/ppermute | solution.py:27
  43.2 1.8 %collective-permute-start.12 = (bf16[32,2560]{1,0:T(8,128)(2,1)S(1)}, bf16[32,2560]{1,0:T(8,128)(2,1)S(1)}, u32[]{:S(2)}, u32[]{:S(2)}) collective-permute-start(bf16[32,2560]{1,0:T(8,128)(2,1)S(1)} %shard_map.105.refs_0_), channel_id=1, source_target_pairs={{0,1},{1,0},{2,3},{3,2},{4,5},{5,4},{6,7},{7,6},{8,9},{9,8},{10,11... | collective-permute-start | bytes 491528 | tf_op jit(solution)/shard_map/ppermute | solution.py:20

commit v5 on v4

--- a/solution.py
+++ b/solution.py
@@ -250,7 +250,7 @@
     )
 
 
-def rejoin(mine, arrived, bit):
+def rejoin(mine, arrived, bit, after):
     rows, features = mine.shape
 
     def body(mine, arrived, out):
@@ -260,7 +260,11 @@
         out[rows:] = jnp.where(upper, one, two).astype(bf16)
 
     return call(
-        body, [mine, arrived], [in_vmem] * 2, [shape_of((2 * rows, features), bf16)]
+        body,
+        [mine, arrived],
+        [in_vmem] * 2,
+        [shape_of((2 * rows, features), bf16)],
+        after=after,
     )[0]
 
 
@@ -476,25 +480,24 @@
         terms = terms + [swap(term, bit, 0) for term in terms]
         pattern = pattern + [step ^ bit for step in pattern]
 
-    back, keep, send = shared_terms(lengths, parts, tokens, scale, [near])
+    cleaned, mark = clean((per_owner,) + near.shape[1:], [near])
+    back, keep, send = shared_terms(lengths, parts, tokens, scale, [mark])
     pieces = [keep, shift(send, "sub", 1)]
 
-    mark = keep
     for bit in bits[:-1]:
         stays, leaves = halve(pieces, bit)
         pieces = [stays, swap(leaves, bit, 0)]
-        mark = leaves
-    cleaned, mark = clean((per_owner,) + near.shape[1:], [mark])
-    total = add_up(pieces, [mark])
+    total = add_up(pieces)
+    near = stack(terms, [total])
+    far = shift(near, "sub", 1)
     kept = arrange(lengths, grad_output, list(zip(early_grads, late_grads)), [total])
     input_gradient, mark = input_side(kept, frozen_value, frozen_other, back, down, [total])
-    near = stack(terms, [total])
-    far = shift(near, "sub", 1)
     if bits:
         total = add_up([total, swap(total, bits[-1], 0)], [mark])
     grad_heads, mark = place_terms(adapter_ids, near, far, pattern, cleaned, [total])
     for bit in reversed(bits[:-1]):
-        total = rejoin(total, swap(total, bit, 0), bit)
+        total = rejoin(total, swap(total, bit, 0), bit, [mark])
+        mark = total
     shared_down_gradient = join_shares(total, shift(total, "sub", 1), [mark]).T
     return (input_gradient, shared_down_gradient, grad_heads)
 

time: 46.1 us -> 45.6 us (0.989)
  starting transfers between devices: 16.9 us -> 15.7 us
  waiting for transfers between devices: 14.1 us -> 14.9 us
    ppermute x9, starting transfers between devices: 12 us -> 10.7 us  [swap(): lax.ppermute(x, ('own', 'sub'), [(i, i ^ other) for i in range(whole)])]
    ppermute x9, waiting for transfers between devices: 10.5 us -> 11.4 us  [swap(): lax.ppermute(x, ('own', 'sub'), [(i, i ^ other) for i in range(whole)])]
  transfers between devices with their start and end apart: 17 -> 17, of which waited for: 5 -> 8; matrix products, arithmetic and copies ran while one was open for 0% -> 0% of each run, Pallas kernels for 26% -> 26%
where the time goes in v5:
time: 45.6 us; the launch traced here: 45.5 us
  starting transfers between devices  15.7 us (34%)
  waiting for transfers between devices  14.9 us (33%)
  Pallas kernels  13.4 us (29%)
  between operations  1.46 us (3%)
    pallas_call x15, Pallas kernels, call(): pl.pallas_call(kernel, out_shape=outs, in_specs=list(specs) + [anywhere]...  13.4 us
    ppermute x9, waiting for transfers between devices, swap(): lax.ppermute(x, ('own', 'sub'), [(i, i ^ other) for i in range(whole)])  11.4 us
    ppermute x9, starting transfers between devices, swap(): lax.ppermute(x, ('own', 'sub'), [(i, i ^ other) for i in range(whole)])  10.7 us
    ppermute x8, starting transfers between devices, shift(): lax.ppermute(x, axis, [(i, (i + step) % count) for i in range(count)])  4.94 us
    ppermute x8, waiting for transfers between devices, shift(): lax.ppermute(x, axis, [(i, (i + step) % count) for i in range(count)])  3.49 us
  transfers between devices with their start and end apart: 17, of which 8 were waited for; matrix products, arithmetic and copies ran while one was open for 0% of the time, Pallas kernels for 26%

profile of v5, /device:TPU:0, one launch (start us, length us, event | category | flops | bytes accessed | tf_op | source)
XLA Modules:
  0.0 45.5 jit_solution(4038320847866863182)
XLA Ops:
  0.6 0.5 %collective-permute-start.5 = (bf16[2560,512]{1,0:T(8,128)(2,1)}, bf16[2560,512]{1,0:T(8,128)(2,1)S(1)}, u32[]{:S(2)}, u32[]{:S(2)}) collective-permute-start(bf16[2560,512]{1,0:T(8,128)(2,1)} %refs_1_.5), channel_id=1, source_target_pairs={{0,1},{1,0},{2,3},{3,2},{4,5},{5,4},{6,7},{7,6},{8,9},{9,8},{10,11... | collective-permute-start | bytes 7864328 | tf_op jit(solution)/shard_map/ppermute | solution.py:20
  1.2 1.3 %shard_map.94 = (bf16[64,512]{1,0:T(8,128)(2,1)S(1)}, bf16[64,512]{1,0:T(8,128)(2,1)S(1)}, bf16[64,512]{1,0:T(8,128)(2,1)S(1)}, bf16[64,512]{1,0:T(8,128)(2,1)S(...) custom-call(s32[8]{0:T(128)} %refs_0_.8, bf16[16,64,512]{2,1,0:T(8,128)(2,1)} %refs_1_.3, bf16[512,512]{1,0:T(8,128)(2,1)} %refs_1_.4), custom_call_target="tpu_custom_call" | custom-call | bytes 2101280 | tf_op jit(solution)/shard_map/pallas_call | solution.py:49
  2.5 2.6 %collective-permute-start = (bf16[256,512]{1,0:T(8,128)(2,1)S(1)}, bf16[256,512]{1,0:T(8,128)(2,1)S(1)}, u32[]{:S(2)}, u32[]{:S(2)}) collective-permute-start(bf16[256,512]{1,0:T(8,128)(2,1)S(1)} %get-tuple-element.25), channel_id=1, source_target_pairs={{0,2},{2,0},{1,3},{3,1},{4,6},{6,4},{5,7},{7,5},{8,10},{10,8},{9,1... | collective-permute-start | bytes 786440 | tf_op jit(solution)/shard_map/ppermute | solution.py:20
  5.1 1.6 %collective-permute-start.1 = (bf16[64,512]{1,0:T(8,128)(2,1)S(1)}, bf16[64,512]{1,0:T(8,128)(2,1)S(1)}, u32[]{:S(2)}, u32[]{:S(2)}) collective-permute-start(bf16[64,512]{1,0:T(8,128)(2,1)S(1)} %get-tuple-element.26), channel_id=1, source_target_pairs={{0,4},{1,5},{4,0},{5,1},{8,12},{9,13},{12,8},{13,9},{2,6},{3,7},{6... | collective-permute-start | bytes 196616 | tf_op jit(solution)/shard_map/ppermute | solution.py:27
  6.7 2.6 %collective-permute-start.3 = (bf16[64,512]{1,0:T(8,128)(2,1)S(1)}, bf16[64,512]{1,0:T(8,128)(2,1)S(1)}, u32[]{:S(2)}, u32[]{:S(2)}) collective-permute-start(bf16[64,512]{1,0:T(8,128)(2,1)S(1)} %get-tuple-element.30), channel_id=1, source_target_pairs={{0,8},{1,9},{4,12},{5,13},{8,0},{9,1},{12,4},{13,5},{2,10},{3,11},... | collective-permute-start | bytes 196616 | tf_op jit(solution)/shard_map/ppermute | solution.py:27
  9.5 2.3 %shard_map.95 = (f32[64,512]{1,0:T(8,128)S(1)}, bf16[512,2560]{1,0:T(8,128)(2,1)S(1)}, bf16[64,2560]{1,0:T(8,128)(2,1)S(1)}) custom-call(bf16[512,2560]{1,0:T(8,128)(2,1)} %refs_0_.7, bf16[64,2560]{1,0:T(8,128)(2,1)} %bitcast.3, bf16[64,512]{1,0:T(8,128)(2,1)S(1)} %collective-permute-done.1.refs_2_), custom_call_target="tpu_custom_call" | custom-call | flops 167772160 | bytes 6029312 | tf_op jit(solution)/shard_map/pallas_call | solution.py:49
  12.2 2.0 %collective-permute-done.3.refs_3_ = bf16[64,512]{1,0:T(8,128)(2,1)S(1)} collective-permute-done((bf16[64,512]{1,0:T(8,128)(2,1)S(1)}, bf16[64,512]{1,0:T(8,128)(2,1)S(1)}, u32[]{:S(2)}, u32[]{:S(2)}) %collective-permute-start.3) | collective-permute-done | bytes 65568 | tf_op jit(solution)/shard_map/ppermute | solution.py:27
  14.2 1.2 %collective-permute-done.4.refs_4_ = bf16[64,512]{1,0:T(8,128)(2,1)S(1)} collective-permute-done((bf16[64,512]{1,0:T(8,128)(2,1)S(1)}, bf16[64,512]{1,0:T(8,128)(2,1)S(1)}, u32[]{:S(2)}, u32[]{:S(2)}) %collective-permute-start.4) | collective-permute-done | bytes 65568 | tf_op jit(solution)/shard_map/ppermute | solution.py:27
  15.7 0.6 %collective-permute-start.7 = (f32[64,512]{1,0:T(8,128)S(1)}, f32[64,512]{1,0:T(8,128)S(1)}, u32[]{:S(2)}, u32[]{:S(2)}) collective-permute-start(f32[64,512]{1,0:T(8,128)S(1)} %shard_map.96.refs_4_.refs_1_), channel_id=1, source_target_pairs={{0,2},{2,0},{1,3},{3,1},{4,6},{6,4},{5,7},{7,5},{8,10},{10,8},{9,1... | collective-permute-start | bytes 393224 | tf_op jit(solution)/shard_map/ppermute | solution.py:20
  17.2 1.4 %shard_map.98 = (f32[16,64,512]{2,1,0:T(8,128)}, f32[8,128]{1,0:T(8,128)S(1)}) custom-call(bf16[1,64,512]{2,1,0:T(8,128)(2,1)S(1)} %get-tuple-element.34.refs_0_), custom_call_target="tpu_custom_call" | custom-call | bytes 2101248 | tf_op jit(solution)/shard_map/pallas_call | solution.py:49
  18.7 2.1 %collective-permute-done.7.refs_2_ = f32[64,512]{1,0:T(8,128)S(1)} collective-permute-done((f32[64,512]{1,0:T(8,128)S(1)}, f32[64,512]{1,0:T(8,128)S(1)}, u32[]{:S(2)}, u32[]{:S(2)}) %collective-permute-start.7) | collective-permute-done | bytes 131104 | tf_op jit(solution)/shard_map/ppermute | solution.py:20
  20.7 0.6 %shard_map.99 = (bf16[64,512]{1,0:T(8,128)(2,1)S(1)}, f32[32,2560]{1,0:T(8,128)S(1)}, f32[32,2560]{1,0:T(8,128)S(1)}) custom-call(s32[1]{0:T(128)S(6)} %copy.12.refs_0_, f32[64,512]{1,0:T(8,128)S(1)} %shard_map.96.refs_4_.refs_1_, f32[64,512]{1,0:T(8,128)S(1)} %collective-permute-done.7.refs_2_, bf16[512,2560]{1,0:T(8,128)(2,1)S(1)} %get-tuple-element.33.refs_3_, ...), custom_call_target="tpu_custom_call" | custom-call | flops 167772160 | bytes 3604484 | tf_op jit(solution)/shard_map/pallas_call | solution.py:49
  21.4 0.6 %collective-permute-start.6 = (bf16[256,512]{1,0:T(8,128)(2,1)S(1)}, bf16[256,512]{1,0:T(8,128)(2,1)S(1)}, u32[]{:S(2)}, u32[]{:S(2)}) collective-permute-start(bf16[256,512]{1,0:T(8,128)(2,1)S(1)} %get-tuple-element.32), channel_id=1, source_target_pairs={{0,2},{2,0},{1,3},{3,1},{4,6},{6,4},{5,7},{7,5},{8,10},{10,8},{9,1... | collective-permute-start | bytes 786440 | tf_op jit(solution)/shard_map/ppermute | solution.py:20
  22.0 1.9 %collective-permute-start.12 = (bf16[1,64,512]{2,1,0:T(8,128)(2,1)S(1)}, bf16[1,64,512]{2,1,0:T(8,128)(2,1)S(1)}, u32[]{:S(2)}, u32[]{:S(2)}) collective-permute-start(bf16[1,64,512]{2,1,0:T(8,128)(2,1)S(1)} %get-tuple-element.34.refs_0_), channel_id=1, source_target_pairs={{0,8},{1,9},{4,12},{5,13},{8,0},{9,1},{12,4},{13,5},{2,10},{3,11},... | collective-permute-start | bytes 196616 | tf_op jit(solution)/shard_map/ppermute | solution.py:27
  24.0 1.8 %collective-permute-start.9 = (bf16[16,2560]{1,0:T(8,128)(2,1)S(1)}, bf16[16,2560]{1,0:T(8,128)(2,1)S(1)}, u32[]{:S(2)}, u32[]{:S(2)}) collective-permute-start(bf16[16,2560]{1,0:T(8,128)(2,1)S(1)} %get-tuple-element.39), channel_id=1, source_target_pairs={{0,4},{1,5},{4,0},{5,1},{8,12},{9,13},{12,8},{13,9},{2,6},{3,7},{6... | collective-permute-start | bytes 245768 | tf_op jit(solution)/shard_map/ppermute | solution.py:27
  26.1 2.5 %collective-permute-done.12.refs_1_ = bf16[1,64,512]{2,1,0:T(8,128)(2,1)S(1)} collective-permute-done((bf16[1,64,512]{2,1,0:T(8,128)(2,1)S(1)}, bf16[1,64,512]{2,1,0:T(8,128)(2,1)S(1)}, u32[]{:S(2)}, u32[]{:S(2)}) %collective-permute-start.12) | collective-permute-done | bytes 65568 | tf_op jit(solution)/shard_map/ppermute | solution.py:27
  28.6 1.2 %collective-permute-done.9.refs_1_ = bf16[16,2560]{1,0:T(8,128)(2,1)S(1)} collective-permute-done((bf16[16,2560]{1,0:T(8,128)(2,1)S(1)}, bf16[16,2560]{1,0:T(8,128)(2,1)S(1)}, u32[]{:S(2)}, u32[]{:S(2)}) %collective-permute-start.9) | collective-permute-done | bytes 81952 | tf_op jit(solution)/shard_map/ppermute | solution.py:27
  29.9 2.2 %collective-permute-start.10 = (bf16[16,2560]{1,0:T(8,128)(2,1)S(1)}, bf16[16,2560]{1,0:T(8,128)(2,1)S(1)}, u32[]{:S(2)}, u32[]{:S(2)}) collective-permute-start(bf16[16,2560]{1,0:T(8,128)(2,1)S(1)} %shard_map.101.refs_4_.refs_5_.refs_0_), channel_id=1, source_target_pairs={{0,8},{1,9},{4,12},{5,13},{8,0},{9,1},{12,4},{13,5},{2,10},{3,11},... | collective-permute-start | bytes 245768 | tf_op jit(solution)/shard_map/ppermute | solution.py:27
  32.1 1.3 %collective-permute-done.14.refs_3_ = bf16[1,64,512]{2,1,0:T(8,128)(2,1)S(1)} collective-permute-done((bf16[1,64,512]{2,1,0:T(8,128)(2,1)S(1)}, bf16[1,64,512]{2,1,0:T(8,128)(2,1)S(1)}, u32[]{:S(2)}, u32[]{:S(2)}) %collective-permute-start.14) | collective-permute-done | bytes 65568 | tf_op jit(solution)/shard_map/ppermute | solution.py:27
  33.7 4.4 %shard_map.103 = (bf16[512,2560]{1,0:T(8,128)(2,1)}, f32[8,128]{1,0:T(8,128)S(1)}) custom-call(bf16[512,1024]{1,0:T(8,128)(2,1)S(1)} %shard_map.102.refs_0_, bf16[2560,512]{1,0:T(8,128)(2,1)S(1)} %copy-done.1, bf16[2560,512]{1,0:T(8,128)(2,1)S(1)} %collective-permute-done.5.refs_7_.refs_2_, bf16[64,512]{1,0:T(8,128)(2,1)S(1)} %get-tuple-element.40.refs_3_, ...), custom_call_target="tpu_custom_call" | custom-call | flops 2852126720 | bytes 9310208 | tf_op jit(solution)/shard_map/pallas_call | solution.py:49
  38.2 1.7 %shard_map.106 = (f32[16,64,512]{2,1,0:T(8,128)}, f32[8,128]{1,0:T(8,128)S(1)}) custom-call(s32[8]{0:T(128)} %refs_0_.8, bf16[4,64,512]{2,1,0:T(8,128)(2,1)S(1)} %shard_map.105.refs_1_, bf16[4,64,512]{2,1,0:T(8,128)(2,1)S(1)} %collective-permute-done.15.refs_2_, f32[16,64,512]{2,1,0:T(8,128)} %get-tuple-element.44.refs_3_, ...), custom_call_target="tpu_custom_call", output_to_operand_aliasing={{0}: (3, {})} | custom-call | bytes 4722720 | tf_op jit(solution)/shard_map/pallas_call | solution.py:49
  39.9 3.1 %collective-permute-done.11.refs_1_ = bf16[16,2560]{1,0:T(8,128)(2,1)S(1)} collective-permute-done((bf16[16,2560]{1,0:T(8,128)(2,1)S(1)}, bf16[16,2560]{1,0:T(8,128)(2,1)S(1)}, u32[]{:S(2)}, u32[]{:S(2)}) %collective-permute-start.11) | collective-permute-done | bytes 81952 | tf_op jit(solution)/shard_map/ppermute | solution.py:27
  43.2 1.4 %collective-permute-done.16.refs_1_ = bf16[32,2560]{1,0:T(8,128)(2,1)S(1)} collective-permute-done((bf16[32,2560]{1,0:T(8,128)(2,1)S(1)}, bf16[32,2560]{1,0:T(8,128)(2,1)S(1)}, u32[]{:S(2)}, u32[]{:S(2)}) %collective-permute-start.16) | collective-permute-done | bytes 163872 | tf_op jit(solution)/shard_map/ppermute | solution.py:20
  44.6 0.9 %shard_map.108 = f32[64,2560]{1,0:T(8,128)} custom-call(bf16[32,2560]{1,0:T(8,128)(2,1)S(1)} %shard_map.107.refs_0_.refs_2_, bf16[32,2560]{1,0:T(8,128)(2,1)S(1)} %collective-permute-done.16.refs_1_, bf16[32,2560]{1,0:T(8,128)(2,1)S(1)} %shard_map.107.refs_0_.refs_2_), custom_call_target="tpu_custom_call" | custom-call | bytes 983040 | tf_op jit(solution)/shard_map/pallas_call | solution.py:49
  (29 shorter events, 1.9 us)
Async XLA Ops:
  0.6 14.8 %copy-start = (bf16[512,512]{1,0:T(8,128)(2,1)S(1)}, bf16[512,512]{1,0:T(8,128)(2,1)}, u32[]{:S(2)}) copy-start(bf16[512,512]{1,0:T(8,128)(2,1)} %refs_1_.4) | copy-start | bytes 1572868
  0.6 14.8 %collective-permute-start.5 = (bf16[2560,512]{1,0:T(8,128)(2,1)}, bf16[2560,512]{1,0:T(8,128)(2,1)S(1)}, u32[]{:S(2)}, u32[]{:S(2)}) collective-permute-start(bf16[2560,512]{1,0:T(8,128)(2,1)} %refs_1_.5), channel_id=1, source_target_pairs={{0,1},{1,0},{2,3},{3,2},{4,5},{5,4},{6,7},{7,6},{8,9},{9,8},{10,11... | collective-permute-start | bytes 7864328 | tf_op jit(solution)/shard_map/ppermute | solution.py:20
  2.5 13.0 %collective-permute-start = (bf16[256,512]{1,0:T(8,128)(2,1)S(1)}, bf16[256,512]{1,0:T(8,128)(2,1)S(1)}, u32[]{:S(2)}, u32[]{:S(2)}) collective-permute-start(bf16[256,512]{1,0:T(8,128)(2,1)S(1)} %get-tuple-element.25), channel_id=1, source_target_pairs={{0,2},{2,0},{1,3},{3,1},{4,6},{6,4},{5,7},{7,5},{8,10},{10,8},{9,1... | collective-permute-start | bytes 786440 | tf_op jit(solution)/shard_map/ppermute | solution.py:20
  5.1 4.4 %collective-permute-start.1 = (bf16[64,512]{1,0:T(8,128)(2,1)S(1)}, bf16[64,512]{1,0:T(8,128)(2,1)S(1)}, u32[]{:S(2)}, u32[]{:S(2)}) collective-permute-start(bf16[64,512]{1,0:T(8,128)(2,1)S(1)} %get-tuple-element.26), channel_id=1, source_target_pairs={{0,4},{1,5},{4,0},{5,1},{8,12},{9,13},{12,8},{13,9},{2,6},{3,7},{6... | collective-permute-start | bytes 196616 | tf_op jit(solution)/shard_map/ppermute | solution.py:27
  6.7 7.5 %collective-permute-start.3 = (bf16[64,512]{1,0:T(8,128)(2,1)S(1)}, bf16[64,512]{1,0:T(8,128)(2,1)S(1)}, u32[]{:S(2)}, u32[]{:S(2)}) collective-permute-start(bf16[64,512]{1,0:T(8,128)(2,1)S(1)} %get-tuple-element.30), channel_id=1, source_target_pairs={{0,8},{1,9},{4,12},{5,13},{8,0},{9,1},{12,4},{13,5},{2,10},{3,11},... | collective-permute-start | bytes 196616 | tf_op jit(solution)/shard_map/ppermute | solution.py:27
  9.2 6.2 %collective-permute-start.4 = (bf16[64,512]{1,0:T(8,128)(2,1)S(1)}, bf16[64,512]{1,0:T(8,128)(2,1)S(1)}, u32[]{:S(2)}, u32[]{:S(2)}) collective-permute-start(bf16[64,512]{1,0:T(8,128)(2,1)S(1)} %get-tuple-element.31), channel_id=1, source_target_pairs={{0,12},{1,13},{4,8},{5,9},{8,4},{9,5},{12,0},{13,1},{2,14},{3,15},... | collective-permute-start | bytes 196616 | tf_op jit(solution)/shard_map/ppermute | solution.py:27
  11.8 5.2 %collective-permute-start.2 = (f32[64,512]{1,0:T(8,128)S(1)}, f32[64,512]{1,0:T(8,128)S(1)}, u32[]{:S(2)}, u32[]{:S(2)}) collective-permute-start(f32[64,512]{1,0:T(8,128)S(1)} %get-tuple-element.27.refs_6_.refs_1_), channel_id=1, source_target_pairs={{0,2},{2,0},{1,3},{3,1},{4,6},{6,4},{5,7},{7,5},{8,10},{10,8},{9,1... | collective-permute-start | bytes 393224 | tf_op jit(solution)/shard_map/ppermute | solution.py:20
  15.7 5.0 %collective-permute-start.7 = (f32[64,512]{1,0:T(8,128)S(1)}, f32[64,512]{1,0:T(8,128)S(1)}, u32[]{:S(2)}, u32[]{:S(2)}) collective-permute-start(f32[64,512]{1,0:T(8,128)S(1)} %shard_map.96.refs_4_.refs_1_), channel_id=1, source_target_pairs={{0,2},{2,0},{1,3},{3,1},{4,6},{6,4},{5,7},{7,5},{8,10},{10,8},{9,1... | collective-permute-start | bytes 393224 | tf_op jit(solution)/shard_map/ppermute | solution.py:20
  20.7 12.9 %copy-start.1 = (bf16[2560,512]{1,0:T(8,128)(2,1)S(1)}, bf16[2560,512]{1,0:T(8,128)(2,1)}, u32[]{:S(2)}) copy-start(bf16[2560,512]{1,0:T(8,128)(2,1)} %refs_1_.5) | copy-start | bytes 7864324
  21.3 2.6 %collective-permute-start.8 = (f32[32,2560]{1,0:T(8,128)S(1)}, f32[32,2560]{1,0:T(8,128)S(1)}, u32[]{:S(2)}, u32[]{:S(2)}) collective-permute-start(f32[32,2560]{1,0:T(8,128)S(1)} %get-tuple-element.37), channel_id=1, source_target_pairs={{0,1},{1,0},{2,3},{3,2},{4,5},{5,4},{6,7},{7,6},{8,9},{9,8},{10,11... | collective-permute-start | bytes 983048 | tf_op jit(solution)/shard_map/ppermute | solution.py:20
  21.4 12.1 %collective-permute-start.6 = (bf16[256,512]{1,0:T(8,128)(2,1)S(1)}, bf16[256,512]{1,0:T(8,128)(2,1)S(1)}, u32[]{:S(2)}, u32[]{:S(2)}) collective-permute-start(bf16[256,512]{1,0:T(8,128)(2,1)S(1)} %get-tuple-element.32), channel_id=1, source_target_pairs={{0,2},{2,0},{1,3},{3,1},{4,6},{6,4},{5,7},{7,5},{8,10},{10,8},{9,1... | collective-permute-start | bytes 786440 | tf_op jit(solution)/shard_map/ppermute | solution.py:20
  22.0 6.6 %collective-permute-start.12 = (bf16[1,64,512]{2,1,0:T(8,128)(2,1)S(1)}, bf16[1,64,512]{2,1,0:T(8,128)(2,1)S(1)}, u32[]{:S(2)}, u32[]{:S(2)}) collective-permute-start(bf16[1,64,512]{2,1,0:T(8,128)(2,1)S(1)} %get-tuple-element.34.refs_0_), channel_id=1, source_target_pairs={{0,8},{1,9},{4,12},{5,13},{8,0},{9,1},{12,4},{13,5},{2,10},{3,11},... | collective-permute-start | bytes 196616 | tf_op jit(solution)/shard_map/ppermute | solution.py:27
  24.0 5.8 %collective-permute-start.9 = (bf16[16,2560]{1,0:T(8,128)(2,1)S(1)}, bf16[16,2560]{1,0:T(8,128)(2,1)S(1)}, u32[]{:S(2)}, u32[]{:S(2)}) collective-permute-start(bf16[16,2560]{1,0:T(8,128)(2,1)S(1)} %get-tuple-element.39), channel_id=1, source_target_pairs={{0,4},{1,5},{4,0},{5,1},{8,12},{9,13},{12,8},{13,9},{2,6},{3,7},{6... | collective-permute-start | bytes 245768 | tf_op jit(solution)/shard_map/ppermute | solution.py:27
  25.9 6.2 %collective-permute-start.13 = (bf16[1,64,512]{2,1,0:T(8,128)(2,1)S(1)}, bf16[1,64,512]{2,1,0:T(8,128)(2,1)S(1)}, u32[]{:S(2)}, u32[]{:S(2)}) collective-permute-start(bf16[1,64,512]{2,1,0:T(8,128)(2,1)S(1)} %get-tuple-element.34.refs_0_), channel_id=1, source_target_pairs={{0,4},{1,5},{4,0},{5,1},{8,12},{9,13},{12,8},{13,9},{2,6},{3,7},{6... | collective-permute-start | bytes 196616 | tf_op jit(solution)/shard_map/ppermute | solution.py:27
  28.6 4.8 %collective-permute-start.14 = (bf16[1,64,512]{2,1,0:T(8,128)(2,1)S(1)}, bf16[1,64,512]{2,1,0:T(8,128)(2,1)S(1)}, u32[]{:S(2)}, u32[]{:S(2)}) collective-permute-start(bf16[1,64,512]{2,1,0:T(8,128)(2,1)S(1)} %collective-permute-done.12.refs_1_), channel_id=1, source_target_pairs={{0,4},{1,5},{4,0},{5,1},{8,12},{9,13},{12,8},{13,9},{2,6},{3,7},{6... | collective-permute-start | bytes 196616 | tf_op jit(solution)/shard_map/ppermute | solution.py:27
  29.9 8.3 %collective-permute-start.10 = (bf16[16,2560]{1,0:T(8,128)(2,1)S(1)}, bf16[16,2560]{1,0:T(8,128)(2,1)S(1)}, u32[]{:S(2)}, u32[]{:S(2)}) collective-permute-start(bf16[16,2560]{1,0:T(8,128)(2,1)S(1)} %shard_map.101.refs_4_.refs_5_.refs_0_), channel_id=1, source_target_pairs={{0,8},{1,9},{4,12},{5,13},{8,0},{9,1},{12,4},{13,5},{2,10},{3,11},... | collective-permute-start | bytes 245768 | tf_op jit(solution)/shard_map/ppermute | solution.py:27
  33.5 4.8 %collective-permute-start.15 = (bf16[4,64,512]{2,1,0:T(8,128)(2,1)S(1)}, bf16[4,64,512]{2,1,0:T(8,128)(2,1)S(1)}, u32[]{:S(2)}, u32[]{:S(2)}) collective-permute-start(bf16[4,64,512]{2,1,0:T(8,128)(2,1)S(1)} %shard_map.105.refs_1_), channel_id=1, source_target_pairs={{0,1},{1,0},{2,3},{3,2},{4,5},{5,4},{6,7},{7,6},{8,9},{9,8},{10,11... | collective-permute-start | bytes 786440 | tf_op jit(solution)/shard_map/ppermute | solution.py:20
  38.2 4.9 %collective-permute-start.11 = (bf16[16,2560]{1,0:T(8,128)(2,1)S(1)}, bf16[16,2560]{1,0:T(8,128)(2,1)S(1)}, u32[]{:S(2)}, u32[]{:S(2)}) collective-permute-start(bf16[16,2560]{1,0:T(8,128)(2,1)S(1)} %shard_map.104.refs_4_.refs_0_), channel_id=1, source_target_pairs={{0,4},{1,5},{4,0},{5,1},{8,12},{9,13},{12,8},{13,9},{2,6},{3,7},{6... | collective-permute-start | bytes 245768 | tf_op jit(solution)/shard_map/ppermute | solution.py:27
  43.1 1.5 %collective-permute-start.16 = (bf16[32,2560]{1,0:T(8,128)(2,1)S(1)}, bf16[32,2560]{1,0:T(8,128)(2,1)S(1)}, u32[]{:S(2)}, u32[]{:S(2)}) collective-permute-start(bf16[32,2560]{1,0:T(8,128)(2,1)S(1)} %shard_map.107.refs_0_.refs_2_), channel_id=1, source_target_pairs={{0,1},{1,0},{2,3},{3,2},{4,5},{5,4},{6,7},{7,6},{8,9},{9,8},{10,11... | collective-permute-start | bytes 491528 | tf_op jit(solution)/shard_map/ppermute | solution.py:20

commit v6 on v4

--- a/solution.py
+++ b/solution.py
@@ -8,6 +8,9 @@
 adapter_scale = 2.0
 f32 = jnp.float32
 bf16 = jnp.bfloat16
+
+busy = 10**10
+brief = 3 * 10**9
 
 anywhere = pl.BlockSpec(memory_space=pl.ANY)
 in_hbm = pl.BlockSpec(memory_space=pltpu.HBM)
@@ -260,7 +263,11 @@
         out[rows:] = jnp.where(upper, one, two).astype(bf16)
 
     return call(
-        body, [mine, arrived], [in_vmem] * 2, [shape_of((2 * rows, features), bf16)]
+        body,
+        [mine, arrived],
+        [in_vmem] * 2,
+        [shape_of((2 * rows, features), bf16)],
+        flops=busy,
     )[0]
 
 
@@ -281,7 +288,7 @@
     )[0]
 
 
-def stack(pieces, after=()):
+def stack(pieces, after=(), flops=0):
     depths = [piece.shape[0] for piece in pieces]
 
     def body(*refs):
@@ -296,6 +303,7 @@
         [in_vmem] * len(pieces),
         [shape_of((sum(depths),) + pieces[0].shape[1:], bf16)],
         after=after,
+        flops=flops,
     )[0]
 
 
@@ -317,6 +325,7 @@
         out_specs=[in_hbm, in_vmem],
         after=after,
         scratch_shapes=[pltpu.VMEM(dims[1:], f32), pltpu.SemaphoreType.DMA((dims[0],))],
+        flops=busy,
     )
 
 
@@ -472,29 +481,36 @@
     late_grads = [shift(late, "tp", step) for step in tp_steps]
     bits = [1 << i for i in range(own_count.bit_length() - 1)]
     terms, pattern = [near], [0]
-    for bit in reversed(bits):
+    for bit in reversed(bits[1:]):
         terms = terms + [swap(term, bit, 0) for term in terms]
         pattern = pattern + [step ^ bit for step in pattern]
+    nearby = [swap(near, 1, 0)] if bits else []
 
     back, keep, send = shared_terms(lengths, parts, tokens, scale, [near])
     pieces = [keep, shift(send, "sub", 1)]
-
-    mark = keep
+    met = stack(terms[1:] + nearby, flops=brief) if bits else near
+
+    mark = met
     for bit in bits[:-1]:
-        stays, leaves = halve(pieces, bit)
+        stays, leaves = halve(pieces, bit, [mark])
         pieces = [stays, swap(leaves, bit, 0)]
         mark = leaves
     cleaned, mark = clean((per_owner,) + near.shape[1:], [mark])
     total = add_up(pieces, [mark])
+    relays = [total]
+    if bits:
+        relays = [stack([term], [total]) for term in terms[1:]]
+        terms = terms + nearby + [swap(relay, 1, 0) for relay in relays]
+        pattern = pattern + [step ^ 1 for step in pattern]
     kept = arrange(lengths, grad_output, list(zip(early_grads, late_grads)), [total])
-    input_gradient, mark = input_side(kept, frozen_value, frozen_other, back, down, [total])
-    near = stack(terms, [total])
+    input_gradient, mark = input_side(kept, frozen_value, frozen_other, back, down, relays)
+    near = stack(terms, [mark])
+    if bits:
+        total = add_up([total, swap(total, bits[-1], 0)], [near])
     far = shift(near, "sub", 1)
-    if bits:
-        total = add_up([total, swap(total, bits[-1], 0)], [mark])
-    grad_heads, mark = place_terms(adapter_ids, near, far, pattern, cleaned, [total])
     for bit in reversed(bits[:-1]):
         total = rejoin(total, swap(total, bit, 0), bit)
+    grad_heads, mark = place_terms(adapter_ids, near, far, pattern, cleaned, [total])
     shared_down_gradient = join_shares(total, shift(total, "sub", 1), [mark]).T
     return (input_gradient, shared_down_gradient, grad_heads)
 

time: 46.1 us -> 45.1 us (0.978)
  waiting for transfers between devices: 14.1 us -> 10.4 us
  starting transfers between devices: 16.9 us -> 19.6 us
    ppermute x8, waiting for transfers between devices: 3.57 us -> 0.02 us  [shift(): lax.ppermute(x, axis, [(i, (i + step) % count) for i in range(count)])]
    ppermute x9, starting transfers between devices: 12 us -> 14.1 us  [swap(): lax.ppermute(x, ('own', 'sub'), [(i, i ^ other) for i in range(whole)])]
    ppermute x8, starting transfers between devices: 4.93 us -> 5.49 us  [shift(): lax.ppermute(x, axis, [(i, (i + step) % count) for i in range(count)])]
    pallas_call x15 -> x17, Pallas kernels: 13.4 us -> 13.3 us  [call(): pl.pallas_call(kernel, out_shape=outs, in_specs=list(specs) + [anywhere]...]
  transfers between devices with their start and end apart: 17 -> 17, of which waited for: 5 -> 5; matrix products, arithmetic and copies ran while one was open for 0% -> 0% of each run, Pallas kernels for 26% -> 28%
where the time goes in v6:
time: 45.1 us; the launch traced here: 44.8 us
  starting transfers between devices  19.6 us (43%)
  Pallas kernels  13.3 us (29%)
  waiting for transfers between devices  10.4 us (23%)
  between operations  1.48 us (3%)
    ppermute x9, starting transfers between devices, swap(): lax.ppermute(x, ('own', 'sub'), [(i, i ^ other) for i in range(whole)])  14.1 us
    pallas_call x17, Pallas kernels, call(): pl.pallas_call(kernel, out_shape=outs, in_specs=list(specs) + [anywhere]...  13.3 us
    ppermute x9, waiting for transfers between devices, swap(): lax.ppermute(x, ('own', 'sub'), [(i, i ^ other) for i in range(whole)])  10.4 us
    ppermute x8, starting transfers between devices, shift(): lax.ppermute(x, axis, [(i, (i + step) % count) for i in range(count)])  5.49 us
  transfers between devices with their start and end apart: 17, of which 5 were waited for; matrix products, arithmetic and copies ran while one was open for 0% of the time, Pallas kernels for 28%

profile of v6, /device:TPU:0, one launch (start us, length us, event | category | flops | bytes accessed | tf_op | source)
XLA Modules:
  0.0 44.8 jit_solution(9730956352598991077)
XLA Ops:
  0.6 0.5 %collective-permute-start.5 = (bf16[2560,512]{1,0:T(8,128)(2,1)}, bf16[2560,512]{1,0:T(8,128)(2,1)S(1)}, u32[]{:S(2)}, u32[]{:S(2)}) collective-permute-start(bf16[2560,512]{1,0:T(8,128)(2,1)} %refs_1_.5), channel_id=1, source_target_pairs={{0,1},{1,0},{2,3},{3,2},{4,5},{5,4},{6,7},{7,6},{8,9},{9,8},{10,11... | collective-permute-start | bytes 7864328 | tf_op jit(solution)/shard_map/ppermute | solution.py:23
  1.2 1.3 %shard_map.94 = (bf16[64,512]{1,0:T(8,128)(2,1)S(1)}, bf16[64,512]{1,0:T(8,128)(2,1)S(1)}, bf16[64,512]{1,0:T(8,128)(2,1)S(1)}, bf16[64,512]{1,0:T(8,128)(2,1)S(...) custom-call(s32[8]{0:T(128)} %refs_0_.8, bf16[16,64,512]{2,1,0:T(8,128)(2,1)} %refs_1_.3, bf16[512,512]{1,0:T(8,128)(2,1)} %refs_1_.4), custom_call_target="tpu_custom_call" | custom-call | bytes 2101280 | tf_op jit(solution)/shard_map/pallas_call | solution.py:52
  2.5 2.6 %collective-permute-start = (bf16[256,512]{1,0:T(8,128)(2,1)S(1)}, bf16[256,512]{1,0:T(8,128)(2,1)S(1)}, u32[]{:S(2)}, u32[]{:S(2)}) collective-permute-start(bf16[256,512]{1,0:T(8,128)(2,1)S(1)} %get-tuple-element.25), channel_id=1, source_target_pairs={{0,2},{2,0},{1,3},{3,1},{4,6},{6,4},{5,7},{7,5},{8,10},{10,8},{9,1... | collective-permute-start | bytes 786440 | tf_op jit(solution)/shard_map/ppermute | solution.py:23
  5.1 1.6 %collective-permute-start.1 = (bf16[64,512]{1,0:T(8,128)(2,1)S(1)}, bf16[64,512]{1,0:T(8,128)(2,1)S(1)}, u32[]{:S(2)}, u32[]{:S(2)}) collective-permute-start(bf16[64,512]{1,0:T(8,128)(2,1)S(1)} %get-tuple-element.26), channel_id=1, source_target_pairs={{0,4},{1,5},{4,0},{5,1},{8,12},{9,13},{12,8},{13,9},{2,6},{3,7},{6... | collective-permute-start | bytes 196616 | tf_op jit(solution)/shard_map/ppermute | solution.py:30
  6.7 2.6 %collective-permute-start.3 = (bf16[64,512]{1,0:T(8,128)(2,1)S(1)}, bf16[64,512]{1,0:T(8,128)(2,1)S(1)}, u32[]{:S(2)}, u32[]{:S(2)}) collective-permute-start(bf16[64,512]{1,0:T(8,128)(2,1)S(1)} %get-tuple-element.30), channel_id=1, source_target_pairs={{0,8},{1,9},{4,12},{5,13},{8,0},{9,1},{12,4},{13,5},{2,10},{3,11},... | collective-permute-start | bytes 196616 | tf_op jit(solution)/shard_map/ppermute | solution.py:30
  9.5 2.3 %shard_map.95 = (f32[64,512]{1,0:T(8,128)S(1)}, bf16[512,2560]{1,0:T(8,128)(2,1)S(1)}, bf16[64,2560]{1,0:T(8,128)(2,1)S(1)}) custom-call(bf16[512,2560]{1,0:T(8,128)(2,1)} %refs_0_.7, bf16[64,2560]{1,0:T(8,128)(2,1)} %bitcast.3, bf16[64,512]{1,0:T(8,128)(2,1)S(1)} %collective-permute-done.1.refs_2_), custom_call_target="tpu_custom_call" | custom-call | flops 167772160 | bytes 6029312 | tf_op jit(solution)/shard_map/pallas_call | solution.py:52
  11.8 0.4 collective-permute-start.2
  12.2 2.0 %collective-permute-done.3.refs_3_ = bf16[64,512]{1,0:T(8,128)(2,1)S(1)} collective-permute-done((bf16[64,512]{1,0:T(8,128)(2,1)S(1)}, bf16[64,512]{1,0:T(8,128)(2,1)S(1)}, u32[]{:S(2)}, u32[]{:S(2)}) %collective-permute-start.3) | collective-permute-done | bytes 65568 | tf_op jit(solution)/shard_map/ppermute | solution.py:30
  14.2 1.2 %collective-permute-done.4.refs_4_ = bf16[64,512]{1,0:T(8,128)(2,1)S(1)} collective-permute-done((bf16[64,512]{1,0:T(8,128)(2,1)S(1)}, bf16[64,512]{1,0:T(8,128)(2,1)S(1)}, u32[]{:S(2)}, u32[]{:S(2)}) %collective-permute-start.4) | collective-permute-done | bytes 65568 | tf_op jit(solution)/shard_map/ppermute | solution.py:30
  15.7 0.6 %collective-permute-start.7 = (f32[64,512]{1,0:T(8,128)S(1)}, f32[64,512]{1,0:T(8,128)S(1)}, u32[]{:S(2)}, u32[]{:S(2)}) collective-permute-start(f32[64,512]{1,0:T(8,128)S(1)} %shard_map.96.refs_4_.refs_1_), channel_id=1, source_target_pairs={{0,2},{2,0},{1,3},{3,1},{4,6},{6,4},{5,7},{7,5},{8,10},{10,8},{9,1... | collective-permute-start | bytes 393224 | tf_op jit(solution)/shard_map/ppermute | solution.py:23
  17.2 4.0 %collective-permute-start.9 = (bf16[1,64,512]{2,1,0:T(8,128)(2,1)S(1)}, bf16[1,64,512]{2,1,0:T(8,128)(2,1)S(1)}, u32[]{:S(2)}, u32[]{:S(2)}) collective-permute-start(bf16[1,64,512]{2,1,0:T(8,128)(2,1)S(1)} %get-tuple-element.34.refs_4_.refs_0_), channel_id=1, source_target_pairs={{0,8},{1,9},{4,12},{5,13},{8,0},{9,1},{12,4},{13,5},{2,10},{3,11},... | collective-permute-start | bytes 196616 | tf_op jit(solution)/shard_map/ppermute | solution.py:30
  21.2 1.2 %collective-permute-start.10 = (bf16[1,64,512]{2,1,0:T(8,128)(2,1)S(1)}, bf16[1,64,512]{2,1,0:T(8,128)(2,1)S(1)}, u32[]{:S(2)}, u32[]{:S(2)}) collective-permute-start(bf16[1,64,512]{2,1,0:T(8,128)(2,1)S(1)} %get-tuple-element.34.refs_4_.refs_0_), channel_id=1, source_target_pairs={{0,4},{1,5},{4,0},{5,1},{8,12},{9,13},{12,8},{13,9},{2,6},{3,7},{6... | collective-permute-start | bytes 196616 | tf_op jit(solution)/shard_map/ppermute | solution.py:30
  22.4 0.6 %shard_map.98 = (bf16[64,512]{1,0:T(8,128)(2,1)S(1)}, f32[32,2560]{1,0:T(8,128)S(1)}, f32[32,2560]{1,0:T(8,128)S(1)}) custom-call(s32[1]{0:T(128)S(6)} %copy.12.refs_0_, f32[64,512]{1,0:T(8,128)S(1)} %shard_map.96.refs_4_.refs_1_, f32[64,512]{1,0:T(8,128)S(1)} %collective-permute-done.7.refs_2_, bf16[512,2560]{1,0:T(8,128)(2,1)S(1)} %get-tuple-element.33.refs_3_, ...), custom_call_target="tpu_custom_call" | custom-call | flops 167772160 | bytes 3604484 | tf_op jit(solution)/shard_map/pallas_call | solution.py:52
  23.1 1.2 %collective-permute-start.6 = (bf16[256,512]{1,0:T(8,128)(2,1)S(1)}, bf16[256,512]{1,0:T(8,128)(2,1)S(1)}, u32[]{:S(2)}, u32[]{:S(2)}) collective-permute-start(bf16[256,512]{1,0:T(8,128)(2,1)S(1)} %get-tuple-element.32), channel_id=1, source_target_pairs={{0,2},{2,0},{1,3},{3,1},{4,6},{6,4},{5,7},{7,5},{8,10},{10,8},{9,1... | collective-permute-start | bytes 786440 | tf_op jit(solution)/shard_map/ppermute | solution.py:23
  24.3 1.1 %collective-permute-done.10.refs_1_.refs_2_ = bf16[1,64,512]{2,1,0:T(8,128)(2,1)S(1)} collective-permute-done((bf16[1,64,512]{2,1,0:T(8,128)(2,1)S(1)}, bf16[1,64,512]{2,1,0:T(8,128)(2,1)S(1)}, u32[]{:S(2)}, u32[]{:S(2)}) %collective-permute-start.10) | collective-permute-done | bytes 65568 | tf_op jit(solution)/shard_map/ppermute | solution.py:30
  25.6 1.3 %collective-permute-start.11 = (bf16[16,2560]{1,0:T(8,128)(2,1)S(1)}, bf16[16,2560]{1,0:T(8,128)(2,1)S(1)}, u32[]{:S(2)}, u32[]{:S(2)}) collective-permute-start(bf16[16,2560]{1,0:T(8,128)(2,1)S(1)} %get-tuple-element.38.refs_0_), channel_id=1, source_target_pairs={{0,4},{1,5},{4,0},{5,1},{8,12},{9,13},{12,8},{13,9},{2,6},{3,7},{6... | collective-permute-start | bytes 245768 | tf_op jit(solution)/shard_map/ppermute | solution.py:30
  26.8 1.4 %shard_map.101 = (f32[16,64,512]{2,1,0:T(8,128)}, f32[8,128]{1,0:T(8,128)S(1)}) custom-call(bf16[16,2560]{1,0:T(8,128)(2,1)S(1)} %get-tuple-element.38.refs_0_), custom_call_target="tpu_custom_call" | custom-call | flops 10000000000 | bytes 2101248 | tf_op jit(solution)/shard_map/pallas_call | solution.py:52
  28.3 1.8 %collective-permute-done.11.refs_1_ = bf16[16,2560]{1,0:T(8,128)(2,1)S(1)} collective-permute-done((bf16[16,2560]{1,0:T(8,128)(2,1)S(1)}, bf16[16,2560]{1,0:T(8,128)(2,1)S(1)}, u32[]{:S(2)}, u32[]{:S(2)}) %collective-permute-start.11) | collective-permute-done | bytes 81952 | tf_op jit(solution)/shard_map/ppermute | solution.py:30
  30.1 1.1 %collective-permute-start.12 = (bf16[16,2560]{1,0:T(8,128)(2,1)S(1)}, bf16[16,2560]{1,0:T(8,128)(2,1)S(1)}, u32[]{:S(2)}, u32[]{:S(2)}) collective-permute-start(bf16[16,2560]{1,0:T(8,128)(2,1)S(1)} %shard_map.102.refs_4_.refs_1_.refs_0_), channel_id=1, source_target_pairs={{0,8},{1,9},{4,12},{5,13},{8,0},{9,1},{12,4},{13,5},{2,10},{3,11},... | collective-permute-start | bytes 245768 | tf_op jit(solution)/shard_map/ppermute | solution.py:30
  31.2 1.8 %collective-permute-start.13 = (bf16[1,64,512]{2,1,0:T(8,128)(2,1)S(1)}, bf16[1,64,512]{2,1,0:T(8,128)(2,1)S(1)}, u32[]{:S(2)}, u32[]{:S(2)}) collective-permute-start(bf16[1,64,512]{2,1,0:T(8,128)(2,1)S(1)} %shard_map.104.refs_5_), channel_id=1, source_target_pairs={{0,4},{1,5},{4,0},{5,1},{8,12},{9,13},{12,8},{13,9},{2,6},{3,7},{6... | collective-permute-start | bytes 196616 | tf_op jit(solution)/shard_map/ppermute | solution.py:30
  33.1 4.4 %shard_map.105 = (bf16[512,2560]{1,0:T(8,128)(2,1)}, f32[8,128]{1,0:T(8,128)S(1)}) custom-call(bf16[512,1024]{1,0:T(8,128)(2,1)S(1)} %shard_map.103.refs_0_, bf16[2560,512]{1,0:T(8,128)(2,1)S(1)} %copy-done.1, bf16[2560,512]{1,0:T(8,128)(2,1)S(1)} %collective-permute-done.5.refs_7_.refs_2_, bf16[64,512]{1,0:T(8,128)(2,1)S(1)} %get-tuple-element.40.refs_3_, ...), custom_call_target="tpu_custom_call" | custom-call | flops 2852126720 | bytes 9310208 | tf_op jit(solution)/shard_map/pallas_call | solution.py:52
  37.9 4.2 %collective-permute-done.14.refs_1_ = bf16[16,2560]{1,0:T(8,128)(2,1)S(1)} collective-permute-done((bf16[16,2560]{1,0:T(8,128)(2,1)S(1)}, bf16[16,2560]{1,0:T(8,128)(2,1)S(1)}, u32[]{:S(2)}, u32[]{:S(2)}) %collective-permute-start.14) | collective-permute-done | bytes 81952 | tf_op jit(solution)/shard_map/ppermute | solution.py:30
  42.3 1.6 %shard_map.109 = (f32[16,64,512]{2,1,0:T(8,128)}, f32[8,128]{1,0:T(8,128)S(1)}) custom-call(s32[8]{0:T(128)} %refs_0_.8, bf16[4,64,512]{2,1,0:T(8,128)(2,1)S(1)} %shard_map.106.refs_2_.refs_1_, bf16[4,64,512]{2,1,0:T(8,128)(2,1)S(1)} %collective-permute-done.16.refs_2_, f32[16,64,512]{2,1,0:T(8,128)} %get-tuple-element.44.refs_3_, ...), custom_call_target="tpu_custom_call", output_to_operand_aliasing={{0}: (3, {})} | custom-call | bytes 4722720 | tf_op jit(solution)/shard_map/pallas_call | solution.py:52
  43.9 0.9 %shard_map.110 = f32[64,2560]{1,0:T(8,128)} custom-call(bf16[32,2560]{1,0:T(8,128)(2,1)S(1)} %shard_map.108.refs_4_.refs_0_, bf16[32,2560]{1,0:T(8,128)(2,1)S(1)} %collective-permute-done.15.refs_1_, f32[8,128]{1,0:T(8,128)S(1)} %get-tuple-element.45.refs_2_), custom_call_target="tpu_custom_call" | custom-call | bytes 983040 | tf_op jit(solution)/shard_map/pallas_call | solution.py:52
  (31 shorter events, 1.5 us)
Async XLA Ops:
  0.6 14.8 %copy-start = (bf16[512,512]{1,0:T(8,128)(2,1)S(1)}, bf16[512,512]{1,0:T(8,128)(2,1)}, u32[]{:S(2)}) copy-start(bf16[512,512]{1,0:T(8,128)(2,1)} %refs_1_.4) | copy-start | bytes 1572868
  0.6 14.8 %collective-permute-start.5 = (bf16[2560,512]{1,0:T(8,128)(2,1)}, bf16[2560,512]{1,0:T(8,128)(2,1)S(1)}, u32[]{:S(2)}, u32[]{:S(2)}) collective-permute-start(bf16[2560,512]{1,0:T(8,128)(2,1)} %refs_1_.5), channel_id=1, source_target_pairs={{0,1},{1,0},{2,3},{3,2},{4,5},{5,4},{6,7},{7,6},{8,9},{9,8},{10,11... | collective-permute-start | bytes 7864328 | tf_op jit(solution)/shard_map/ppermute | solution.py:23
  2.5 13.0 %collective-permute-start = (bf16[256,512]{1,0:T(8,128)(2,1)S(1)}, bf16[256,512]{1,0:T(8,128)(2,1)S(1)}, u32[]{:S(2)}, u32[]{:S(2)}) collective-permute-start(bf16[256,512]{1,0:T(8,128)(2,1)S(1)} %get-tuple-element.25), channel_id=1, source_target_pairs={{0,2},{2,0},{1,3},{3,1},{4,6},{6,4},{5,7},{7,5},{8,10},{10,8},{9,1... | collective-permute-start | bytes 786440 | tf_op jit(solution)/shard_map/ppermute | solution.py:23
  5.1 4.4 %collective-permute-start.1 = (bf16[64,512]{1,0:T(8,128)(2,1)S(1)}, bf16[64,512]{1,0:T(8,128)(2,1)S(1)}, u32[]{:S(2)}, u32[]{:S(2)}) collective-permute-start(bf16[64,512]{1,0:T(8,128)(2,1)S(1)} %get-tuple-element.26), channel_id=1, source_target_pairs={{0,4},{1,5},{4,0},{5,1},{8,12},{9,13},{12,8},{13,9},{2,6},{3,7},{6... | collective-permute-start | bytes 196616 | tf_op jit(solution)/shard_map/ppermute | solution.py:30
  6.7 7.5 %collective-permute-start.3 = (bf16[64,512]{1,0:T(8,128)(2,1)S(1)}, bf16[64,512]{1,0:T(8,128)(2,1)S(1)}, u32[]{:S(2)}, u32[]{:S(2)}) collective-permute-start(bf16[64,512]{1,0:T(8,128)(2,1)S(1)} %get-tuple-element.30), channel_id=1, source_target_pairs={{0,8},{1,9},{4,12},{5,13},{8,0},{9,1},{12,4},{13,5},{2,10},{3,11},... | collective-permute-start | bytes 196616 | tf_op jit(solution)/shard_map/ppermute | solution.py:30
  9.2 6.2 %collective-permute-start.4 = (bf16[64,512]{1,0:T(8,128)(2,1)S(1)}, bf16[64,512]{1,0:T(8,128)(2,1)S(1)}, u32[]{:S(2)}, u32[]{:S(2)}) collective-permute-start(bf16[64,512]{1,0:T(8,128)(2,1)S(1)} %get-tuple-element.31), channel_id=1, source_target_pairs={{0,12},{1,13},{4,8},{5,9},{8,4},{9,5},{12,0},{13,1},{2,14},{3,15},... | collective-permute-start | bytes 196616 | tf_op jit(solution)/shard_map/ppermute | solution.py:30
  11.8 5.2 %collective-permute-start.2 = (f32[64,512]{1,0:T(8,128)S(1)}, f32[64,512]{1,0:T(8,128)S(1)}, u32[]{:S(2)}, u32[]{:S(2)}) collective-permute-start(f32[64,512]{1,0:T(8,128)S(1)} %get-tuple-element.27.refs_6_.refs_1_), channel_id=1, source_target_pairs={{0,2},{2,0},{1,3},{3,1},{4,6},{6,4},{5,7},{7,5},{8,10},{10,8},{9,1... | collective-permute-start | bytes 393224 | tf_op jit(solution)/shard_map/ppermute | solution.py:23
  15.7 6.7 %collective-permute-start.7 = (f32[64,512]{1,0:T(8,128)S(1)}, f32[64,512]{1,0:T(8,128)S(1)}, u32[]{:S(2)}, u32[]{:S(2)}) collective-permute-start(f32[64,512]{1,0:T(8,128)S(1)} %shard_map.96.refs_4_.refs_1_), channel_id=1, source_target_pairs={{0,2},{2,0},{1,3},{3,1},{4,6},{6,4},{5,7},{7,5},{8,10},{10,8},{9,1... | collective-permute-start | bytes 393224 | tf_op jit(solution)/shard_map/ppermute | solution.py:23
  17.2 7.2 %collective-permute-start.9 = (bf16[1,64,512]{2,1,0:T(8,128)(2,1)S(1)}, bf16[1,64,512]{2,1,0:T(8,128)(2,1)S(1)}, u32[]{:S(2)}, u32[]{:S(2)}) collective-permute-start(bf16[1,64,512]{2,1,0:T(8,128)(2,1)S(1)} %get-tuple-element.34.refs_4_.refs_0_), channel_id=1, source_target_pairs={{0,8},{1,9},{4,12},{5,13},{8,0},{9,1},{12,4},{13,5},{2,10},{3,11},... | collective-permute-start | bytes 196616 | tf_op jit(solution)/shard_map/ppermute | solution.py:30
  21.2 4.3 %collective-permute-start.10 = (bf16[1,64,512]{2,1,0:T(8,128)(2,1)S(1)}, bf16[1,64,512]{2,1,0:T(8,128)(2,1)S(1)}, u32[]{:S(2)}, u32[]{:S(2)}) collective-permute-start(bf16[1,64,512]{2,1,0:T(8,128)(2,1)S(1)} %get-tuple-element.34.refs_4_.refs_0_), channel_id=1, source_target_pairs={{0,4},{1,5},{4,0},{5,1},{8,12},{9,13},{12,8},{13,9},{2,6},{3,7},{6... | collective-permute-start | bytes 196616 | tf_op jit(solution)/shard_map/ppermute | solution.py:30
  23.0 2.5 %collective-permute-start.8 = (f32[32,2560]{1,0:T(8,128)S(1)}, f32[32,2560]{1,0:T(8,128)S(1)}, u32[]{:S(2)}, u32[]{:S(2)}) collective-permute-start(f32[32,2560]{1,0:T(8,128)S(1)} %get-tuple-element.36), channel_id=1, source_target_pairs={{0,1},{1,0},{2,3},{3,2},{4,5},{5,4},{6,7},{7,6},{8,9},{9,8},{10,11... | collective-permute-start | bytes 983048 | tf_op jit(solution)/shard_map/ppermute | solution.py:23
  23.1 9.9 %collective-permute-start.6 = (bf16[256,512]{1,0:T(8,128)(2,1)S(1)}, bf16[256,512]{1,0:T(8,128)(2,1)S(1)}, u32[]{:S(2)}, u32[]{:S(2)}) collective-permute-start(bf16[256,512]{1,0:T(8,128)(2,1)S(1)} %get-tuple-element.32), channel_id=1, source_target_pairs={{0,2},{2,0},{1,3},{3,1},{4,6},{6,4},{5,7},{7,5},{8,10},{10,8},{9,1... | collective-permute-start | bytes 786440 | tf_op jit(solution)/shard_map/ppermute | solution.py:23
  25.6 4.5 %collective-permute-start.11 = (bf16[16,2560]{1,0:T(8,128)(2,1)S(1)}, bf16[16,2560]{1,0:T(8,128)(2,1)S(1)}, u32[]{:S(2)}, u32[]{:S(2)}) collective-permute-start(bf16[16,2560]{1,0:T(8,128)(2,1)S(1)} %get-tuple-element.38.refs_0_), channel_id=1, source_target_pairs={{0,4},{1,5},{4,0},{5,1},{8,12},{9,13},{12,8},{13,9},{2,6},{3,7},{6... | collective-permute-start | bytes 245768 | tf_op jit(solution)/shard_map/ppermute | solution.py:30
  28.3 4.8 %copy-start.1 = (bf16[2560,512]{1,0:T(8,128)(2,1)S(1)}, bf16[2560,512]{1,0:T(8,128)(2,1)}, u32[]{:S(2)}) copy-start(bf16[2560,512]{1,0:T(8,128)(2,1)} %refs_1_.5) | copy-start | bytes 7864324
  30.1 7.5 %collective-permute-start.12 = (bf16[16,2560]{1,0:T(8,128)(2,1)S(1)}, bf16[16,2560]{1,0:T(8,128)(2,1)S(1)}, u32[]{:S(2)}, u32[]{:S(2)}) collective-permute-start(bf16[16,2560]{1,0:T(8,128)(2,1)S(1)} %shard_map.102.refs_4_.refs_1_.refs_0_), channel_id=1, source_target_pairs={{0,8},{1,9},{4,12},{5,13},{8,0},{9,1},{12,4},{13,5},{2,10},{3,11},... | collective-permute-start | bytes 245768 | tf_op jit(solution)/shard_map/ppermute | solution.py:30
  31.2 6.4 %collective-permute-start.13 = (bf16[1,64,512]{2,1,0:T(8,128)(2,1)S(1)}, bf16[1,64,512]{2,1,0:T(8,128)(2,1)S(1)}, u32[]{:S(2)}, u32[]{:S(2)}) collective-permute-start(bf16[1,64,512]{2,1,0:T(8,128)(2,1)S(1)} %shard_map.104.refs_5_), channel_id=1, source_target_pairs={{0,4},{1,5},{4,0},{5,1},{8,12},{9,13},{12,8},{13,9},{2,6},{3,7},{6... | collective-permute-start | bytes 196616 | tf_op jit(solution)/shard_map/ppermute | solution.py:30
  37.6 4.5 %collective-permute-start.14 = (bf16[16,2560]{1,0:T(8,128)(2,1)S(1)}, bf16[16,2560]{1,0:T(8,128)(2,1)S(1)}, u32[]{:S(2)}, u32[]{:S(2)}) collective-permute-start(bf16[16,2560]{1,0:T(8,128)(2,1)S(1)} %shard_map.107.refs_0_), channel_id=1, source_target_pairs={{0,4},{1,5},{4,0},{5,1},{8,12},{9,13},{12,8},{13,9},{2,6},{3,7},{6... | collective-permute-start | bytes 245768 | tf_op jit(solution)/shard_map/ppermute | solution.py:30
  37.9 4.4 %collective-permute-start.16 = (bf16[4,64,512]{2,1,0:T(8,128)(2,1)S(1)}, bf16[4,64,512]{2,1,0:T(8,128)(2,1)S(1)}, u32[]{:S(2)}, u32[]{:S(2)}) collective-permute-start(bf16[4,64,512]{2,1,0:T(8,128)(2,1)S(1)} %shard_map.106.refs_2_.refs_1_), channel_id=1, source_target_pairs={{0,1},{1,0},{2,3},{3,2},{4,5},{5,4},{6,7},{7,6},{8,9},{9,8},{10,11... | collective-permute-start | bytes 786440 | tf_op jit(solution)/shard_map/ppermute | solution.py:23
  42.2 1.7 %collective-permute-start.15 = (bf16[32,2560]{1,0:T(8,128)(2,1)S(1)}, bf16[32,2560]{1,0:T(8,128)(2,1)S(1)}, u32[]{:S(2)}, u32[]{:S(2)}) collective-permute-start(bf16[32,2560]{1,0:T(8,128)(2,1)S(1)} %shard_map.108.refs_4_.refs_0_), channel_id=1, source_target_pairs={{0,1},{1,0},{2,3},{3,2},{4,5},{5,4},{6,7},{7,6},{8,9},{9,8},{10,11... | collective-permute-start | bytes 491528 | tf_op jit(solution)/shard_map/ppermute | solution.py:23

commit v7 on v6

--- a/solution.py
+++ b/solution.py
@@ -9,8 +9,9 @@
 f32 = jnp.float32
 bf16 = jnp.bfloat16
 
-busy = 10**10
-brief = 3 * 10**9
+early_part = 4
+
+busy, middling, brief = 10**10, 5 * 10**9, 3 * 10**9
 
 anywhere = pl.BlockSpec(memory_space=pl.ANY)
 in_hbm = pl.BlockSpec(memory_space=pltpu.HBM)
@@ -63,7 +64,7 @@
 def pick_heads(adapter_ids, head_up, grad):
     per_owner, rank, width = head_up.shape
     own_count, sub_count = lax.axis_size("own"), lax.axis_size("sub")
-    first = grad.shape[0] // 2
+    first = grad.shape[0] // early_part
 
     def body(ids_far, head_up, grad, *refs):
         outs, early, away, ids, maps, sems = refs[:own_count], *refs[own_count:]
@@ -105,7 +106,7 @@
     width = width_of(features)
     blocks = features // width
 
-    def body(tokens, down, low, near_tokens, near_down, sems):
+    def body(tokens, down, low, rounded, near_tokens, near_down, sems):
         copies = [pltpu.make_async_copy(down, near_down, sems.at[blocks])]
         for at in range(blocks):
             here = pl.ds(at * width, width)
@@ -125,12 +126,14 @@
             )
             total = part if total is None else total + part
         low[...] = total
+        rounded[...] = total.astype(bf16)
 
     return call(
         body,
         [stay(tokens), stay(down)],
         [in_hbm] * 2,
-        [shape_of((rank, rows), f32), shape_of(tokens.shape, bf16), shape_of(down.shape, bf16)],
+        [shape_of((rank, rows), f32), shape_of((rank, rows), bf16)]
+        + [shape_of(tokens.shape, bf16), shape_of(down.shape, bf16)],
         after=after,
         flops=2 * rows * rank * features,
         scratch_shapes=[pltpu.SemaphoreType.DMA((blocks + 1,))],
@@ -164,16 +167,20 @@
 def head_term(lengths, lows, grad, scale, after):
     rank, rows = lows[0].shape
     columns = grad.shape[1]
-    first = rows // 2
+    first = rows // early_part
 
     def body(lengths, *refs):
         *lows, grad, term, late = refs
         total = lows[0][...]
         for low in lows[1:]:
-            total = total + low[...]
+            total = total + low[...].astype(f32)
         live = lax.broadcasted_iota(jnp.int32, total.shape, 1) < lengths[0]
-        kept = jnp.where(live, total, 0.0).astype(bf16)
-        term[0] = (scale * jnp.dot(kept, grad[...], preferred_element_type=f32)).astype(bf16)
+        total = jnp.where(live, total, 0.0)
+        kept = total.astype(bf16)
+        rest = (total - kept.astype(f32)).astype(bf16)
+        product = jnp.dot(kept, grad[...], preferred_element_type=f32)
+        product += jnp.dot(rest, grad[...], preferred_element_type=f32)
+        term[0] = (scale * product).astype(bf16)
         late[...] = grad[first:, :]
 
     return call(
@@ -182,7 +189,7 @@
         [in_smem] + [in_vmem] * (len(lows) + 1),
         [shape_of((1, rank, columns), bf16), shape_of((rows - first, columns), bf16)],
         after=after,
-        flops=2 * rows * rank * columns,
+        flops=brief,
     )
 
 
@@ -388,7 +395,7 @@
 def arrange(lengths, grad, pieces, after):
     rows, columns = grad.shape
     count = 1 + len(pieces)
-    first = rows // 2
+    first = rows // early_part
 
     def body(lengths, grad, *refs):
         pieces, kept = refs[:-1], refs[-1]
@@ -471,8 +478,8 @@
     offered = [picked[0]] + [swap(picked[step], step, 0) for step in own_steps]
     early_grads = [shift(early, "tp", step) for step in tp_steps]
 
-    low, tokens, down = project_low(tokens, shared_down.T, offered[1:2] or picked[:1])
-    lows = [low] + [shift(low, "tp", step) for step in tp_steps]
+    low, rounded, tokens, down = project_low(tokens, shared_down.T, offered[1:2] or picked[:1])
+    lows = [low] + [shift(rounded, "tp", step) for step in tp_steps]
 
     part = project_back(away, offered, grad_output, [low, frozen_other, *early_grads])
     parts = [part] + [shift(part, "tp", step) for step in tp_steps]
@@ -488,7 +495,7 @@
 
     back, keep, send = shared_terms(lengths, parts, tokens, scale, [near])
     pieces = [keep, shift(send, "sub", 1)]
-    met = stack(terms[1:] + nearby, flops=brief) if bits else near
+    met = stack(terms[1:] + nearby, flops=middling) if bits else near
 
     mark = met
     for bit in bits[:-1]:

time: 45.1 us -> 43.7 us (0.969)
  waiting for transfers between devices: 10.4 us -> 8.43 us
  starting transfers between devices: 19.6 us -> 20.1 us
    ppermute x9, starting transfers between devices: 14.1 us -> 17 us  [swap(): lax.ppermute(x, ('own', 'sub'), [(i, i ^ other) for i in range(whole)])]
    ppermute x8, starting transfers between devices: 5.49 us -> 3.13 us  [shift(): lax.ppermute(x, axis, [(i, (i + step) % count) for i in range(count)])]
    ppermute x9, waiting for transfers between devices: 10.4 us -> 8.35 us  [swap(): lax.ppermute(x, ('own', 'sub'), [(i, i ^ other) for i in range(whole)])]
  transfers between devices with their start and end apart: 17 -> 17, of which waited for: 5 -> 6; matrix products, arithmetic and copies ran while one was open for 0% -> 0% of each run, Pallas kernels for 28% -> 29%
where the time goes in v7:
time: 43.7 us; the launch traced here: 43.5 us
  starting transfers between devices  20.1 us (46%)
  Pallas kernels  13.5 us (31%)
  waiting for transfers between devices  8.43 us (19%)
  between operations  1.47 us (3%)
    ppermute x9, starting transfers between devices, swap(): lax.ppermute(x, ('own', 'sub'), [(i, i ^ other) for i in range(whole)])  17 us
    pallas_call x17, Pallas kernels, call(): pl.pallas_call(kernel, out_shape=outs, in_specs=list(specs) + [anywhere]...  13.5 us
    ppermute x9, waiting for transfers between devices, swap(): lax.ppermute(x, ('own', 'sub'), [(i, i ^ other) for i in range(whole)])  8.35 us
    ppermute x8, starting transfers between devices, shift(): lax.ppermute(x, axis, [(i, (i + step) % count) for i in range(count)])  3.13 us
  transfers between devices with their start and end apart: 17, of which 6 were waited for; matrix products, arithmetic and copies ran while one was open for 0% of the time, Pallas kernels for 29%

profile of v7, /device:TPU:0, one launch (start us, length us, event | category | flops | bytes accessed | tf_op | source)
XLA Modules:
  0.0 43.5 jit_solution(2858375852992137254)
XLA Ops:
  0.6 0.5 %collective-permute-start.5 = (bf16[2560,512]{1,0:T(8,128)(2,1)}, bf16[2560,512]{1,0:T(8,128)(2,1)S(1)}, u32[]{:S(2)}, u32[]{:S(2)}) collective-permute-start(bf16[2560,512]{1,0:T(8,128)(2,1)} %refs_1_.5), channel_id=1, source_target_pairs={{0,1},{1,0},{2,3},{3,2},{4,5},{5,4},{6,7},{7,6},{8,9},{9,8},{10,11... | collective-permute-start | bytes 7864328 | tf_op jit(solution)/shard_map/ppermute | solution.py:24
  1.2 1.3 %shard_map.94 = (bf16[64,512]{1,0:T(8,128)(2,1)S(1)}, bf16[64,512]{1,0:T(8,128)(2,1)S(1)}, bf16[64,512]{1,0:T(8,128)(2,1)S(1)}, bf16[64,512]{1,0:T(8,128)(2,1)S(...) custom-call(s32[8]{0:T(128)} %refs_0_.8, bf16[16,64,512]{2,1,0:T(8,128)(2,1)} %refs_1_.3, bf16[512,512]{1,0:T(8,128)(2,1)} %refs_1_.4), custom_call_target="tpu_custom_call" | custom-call | bytes 1970208 | tf_op jit(solution)/shard_map/pallas_call | solution.py:53
  2.4 2.7 %collective-permute-start.1 = (bf16[64,512]{1,0:T(8,128)(2,1)S(1)}, bf16[64,512]{1,0:T(8,128)(2,1)S(1)}, u32[]{:S(2)}, u32[]{:S(2)}) collective-permute-start(bf16[64,512]{1,0:T(8,128)(2,1)S(1)} %get-tuple-element.27), channel_id=1, source_target_pairs={{0,4},{1,5},{4,0},{5,1},{8,12},{9,13},{12,8},{13,9},{2,6},{3,7},{6... | collective-permute-start | bytes 196616 | tf_op jit(solution)/shard_map/ppermute | solution.py:31
  5.1 1.5 %collective-permute-start = (bf16[128,512]{1,0:T(8,128)(2,1)S(1)}, bf16[128,512]{1,0:T(8,128)(2,1)S(1)}, u32[]{:S(2)}, u32[]{:S(2)}) collective-permute-start(bf16[128,512]{1,0:T(8,128)(2,1)S(1)} %get-tuple-element.26), channel_id=1, source_target_pairs={{0,2},{2,0},{1,3},{3,1},{4,6},{6,4},{5,7},{7,5},{8,10},{10,8},{9,1... | collective-permute-start | bytes 393224 | tf_op jit(solution)/shard_map/ppermute | solution.py:24
  6.6 2.6 %collective-permute-start.3 = (bf16[64,512]{1,0:T(8,128)(2,1)S(1)}, bf16[64,512]{1,0:T(8,128)(2,1)S(1)}, u32[]{:S(2)}, u32[]{:S(2)}) collective-permute-start(bf16[64,512]{1,0:T(8,128)(2,1)S(1)} %get-tuple-element.32), channel_id=1, source_target_pairs={{0,8},{1,9},{4,12},{5,13},{8,0},{9,1},{12,4},{13,5},{2,10},{3,11},... | collective-permute-start | bytes 196616 | tf_op jit(solution)/shard_map/ppermute | solution.py:31
  9.4 2.3 %shard_map.95 = (f32[64,512]{1,0:T(8,128)S(1)}, bf16[64,512]{1,0:T(8,128)(2,1)S(1)}, bf16[512,2560]{1,0:T(8,128)(2,1)S(1)}, bf16[64,2560]{1,0:T(8,128)(2,1)S(1)}) custom-call(bf16[512,2560]{1,0:T(8,128)(2,1)} %refs_0_.7, bf16[64,2560]{1,0:T(8,128)(2,1)} %bitcast.3, bf16[64,512]{1,0:T(8,128)(2,1)S(1)} %collective-permute-done.1.refs_2_), custom_call_target="tpu_custom_call" | custom-call | flops 167772160 | bytes 6094848 | tf_op jit(solution)/shard_map/pallas_call | solution.py:53
  11.8 0.4 collective-permute-start.2
  13.1 2.3 %collective-permute-done.4.refs_4_ = bf16[64,512]{1,0:T(8,128)(2,1)S(1)} collective-permute-done((bf16[64,512]{1,0:T(8,128)(2,1)S(1)}, bf16[64,512]{1,0:T(8,128)(2,1)S(1)}, u32[]{:S(2)}, u32[]{:S(2)}) %collective-permute-start.4) | collective-permute-done | bytes 65568 | tf_op jit(solution)/shard_map/ppermute | solution.py:31
  15.7 0.6 %collective-permute-start.7 = (f32[64,512]{1,0:T(8,128)S(1)}, f32[64,512]{1,0:T(8,128)S(1)}, u32[]{:S(2)}, u32[]{:S(2)}) collective-permute-start(f32[64,512]{1,0:T(8,128)S(1)} %shard_map.96.refs_4_.refs_1_), channel_id=1, source_target_pairs={{0,2},{2,0},{1,3},{3,1},{4,6},{6,4},{5,7},{7,5},{8,10},{10,8},{9,1... | collective-permute-start | bytes 393224 | tf_op jit(solution)/shard_map/ppermute | solution.py:24
  16.3 0.3 shard_map.97
  16.6 1.9 %collective-permute-start.9 = (bf16[1,64,512]{2,1,0:T(8,128)(2,1)S(1)}, bf16[1,64,512]{2,1,0:T(8,128)(2,1)S(1)}, u32[]{:S(2)}, u32[]{:S(2)}) collective-permute-start(bf16[1,64,512]{2,1,0:T(8,128)(2,1)S(1)} %get-tuple-element.36.refs_4_.refs_0_), channel_id=1, source_target_pairs={{0,8},{1,9},{4,12},{5,13},{8,0},{9,1},{12,4},{13,5},{2,10},{3,11},... | collective-permute-start | bytes 196616 | tf_op jit(solution)/shard_map/ppermute | solution.py:31
  18.5 2.9 %collective-permute-start.10 = (bf16[1,64,512]{2,1,0:T(8,128)(2,1)S(1)}, bf16[1,64,512]{2,1,0:T(8,128)(2,1)S(1)}, u32[]{:S(2)}, u32[]{:S(2)}) collective-permute-start(bf16[1,64,512]{2,1,0:T(8,128)(2,1)S(1)} %get-tuple-element.36.refs_4_.refs_0_), channel_id=1, source_target_pairs={{0,4},{1,5},{4,0},{5,1},{8,12},{9,13},{12,8},{13,9},{2,6},{3,7},{6... | collective-permute-start | bytes 196616 | tf_op jit(solution)/shard_map/ppermute | solution.py:31
  21.3 0.6 %shard_map.98 = (bf16[64,512]{1,0:T(8,128)(2,1)S(1)}, f32[32,2560]{1,0:T(8,128)S(1)}, f32[32,2560]{1,0:T(8,128)S(1)}) custom-call(s32[1]{0:T(128)S(6)} %copy.12.refs_0_, f32[64,512]{1,0:T(8,128)S(1)} %shard_map.96.refs_4_.refs_1_, f32[64,512]{1,0:T(8,128)S(1)} %collective-permute-done.7.refs_2_, bf16[512,2560]{1,0:T(8,128)(2,1)S(1)} %get-tuple-element.35.refs_3_, ...), custom_call_target="tpu_custom_call" | custom-call | flops 167772160 | bytes 3604484 | tf_op jit(solution)/shard_map/pallas_call | solution.py:53
  22.0 1.5 %collective-permute-done.10.refs_1_.refs_2_ = bf16[1,64,512]{2,1,0:T(8,128)(2,1)S(1)} collective-permute-done((bf16[1,64,512]{2,1,0:T(8,128)(2,1)S(1)}, bf16[1,64,512]{2,1,0:T(8,128)(2,1)S(1)}, u32[]{:S(2)}, u32[]{:S(2)}) %collective-permute-start.10) | collective-permute-done | bytes 65568 | tf_op jit(solution)/shard_map/ppermute | solution.py:31
  23.7 2.1 %collective-permute-start.11 = (bf16[16,2560]{1,0:T(8,128)(2,1)S(1)}, bf16[16,2560]{1,0:T(8,128)(2,1)S(1)}, u32[]{:S(2)}, u32[]{:S(2)}) collective-permute-start(bf16[16,2560]{1,0:T(8,128)(2,1)S(1)} %get-tuple-element.40.refs_0_), channel_id=1, source_target_pairs={{0,4},{1,5},{4,0},{5,1},{8,12},{9,13},{12,8},{13,9},{2,6},{3,7},{6... | collective-permute-start | bytes 245768 | tf_op jit(solution)/shard_map/ppermute | solution.py:31
  25.7 1.4 %shard_map.101 = (f32[16,64,512]{2,1,0:T(8,128)}, f32[8,128]{1,0:T(8,128)S(1)}) custom-call(bf16[16,2560]{1,0:T(8,128)(2,1)S(1)} %get-tuple-element.40.refs_0_), custom_call_target="tpu_custom_call" | custom-call | flops 10000000000 | bytes 2101248 | tf_op jit(solution)/shard_map/pallas_call | solution.py:53
  27.2 1.0 %collective-permute-done.11.refs_1_ = bf16[16,2560]{1,0:T(8,128)(2,1)S(1)} collective-permute-done((bf16[16,2560]{1,0:T(8,128)(2,1)S(1)}, bf16[16,2560]{1,0:T(8,128)(2,1)S(1)}, u32[]{:S(2)}, u32[]{:S(2)}) %collective-permute-start.11) | collective-permute-done | bytes 81952 | tf_op jit(solution)/shard_map/ppermute | solution.py:31
  28.3 2.6 %collective-permute-start.12 = (bf16[16,2560]{1,0:T(8,128)(2,1)S(1)}, bf16[16,2560]{1,0:T(8,128)(2,1)S(1)}, u32[]{:S(2)}, u32[]{:S(2)}) collective-permute-start(bf16[16,2560]{1,0:T(8,128)(2,1)S(1)} %shard_map.102.refs_4_.refs_1_.refs_0_), channel_id=1, source_target_pairs={{0,8},{1,9},{4,12},{5,13},{8,0},{9,1},{12,4},{13,5},{2,10},{3,11},... | collective-permute-start | bytes 245768 | tf_op jit(solution)/shard_map/ppermute | solution.py:31
  30.9 0.8 %collective-permute-start.13 = (bf16[1,64,512]{2,1,0:T(8,128)(2,1)S(1)}, bf16[1,64,512]{2,1,0:T(8,128)(2,1)S(1)}, u32[]{:S(2)}, u32[]{:S(2)}) collective-permute-start(bf16[1,64,512]{2,1,0:T(8,128)(2,1)S(1)} %shard_map.104.refs_5_), channel_id=1, source_target_pairs={{0,4},{1,5},{4,0},{5,1},{8,12},{9,13},{12,8},{13,9},{2,6},{3,7},{6... | collective-permute-start | bytes 196616 | tf_op jit(solution)/shard_map/ppermute | solution.py:31
  31.7 4.4 %shard_map.105 = (bf16[512,2560]{1,0:T(8,128)(2,1)}, f32[8,128]{1,0:T(8,128)S(1)}) custom-call(bf16[512,1024]{1,0:T(8,128)(2,1)S(1)} %shard_map.103.refs_0_, bf16[2560,512]{1,0:T(8,128)(2,1)S(1)} %copy-done.1, bf16[2560,512]{1,0:T(8,128)(2,1)S(1)} %collective-permute-done.5.refs_7_.refs_2_, bf16[64,512]{1,0:T(8,128)(2,1)S(1)} %get-tuple-element.42.refs_3_, ...), custom_call_target="tpu_custom_call" | custom-call | flops 2852126720 | bytes 9310208 | tf_op jit(solution)/shard_map/pallas_call | solution.py:53
  36.2 1.3 %collective-permute-start.14 = (bf16[16,2560]{1,0:T(8,128)(2,1)S(1)}, bf16[16,2560]{1,0:T(8,128)(2,1)S(1)}, u32[]{:S(2)}, u32[]{:S(2)}) collective-permute-start(bf16[16,2560]{1,0:T(8,128)(2,1)S(1)} %shard_map.107.refs_0_), channel_id=1, source_target_pairs={{0,4},{1,5},{4,0},{5,1},{8,12},{9,13},{12,8},{13,9},{2,6},{3,7},{6... | collective-permute-start | bytes 245768 | tf_op jit(solution)/shard_map/ppermute | solution.py:31
  37.6 3.2 %collective-permute-done.14.refs_1_ = bf16[16,2560]{1,0:T(8,128)(2,1)S(1)} collective-permute-done((bf16[16,2560]{1,0:T(8,128)(2,1)S(1)}, bf16[16,2560]{1,0:T(8,128)(2,1)S(1)}, u32[]{:S(2)}, u32[]{:S(2)}) %collective-permute-start.14) | collective-permute-done | bytes 81952 | tf_op jit(solution)/shard_map/ppermute | solution.py:31
  40.9 1.7 %shard_map.109 = (f32[16,64,512]{2,1,0:T(8,128)}, f32[8,128]{1,0:T(8,128)S(1)}) custom-call(s32[8]{0:T(128)} %refs_0_.8, bf16[4,64,512]{2,1,0:T(8,128)(2,1)S(1)} %shard_map.106.refs_2_.refs_1_, bf16[4,64,512]{2,1,0:T(8,128)(2,1)S(1)} %collective-permute-done.16.refs_2_, f32[16,64,512]{2,1,0:T(8,128)} %get-tuple-element.46.refs_3_, ...), custom_call_target="tpu_custom_call", output_to_operand_aliasing={{0}: (3, {})} | custom-call | bytes 4722720 | tf_op jit(solution)/shard_map/pallas_call | solution.py:53
  42.6 0.9 %shard_map.110 = f32[64,2560]{1,0:T(8,128)} custom-call(bf16[32,2560]{1,0:T(8,128)(2,1)S(1)} %shard_map.108.refs_4_.refs_0_, bf16[32,2560]{1,0:T(8,128)(2,1)S(1)} %collective-permute-done.15.refs_1_, f32[8,128]{1,0:T(8,128)S(1)} %get-tuple-element.47.refs_2_), custom_call_target="tpu_custom_call" | custom-call | bytes 983040 | tf_op jit(solution)/shard_map/pallas_call | solution.py:53
  (31 shorter events, 1.3 us)
Async XLA Ops:
  0.6 14.8 %copy-start = (bf16[512,512]{1,0:T(8,128)(2,1)S(1)}, bf16[512,512]{1,0:T(8,128)(2,1)}, u32[]{:S(2)}) copy-start(bf16[512,512]{1,0:T(8,128)(2,1)} %refs_1_.4) | copy-start | bytes 1572868
  0.6 14.8 %collective-permute-start.5 = (bf16[2560,512]{1,0:T(8,128)(2,1)}, bf16[2560,512]{1,0:T(8,128)(2,1)S(1)}, u32[]{:S(2)}, u32[]{:S(2)}) collective-permute-start(bf16[2560,512]{1,0:T(8,128)(2,1)} %refs_1_.5), channel_id=1, source_target_pairs={{0,1},{1,0},{2,3},{3,2},{4,5},{5,4},{6,7},{7,6},{8,9},{9,8},{10,11... | collective-permute-start | bytes 7864328 | tf_op jit(solution)/shard_map/ppermute | solution.py:24
  2.4 7.0 %collective-permute-start.1 = (bf16[64,512]{1,0:T(8,128)(2,1)S(1)}, bf16[64,512]{1,0:T(8,128)(2,1)S(1)}, u32[]{:S(2)}, u32[]{:S(2)}) collective-permute-start(bf16[64,512]{1,0:T(8,128)(2,1)S(1)} %get-tuple-element.27), channel_id=1, source_target_pairs={{0,4},{1,5},{4,0},{5,1},{8,12},{9,13},{12,8},{13,9},{2,6},{3,7},{6... | collective-permute-start | bytes 196616 | tf_op jit(solution)/shard_map/ppermute | solution.py:31
  5.1 10.3 %collective-permute-start = (bf16[128,512]{1,0:T(8,128)(2,1)S(1)}, bf16[128,512]{1,0:T(8,128)(2,1)S(1)}, u32[]{:S(2)}, u32[]{:S(2)}) collective-permute-start(bf16[128,512]{1,0:T(8,128)(2,1)S(1)} %get-tuple-element.26), channel_id=1, source_target_pairs={{0,2},{2,0},{1,3},{3,1},{4,6},{6,4},{5,7},{7,5},{8,10},{10,8},{9,1... | collective-permute-start | bytes 393224 | tf_op jit(solution)/shard_map/ppermute | solution.py:24
  6.6 6.5 %collective-permute-start.3 = (bf16[64,512]{1,0:T(8,128)(2,1)S(1)}, bf16[64,512]{1,0:T(8,128)(2,1)S(1)}, u32[]{:S(2)}, u32[]{:S(2)}) collective-permute-start(bf16[64,512]{1,0:T(8,128)(2,1)S(1)} %get-tuple-element.32), channel_id=1, source_target_pairs={{0,8},{1,9},{4,12},{5,13},{8,0},{9,1},{12,4},{13,5},{2,10},{3,11},... | collective-permute-start | bytes 196616 | tf_op jit(solution)/shard_map/ppermute | solution.py:31
  9.2 6.2 %collective-permute-start.4 = (bf16[64,512]{1,0:T(8,128)(2,1)S(1)}, bf16[64,512]{1,0:T(8,128)(2,1)S(1)}, u32[]{:S(2)}, u32[]{:S(2)}) collective-permute-start(bf16[64,512]{1,0:T(8,128)(2,1)S(1)} %get-tuple-element.33), channel_id=1, source_target_pairs={{0,12},{1,13},{4,8},{5,9},{8,4},{9,5},{12,0},{13,1},{2,14},{3,15},... | collective-permute-start | bytes 196616 | tf_op jit(solution)/shard_map/ppermute | solution.py:31
  11.8 4.5 %collective-permute-start.2 = (bf16[64,512]{1,0:T(8,128)(2,1)S(1)}, bf16[64,512]{1,0:T(8,128)(2,1)S(1)}, u32[]{:S(2)}, u32[]{:S(2)}) collective-permute-start(bf16[64,512]{1,0:T(8,128)(2,1)S(1)} %get-tuple-element.29), channel_id=1, source_target_pairs={{0,2},{2,0},{1,3},{3,1},{4,6},{6,4},{5,7},{7,5},{8,10},{10,8},{9,1... | collective-permute-start | bytes 196616 | tf_op jit(solution)/shard_map/ppermute | solution.py:24
  15.7 5.6 %collective-permute-start.7 = (f32[64,512]{1,0:T(8,128)S(1)}, f32[64,512]{1,0:T(8,128)S(1)}, u32[]{:S(2)}, u32[]{:S(2)}) collective-permute-start(f32[64,512]{1,0:T(8,128)S(1)} %shard_map.96.refs_4_.refs_1_), channel_id=1, source_target_pairs={{0,2},{2,0},{1,3},{3,1},{4,6},{6,4},{5,7},{7,5},{8,10},{10,8},{9,1... | collective-permute-start | bytes 393224 | tf_op jit(solution)/shard_map/ppermute | solution.py:24
  16.6 5.4 %collective-permute-start.9 = (bf16[1,64,512]{2,1,0:T(8,128)(2,1)S(1)}, bf16[1,64,512]{2,1,0:T(8,128)(2,1)S(1)}, u32[]{:S(2)}, u32[]{:S(2)}) collective-permute-start(bf16[1,64,512]{2,1,0:T(8,128)(2,1)S(1)} %get-tuple-element.36.refs_4_.refs_0_), channel_id=1, source_target_pairs={{0,8},{1,9},{4,12},{5,13},{8,0},{9,1},{12,4},{13,5},{2,10},{3,11},... | collective-permute-start | bytes 196616 | tf_op jit(solution)/shard_map/ppermute | solution.py:31
  18.5 5.1 %collective-permute-start.10 = (bf16[1,64,512]{2,1,0:T(8,128)(2,1)S(1)}, bf16[1,64,512]{2,1,0:T(8,128)(2,1)S(1)}, u32[]{:S(2)}, u32[]{:S(2)}) collective-permute-start(bf16[1,64,512]{2,1,0:T(8,128)(2,1)S(1)} %get-tuple-element.36.refs_4_.refs_0_), channel_id=1, source_target_pairs={{0,4},{1,5},{4,0},{5,1},{8,12},{9,13},{12,8},{13,9},{2,6},{3,7},{6... | collective-permute-start | bytes 196616 | tf_op jit(solution)/shard_map/ppermute | solution.py:31
  21.3 10.3 %collective-permute-start.6 = (bf16[384,512]{1,0:T(8,128)(2,1)S(1)}, bf16[384,512]{1,0:T(8,128)(2,1)S(1)}, u32[]{:S(2)}, u32[]{:S(2)}) collective-permute-start(bf16[384,512]{1,0:T(8,128)(2,1)S(1)} %get-tuple-element.34), channel_id=1, source_target_pairs={{0,2},{2,0},{1,3},{3,1},{4,6},{6,4},{5,7},{7,5},{8,10},{10,8},{9,1... | collective-permute-start | bytes 1179656 | tf_op jit(solution)/shard_map/ppermute | solution.py:24
  22.0 1.7 %collective-permute-start.8 = (f32[32,2560]{1,0:T(8,128)S(1)}, f32[32,2560]{1,0:T(8,128)S(1)}, u32[]{:S(2)}, u32[]{:S(2)}) collective-permute-start(f32[32,2560]{1,0:T(8,128)S(1)} %get-tuple-element.38), channel_id=1, source_target_pairs={{0,1},{1,0},{2,3},{3,2},{4,5},{5,4},{6,7},{7,6},{8,9},{9,8},{10,11... | collective-permute-start | bytes 983048 | tf_op jit(solution)/shard_map/ppermute | solution.py:24
  23.7 4.6 %collective-permute-start.11 = (bf16[16,2560]{1,0:T(8,128)(2,1)S(1)}, bf16[16,2560]{1,0:T(8,128)(2,1)S(1)}, u32[]{:S(2)}, u32[]{:S(2)}) collective-permute-start(bf16[16,2560]{1,0:T(8,128)(2,1)S(1)} %get-tuple-element.40.refs_0_), channel_id=1, source_target_pairs={{0,4},{1,5},{4,0},{5,1},{8,12},{9,13},{12,8},{13,9},{2,6},{3,7},{6... | collective-permute-start | bytes 245768 | tf_op jit(solution)/shard_map/ppermute | solution.py:31
  27.2 4.5 %copy-start.1 = (bf16[2560,512]{1,0:T(8,128)(2,1)S(1)}, bf16[2560,512]{1,0:T(8,128)(2,1)}, u32[]{:S(2)}) copy-start(bf16[2560,512]{1,0:T(8,128)(2,1)} %refs_1_.5) | copy-start | bytes 7864324
  28.3 7.9 %collective-permute-start.12 = (bf16[16,2560]{1,0:T(8,128)(2,1)S(1)}, bf16[16,2560]{1,0:T(8,128)(2,1)S(1)}, u32[]{:S(2)}, u32[]{:S(2)}) collective-permute-start(bf16[16,2560]{1,0:T(8,128)(2,1)S(1)} %shard_map.102.refs_4_.refs_1_.refs_0_), channel_id=1, source_target_pairs={{0,8},{1,9},{4,12},{5,13},{8,0},{9,1},{12,4},{13,5},{2,10},{3,11},... | collective-permute-start | bytes 245768 | tf_op jit(solution)/shard_map/ppermute | solution.py:31
  30.9 5.3 %collective-permute-start.13 = (bf16[1,64,512]{2,1,0:T(8,128)(2,1)S(1)}, bf16[1,64,512]{2,1,0:T(8,128)(2,1)S(1)}, u32[]{:S(2)}, u32[]{:S(2)}) collective-permute-start(bf16[1,64,512]{2,1,0:T(8,128)(2,1)S(1)} %shard_map.104.refs_5_), channel_id=1, source_target_pairs={{0,4},{1,5},{4,0},{5,1},{8,12},{9,13},{12,8},{13,9},{2,6},{3,7},{6... | collective-permute-start | bytes 196616 | tf_op jit(solution)/shard_map/ppermute | solution.py:31
  36.2 4.5 %collective-permute-start.14 = (bf16[16,2560]{1,0:T(8,128)(2,1)S(1)}, bf16[16,2560]{1,0:T(8,128)(2,1)S(1)}, u32[]{:S(2)}, u32[]{:S(2)}) collective-permute-start(bf16[16,2560]{1,0:T(8,128)(2,1)S(1)} %shard_map.107.refs_0_), channel_id=1, source_target_pairs={{0,4},{1,5},{4,0},{5,1},{8,12},{9,13},{12,8},{13,9},{2,6},{3,7},{6... | collective-permute-start | bytes 245768 | tf_op jit(solution)/shard_map/ppermute | solution.py:31
  37.6 3.3 %collective-permute-start.16 = (bf16[4,64,512]{2,1,0:T(8,128)(2,1)S(1)}, bf16[4,64,512]{2,1,0:T(8,128)(2,1)S(1)}, u32[]{:S(2)}, u32[]{:S(2)}) collective-permute-start(bf16[4,64,512]{2,1,0:T(8,128)(2,1)S(1)} %shard_map.106.refs_2_.refs_1_), channel_id=1, source_target_pairs={{0,1},{1,0},{2,3},{3,2},{4,5},{5,4},{6,7},{7,6},{8,9},{9,8},{10,11... | collective-permute-start | bytes 786440 | tf_op jit(solution)/shard_map/ppermute | solution.py:24
  40.8 1.8 %collective-permute-start.15 = (bf16[32,2560]{1,0:T(8,128)(2,1)S(1)}, bf16[32,2560]{1,0:T(8,128)(2,1)S(1)}, u32[]{:S(2)}, u32[]{:S(2)}) collective-permute-start(bf16[32,2560]{1,0:T(8,128)(2,1)S(1)} %shard_map.108.refs_4_.refs_0_), channel_id=1, source_target_pairs={{0,1},{1,0},{2,3},{3,2},{4,5},{5,4},{6,7},{7,6},{8,9},{9,8},{10,11... | collective-permute-start | bytes 491528 | tf_op jit(solution)/shard_map/ppermute | solution.py:24

commit v8 on v7

--- a/solution.py
+++ b/solution.py
@@ -11,7 +11,7 @@
 
 early_part = 4
 
-busy, middling, brief = 10**10, 5 * 10**9, 3 * 10**9
+busy, middling, brief, slight = 10**10, 5 * 10**9, 3 * 10**9, 15 * 10**8
 
 anywhere = pl.BlockSpec(memory_space=pl.ANY)
 in_hbm = pl.BlockSpec(memory_space=pltpu.HBM)
@@ -140,7 +140,7 @@
     )
 
 
-def project_back(away, offered, grad, after):
+def project_back(away, offered, steps, grad, after):
     rank, columns = offered[0].shape
     rows = grad.shape[0]
 
@@ -148,8 +148,8 @@
         *offered, grad, part = refs
         step = jnp.broadcast_to(away[:1, :1], (rank, columns))
         head = offered[0][...].astype(f32)
-        for at in range(1, len(offered)):
-            head = jnp.where(step == at, offered[at][...].astype(f32), head)
+        for at, block in zip(steps, offered[1:]):
+            head = jnp.where(step == at, block[...].astype(f32), head)
         part[...] = lax.dot_general(
             head.astype(bf16), grad[...], (((1,), (1,)), ((), ())), preferred_element_type=f32
         )
@@ -160,7 +160,7 @@
         [in_vmem] * (len(offered) + 2),
         [shape_of((rank, rows), f32)],
         after=after,
-        flops=2 * rows * rank * columns,
+        flops=slight,
     )[0]
 
 
@@ -475,16 +475,19 @@
 
     frozen_other = shift(frozen_value, "sub", 1)
     picked, early, away = pick_heads(adapter_ids, head_up, grad_output)
-    offered = [picked[0]] + [swap(picked[step], step, 0) for step in own_steps]
+    steps = sorted(own_steps, key=lambda step: (-step.bit_length(), step))
+    offered = [picked[0]] + [swap(picked[step], step, 0) for step in steps]
     early_grads = [shift(early, "tp", step) for step in tp_steps]
 
-    low, rounded, tokens, down = project_low(tokens, shared_down.T, offered[1:2] or picked[:1])
+    low, rounded, tokens, down = project_low(
+        tokens, shared_down.T, [picked[0], frozen_other]
+    )
     lows = [low] + [shift(rounded, "tp", step) for step in tp_steps]
 
-    part = project_back(away, offered, grad_output, [low, frozen_other, *early_grads])
+    part = project_back(away, offered, steps, grad_output, [low])
     parts = [part] + [shift(part, "tp", step) for step in tp_steps]
 
-    near, late = head_term(lengths, lows, grad_output, scale, [part])
+    near, late = head_term(lengths, lows, grad_output, scale, [part, *early_grads])
     late_grads = [shift(late, "tp", step) for step in tp_steps]
     bits = [1 << i for i in range(own_count.bit_length() - 1)]
     terms, pattern = [near], [0]

time: 43.7 us -> 43.4 us (level)
  starting transfers between devices: 20.1 us -> 16.8 us
  waiting for transfers between devices: 8.43 us -> 11.4 us
    ppermute x9, starting transfers between devices: 17 us -> 12.3 us  [swap(): lax.ppermute(x, ('own', 'sub'), [(i, i ^ other) for i in range(whole)])]
    ppermute x8, waiting for transfers between devices: 0.07 us -> 2.38 us  [shift(): lax.ppermute(x, axis, [(i, (i + step) % count) for i in range(count)])]
    ppermute x8, starting transfers between devices: 3.13 us -> 4.48 us  [shift(): lax.ppermute(x, axis, [(i, (i + step) % count) for i in range(count)])]
    ppermute x9, waiting for transfers between devices: 8.35 us -> 9.05 us  [swap(): lax.ppermute(x, ('own', 'sub'), [(i, i ^ other) for i in range(whole)])]
where the time goes in v8:
time: 43.4 us; the launch traced here: 43.1 us
  starting transfers between devices  16.8 us (39%)
  Pallas kernels  13.4 us (31%)
  waiting for transfers between devices  11.4 us (26%)
  between operations  1.48 us (3%)
    pallas_call x17, Pallas kernels, call(): pl.pallas_call(kernel, out_shape=outs, in_specs=list(specs) + [anywhere]...  13.4 us
    ppermute x9, starting transfers between devices, swap(): lax.ppermute(x, ('own', 'sub'), [(i, i ^ other) for i in range(whole)])  12.3 us
    ppermute x9, waiting for transfers between devices, swap(): lax.ppermute(x, ('own', 'sub'), [(i, i ^ other) for i in range(whole)])  9.05 us
    ppermute x8, starting transfers between devices, shift(): lax.ppermute(x, axis, [(i, (i + step) % count) for i in range(count)])  4.48 us
    ppermute x8, waiting for transfers between devices, shift(): lax.ppermute(x, axis, [(i, (i + step) % count) for i in range(count)])  2.38 us
  transfers between devices with their start and end apart: 17, of which 6 were waited for; matrix products, arithmetic and copies ran while one was open for 0% of the time, Pallas kernels for 29%

profile of v8, /device:TPU:0, one launch (start us, length us, event | category | flops | bytes accessed | tf_op | source)
XLA Modules:
  0.0 43.1 jit_solution(11217701001042229158)
XLA Ops:
  0.6 0.5 %collective-permute-start.1 = (bf16[2560,512]{1,0:T(8,128)(2,1)}, bf16[2560,512]{1,0:T(8,128)(2,1)S(1)}, u32[]{:S(2)}, u32[]{:S(2)}) collective-permute-start(bf16[2560,512]{1,0:T(8,128)(2,1)} %refs_1_.5), channel_id=1, source_target_pairs={{0,1},{1,0},{2,3},{3,2},{4,5},{5,4},{6,7},{7,6},{8,9},{9,8},{10,11... | collective-permute-start | bytes 7864328 | tf_op jit(solution)/shard_map/ppermute | solution.py:24
  1.1 1.3 %shard_map.94 = (bf16[64,512]{1,0:T(8,128)(2,1)S(1)}, bf16[64,512]{1,0:T(8,128)(2,1)S(1)}, bf16[64,512]{1,0:T(8,128)(2,1)S(1)}, bf16[64,512]{1,0:T(8,128)(2,1)S(...) custom-call(s32[8]{0:T(128)} %refs_0_.8, bf16[16,64,512]{2,1,0:T(8,128)(2,1)} %refs_1_.3, bf16[512,512]{1,0:T(8,128)(2,1)} %refs_1_.4), custom_call_target="tpu_custom_call" | custom-call | bytes 1970208 | tf_op jit(solution)/shard_map/pallas_call | solution.py:53
  2.4 3.7 %collective-permute-start.3 = (bf16[64,512]{1,0:T(8,128)(2,1)S(1)}, bf16[64,512]{1,0:T(8,128)(2,1)S(1)}, u32[]{:S(2)}, u32[]{:S(2)}) collective-permute-start(bf16[64,512]{1,0:T(8,128)(2,1)S(1)} %get-tuple-element.31), channel_id=1, source_target_pairs={{0,8},{1,9},{4,12},{5,13},{8,0},{9,1},{12,4},{13,5},{2,10},{3,11},... | collective-permute-start | bytes 196616 | tf_op jit(solution)/shard_map/ppermute | solution.py:31
  6.1 1.3 %collective-permute-start.4 = (bf16[64,512]{1,0:T(8,128)(2,1)S(1)}, bf16[64,512]{1,0:T(8,128)(2,1)S(1)}, u32[]{:S(2)}, u32[]{:S(2)}) collective-permute-start(bf16[64,512]{1,0:T(8,128)(2,1)S(1)} %get-tuple-element.32), channel_id=1, source_target_pairs={{0,12},{1,13},{4,8},{5,9},{8,4},{9,5},{12,0},{13,1},{2,14},{3,15},... | collective-permute-start | bytes 196616 | tf_op jit(solution)/shard_map/ppermute | solution.py:31
  7.7 1.5 %collective-permute-start = (bf16[128,512]{1,0:T(8,128)(2,1)S(1)}, bf16[128,512]{1,0:T(8,128)(2,1)S(1)}, u32[]{:S(2)}, u32[]{:S(2)}) collective-permute-start(bf16[128,512]{1,0:T(8,128)(2,1)S(1)} %get-tuple-element.26), channel_id=1, source_target_pairs={{0,2},{2,0},{1,3},{3,1},{4,6},{6,4},{5,7},{7,5},{8,10},{10,8},{9,1... | collective-permute-start | bytes 393224 | tf_op jit(solution)/shard_map/ppermute | solution.py:24
  9.8 2.4 %shard_map.95 = (f32[64,512]{1,0:T(8,128)S(1)}, bf16[64,512]{1,0:T(8,128)(2,1)S(1)}, bf16[512,2560]{1,0:T(8,128)(2,1)S(1)}, bf16[64,2560]{1,0:T(8,128)(2,1)S(1)}) custom-call(bf16[512,2560]{1,0:T(8,128)(2,1)} %refs_0_.7, bf16[64,2560]{1,0:T(8,128)(2,1)} %bitcast.3, bf16[64,512]{1,0:T(8,128)(2,1)S(1)} %get-tuple-element.27.refs_2_.refs_1_, ...), custom_call_target="tpu_custom_call" | custom-call | flops 167772160 | bytes 6094848 | tf_op jit(solution)/shard_map/pallas_call | solution.py:53
  12.2 0.6 %collective-permute-start.2 = (bf16[64,512]{1,0:T(8,128)(2,1)S(1)}, bf16[64,512]{1,0:T(8,128)(2,1)S(1)}, u32[]{:S(2)}, u32[]{:S(2)}) collective-permute-start(bf16[64,512]{1,0:T(8,128)(2,1)S(1)} %get-tuple-element.29), channel_id=1, source_target_pairs={{0,2},{2,0},{1,3},{3,1},{4,6},{6,4},{5,7},{7,5},{8,10},{10,8},{9,1... | collective-permute-start | bytes 196616 | tf_op jit(solution)/shard_map/ppermute | solution.py:24
  13.3 1.6 %collective-permute-start.7 = (f32[64,512]{1,0:T(8,128)S(1)}, f32[64,512]{1,0:T(8,128)S(1)}, u32[]{:S(2)}, u32[]{:S(2)}) collective-permute-start(f32[64,512]{1,0:T(8,128)S(1)} %shard_map.96.refs_4_.refs_1_), channel_id=1, source_target_pairs={{0,2},{2,0},{1,3},{3,1},{4,6},{6,4},{5,7},{7,5},{8,10},{10,8},{9,1... | collective-permute-start | bytes 393224 | tf_op jit(solution)/shard_map/ppermute | solution.py:24
  14.9 2.4 %collective-permute-done.2.refs_2_ = bf16[64,512]{1,0:T(8,128)(2,1)S(1)} collective-permute-done((bf16[64,512]{1,0:T(8,128)(2,1)S(1)}, bf16[64,512]{1,0:T(8,128)(2,1)S(1)}, u32[]{:S(2)}, u32[]{:S(2)}) %collective-permute-start.2) | collective-permute-done | bytes 65568 | tf_op jit(solution)/shard_map/ppermute | solution.py:24
  17.6 2.7 %collective-permute-start.9 = (bf16[1,64,512]{2,1,0:T(8,128)(2,1)S(1)}, bf16[1,64,512]{2,1,0:T(8,128)(2,1)S(1)}, u32[]{:S(2)}, u32[]{:S(2)}) collective-permute-start(bf16[1,64,512]{2,1,0:T(8,128)(2,1)S(1)} %get-tuple-element.36.refs_4_.refs_0_), channel_id=1, source_target_pairs={{0,8},{1,9},{4,12},{5,13},{8,0},{9,1},{12,4},{13,5},{2,10},{3,11},... | collective-permute-start | bytes 196616 | tf_op jit(solution)/shard_map/ppermute | solution.py:31
  20.3 0.5 %collective-permute-start.10 = (bf16[1,64,512]{2,1,0:T(8,128)(2,1)S(1)}, bf16[1,64,512]{2,1,0:T(8,128)(2,1)S(1)}, u32[]{:S(2)}, u32[]{:S(2)}) collective-permute-start(bf16[1,64,512]{2,1,0:T(8,128)(2,1)S(1)} %get-tuple-element.36.refs_4_.refs_0_), channel_id=1, source_target_pairs={{0,4},{1,5},{4,0},{5,1},{8,12},{9,13},{12,8},{13,9},{2,6},{3,7},{6... | collective-permute-start | bytes 196616 | tf_op jit(solution)/shard_map/ppermute | solution.py:31
  20.9 0.6 %shard_map.98 = (bf16[64,512]{1,0:T(8,128)(2,1)S(1)}, f32[32,2560]{1,0:T(8,128)S(1)}, f32[32,2560]{1,0:T(8,128)S(1)}) custom-call(s32[1]{0:T(128)S(6)} %copy.12.refs_0_, f32[64,512]{1,0:T(8,128)S(1)} %shard_map.96.refs_4_.refs_1_, f32[64,512]{1,0:T(8,128)S(1)} %collective-permute-done.7.refs_2_, bf16[512,2560]{1,0:T(8,128)(2,1)S(1)} %get-tuple-element.35.refs_3_, ...), custom_call_target="tpu_custom_call" | custom-call | flops 167772160 | bytes 3604484 | tf_op jit(solution)/shard_map/pallas_call | solution.py:53
  21.6 1.2 %collective-permute-done.9.refs_0_.refs_1_ = bf16[1,64,512]{2,1,0:T(8,128)(2,1)S(1)} collective-permute-done((bf16[1,64,512]{2,1,0:T(8,128)(2,1)S(1)}, bf16[1,64,512]{2,1,0:T(8,128)(2,1)S(1)}, u32[]{:S(2)}, u32[]{:S(2)}) %collective-permute-start.9) | collective-permute-done | bytes 65568 | tf_op jit(solution)/shard_map/ppermute | solution.py:31
  22.8 1.8 %collective-permute-done.10.refs_1_.refs_2_ = bf16[1,64,512]{2,1,0:T(8,128)(2,1)S(1)} collective-permute-done((bf16[1,64,512]{2,1,0:T(8,128)(2,1)S(1)}, bf16[1,64,512]{2,1,0:T(8,128)(2,1)S(1)}, u32[]{:S(2)}, u32[]{:S(2)}) %collective-permute-start.10) | collective-permute-done | bytes 65568 | tf_op jit(solution)/shard_map/ppermute | solution.py:31
  24.7 0.8 %collective-permute-start.11 = (bf16[16,2560]{1,0:T(8,128)(2,1)S(1)}, bf16[16,2560]{1,0:T(8,128)(2,1)S(1)}, u32[]{:S(2)}, u32[]{:S(2)}) collective-permute-start(bf16[16,2560]{1,0:T(8,128)(2,1)S(1)} %get-tuple-element.40.refs_0_), channel_id=1, source_target_pairs={{0,4},{1,5},{4,0},{5,1},{8,12},{9,13},{12,8},{13,9},{2,6},{3,7},{6... | collective-permute-start | bytes 245768 | tf_op jit(solution)/shard_map/ppermute | solution.py:31
  25.4 1.4 %shard_map.101 = (f32[16,64,512]{2,1,0:T(8,128)}, f32[8,128]{1,0:T(8,128)S(1)}) custom-call(bf16[16,2560]{1,0:T(8,128)(2,1)S(1)} %get-tuple-element.40.refs_0_), custom_call_target="tpu_custom_call" | custom-call | flops 10000000000 | bytes 2101248 | tf_op jit(solution)/shard_map/pallas_call | solution.py:53
  26.9 2.3 %collective-permute-done.11.refs_1_ = bf16[16,2560]{1,0:T(8,128)(2,1)S(1)} collective-permute-done((bf16[16,2560]{1,0:T(8,128)(2,1)S(1)}, bf16[16,2560]{1,0:T(8,128)(2,1)S(1)}, u32[]{:S(2)}, u32[]{:S(2)}) %collective-permute-start.11) | collective-permute-done | bytes 81952 | tf_op jit(solution)/shard_map/ppermute | solution.py:31
  29.2 1.0 %collective-permute-start.12 = (bf16[16,2560]{1,0:T(8,128)(2,1)S(1)}, bf16[16,2560]{1,0:T(8,128)(2,1)S(1)}, u32[]{:S(2)}, u32[]{:S(2)}) collective-permute-start(bf16[16,2560]{1,0:T(8,128)(2,1)S(1)} %shard_map.102.refs_4_.refs_1_.refs_0_), channel_id=1, source_target_pairs={{0,8},{1,9},{4,12},{5,13},{8,0},{9,1},{12,4},{13,5},{2,10},{3,11},... | collective-permute-start | bytes 245768 | tf_op jit(solution)/shard_map/ppermute | solution.py:31
  30.2 1.2 %collective-permute-start.13 = (bf16[1,64,512]{2,1,0:T(8,128)(2,1)S(1)}, bf16[1,64,512]{2,1,0:T(8,128)(2,1)S(1)}, u32[]{:S(2)}, u32[]{:S(2)}) collective-permute-start(bf16[1,64,512]{2,1,0:T(8,128)(2,1)S(1)} %shard_map.104.refs_5_), channel_id=1, source_target_pairs={{0,4},{1,5},{4,0},{5,1},{8,12},{9,13},{12,8},{13,9},{2,6},{3,7},{6... | collective-permute-start | bytes 196616 | tf_op jit(solution)/shard_map/ppermute | solution.py:31
  31.5 4.4 %shard_map.105 = (bf16[512,2560]{1,0:T(8,128)(2,1)}, f32[8,128]{1,0:T(8,128)S(1)}) custom-call(bf16[512,1024]{1,0:T(8,128)(2,1)S(1)} %shard_map.103.refs_0_, bf16[2560,512]{1,0:T(8,128)(2,1)S(1)} %copy-done.1, bf16[2560,512]{1,0:T(8,128)(2,1)S(1)} %collective-permute-done.1.refs_3_.refs_2_, bf16[64,512]{1,0:T(8,128)(2,1)S(1)} %get-tuple-element.42.refs_3_, ...), custom_call_target="tpu_custom_call" | custom-call | flops 2852126720 | bytes 9310208 | tf_op jit(solution)/shard_map/pallas_call | solution.py:53
  36.0 0.9 %collective-permute-start.14 = (bf16[16,2560]{1,0:T(8,128)(2,1)S(1)}, bf16[16,2560]{1,0:T(8,128)(2,1)S(1)}, u32[]{:S(2)}, u32[]{:S(2)}) collective-permute-start(bf16[16,2560]{1,0:T(8,128)(2,1)S(1)} %shard_map.107.refs_0_), channel_id=1, source_target_pairs={{0,4},{1,5},{4,0},{5,1},{8,12},{9,13},{12,8},{13,9},{2,6},{3,7},{6... | collective-permute-start | bytes 245768 | tf_op jit(solution)/shard_map/ppermute | solution.py:31
  36.9 3.6 %collective-permute-done.14.refs_1_ = bf16[16,2560]{1,0:T(8,128)(2,1)S(1)} collective-permute-done((bf16[16,2560]{1,0:T(8,128)(2,1)S(1)}, bf16[16,2560]{1,0:T(8,128)(2,1)S(1)}, u32[]{:S(2)}, u32[]{:S(2)}) %collective-permute-start.14) | collective-permute-done | bytes 81952 | tf_op jit(solution)/shard_map/ppermute | solution.py:31
  40.6 1.6 %shard_map.109 = (f32[16,64,512]{2,1,0:T(8,128)}, f32[8,128]{1,0:T(8,128)S(1)}) custom-call(s32[8]{0:T(128)} %refs_0_.8, bf16[4,64,512]{2,1,0:T(8,128)(2,1)S(1)} %shard_map.106.refs_2_.refs_1_, bf16[4,64,512]{2,1,0:T(8,128)(2,1)S(1)} %collective-permute-done.16.refs_2_, f32[16,64,512]{2,1,0:T(8,128)} %get-tuple-element.46.refs_3_, ...), custom_call_target="tpu_custom_call", output_to_operand_aliasing={{0}: (3, {})} | custom-call | bytes 4722720 | tf_op jit(solution)/shard_map/pallas_call | solution.py:53
  42.2 0.9 %shard_map.110 = f32[64,2560]{1,0:T(8,128)} custom-call(bf16[32,2560]{1,0:T(8,128)(2,1)S(1)} %shard_map.108.refs_4_.refs_0_, bf16[32,2560]{1,0:T(8,128)(2,1)S(1)} %collective-permute-done.15.refs_1_, f32[8,128]{1,0:T(8,128)S(1)} %get-tuple-element.47.refs_2_), custom_call_target="tpu_custom_call" | custom-call | bytes 983040 | tf_op jit(solution)/shard_map/pallas_call | solution.py:53
  (31 shorter events, 1.6 us)
Async XLA Ops:
  0.6 9.2 %collective-permute-start.1 = (bf16[2560,512]{1,0:T(8,128)(2,1)}, bf16[2560,512]{1,0:T(8,128)(2,1)S(1)}, u32[]{:S(2)}, u32[]{:S(2)}) collective-permute-start(bf16[2560,512]{1,0:T(8,128)(2,1)} %refs_1_.5), channel_id=1, source_target_pairs={{0,1},{1,0},{2,3},{3,2},{4,5},{5,4},{6,7},{7,6},{8,9},{9,8},{10,11... | collective-permute-start | bytes 7864328 | tf_op jit(solution)/shard_map/ppermute | solution.py:24
  2.4 10.4 %collective-permute-start.3 = (bf16[64,512]{1,0:T(8,128)(2,1)S(1)}, bf16[64,512]{1,0:T(8,128)(2,1)S(1)}, u32[]{:S(2)}, u32[]{:S(2)}) collective-permute-start(bf16[64,512]{1,0:T(8,128)(2,1)S(1)} %get-tuple-element.31), channel_id=1, source_target_pairs={{0,8},{1,9},{4,12},{5,13},{8,0},{9,1},{12,4},{13,5},{2,10},{3,11},... | collective-permute-start | bytes 196616 | tf_op jit(solution)/shard_map/ppermute | solution.py:31
  6.1 6.7 %collective-permute-start.4 = (bf16[64,512]{1,0:T(8,128)(2,1)S(1)}, bf16[64,512]{1,0:T(8,128)(2,1)S(1)}, u32[]{:S(2)}, u32[]{:S(2)}) collective-permute-start(bf16[64,512]{1,0:T(8,128)(2,1)S(1)} %get-tuple-element.32), channel_id=1, source_target_pairs={{0,12},{1,13},{4,8},{5,9},{8,4},{9,5},{12,0},{13,1},{2,14},{3,15},... | collective-permute-start | bytes 196616 | tf_op jit(solution)/shard_map/ppermute | solution.py:31
  7.4 5.6 %collective-permute-start.5 = (bf16[64,512]{1,0:T(8,128)(2,1)S(1)}, bf16[64,512]{1,0:T(8,128)(2,1)S(1)}, u32[]{:S(2)}, u32[]{:S(2)}) collective-permute-start(bf16[64,512]{1,0:T(8,128)(2,1)S(1)} %get-tuple-element.33), channel_id=1, source_target_pairs={{0,4},{1,5},{4,0},{5,1},{8,12},{9,13},{12,8},{13,9},{2,6},{3,7},{6... | collective-permute-start | bytes 196616 | tf_op jit(solution)/shard_map/ppermute | solution.py:31
  7.7 7.3 %collective-permute-start = (bf16[128,512]{1,0:T(8,128)(2,1)S(1)}, bf16[128,512]{1,0:T(8,128)(2,1)S(1)}, u32[]{:S(2)}, u32[]{:S(2)}) collective-permute-start(bf16[128,512]{1,0:T(8,128)(2,1)S(1)} %get-tuple-element.26), channel_id=1, source_target_pairs={{0,2},{2,0},{1,3},{3,1},{4,6},{6,4},{5,7},{7,5},{8,10},{10,8},{9,1... | collective-permute-start | bytes 393224 | tf_op jit(solution)/shard_map/ppermute | solution.py:24
  9.8 3.2 %copy-start = (bf16[512,512]{1,0:T(8,128)(2,1)S(1)}, bf16[512,512]{1,0:T(8,128)(2,1)}, u32[]{:S(2)}) copy-start(bf16[512,512]{1,0:T(8,128)(2,1)} %refs_1_.4) | copy-start | bytes 1572868
  12.2 5.1 %collective-permute-start.2 = (bf16[64,512]{1,0:T(8,128)(2,1)S(1)}, bf16[64,512]{1,0:T(8,128)(2,1)S(1)}, u32[]{:S(2)}, u32[]{:S(2)}) collective-permute-start(bf16[64,512]{1,0:T(8,128)(2,1)S(1)} %get-tuple-element.29), channel_id=1, source_target_pairs={{0,2},{2,0},{1,3},{3,1},{4,6},{6,4},{5,7},{7,5},{8,10},{10,8},{9,1... | collective-permute-start | bytes 196616 | tf_op jit(solution)/shard_map/ppermute | solution.py:24
  13.3 7.6 %collective-permute-start.7 = (f32[64,512]{1,0:T(8,128)S(1)}, f32[64,512]{1,0:T(8,128)S(1)}, u32[]{:S(2)}, u32[]{:S(2)}) collective-permute-start(f32[64,512]{1,0:T(8,128)S(1)} %shard_map.96.refs_4_.refs_1_), channel_id=1, source_target_pairs={{0,2},{2,0},{1,3},{3,1},{4,6},{6,4},{5,7},{7,5},{8,10},{10,8},{9,1... | collective-permute-start | bytes 393224 | tf_op jit(solution)/shard_map/ppermute | solution.py:24
  17.6 5.2 %collective-permute-start.9 = (bf16[1,64,512]{2,1,0:T(8,128)(2,1)S(1)}, bf16[1,64,512]{2,1,0:T(8,128)(2,1)S(1)}, u32[]{:S(2)}, u32[]{:S(2)}) collective-permute-start(bf16[1,64,512]{2,1,0:T(8,128)(2,1)S(1)} %get-tuple-element.36.refs_4_.refs_0_), channel_id=1, source_target_pairs={{0,8},{1,9},{4,12},{5,13},{8,0},{9,1},{12,4},{13,5},{2,10},{3,11},... | collective-permute-start | bytes 196616 | tf_op jit(solution)/shard_map/ppermute | solution.py:31
  20.3 4.3 %collective-permute-start.10 = (bf16[1,64,512]{2,1,0:T(8,128)(2,1)S(1)}, bf16[1,64,512]{2,1,0:T(8,128)(2,1)S(1)}, u32[]{:S(2)}, u32[]{:S(2)}) collective-permute-start(bf16[1,64,512]{2,1,0:T(8,128)(2,1)S(1)} %get-tuple-element.36.refs_4_.refs_0_), channel_id=1, source_target_pairs={{0,4},{1,5},{4,0},{5,1},{8,12},{9,13},{12,8},{13,9},{2,6},{3,7},{6... | collective-permute-start | bytes 196616 | tf_op jit(solution)/shard_map/ppermute | solution.py:31
  20.8 10.5 %collective-permute-start.6 = (bf16[384,512]{1,0:T(8,128)(2,1)S(1)}, bf16[384,512]{1,0:T(8,128)(2,1)S(1)}, u32[]{:S(2)}, u32[]{:S(2)}) collective-permute-start(bf16[384,512]{1,0:T(8,128)(2,1)S(1)} %get-tuple-element.34), channel_id=1, source_target_pairs={{0,2},{2,0},{1,3},{3,1},{4,6},{6,4},{5,7},{7,5},{8,10},{10,8},{9,1... | collective-permute-start | bytes 1179656 | tf_op jit(solution)/shard_map/ppermute | solution.py:24
  21.6 3.1 %collective-permute-start.8 = (f32[32,2560]{1,0:T(8,128)S(1)}, f32[32,2560]{1,0:T(8,128)S(1)}, u32[]{:S(2)}, u32[]{:S(2)}) collective-permute-start(f32[32,2560]{1,0:T(8,128)S(1)} %get-tuple-element.38), channel_id=1, source_target_pairs={{0,1},{1,0},{2,3},{3,2},{4,5},{5,4},{6,7},{7,6},{8,9},{9,8},{10,11... | collective-permute-start | bytes 983048 | tf_op jit(solution)/shard_map/ppermute | solution.py:24
  24.7 4.5 %collective-permute-start.11 = (bf16[16,2560]{1,0:T(8,128)(2,1)S(1)}, bf16[16,2560]{1,0:T(8,128)(2,1)S(1)}, u32[]{:S(2)}, u32[]{:S(2)}) collective-permute-start(bf16[16,2560]{1,0:T(8,128)(2,1)S(1)} %get-tuple-element.40.refs_0_), channel_id=1, source_target_pairs={{0,4},{1,5},{4,0},{5,1},{8,12},{9,13},{12,8},{13,9},{2,6},{3,7},{6... | collective-permute-start | bytes 245768 | tf_op jit(solution)/shard_map/ppermute | solution.py:31
  26.9 4.6 %copy-start.1 = (bf16[2560,512]{1,0:T(8,128)(2,1)S(1)}, bf16[2560,512]{1,0:T(8,128)(2,1)}, u32[]{:S(2)}) copy-start(bf16[2560,512]{1,0:T(8,128)(2,1)} %refs_1_.5) | copy-start | bytes 7864324
  29.2 6.8 %collective-permute-start.12 = (bf16[16,2560]{1,0:T(8,128)(2,1)S(1)}, bf16[16,2560]{1,0:T(8,128)(2,1)S(1)}, u32[]{:S(2)}, u32[]{:S(2)}) collective-permute-start(bf16[16,2560]{1,0:T(8,128)(2,1)S(1)} %shard_map.102.refs_4_.refs_1_.refs_0_), channel_id=1, source_target_pairs={{0,8},{1,9},{4,12},{5,13},{8,0},{9,1},{12,4},{13,5},{2,10},{3,11},... | collective-permute-start | bytes 245768 | tf_op jit(solution)/shard_map/ppermute | solution.py:31
  30.2 5.7 %collective-permute-start.13 = (bf16[1,64,512]{2,1,0:T(8,128)(2,1)S(1)}, bf16[1,64,512]{2,1,0:T(8,128)(2,1)S(1)}, u32[]{:S(2)}, u32[]{:S(2)}) collective-permute-start(bf16[1,64,512]{2,1,0:T(8,128)(2,1)S(1)} %shard_map.104.refs_5_), channel_id=1, source_target_pairs={{0,4},{1,5},{4,0},{5,1},{8,12},{9,13},{12,8},{13,9},{2,6},{3,7},{6... | collective-permute-start | bytes 196616 | tf_op jit(solution)/shard_map/ppermute | solution.py:31
  36.0 4.5 %collective-permute-start.14 = (bf16[16,2560]{1,0:T(8,128)(2,1)S(1)}, bf16[16,2560]{1,0:T(8,128)(2,1)S(1)}, u32[]{:S(2)}, u32[]{:S(2)}) collective-permute-start(bf16[16,2560]{1,0:T(8,128)(2,1)S(1)} %shard_map.107.refs_0_), channel_id=1, source_target_pairs={{0,4},{1,5},{4,0},{5,1},{8,12},{9,13},{12,8},{13,9},{2,6},{3,7},{6... | collective-permute-start | bytes 245768 | tf_op jit(solution)/shard_map/ppermute | solution.py:31
  36.9 3.7 %collective-permute-start.16 = (bf16[4,64,512]{2,1,0:T(8,128)(2,1)S(1)}, bf16[4,64,512]{2,1,0:T(8,128)(2,1)S(1)}, u32[]{:S(2)}, u32[]{:S(2)}) collective-permute-start(bf16[4,64,512]{2,1,0:T(8,128)(2,1)S(1)} %shard_map.106.refs_2_.refs_1_), channel_id=1, source_target_pairs={{0,1},{1,0},{2,3},{3,2},{4,5},{5,4},{6,7},{7,6},{8,9},{9,8},{10,11... | collective-permute-start | bytes 786440 | tf_op jit(solution)/shard_map/ppermute | solution.py:24
  40.5 1.7 %collective-permute-start.15 = (bf16[32,2560]{1,0:T(8,128)(2,1)S(1)}, bf16[32,2560]{1,0:T(8,128)(2,1)S(1)}, u32[]{:S(2)}, u32[]{:S(2)}) collective-permute-start(bf16[32,2560]{1,0:T(8,128)(2,1)S(1)} %shard_map.108.refs_4_.refs_0_), channel_id=1, source_target_pairs={{0,1},{1,0},{2,3},{3,2},{4,5},{5,4},{6,7},{7,6},{8,9},{9,8},{10,11... | collective-permute-start | bytes 491528 | tf_op jit(solution)/shard_map/ppermute | solution.py:24

commit v9 on v8

--- a/solution.py
+++ b/solution.py
@@ -9,9 +9,9 @@
 f32 = jnp.float32
 bf16 = jnp.bfloat16
 
-early_part = 4
-
-busy, middling, brief, slight = 10**10, 5 * 10**9, 3 * 10**9, 15 * 10**8
+(busy, first_cost, middling, filling, brief, slight) = (
+    10**10, 5 * 10**9, 5 * 10**9, 10**10, 3 * 10**9, 15 * 10**8
+)
 
 anywhere = pl.BlockSpec(memory_space=pl.ANY)
 in_hbm = pl.BlockSpec(memory_space=pltpu.HBM)
@@ -61,83 +61,66 @@
     )(*operands, *after)
 
 
-def pick_heads(adapter_ids, head_up, grad):
+def pick_heads(adapter_ids, head_up):
     per_owner, rank, width = head_up.shape
     own_count, sub_count = lax.axis_size("own"), lax.axis_size("sub")
-    first = grad.shape[0] // early_part
-
-    def body(ids_far, head_up, grad, *refs):
-        outs, early, away, ids, maps, sems = refs[:own_count], *refs[own_count:]
+
+    def body(ids_far, head_up, *refs):
+        outs, away, ids, maps, sems = refs[:own_count], *refs[own_count:]
         own, sub = lax.axis_index("own"), lax.axis_index("sub")
         copies = [
             pltpu.make_async_copy(ids_far, ids, sems.at[0]),
             pltpu.make_async_copy(head_up, maps, sems.at[1]),
-            pltpu.make_async_copy(grad.at[pl.ds(0, first)], early, sems.at[2]),
         ]
         for copy in copies:
             copy.start()
-        copies[0].wait()
-        copies[1].wait()
+        for copy in copies:
+            copy.wait()
         for step in range(own_count):
             local = ids[(own ^ step) * sub_count + sub] - own * per_owner
             outs[step][...] = maps[jnp.clip(local, 0, per_owner - 1)]
         step = lax.div(ids[own * sub_count + sub], per_owner) ^ own
         away[...] = jnp.full(away.shape, step, jnp.int32)
-        copies[2].wait()
-
-    *picked, early, away = call(
-        body,
-        [stay(adapter_ids), stay(head_up), stay(grad)],
-        [in_hbm] * 3,
-        [shape_of((rank, width), bf16)] * own_count
-        + [shape_of((first, grad.shape[1]), bf16), shape_of((8, 128), jnp.int32)],
+
+    *picked, away = call(
+        body,
+        [stay(adapter_ids), stay(head_up)],
+        [in_hbm] * 2,
+        [shape_of((rank, width), bf16)] * own_count + [shape_of((8, 128), jnp.int32)],
         scratch_shapes=[
             pltpu.SMEM(adapter_ids.shape, jnp.int32),
             pltpu.VMEM(head_up.shape, bf16),
-            pltpu.SemaphoreType.DMA((3,)),
+            pltpu.SemaphoreType.DMA((2,)),
         ],
-    )
-    return picked, early, away
+        flops=first_cost,
+    )
+    return picked, away
 
 
 def project_low(tokens, down, after):
     rows, features = tokens.shape
     rank = down.shape[0]
-    width = width_of(features)
-    blocks = features // width
-
-    def body(tokens, down, low, rounded, near_tokens, near_down, sems):
-        copies = [pltpu.make_async_copy(down, near_down, sems.at[blocks])]
-        for at in range(blocks):
-            here = pl.ds(at * width, width)
-            copies.append(
-                pltpu.make_async_copy(tokens.at[:, here], near_tokens.at[:, here], sems.at[at])
-            )
-        for copy in copies:
-            copy.start()
-        copies[0].wait()
-        total = None
-        for at in range(blocks):
-            copies[at + 1].wait()
-            here = slice(at * width, (at + 1) * width)
-            part = lax.dot_general(
-                near_down[:, here], near_tokens[:, here], (((1,), (1,)), ((), ())),
-                preferred_element_type=f32,
-            )
-            total = part if total is None else total + part
-        low[...] = total
-        rounded[...] = total.astype(bf16)
-
-    return call(
-        body,
-        [stay(tokens), stay(down)],
-        [in_hbm] * 2,
-        [shape_of((rank, rows), f32), shape_of((rank, rows), bf16)]
-        + [shape_of(tokens.shape, bf16), shape_of(down.shape, bf16)],
+
+    def body(tokens, down, low):
+        low[...] = lax.dot_general(
+            down[...], tokens[...], (((1,), (1,)), ((), ())), preferred_element_type=f32
+        )
+
+    return call(
+        body,
+        [tokens, down],
+        [in_vmem] * 2,
+        [shape_of((rank, rows), f32)],
         after=after,
         flops=2 * rows * rank * features,
-        scratch_shapes=[pltpu.SemaphoreType.DMA((blocks + 1,))],
-    )
+    )[0]
+
+
+def rounded(x, after):
+    def body(x, out):
+        out[...] = x[...].astype(bf16)
+
+    return call(body, [x], [in_vmem], [shape_of(x.shape, bf16)], after=after)[0]
 
 
 def project_back(away, offered, steps, grad, after):
@@ -167,10 +150,9 @@
 def head_term(lengths, lows, grad, scale, after):
     rank, rows = lows[0].shape
     columns = grad.shape[1]
-    first = rows // early_part
 
     def body(lengths, *refs):
-        *lows, grad, term, late = refs
+        *lows, grad, term, again = refs
         total = lows[0][...]
         for low in lows[1:]:
             total = total + low[...].astype(f32)
@@ -181,13 +163,13 @@
         product = jnp.dot(kept, grad[...], preferred_element_type=f32)
         product += jnp.dot(rest, grad[...], preferred_element_type=f32)
         term[0] = (scale * product).astype(bf16)
-        late[...] = grad[first:, :]
+        again[...] = grad[...]
 
     return call(
         body,
         [lengths, *lows, grad],
         [in_smem] + [in_vmem] * (len(lows) + 1),
-        [shape_of((1, rank, columns), bf16), shape_of((rows - first, columns), bf16)],
+        [shape_of((1, rank, columns), bf16), shape_of(grad.shape, bf16)],
         after=after,
         flops=brief,
     )
@@ -260,7 +242,7 @@
     )
 
 
-def rejoin(mine, arrived, bit):
+def rejoin(mine, arrived, bit, after):
     rows, features = mine.shape
 
     def body(mine, arrived, out):
@@ -274,6 +256,7 @@
         [mine, arrived],
         [in_vmem] * 2,
         [shape_of((2 * rows, features), bf16)],
+        after=after,
         flops=busy,
     )[0]
 
@@ -314,25 +297,47 @@
     )[0]
 
 
-def clean(dims, after):
-    def body(out, mark, held, sem):
-        held[...] = jnp.zeros(held.shape, f32)
-        mark[...] = jnp.zeros(mark.shape, f32)
-        copies = [pltpu.make_async_copy(held, out.at[at], sem.at[at]) for at in range(dims[0])]
+def prepare(dims, frozen, frozen_other, down, after):
+    features, half = frozen.shape
+    rank = down.shape[0]
+    padded = -(-rank // 128) * 128
+
+    def body(frozen, frozen_other, down, out, wide, held, sems, weight_sems):
+        sub = lax.axis_index("sub")
+        copies = [
+            pltpu.make_async_copy(
+                piece,
+                wide.at[:, pl.ds(pl.multiple_of(side * half, 128), half)],
+                weight_sems.at[at],
+            )
+            for at, (side, piece) in enumerate(((sub, frozen), (1 - sub, frozen_other)))
+        ]
         for copy in copies:
             copy.start()
-        for copy in copies:
+        held[...] = jnp.zeros(held.shape, f32)
+        zeros = [pltpu.make_async_copy(held, out.at[at], sems.at[at]) for at in range(dims[0])]
+        for copy in zeros:
+            copy.start()
+        down = down[...].astype(f32)
+        if padded > rank:
+            down = jnp.concatenate([down, jnp.zeros((padded - rank, features), f32)], axis=0)
+        wide[:, 2 * half :] = down.T.astype(bf16)
+        for copy in copies + zeros:
             copy.wait()
 
     return call(
         body,
-        [],
-        [],
-        [shape_of(dims, f32), shape_of((8, 128), f32)],
+        [stay(frozen), frozen_other, down],
+        [in_hbm, anywhere, in_vmem],
+        [shape_of(dims, f32), shape_of((features, 2 * half + padded), bf16)],
         out_specs=[in_hbm, in_vmem],
         after=after,
-        scratch_shapes=[pltpu.VMEM(dims[1:], f32), pltpu.SemaphoreType.DMA((dims[0],))],
-        flops=busy,
+        scratch_shapes=[
+            pltpu.VMEM(dims[1:], f32),
+            pltpu.SemaphoreType.DMA((dims[0],)),
+            pltpu.SemaphoreType.DMA((2,)),
+        ],
+        flops=filling,
     )
 
 
@@ -392,57 +397,49 @@
     )
 
 
-def arrange(lengths, grad, pieces, after):
-    rows, columns = grad.shape
-    count = 1 + len(pieces)
-    first = rows // early_part
-
-    def body(lengths, grad, *refs):
-        pieces, kept = refs[:-1], refs[-1]
+def arrange(lengths, grads, back, width, after):
+    rows, columns = grads[0].shape
+    count = len(grads)
+    rank = back.shape[0]
+    padded = width - count * columns
+
+    def body(lengths, *refs):
+        *grads, back, kept = refs
         at = lax.axis_index("tp")
         live = lax.broadcasted_iota(jnp.int32, (rows, columns), 0) < lengths[0]
-        zero = jnp.zeros((rows, columns), bf16)
-        place = pl.multiple_of(at * columns, 128)
-        kept[:, pl.ds(place, columns)] = jnp.where(live, grad[...], zero)
-        for step in range(1, count):
+        for step, grad in enumerate(grads):
             place = pl.multiple_of(lax.rem(at + count - step, count) * columns, 128)
-            early, late = pieces[2 * step - 2 : 2 * step]
-            kept[:first, pl.ds(place, columns)] = jnp.where(live[:first], early[...], zero[:first])
-            kept[first:, pl.ds(place, columns)] = jnp.where(live[first:], late[...], zero[first:])
-
-    flat = [x for pair in pieces for x in pair]
-    return call(
-        body,
-        [lengths, grad, *flat],
-        [in_smem] + [in_vmem] * (1 + len(flat)),
-        [shape_of((rows, count * columns), bf16)],
-        after=after,
-    )[0]
-
-
-def input_side(kept, frozen, frozen_other, back, down, after):
-    rows, whole = kept.shape
-    features, half = frozen.shape
-    rank = back.shape[0]
+            kept[:, pl.ds(place, columns)] = jnp.where(
+                live, grad[...], jnp.zeros((rows, columns), bf16)
+            )
+        twice = adapter_scale * back[...].astype(f32)
+        if padded > rank:
+            twice = jnp.concatenate([twice, jnp.zeros((padded - rank, rows), f32)], axis=0)
+        kept[:, count * columns :] = twice.T.astype(bf16)
+
+    return call(
+        body,
+        [lengths, *grads, back],
+        [in_smem] + [in_vmem] * (count + 1),
+        [shape_of((rows, width), bf16)],
+        after=after,
+    )[0]
+
+
+def input_side(kept, wide, after):
+    rows = kept.shape[0]
+    features = wide.shape[0]
     width = width_of(features)
     blocks = features // width
 
-    def body(kept, frozen, frozen_other, back, down, out, mark, held, sems):
+    def body(kept, wide, out, mark, held, sems):
         mark[...] = jnp.zeros(mark.shape, f32)
-        sub = lax.axis_index("sub")
-        both = (((1,), (1,)), ((), ()))
-        mine = kept[:, pl.ds(pl.multiple_of(sub * half, 128), half)]
-        other = kept[:, pl.ds(pl.multiple_of((1 - sub) * half, 128), half)]
-        twice = adapter_scale * back[...]
         copies = []
         for at in range(blocks):
             here = slice(at * width, (at + 1) * width)
-            total = lax.dot_general(mine, frozen[here, :], both, preferred_element_type=f32)
-            total += lax.dot_general(other, frozen_other[here, :], both, preferred_element_type=f32)
-            total += lax.dot_general(
-                twice, down[:, here], (((0,), (0,)), ((), ())), preferred_element_type=f32
-            )
-            held[:, here] = total.astype(bf16)
+            held[:, here] = lax.dot_general(
+                kept[...], wide[here, :], (((1,), (1,)), ((), ())), preferred_element_type=f32
+            ).astype(bf16)
             copies.append(
                 pltpu.make_async_copy(held.at[:, here], out.at[:, here], sems.at[at])
             )
@@ -452,8 +449,8 @@
 
     return call(
         body,
-        [kept, frozen, frozen_other, back, down],
-        [in_vmem] * 5,
+        [kept, wide],
+        [in_vmem] * 2,
         [shape_of((rows, features), bf16), shape_of((8, 128), f32)],
         out_specs=[in_hbm, in_vmem],
         after=after,
@@ -461,7 +458,7 @@
             pltpu.VMEM((rows, features), bf16),
             pltpu.SemaphoreType.DMA((blocks,)),
         ],
-        flops=2 * rows * features * (2 * half + rank),
+        flops=2 * rows * features * wide.shape[1],
     )
 
 
@@ -474,21 +471,20 @@
     tp_steps, own_steps = range(1, tp_count), range(1, own_count)
 
     frozen_other = shift(frozen_value, "sub", 1)
-    picked, early, away = pick_heads(adapter_ids, head_up, grad_output)
+    picked, away = pick_heads(adapter_ids, head_up)
     steps = sorted(own_steps, key=lambda step: (-step.bit_length(), step))
     offered = [picked[0]] + [swap(picked[step], step, 0) for step in steps]
-    early_grads = [shift(early, "tp", step) for step in tp_steps]
-
-    low, rounded, tokens, down = project_low(
-        tokens, shared_down.T, [picked[0], frozen_other]
-    )
-    lows = [low] + [shift(rounded, "tp", step) for step in tp_steps]
+
+    down = shared_down.T
+    low = project_low(tokens, down, picked[:1])
+    sent = rounded(low, [low])
+    lows = [low] + [shift(sent, "tp", step) for step in tp_steps]
 
     part = project_back(away, offered, steps, grad_output, [low])
     parts = [part] + [shift(part, "tp", step) for step in tp_steps]
 
-    near, late = head_term(lengths, lows, grad_output, scale, [part, *early_grads])
-    late_grads = [shift(late, "tp", step) for step in tp_steps]
+    near, again = head_term(lengths, lows, grad_output, scale, [part])
+    grads = [grad_output] + [shift(again, "tp", step) for step in tp_steps]
     bits = [1 << i for i in range(own_count.bit_length() - 1)]
     terms, pattern = [near], [0]
     for bit in reversed(bits[1:]):
@@ -505,21 +501,22 @@
         stays, leaves = halve(pieces, bit, [mark])
         pieces = [stays, swap(leaves, bit, 0)]
         mark = leaves
-    cleaned, mark = clean((per_owner,) + near.shape[1:], [mark])
-    total = add_up(pieces, [mark])
+    cleaned, wide = prepare((per_owner,) + near.shape[1:], frozen_value, frozen_other, down, [mark])
+    total = add_up(pieces, [wide])
     relays = [total]
     if bits:
         relays = [stack([term], [total]) for term in terms[1:]]
         terms = terms + nearby + [swap(relay, 1, 0) for relay in relays]
         pattern = pattern + [step ^ 1 for step in pattern]
-    kept = arrange(lengths, grad_output, list(zip(early_grads, late_grads)), [total])
-    input_gradient, mark = input_side(kept, frozen_value, frozen_other, back, down, relays)
-    near = stack(terms, [mark])
+    near = stack(terms, [total])
     if bits:
         total = add_up([total, swap(total, bits[-1], 0)], [near])
     far = shift(near, "sub", 1)
+    kept = arrange(lengths, grads, back, wide.shape[1], [total])
+    input_gradient, mark = input_side(kept, wide, [total])
     for bit in reversed(bits[:-1]):
-        total = rejoin(total, swap(total, bit, 0), bit)
+        total = rejoin(total, swap(total, bit, 0), bit, [mark])
+        mark = total
     grad_heads, mark = place_terms(adapter_ids, near, far, pattern, cleaned, [total])
     shared_down_gradient = join_shares(total, shift(total, "sub", 1), [mark]).T
     return (input_gradient, shared_down_gradient, grad_heads)

time: 43.4 us -> 42.1 us (0.970)
  waiting for transfers between devices: 11.4 us -> 8.15 us
  starting transfers between devices: 16.8 us -> 18.7 us
    ppermute x8 -> x7, waiting for transfers between devices: 2.38 us -> 0.02 us  [shift(): lax.ppermute(x, axis, [(i, (i + step) % count) for i in range(count)])]
    ppermute x9, starting transfers between devices: 12.3 us -> 14.1 us  [swap(): lax.ppermute(x, ('own', 'sub'), [(i, i ^ other) for i in range(whole)])]
    ppermute x9, waiting for transfers between devices: 9.05 us -> 8.13 us  [swap(): lax.ppermute(x, ('own', 'sub'), [(i, i ^ other) for i in range(whole)])]
    pallas_call x17 -> x18, Pallas kernels: 13.4 us -> 13.6 us  [call(): pl.pallas_call(kernel, out_shape=outs, in_specs=list(specs) + [anywhere]...]
    ppermute x8 -> x7, starting transfers between devices: 4.48 us -> 4.63 us  [shift(): lax.ppermute(x, axis, [(i, (i + step) % count) for i in range(count)])]
  transfers between devices with their start and end apart: 17 -> 16, of which waited for: 6 -> 6; matrix products, arithmetic and copies ran while one was open for 0% -> 0% of each run, Pallas kernels for 29% -> 30%
where the time goes in v9:
time: 42.1 us; the launch traced here: 42 us
  starting transfers between devices  18.7 us (44%)
  Pallas kernels  13.6 us (32%)
  waiting for transfers between devices  8.15 us (19%)
  between operations  1.47 us (3%)
    ppermute x9, starting transfers between devices, swap(): lax.ppermute(x, ('own', 'sub'), [(i, i ^ other) for i in range(whole)])  14.1 us
    pallas_call x18, Pallas kernels, call(): pl.pallas_call(kernel, out_shape=outs, in_specs=list(specs) + [anywhere]...  13.6 us
    ppermute x9, waiting for transfers between devices, swap(): lax.ppermute(x, ('own', 'sub'), [(i, i ^ other) for i in range(whole)])  8.13 us
    ppermute x7, starting transfers between devices, shift(): lax.ppermute(x, axis, [(i, (i + step) % count) for i in range(count)])  4.63 us
  transfers between devices with their start and end apart: 16, of which 6 were waited for; matrix products, arithmetic and copies ran while one was open for 0% of the time, Pallas kernels for 30%

profile of v9, /device:TPU:0, one launch (start us, length us, event | category | flops | bytes accessed | tf_op | source)
XLA Modules:
  0.0 42.0 jit_solution(15369406268956375541)
XLA Ops:
  0.7 0.5 %collective-permute-start.10 = (bf16[2560,512]{1,0:T(8,128)(2,1)}, bf16[2560,512]{1,0:T(8,128)(2,1)S(1)}, u32[]{:S(2)}, u32[]{:S(2)}) collective-permute-start(bf16[2560,512]{1,0:T(8,128)(2,1)} %refs_0_.9), channel_id=1, source_target_pairs={{0,1},{1,0},{2,3},{3,2},{4,5},{5,4},{6,7},{7,6},{8,9},{9,8},{10,11... | collective-permute-start | bytes 7864328 | tf_op jit(solution)/shard_map/ppermute | solution.py:24
  1.2 1.5 %shard_map.94 = (bf16[64,512]{1,0:T(8,128)(2,1)S(1)}, bf16[64,512]{1,0:T(8,128)(2,1)S(1)}, bf16[64,512]{1,0:T(8,128)(2,1)S(1)}, bf16[64,512]{1,0:T(8,128)(2,1)S(1)}, s32[8,128]{1,0:T(8,128)S(1)}) custom-call(s32[8]{0:T(128)} %refs_0_.10, bf16[16,64,512]{2,1,0:T(8,128)(2,1)} %refs_1_.2), custom_call_target="tpu_custom_call" | custom-call | flops 5000000000 | bytes 1314848 | tf_op jit(solution)/shard_map/pallas_call | solution.py:53
  2.7 3.6 %collective-permute-start.1 = (bf16[64,512]{1,0:T(8,128)(2,1)S(1)}, bf16[64,512]{1,0:T(8,128)(2,1)S(1)}, u32[]{:S(2)}, u32[]{:S(2)}) collective-permute-start(bf16[64,512]{1,0:T(8,128)(2,1)S(1)} %get-tuple-element.23), channel_id=1, source_target_pairs={{0,8},{1,9},{4,12},{5,13},{8,0},{9,1},{12,4},{13,5},{2,10},{3,11},... | collective-permute-start | bytes 196616 | tf_op jit(solution)/shard_map/ppermute | solution.py:31
  6.3 1.3 %collective-permute-start.2 = (bf16[64,512]{1,0:T(8,128)(2,1)S(1)}, bf16[64,512]{1,0:T(8,128)(2,1)S(1)}, u32[]{:S(2)}, u32[]{:S(2)}) collective-permute-start(bf16[64,512]{1,0:T(8,128)(2,1)S(1)} %get-tuple-element.24), channel_id=1, source_target_pairs={{0,12},{1,13},{4,8},{5,9},{8,4},{9,5},{12,0},{13,1},{2,14},{3,15},... | collective-permute-start | bytes 196616 | tf_op jit(solution)/shard_map/ppermute | solution.py:31
  7.9 0.9 %shard_map.95.refs_0_.refs_1_.refs_6_ = f32[64,512]{1,0:T(8,128)S(1)} custom-call(bf16[512,2560]{1,0:T(8,128)(2,1)S(1)} %copy-done, bf16[64,2560]{1,0:T(8,128)(2,1)S(1)} %bitcast.2, bf16[64,512]{1,0:T(8,128)(2,1)S(1)} %get-tuple-element.21.refs_2_.refs_1_), custom_call_target="tpu_custom_call" | custom-call | flops 167772160 | bytes 3080192 | tf_op jit(solution)/shard_map/pallas_call | solution.py:53
  8.8 1.6 %collective-permute-start = (bf16[64,512]{1,0:T(8,128)(2,1)S(1)}, bf16[64,512]{1,0:T(8,128)(2,1)S(1)}, u32[]{:S(2)}, u32[]{:S(2)}) collective-permute-start(bf16[64,512]{1,0:T(8,128)(2,1)S(1)} %shard_map.96), channel_id=1, source_target_pairs={{0,2},{2,0},{1,3},{3,1},{4,6},{6,4},{5,7},{7,5},{8,10},{10,8},{9,1... | collective-permute-start | bytes 196616 | tf_op jit(solution)/shard_map/ppermute | solution.py:24
  11.0 2.0 %collective-permute-done.2.refs_3_ = bf16[64,512]{1,0:T(8,128)(2,1)S(1)} collective-permute-done((bf16[64,512]{1,0:T(8,128)(2,1)S(1)}, bf16[64,512]{1,0:T(8,128)(2,1)S(1)}, u32[]{:S(2)}, u32[]{:S(2)}) %collective-permute-start.2) | collective-permute-done | bytes 65568 | tf_op jit(solution)/shard_map/ppermute | solution.py:31
  13.5 1.6 %collective-permute-start.5 = (f32[64,512]{1,0:T(8,128)S(1)}, f32[64,512]{1,0:T(8,128)S(1)}, u32[]{:S(2)}, u32[]{:S(2)}) collective-permute-start(f32[64,512]{1,0:T(8,128)S(1)} %shard_map.97.refs_4_.refs_1_), channel_id=1, source_target_pairs={{0,2},{2,0},{1,3},{3,1},{4,6},{6,4},{5,7},{7,5},{8,10},{10,8},{9,1... | collective-permute-start | bytes 393224 | tf_op jit(solution)/shard_map/ppermute | solution.py:24
  15.4 2.7 %collective-permute-start.7 = (bf16[1,64,512]{2,1,0:T(8,128)(2,1)S(1)}, bf16[1,64,512]{2,1,0:T(8,128)(2,1)S(1)}, u32[]{:S(2)}, u32[]{:S(2)}) collective-permute-start(bf16[1,64,512]{2,1,0:T(8,128)(2,1)S(1)} %get-tuple-element.27.refs_4_.refs_0_), channel_id=1, source_target_pairs={{0,8},{1,9},{4,12},{5,13},{8,0},{9,1},{12,4},{13,5},{2,10},{3,11},... | collective-permute-start | bytes 196616 | tf_op jit(solution)/shard_map/ppermute | solution.py:31
  18.1 1.2 %collective-permute-start.8 = (bf16[1,64,512]{2,1,0:T(8,128)(2,1)S(1)}, bf16[1,64,512]{2,1,0:T(8,128)(2,1)S(1)}, u32[]{:S(2)}, u32[]{:S(2)}) collective-permute-start(bf16[1,64,512]{2,1,0:T(8,128)(2,1)S(1)} %get-tuple-element.27.refs_4_.refs_0_), channel_id=1, source_target_pairs={{0,4},{1,5},{4,0},{5,1},{8,12},{9,13},{12,8},{13,9},{2,6},{3,7},{6... | collective-permute-start | bytes 196616 | tf_op jit(solution)/shard_map/ppermute | solution.py:31
  19.3 0.5 %collective-permute-start.4 = (bf16[512,512]{1,0:T(8,128)(2,1)S(1)}, bf16[512,512]{1,0:T(8,128)(2,1)S(1)}, u32[]{:S(2)}, u32[]{:S(2)}) collective-permute-start(bf16[512,512]{1,0:T(8,128)(2,1)S(1)} %get-tuple-element.26), channel_id=1, source_target_pairs={{0,2},{2,0},{1,3},{3,1},{4,6},{6,4},{5,7},{7,5},{8,10},{10,8},{9,1... | collective-permute-start | bytes 1572872 | tf_op jit(solution)/shard_map/ppermute | solution.py:24
  19.9 0.6 %shard_map.99 = (bf16[64,512]{1,0:T(8,128)(2,1)S(1)}, f32[32,2560]{1,0:T(8,128)S(1)}, f32[32,2560]{1,0:T(8,128)S(1)}) custom-call(s32[1]{0:T(128)S(6)} %copy.12.refs_0_, f32[64,512]{1,0:T(8,128)S(1)} %shard_map.97.refs_4_.refs_1_, f32[64,512]{1,0:T(8,128)S(1)} %collective-permute-done.5.refs_2_, bf16[512,2560]{1,0:T(8,128)(2,1)S(1)} %copy-done, ...), custom_call_target="tpu_custom_call" | custom-call | flops 167772160 | bytes 3604484 | tf_op jit(solution)/shard_map/pallas_call | solution.py:53
  20.6 1.0 %collective-permute-done.7.refs_0_.refs_1_ = bf16[1,64,512]{2,1,0:T(8,128)(2,1)S(1)} collective-permute-done((bf16[1,64,512]{2,1,0:T(8,128)(2,1)S(1)}, bf16[1,64,512]{2,1,0:T(8,128)(2,1)S(1)}, u32[]{:S(2)}, u32[]{:S(2)}) %collective-permute-start.7) | collective-permute-done | bytes 65568 | tf_op jit(solution)/shard_map/ppermute | solution.py:31
  21.6 0.8 %collective-permute-done.8.refs_1_.refs_2_ = bf16[1,64,512]{2,1,0:T(8,128)(2,1)S(1)} collective-permute-done((bf16[1,64,512]{2,1,0:T(8,128)(2,1)S(1)}, bf16[1,64,512]{2,1,0:T(8,128)(2,1)S(1)}, u32[]{:S(2)}, u32[]{:S(2)}) %collective-permute-start.8) | collective-permute-done | bytes 65568 | tf_op jit(solution)/shard_map/ppermute | solution.py:31
  22.5 1.3 %collective-permute-start.9 = (bf16[16,2560]{1,0:T(8,128)(2,1)S(1)}, bf16[16,2560]{1,0:T(8,128)(2,1)S(1)}, u32[]{:S(2)}, u32[]{:S(2)}) collective-permute-start(bf16[16,2560]{1,0:T(8,128)(2,1)S(1)} %get-tuple-element.32.refs_3_), channel_id=1, source_target_pairs={{0,4},{1,5},{4,0},{5,1},{8,12},{9,13},{12,8},{13,9},{2,6},{3,7},{6... | collective-permute-start | bytes 245768 | tf_op jit(solution)/shard_map/ppermute | solution.py:31
  23.7 2.7 %shard_map.102 = (f32[16,64,512]{2,1,0:T(8,128)}, bf16[2560,1152]{1,0:T(8,128)(2,1)S(1)}) custom-call(bf16[2560,512]{1,0:T(8,128)(2,1)} %refs_0_.9, bf16[2560,512]{1,0:T(8,128)(2,1)S(1)} %collective-permute-done.10.refs_1_, bf16[64,2560]{1,0:T(8,128)(2,1)S(1)} %bitcast.3, bf16[16,2560]{1,0:T(8,128)(2,1)S(1)} %get-tuple-element.32.refs_3_), custom_call_target="tpu_custom_call" | custom-call | flops 10000000000 | bytes 13565952 | tf_op jit(solution)/shard_map/pallas_call | solution.py:53
  26.4 0.5 %collective-permute-done.9.refs_1_ = bf16[16,2560]{1,0:T(8,128)(2,1)S(1)} collective-permute-done((bf16[16,2560]{1,0:T(8,128)(2,1)S(1)}, bf16[16,2560]{1,0:T(8,128)(2,1)S(1)}, u32[]{:S(2)}, u32[]{:S(2)}) %collective-permute-start.9) | collective-permute-done | bytes 81952 | tf_op jit(solution)/shard_map/ppermute | solution.py:31
  27.0 2.1 %collective-permute-start.11 = (bf16[16,2560]{1,0:T(8,128)(2,1)S(1)}, bf16[16,2560]{1,0:T(8,128)(2,1)S(1)}, u32[]{:S(2)}, u32[]{:S(2)}) collective-permute-start(bf16[16,2560]{1,0:T(8,128)(2,1)S(1)} %shard_map.103.refs_1_.refs_4_.refs_0_), channel_id=1, source_target_pairs={{0,8},{1,9},{4,12},{5,13},{8,0},{9,1},{12,4},{13,5},{2,10},{3,11},... | collective-permute-start | bytes 245768 | tf_op jit(solution)/shard_map/ppermute | solution.py:31
  29.1 0.8 %collective-permute-start.12 = (bf16[1,64,512]{2,1,0:T(8,128)(2,1)S(1)}, bf16[1,64,512]{2,1,0:T(8,128)(2,1)S(1)}, u32[]{:S(2)}, u32[]{:S(2)}) collective-permute-start(bf16[1,64,512]{2,1,0:T(8,128)(2,1)S(1)} %shard_map.104), channel_id=1, source_target_pairs={{0,4},{1,5},{4,0},{5,1},{8,12},{9,13},{12,8},{13,9},{2,6},{3,7},{6... | collective-permute-start | bytes 196616 | tf_op jit(solution)/shard_map/ppermute | solution.py:31
  30.0 3.6 %collective-permute-done.12.refs_3_ = bf16[1,64,512]{2,1,0:T(8,128)(2,1)S(1)} collective-permute-done((bf16[1,64,512]{2,1,0:T(8,128)(2,1)S(1)}, bf16[1,64,512]{2,1,0:T(8,128)(2,1)S(1)}, u32[]{:S(2)}, u32[]{:S(2)}) %collective-permute-start.12) | collective-permute-done | bytes 65568 | tf_op jit(solution)/shard_map/ppermute | solution.py:31
  33.6 0.8 %collective-permute-start.13 = (bf16[16,2560]{1,0:T(8,128)(2,1)S(1)}, bf16[16,2560]{1,0:T(8,128)(2,1)S(1)}, u32[]{:S(2)}, u32[]{:S(2)}) collective-permute-start(bf16[16,2560]{1,0:T(8,128)(2,1)S(1)} %shard_map.106.refs_4_.refs_2_.refs_0_), channel_id=1, source_target_pairs={{0,4},{1,5},{4,0},{5,1},{8,12},{9,13},{12,8},{13,9},{2,6},{3,7},{6... | collective-permute-start | bytes 245768 | tf_op jit(solution)/shard_map/ppermute | solution.py:31
  34.6 4.4 %shard_map.108 = (bf16[512,2560]{1,0:T(8,128)(2,1)}, f32[8,128]{1,0:T(8,128)S(1)}) custom-call(bf16[512,1152]{1,0:T(8,128)(2,1)S(1)} %shard_map.107.refs_0_, bf16[2560,1152]{1,0:T(8,128)(2,1)S(1)} %get-tuple-element.33.refs_2_.refs_1_, bf16[16,2560]{1,0:T(8,128)(2,1)S(1)} %shard_map.106.refs_4_.refs_2_.refs_0_), custom_call_target="tpu_custom_call" | custom-call | flops 3019898880 | bytes 9703424 | tf_op jit(solution)/shard_map/pallas_call | solution.py:53
  39.4 1.7 %shard_map.110 = (f32[16,64,512]{2,1,0:T(8,128)}, f32[8,128]{1,0:T(8,128)S(1)}) custom-call(s32[8]{0:T(128)} %refs_0_.10, bf16[4,64,512]{2,1,0:T(8,128)(2,1)S(1)} %shard_map.105.refs_2_.refs_1_, bf16[4,64,512]{2,1,0:T(8,128)(2,1)S(1)} %collective-permute-done.15.refs_2_, f32[16,64,512]{2,1,0:T(8,128)} %get-tuple-element.36.refs_3_, ...), custom_call_target="tpu_custom_call", output_to_operand_aliasing={{0}: (3, {})} | custom-call | bytes 4722720 | tf_op jit(solution)/shard_map/pallas_call | solution.py:53
  41.1 0.9 %shard_map.111 = f32[64,2560]{1,0:T(8,128)} custom-call(bf16[32,2560]{1,0:T(8,128)(2,1)S(1)} %shard_map.109.refs_4_.refs_0_, bf16[32,2560]{1,0:T(8,128)(2,1)S(1)} %collective-permute-done.14.refs_1_, f32[8,128]{1,0:T(8,128)S(1)} %get-tuple-element.37.refs_2_), custom_call_target="tpu_custom_call" | custom-call | bytes 983040 | tf_op jit(solution)/shard_map/pallas_call | solution.py:53
  (32 shorter events, 1.8 us)
Async XLA Ops:
  0.6 7.2 %copy-start.2 = (bf16[2560,64]{0,1:T(8,128)(2,1)S(1)}, bf16[2560,64]{0,1:T(8,128)(2,1)}, u32[]{:S(2)}) copy-start(bf16[2560,64]{0,1:T(8,128)(2,1)} %param.10) | copy-start | bytes 983044
  0.6 7.2 %copy-start = (bf16[512,2560]{1,0:T(8,128)(2,1)S(1)}, bf16[512,2560]{1,0:T(8,128)(2,1)}, u32[]{:S(2)}) copy-start(bf16[512,2560]{1,0:T(8,128)(2,1)} %refs_3_.3) | copy-start | bytes 7864324
  0.7 23.1 %collective-permute-start.10 = (bf16[2560,512]{1,0:T(8,128)(2,1)}, bf16[2560,512]{1,0:T(8,128)(2,1)S(1)}, u32[]{:S(2)}, u32[]{:S(2)}) collective-permute-start(bf16[2560,512]{1,0:T(8,128)(2,1)} %refs_0_.9), channel_id=1, source_target_pairs={{0,1},{1,0},{2,3},{3,2},{4,5},{5,4},{6,7},{7,6},{8,9},{9,8},{10,11... | collective-permute-start | bytes 7864328 | tf_op jit(solution)/shard_map/ppermute | solution.py:24
  2.7 10.5 %copy-start.1 = (bf16[512,512]{1,0:T(8,128)(2,1)S(1)}, bf16[512,512]{1,0:T(8,128)(2,1)}, u32[]{:S(2)}) copy-start(bf16[512,512]{1,0:T(8,128)(2,1)} %refs_1_.3) | copy-start | bytes 1572868
  2.7 8.3 %collective-permute-start.1 = (bf16[64,512]{1,0:T(8,128)(2,1)S(1)}, bf16[64,512]{1,0:T(8,128)(2,1)S(1)}, u32[]{:S(2)}, u32[]{:S(2)}) collective-permute-start(bf16[64,512]{1,0:T(8,128)(2,1)S(1)} %get-tuple-element.23), channel_id=1, source_target_pairs={{0,8},{1,9},{4,12},{5,13},{8,0},{9,1},{12,4},{13,5},{2,10},{3,11},... | collective-permute-start | bytes 196616 | tf_op jit(solution)/shard_map/ppermute | solution.py:31
  6.3 6.7 %collective-permute-start.2 = (bf16[64,512]{1,0:T(8,128)(2,1)S(1)}, bf16[64,512]{1,0:T(8,128)(2,1)S(1)}, u32[]{:S(2)}, u32[]{:S(2)}) collective-permute-start(bf16[64,512]{1,0:T(8,128)(2,1)S(1)} %get-tuple-element.24), channel_id=1, source_target_pairs={{0,12},{1,13},{4,8},{5,9},{8,4},{9,5},{12,0},{13,1},{2,14},{3,15},... | collective-permute-start | bytes 196616 | tf_op jit(solution)/shard_map/ppermute | solution.py:31
  7.6 5.6 %collective-permute-start.3 = (bf16[64,512]{1,0:T(8,128)(2,1)S(1)}, bf16[64,512]{1,0:T(8,128)(2,1)S(1)}, u32[]{:S(2)}, u32[]{:S(2)}) collective-permute-start(bf16[64,512]{1,0:T(8,128)(2,1)S(1)} %get-tuple-element.25), channel_id=1, source_target_pairs={{0,4},{1,5},{4,0},{5,1},{8,12},{9,13},{12,8},{13,9},{2,6},{3,7},{6... | collective-permute-start | bytes 196616 | tf_op jit(solution)/shard_map/ppermute | solution.py:31
  8.8 6.3 %collective-permute-start = (bf16[64,512]{1,0:T(8,128)(2,1)S(1)}, bf16[64,512]{1,0:T(8,128)(2,1)S(1)}, u32[]{:S(2)}, u32[]{:S(2)}) collective-permute-start(bf16[64,512]{1,0:T(8,128)(2,1)S(1)} %shard_map.96), channel_id=1, source_target_pairs={{0,2},{2,0},{1,3},{3,1},{4,6},{6,4},{5,7},{7,5},{8,10},{10,8},{9,1... | collective-permute-start | bytes 196616 | tf_op jit(solution)/shard_map/ppermute | solution.py:24
  13.5 6.4 %collective-permute-start.5 = (f32[64,512]{1,0:T(8,128)S(1)}, f32[64,512]{1,0:T(8,128)S(1)}, u32[]{:S(2)}, u32[]{:S(2)}) collective-permute-start(f32[64,512]{1,0:T(8,128)S(1)} %shard_map.97.refs_4_.refs_1_), channel_id=1, source_target_pairs={{0,2},{2,0},{1,3},{3,1},{4,6},{6,4},{5,7},{7,5},{8,10},{10,8},{9,1... | collective-permute-start | bytes 393224 | tf_op jit(solution)/shard_map/ppermute | solution.py:24
  15.4 6.2 %collective-permute-start.7 = (bf16[1,64,512]{2,1,0:T(8,128)(2,1)S(1)}, bf16[1,64,512]{2,1,0:T(8,128)(2,1)S(1)}, u32[]{:S(2)}, u32[]{:S(2)}) collective-permute-start(bf16[1,64,512]{2,1,0:T(8,128)(2,1)S(1)} %get-tuple-element.27.refs_4_.refs_0_), channel_id=1, source_target_pairs={{0,8},{1,9},{4,12},{5,13},{8,0},{9,1},{12,4},{13,5},{2,10},{3,11},... | collective-permute-start | bytes 196616 | tf_op jit(solution)/shard_map/ppermute | solution.py:31
  18.1 4.3 %collective-permute-start.8 = (bf16[1,64,512]{2,1,0:T(8,128)(2,1)S(1)}, bf16[1,64,512]{2,1,0:T(8,128)(2,1)S(1)}, u32[]{:S(2)}, u32[]{:S(2)}) collective-permute-start(bf16[1,64,512]{2,1,0:T(8,128)(2,1)S(1)} %get-tuple-element.27.refs_4_.refs_0_), channel_id=1, source_target_pairs={{0,4},{1,5},{4,0},{5,1},{8,12},{9,13},{12,8},{13,9},{2,6},{3,7},{6... | collective-permute-start | bytes 196616 | tf_op jit(solution)/shard_map/ppermute | solution.py:31
  19.3 15.1 %collective-permute-start.4 = (bf16[512,512]{1,0:T(8,128)(2,1)S(1)}, bf16[512,512]{1,0:T(8,128)(2,1)S(1)}, u32[]{:S(2)}, u32[]{:S(2)}) collective-permute-start(bf16[512,512]{1,0:T(8,128)(2,1)S(1)} %get-tuple-element.26), channel_id=1, source_target_pairs={{0,2},{2,0},{1,3},{3,1},{4,6},{6,4},{5,7},{7,5},{8,10},{10,8},{9,1... | collective-permute-start | bytes 1572872 | tf_op jit(solution)/shard_map/ppermute | solution.py:24
  20.5 1.9 %collective-permute-start.6 = (f32[32,2560]{1,0:T(8,128)S(1)}, f32[32,2560]{1,0:T(8,128)S(1)}, u32[]{:S(2)}, u32[]{:S(2)}) collective-permute-start(f32[32,2560]{1,0:T(8,128)S(1)} %get-tuple-element.30), channel_id=1, source_target_pairs={{0,1},{1,0},{2,3},{3,2},{4,5},{5,4},{6,7},{7,6},{8,9},{9,8},{10,11... | collective-permute-start | bytes 983048 | tf_op jit(solution)/shard_map/ppermute | solution.py:24
  22.5 4.5 %collective-permute-start.9 = (bf16[16,2560]{1,0:T(8,128)(2,1)S(1)}, bf16[16,2560]{1,0:T(8,128)(2,1)S(1)}, u32[]{:S(2)}, u32[]{:S(2)}) collective-permute-start(bf16[16,2560]{1,0:T(8,128)(2,1)S(1)} %get-tuple-element.32.refs_3_), channel_id=1, source_target_pairs={{0,4},{1,5},{4,0},{5,1},{8,12},{9,13},{12,8},{13,9},{2,6},{3,7},{6... | collective-permute-start | bytes 245768 | tf_op jit(solution)/shard_map/ppermute | solution.py:31
  27.0 6.6 %collective-permute-start.11 = (bf16[16,2560]{1,0:T(8,128)(2,1)S(1)}, bf16[16,2560]{1,0:T(8,128)(2,1)S(1)}, u32[]{:S(2)}, u32[]{:S(2)}) collective-permute-start(bf16[16,2560]{1,0:T(8,128)(2,1)S(1)} %shard_map.103.refs_1_.refs_4_.refs_0_), channel_id=1, source_target_pairs={{0,8},{1,9},{4,12},{5,13},{8,0},{9,1},{12,4},{13,5},{2,10},{3,11},... | collective-permute-start | bytes 245768 | tf_op jit(solution)/shard_map/ppermute | solution.py:31
  29.1 4.4 %collective-permute-start.12 = (bf16[1,64,512]{2,1,0:T(8,128)(2,1)S(1)}, bf16[1,64,512]{2,1,0:T(8,128)(2,1)S(1)}, u32[]{:S(2)}, u32[]{:S(2)}) collective-permute-start(bf16[1,64,512]{2,1,0:T(8,128)(2,1)S(1)} %shard_map.104), channel_id=1, source_target_pairs={{0,4},{1,5},{4,0},{5,1},{8,12},{9,13},{12,8},{13,9},{2,6},{3,7},{6... | collective-permute-start | bytes 196616 | tf_op jit(solution)/shard_map/ppermute | solution.py:31
  33.5 5.8 %collective-permute-start.15 = (bf16[4,64,512]{2,1,0:T(8,128)(2,1)S(1)}, bf16[4,64,512]{2,1,0:T(8,128)(2,1)S(1)}, u32[]{:S(2)}, u32[]{:S(2)}) collective-permute-start(bf16[4,64,512]{2,1,0:T(8,128)(2,1)S(1)} %shard_map.105.refs_2_.refs_1_), channel_id=1, source_target_pairs={{0,1},{1,0},{2,3},{3,2},{4,5},{5,4},{6,7},{7,6},{8,9},{9,8},{10,11... | collective-permute-start | bytes 786440 | tf_op jit(solution)/shard_map/ppermute | solution.py:24
  33.6 5.4 %collective-permute-start.13 = (bf16[16,2560]{1,0:T(8,128)(2,1)S(1)}, bf16[16,2560]{1,0:T(8,128)(2,1)S(1)}, u32[]{:S(2)}, u32[]{:S(2)}) collective-permute-start(bf16[16,2560]{1,0:T(8,128)(2,1)S(1)} %shard_map.106.refs_4_.refs_2_.refs_0_), channel_id=1, source_target_pairs={{0,4},{1,5},{4,0},{5,1},{8,12},{9,13},{12,8},{13,9},{2,6},{3,7},{6... | collective-permute-start | bytes 245768 | tf_op jit(solution)/shard_map/ppermute | solution.py:31
  39.1 2.0 %collective-permute-start.14 = (bf16[32,2560]{1,0:T(8,128)(2,1)S(1)}, bf16[32,2560]{1,0:T(8,128)(2,1)S(1)}, u32[]{:S(2)}, u32[]{:S(2)}) collective-permute-start(bf16[32,2560]{1,0:T(8,128)(2,1)S(1)} %shard_map.109.refs_4_.refs_0_), channel_id=1, source_target_pairs={{0,1},{1,0},{2,3},{3,2},{4,5},{5,4},{6,7},{7,6},{8,9},{9,8},{10,11... | collective-permute-start | bytes 491528 | tf_op jit(solution)/shard_map/ppermute | solution.py:24

commit v10 on v8

--- a/solution.py
+++ b/solution.py
@@ -11,7 +11,9 @@
 
 early_part = 4
 
-busy, middling, brief, slight = 10**10, 5 * 10**9, 3 * 10**9, 15 * 10**8
+(busy, first_cost, middling, filling, brief, slight) = (
+    10**10, 5 * 10**9, 5 * 10**9, 10**10, 3 * 10**9, 15 * 10**8
+)
 
 anywhere = pl.BlockSpec(memory_space=pl.ANY)
 in_hbm = pl.BlockSpec(memory_space=pltpu.HBM)
@@ -96,6 +98,7 @@
             pltpu.VMEM(head_up.shape, bf16),
             pltpu.SemaphoreType.DMA((3,)),
         ],
+        flops=first_cost,
     )
     return picked, early, away
 
@@ -103,41 +106,27 @@
 def project_low(tokens, down, after):
     rows, features = tokens.shape
     rank = down.shape[0]
-    width = width_of(features)
-    blocks = features // width
-
-    def body(tokens, down, low, rounded, near_tokens, near_down, sems):
-        copies = [pltpu.make_async_copy(down, near_down, sems.at[blocks])]
-        for at in range(blocks):
-            here = pl.ds(at * width, width)
-            copies.append(
-                pltpu.make_async_copy(tokens.at[:, here], near_tokens.at[:, here], sems.at[at])
-            )
-        for copy in copies:
-            copy.start()
-        copies[0].wait()
-        total = None
-        for at in range(blocks):
-            copies[at + 1].wait()
-            here = slice(at * width, (at + 1) * width)
-            part = lax.dot_general(
-                near_down[:, here], near_tokens[:, here], (((1,), (1,)), ((), ())),
-                preferred_element_type=f32,
-            )
-            total = part if total is None else total + part
-        low[...] = total
-        rounded[...] = total.astype(bf16)
-
-    return call(
-        body,
-        [stay(tokens), stay(down)],
-        [in_hbm] * 2,
-        [shape_of((rank, rows), f32), shape_of((rank, rows), bf16)]
-        + [shape_of(tokens.shape, bf16), shape_of(down.shape, bf16)],
+
+    def body(tokens, down, low):
+        low[...] = lax.dot_general(
+            down[...], tokens[...], (((1,), (1,)), ((), ())), preferred_element_type=f32
+        )
+
+    return call(
+        body,
+        [tokens, down],
+        [in_vmem] * 2,
+        [shape_of((rank, rows), f32)],
         after=after,
         flops=2 * rows * rank * features,
-        scratch_shapes=[pltpu.SemaphoreType.DMA((blocks + 1,))],
-    )
+    )[0]
+
+
+def rounded(x, after):
+    def body(x, out):
+        out[...] = x[...].astype(bf16)
+
+    return call(body, [x], [in_vmem], [shape_of(x.shape, bf16)], after=after)[0]
 
 
 def project_back(away, offered, steps, grad, after):
@@ -222,7 +211,7 @@
     )
 
 
-def add_up(pieces, after=()):
+def add_up(pieces, after=(), flops=0):
     def body(*refs):
         total = refs[0][...].astype(f32)
         for piece in refs[1:-1]:
@@ -235,6 +224,7 @@
         [in_vmem] * len(pieces),
         [shape_of(pieces[0].shape, bf16)],
         after=after,
+        flops=flops,
     )[0]
 
 
@@ -260,7 +250,7 @@
     )
 
 
-def rejoin(mine, arrived, bit):
+def rejoin(mine, arrived, bit, after):
     rows, features = mine.shape
 
     def body(mine, arrived, out):
@@ -274,6 +264,7 @@
         [mine, arrived],
         [in_vmem] * 2,
         [shape_of((2 * rows, features), bf16)],
+        after=after,
         flops=busy,
     )[0]
 
@@ -332,7 +323,7 @@
         out_specs=[in_hbm, in_vmem],
         after=after,
         scratch_shapes=[pltpu.VMEM(dims[1:], f32), pltpu.SemaphoreType.DMA((dims[0],))],
-        flops=busy,
+        flops=filling,
     )
 
 
@@ -420,14 +411,14 @@
     )[0]
 
 
-def input_side(kept, frozen, frozen_other, back, down, after):
-    rows, whole = kept.shape
+def input_side(kept, frozen, frozen_other, back, down, begin, count, before, after):
+    rows = kept.shape[0]
     features, half = frozen.shape
-    rank = back.shape[0]
     width = width_of(features)
-    blocks = features // width
-
-    def body(kept, frozen, frozen_other, back, down, out, mark, held, sems):
+    held_in = [] if before is None else [before]
+
+    def body(kept, frozen, frozen_other, back, down, *refs):
+        out, mark, held, sems = refs[len(held_in) :]
         mark[...] = jnp.zeros(mark.shape, f32)
         sub = lax.axis_index("sub")
         both = (((1,), (1,)), ((), ()))
@@ -435,16 +426,17 @@
         other = kept[:, pl.ds(pl.multiple_of((1 - sub) * half, 128), half)]
         twice = adapter_scale * back[...]
         copies = []
-        for at in range(blocks):
-            here = slice(at * width, (at + 1) * width)
+        for at in range(count):
+            here = slice((begin + at) * width, (begin + at + 1) * width)
             total = lax.dot_general(mine, frozen[here, :], both, preferred_element_type=f32)
             total += lax.dot_general(other, frozen_other[here, :], both, preferred_element_type=f32)
             total += lax.dot_general(
                 twice, down[:, here], (((0,), (0,)), ((), ())), preferred_element_type=f32
             )
-            held[:, here] = total.astype(bf16)
+            there = slice(at * width, (at + 1) * width)
+            held[:, there] = total.astype(bf16)
             copies.append(
-                pltpu.make_async_copy(held.at[:, here], out.at[:, here], sems.at[at])
+                pltpu.make_async_copy(held.at[:, there], out.at[:, here], sems.at[at])
             )
             copies[-1].start()
         for copy in copies:
@@ -452,21 +444,22 @@
 
     return call(
         body,
-        [kept, frozen, frozen_other, back, down],
-        [in_vmem] * 5,
+        [kept, frozen, frozen_other, back, down, *held_in],
+        [in_vmem] * 5 + [in_hbm] * len(held_in),
         [shape_of((rows, features), bf16), shape_of((8, 128), f32)],
         out_specs=[in_hbm, in_vmem],
         after=after,
+        input_output_aliases={5: 0} if held_in else {},
         scratch_shapes=[
-            pltpu.VMEM((rows, features), bf16),
-            pltpu.SemaphoreType.DMA((blocks,)),
+            pltpu.VMEM((rows, count * width), bf16),
+            pltpu.SemaphoreType.DMA((count,)),
         ],
-        flops=2 * rows * features * (2 * half + rank),
+        flops=2 * rows * width * count * (2 * half + back.shape[0]),
     )
 
 
 def on_device(tokens, grad_output, frozen_value, shared_down, head_up, adapter_ids, lengths):
-    rows = tokens.shape[0]
+    rows, features = tokens.shape
     own_count = lax.axis_size("own")
     tp_count = lax.axis_size("tp")
     per_owner = head_up.shape[0]
@@ -479,48 +472,47 @@
     offered = [picked[0]] + [swap(picked[step], step, 0) for step in steps]
     early_grads = [shift(early, "tp", step) for step in tp_steps]
 
-    low, rounded, tokens, down = project_low(
-        tokens, shared_down.T, [picked[0], frozen_other]
-    )
-    lows = [low] + [shift(rounded, "tp", step) for step in tp_steps]
+    down = shared_down.T
+    low = project_low(tokens, down, picked[:1])
+    sent = rounded(low, [frozen_other])
+    lows = [low] + [shift(sent, "tp", step) for step in tp_steps]
 
     part = project_back(away, offered, steps, grad_output, [low])
     parts = [part] + [shift(part, "tp", step) for step in tp_steps]
 
     near, late = head_term(lengths, lows, grad_output, scale, [part, *early_grads])
     late_grads = [shift(late, "tp", step) for step in tp_steps]
-    bits = [1 << i for i in range(own_count.bit_length() - 1)]
-    terms, pattern = [near], [0]
-    for bit in reversed(bits[1:]):
-        terms = terms + [swap(term, bit, 0) for term in terms]
-        pattern = pattern + [step ^ bit for step in pattern]
-    nearby = [swap(near, 1, 0)] if bits else []
-
+    terms = [near] + [swap(near, step, 0) for step in own_steps]
     back, keep, send = shared_terms(lengths, parts, tokens, scale, [near])
     pieces = [keep, shift(send, "sub", 1)]
-    met = stack(terms[1:] + nearby, flops=middling) if bits else near
-
+    met = stack(terms[1:3], flops=middling) if own_count > 1 else near
+
+    bits = [1 << i for i in range(own_count.bit_length() - 1)]
     mark = met
     for bit in bits[:-1]:
         stays, leaves = halve(pieces, bit, [mark])
         pieces = [stays, swap(leaves, bit, 0)]
         mark = leaves
     cleaned, mark = clean((per_owner,) + near.shape[1:], [mark])
-    total = add_up(pieces, [mark])
-    relays = [total]
+    near = stack(terms, [mark])
+    far = shift(near, "sub", 1)
+    total = add_up(pieces, [near], flops=busy)
+    grad_heads, mark = place_terms(
+        adapter_ids, near, far, range(own_count), cleaned, [total]
+    )
+    kept = arrange(lengths, grad_output, list(zip(early_grads, late_grads)), [mark])
+    sides = (frozen_value, frozen_other, back, down)
+    blocks = features // width_of(features)
+    input_gradient, mark = input_side(kept, *sides, 0, 1, None, [mark])
     if bits:
-        relays = [stack([term], [total]) for term in terms[1:]]
-        terms = terms + nearby + [swap(relay, 1, 0) for relay in relays]
-        pattern = pattern + [step ^ 1 for step in pattern]
-    kept = arrange(lengths, grad_output, list(zip(early_grads, late_grads)), [total])
-    input_gradient, mark = input_side(kept, frozen_value, frozen_other, back, down, relays)
-    near = stack(terms, [mark])
-    if bits:
-        total = add_up([total, swap(total, bits[-1], 0)], [near])
-    far = shift(near, "sub", 1)
+        total = add_up([total, swap(total, bits[-1], 0)], [mark])
+    if blocks > 1:
+        input_gradient, mark = input_side(
+            kept, *sides, 1, blocks - 1, input_gradient, [total]
+        )
     for bit in reversed(bits[:-1]):
-        total = rejoin(total, swap(total, bit, 0), bit)
-    grad_heads, mark = place_terms(adapter_ids, near, far, pattern, cleaned, [total])
+        total = rejoin(total, swap(total, bit, 0), bit, [mark])
+        mark = total
     shared_down_gradient = join_shares(total, shift(total, "sub", 1), [mark]).T
     return (input_gradient, shared_down_gradient, grad_heads)
 

time: 43.4 us -> 41.8 us (0.963)
  waiting for transfers between devices: 11.4 us -> 7.67 us
  starting transfers between devices: 16.8 us -> 19.3 us
    ppermute x9, waiting for transfers between devices: 9.05 us -> 5.63 us  [swap(): lax.ppermute(x, ('own', 'sub'), [(i, i ^ other) for i in range(whole)])]
    ppermute x9, starting transfers between devices: 12.3 us -> 14.2 us  [swap(): lax.ppermute(x, ('own', 'sub'), [(i, i ^ other) for i in range(whole)])]
    ppermute x8, starting transfers between devices: 4.48 us -> 5.11 us  [shift(): lax.ppermute(x, axis, [(i, (i + step) % count) for i in range(count)])]
    pallas_call x17 -> x18, Pallas kernels: 13.4 us -> 13.2 us  [call(): pl.pallas_call(kernel, out_shape=outs, in_specs=list(specs) + [anywhere]...]
  transfers between devices with their start and end apart: 17 -> 17, of which waited for: 6 -> 8; matrix products, arithmetic and copies ran while one was open for 0% -> 0% of each run, Pallas kernels for 29% -> 29%
where the time goes in v10:
time: 41.8 us; the launch traced here: 41.7 us
  starting transfers between devices  19.3 us (46%)
  Pallas kernels  13.2 us (32%)
  waiting for transfers between devices  7.67 us (18%)
  between operations  1.52 us (4%)
    ppermute x9, starting transfers between devices, swap(): lax.ppermute(x, ('own', 'sub'), [(i, i ^ other) for i in range(whole)])  14.2 us
    pallas_call x18, Pallas kernels, call(): pl.pallas_call(kernel, out_shape=outs, in_specs=list(specs) + [anywhere]...  13.2 us
    ppermute x9, waiting for transfers between devices, swap(): lax.ppermute(x, ('own', 'sub'), [(i, i ^ other) for i in range(whole)])  5.63 us
    ppermute x8, starting transfers between devices, shift(): lax.ppermute(x, axis, [(i, (i + step) % count) for i in range(count)])  5.11 us
    ppermute x8, waiting for transfers between devices, shift(): lax.ppermute(x, axis, [(i, (i + step) % count) for i in range(count)])  2.04 us
  transfers between devices with their start and end apart: 17, of which 8 were waited for; matrix products, arithmetic and copies ran while one was open for 0% of the time, Pallas kernels for 29%

profile of v10, /device:TPU:0, one launch (start us, length us, event | category | flops | bytes accessed | tf_op | source)
XLA Modules:
  0.0 41.7 jit_solution(9483361979100452240)
XLA Ops:
  1.2 1.5 %shard_map.94 = (bf16[64,512]{1,0:T(8,128)(2,1)S(1)}, bf16[64,512]{1,0:T(8,128)(2,1)S(1)}, bf16[64,512]{1,0:T(8,128)(2,1)S(1)}, bf16[64,512]{1,0:T(8,128)(2,1)S(...) custom-call(s32[8]{0:T(128)} %refs_0_.8, bf16[16,64,512]{2,1,0:T(8,128)(2,1)} %refs_1_.4, bf16[512,512]{1,0:T(8,128)(2,1)} %refs_1_.5), custom_call_target="tpu_custom_call" | custom-call | flops 5000000000 | bytes 1970208 | tf_op jit(solution)/shard_map/pallas_call | solution.py:55
  2.7 3.6 %collective-permute-start.3 = (bf16[64,512]{1,0:T(8,128)(2,1)S(1)}, bf16[64,512]{1,0:T(8,128)(2,1)S(1)}, u32[]{:S(2)}, u32[]{:S(2)}) collective-permute-start(bf16[64,512]{1,0:T(8,128)(2,1)S(1)} %get-tuple-element.27), channel_id=1, source_target_pairs={{0,8},{1,9},{4,12},{5,13},{8,0},{9,1},{12,4},{13,5},{2,10},{3,11},... | collective-permute-start | bytes 196616 | tf_op jit(solution)/shard_map/ppermute | solution.py:33
  6.3 1.3 %collective-permute-start.4 = (bf16[64,512]{1,0:T(8,128)(2,1)S(1)}, bf16[64,512]{1,0:T(8,128)(2,1)S(1)}, u32[]{:S(2)}, u32[]{:S(2)}) collective-permute-start(bf16[64,512]{1,0:T(8,128)(2,1)S(1)} %get-tuple-element.28), channel_id=1, source_target_pairs={{0,12},{1,13},{4,8},{5,9},{8,4},{9,5},{12,0},{13,1},{2,14},{3,15},... | collective-permute-start | bytes 196616 | tf_op jit(solution)/shard_map/ppermute | solution.py:33
  7.8 1.5 %collective-permute-start = (bf16[128,512]{1,0:T(8,128)(2,1)S(1)}, bf16[128,512]{1,0:T(8,128)(2,1)S(1)}, u32[]{:S(2)}, u32[]{:S(2)}) collective-permute-start(bf16[128,512]{1,0:T(8,128)(2,1)S(1)} %get-tuple-element.24), channel_id=1, source_target_pairs={{0,2},{2,0},{1,3},{3,1},{4,6},{6,4},{5,7},{7,5},{8,10},{10,8},{9,1... | collective-permute-start | bytes 393224 | tf_op jit(solution)/shard_map/ppermute | solution.py:26
  10.0 0.9 %shard_map.95.refs_0_.refs_6_.refs_1_ = f32[64,512]{1,0:T(8,128)S(1)} custom-call(bf16[512,2560]{1,0:T(8,128)(2,1)S(1)} %copy-done, bf16[64,2560]{1,0:T(8,128)(2,1)S(1)} %bitcast.2, bf16[64,512]{1,0:T(8,128)(2,1)S(1)} %get-tuple-element.25.refs_2_.refs_1_), custom_call_target="tpu_custom_call" | custom-call | flops 167772160 | bytes 3080192 | tf_op jit(solution)/shard_map/pallas_call | solution.py:55
  11.0 0.6 %collective-permute-start.2 = (bf16[64,512]{1,0:T(8,128)(2,1)S(1)}, bf16[64,512]{1,0:T(8,128)(2,1)S(1)}, u32[]{:S(2)}, u32[]{:S(2)}) collective-permute-start(bf16[64,512]{1,0:T(8,128)(2,1)S(1)} %shard_map.96), channel_id=1, source_target_pairs={{0,2},{2,0},{1,3},{3,1},{4,6},{6,4},{5,7},{7,5},{8,10},{10,8},{9,1... | collective-permute-start | bytes 196616 | tf_op jit(solution)/shard_map/ppermute | solution.py:26
  11.6 1.4 %collective-permute-done.4.refs_3_ = bf16[64,512]{1,0:T(8,128)(2,1)S(1)} collective-permute-done((bf16[64,512]{1,0:T(8,128)(2,1)S(1)}, bf16[64,512]{1,0:T(8,128)(2,1)S(1)}, u32[]{:S(2)}, u32[]{:S(2)}) %collective-permute-start.4) | collective-permute-done | bytes 65568 | tf_op jit(solution)/shard_map/ppermute | solution.py:33
  13.5 1.6 %collective-permute-start.10 = (f32[64,512]{1,0:T(8,128)S(1)}, f32[64,512]{1,0:T(8,128)S(1)}, u32[]{:S(2)}, u32[]{:S(2)}) collective-permute-start(f32[64,512]{1,0:T(8,128)S(1)} %shard_map.97.refs_4_.refs_1_), channel_id=1, source_target_pairs={{0,2},{2,0},{1,3},{3,1},{4,6},{6,4},{5,7},{7,5},{8,10},{10,8},{9,1... | collective-permute-start | bytes 393224 | tf_op jit(solution)/shard_map/ppermute | solution.py:26
  15.7 2.8 %collective-permute-start.8 = (bf16[1,64,512]{2,1,0:T(8,128)(2,1)S(1)}, bf16[1,64,512]{2,1,0:T(8,128)(2,1)S(1)}, u32[]{:S(2)}, u32[]{:S(2)}) collective-permute-start(bf16[1,64,512]{2,1,0:T(8,128)(2,1)S(1)} %get-tuple-element.31.refs_4_.refs_0_), channel_id=1, source_target_pairs={{0,8},{1,9},{4,12},{5,13},{8,0},{9,1},{12,4},{13,5},{2,10},{3,11},... | collective-permute-start | bytes 196616 | tf_op jit(solution)/shard_map/ppermute | solution.py:33
  18.5 0.9 %collective-permute-start.7 = (bf16[1,64,512]{2,1,0:T(8,128)(2,1)S(1)}, bf16[1,64,512]{2,1,0:T(8,128)(2,1)S(1)}, u32[]{:S(2)}, u32[]{:S(2)}) collective-permute-start(bf16[1,64,512]{2,1,0:T(8,128)(2,1)S(1)} %get-tuple-element.31.refs_4_.refs_0_), channel_id=1, source_target_pairs={{0,4},{1,5},{4,0},{5,1},{8,12},{9,13},{12,8},{13,9},{2,6},{3,7},{6... | collective-permute-start | bytes 196616 | tf_op jit(solution)/shard_map/ppermute | solution.py:33
  19.3 0.8 %collective-permute-start.9 = (bf16[1,64,512]{2,1,0:T(8,128)(2,1)S(1)}, bf16[1,64,512]{2,1,0:T(8,128)(2,1)S(1)}, u32[]{:S(2)}, u32[]{:S(2)}) collective-permute-start(bf16[1,64,512]{2,1,0:T(8,128)(2,1)S(1)} %get-tuple-element.31.refs_4_.refs_0_), channel_id=1, source_target_pairs={{0,12},{1,13},{4,8},{5,9},{8,4},{9,5},{12,0},{13,1},{2,14},{3,15},... | collective-permute-start | bytes 196616 | tf_op jit(solution)/shard_map/ppermute | solution.py:33
  20.1 0.7 %collective-permute-start.6 = (bf16[384,512]{1,0:T(8,128)(2,1)S(1)}, bf16[384,512]{1,0:T(8,128)(2,1)S(1)}, u32[]{:S(2)}, u32[]{:S(2)}) collective-permute-start(bf16[384,512]{1,0:T(8,128)(2,1)S(1)} %get-tuple-element.30), channel_id=1, source_target_pairs={{0,2},{2,0},{1,3},{3,1},{4,6},{6,4},{5,7},{7,5},{8,10},{10,8},{9,1... | collective-permute-start | bytes 1179656 | tf_op jit(solution)/shard_map/ppermute | solution.py:26
  21.5 1.2 %collective-permute-done.7.refs_0_.refs_1_ = bf16[1,64,512]{2,1,0:T(8,128)(2,1)S(1)} collective-permute-done((bf16[1,64,512]{2,1,0:T(8,128)(2,1)S(1)}, bf16[1,64,512]{2,1,0:T(8,128)(2,1)S(1)}, u32[]{:S(2)}, u32[]{:S(2)}) %collective-permute-start.7) | collective-permute-done | bytes 65568 | tf_op jit(solution)/shard_map/ppermute | solution.py:33
  23.2 1.0 %collective-permute-start.13 = (bf16[16,2560]{1,0:T(8,128)(2,1)S(1)}, bf16[16,2560]{1,0:T(8,128)(2,1)S(1)}, u32[]{:S(2)}, u32[]{:S(2)}) collective-permute-start(bf16[16,2560]{1,0:T(8,128)(2,1)S(1)} %get-tuple-element.34.refs_0_), channel_id=1, source_target_pairs={{0,4},{1,5},{4,0},{5,1},{8,12},{9,13},{12,8},{13,9},{2,6},{3,7},{6... | collective-permute-start | bytes 245768 | tf_op jit(solution)/shard_map/ppermute | solution.py:33
  24.2 1.4 %shard_map.102 = (f32[16,64,512]{2,1,0:T(8,128)}, f32[8,128]{1,0:T(8,128)S(1)}) custom-call(bf16[16,2560]{1,0:T(8,128)(2,1)S(1)} %get-tuple-element.34.refs_0_), custom_call_target="tpu_custom_call" | custom-call | flops 10000000000 | bytes 2101248 | tf_op jit(solution)/shard_map/pallas_call | solution.py:55
  25.8 2.0 %collective-permute-done.13.refs_1_ = bf16[16,2560]{1,0:T(8,128)(2,1)S(1)} collective-permute-done((bf16[16,2560]{1,0:T(8,128)(2,1)S(1)}, bf16[16,2560]{1,0:T(8,128)(2,1)S(1)}, u32[]{:S(2)}, u32[]{:S(2)}) %collective-permute-start.13) | collective-permute-done | bytes 81952 | tf_op jit(solution)/shard_map/ppermute | solution.py:33
  27.8 2.2 %collective-permute-start.14 = (bf16[16,2560]{1,0:T(8,128)(2,1)S(1)}, bf16[16,2560]{1,0:T(8,128)(2,1)S(1)}, u32[]{:S(2)}, u32[]{:S(2)}) collective-permute-start(bf16[16,2560]{1,0:T(8,128)(2,1)S(1)} %shard_map.104.refs_4_.refs_0_), channel_id=1, source_target_pairs={{0,8},{1,9},{4,12},{5,13},{8,0},{9,1},{12,4},{13,5},{2,10},{3,11},... | collective-permute-start | bytes 245768 | tf_op jit(solution)/shard_map/ppermute | solution.py:33
  29.9 1.6 %shard_map.105 = (f32[16,64,512]{2,1,0:T(8,128)}, f32[8,128]{1,0:T(8,128)S(1)}) custom-call(s32[8]{0:T(128)} %refs_0_.8, bf16[4,64,512]{2,1,0:T(8,128)(2,1)S(1)} %shard_map.103.refs_2_.refs_1_, bf16[4,64,512]{2,1,0:T(8,128)(2,1)S(1)} %collective-permute-done.12.refs_2_, f32[16,64,512]{2,1,0:T(8,128)} %get-tuple-element.36.refs_3_, ...), custom_call_target="tpu_custom_call", output_to_operand_aliasing={{0}: (3, {})} | custom-call | bytes 4722720 | tf_op jit(solution)/shard_map/pallas_call | solution.py:55
  31.7 1.7 %shard_map.107 = (bf16[512,2560]{1,0:T(8,128)(2,1)}, f32[8,128]{1,0:T(8,128)S(1)}) custom-call(bf16[512,1024]{1,0:T(8,128)(2,1)S(1)} %shard_map.106.refs_0_, bf16[2560,512]{1,0:T(8,128)(2,1)S(1)} %copy-done.1, bf16[2560,512]{1,0:T(8,128)(2,1)S(1)} %collective-permute-done.1.refs_1_.refs_2_, bf16[64,512]{1,0:T(8,128)(2,1)S(1)} %get-tuple-element.39.refs_3_, ...), custom_call_target="tpu_custom_call" | custom-call | flops 570425344 | bytes 9310208 | tf_op jit(solution)/shard_map/pallas_call | solution.py:55
  33.3 0.8 %collective-permute-done.14.refs_1_ = bf16[16,2560]{1,0:T(8,128)(2,1)S(1)} collective-permute-done((bf16[16,2560]{1,0:T(8,128)(2,1)S(1)}, bf16[16,2560]{1,0:T(8,128)(2,1)S(1)}, u32[]{:S(2)}, u32[]{:S(2)}) %collective-permute-start.14) | collective-permute-done | bytes 81952 | tf_op jit(solution)/shard_map/ppermute | solution.py:33
  34.2 1.4 %collective-permute-start.15 = (bf16[16,2560]{1,0:T(8,128)(2,1)S(1)}, bf16[16,2560]{1,0:T(8,128)(2,1)S(1)}, u32[]{:S(2)}, u32[]{:S(2)}) collective-permute-start(bf16[16,2560]{1,0:T(8,128)(2,1)S(1)} %shard_map.108.refs_6_.refs_0_), channel_id=1, source_target_pairs={{0,4},{1,5},{4,0},{5,1},{8,12},{9,13},{12,8},{13,9},{2,6},{3,7},{6... | collective-permute-start | bytes 245768 | tf_op jit(solution)/shard_map/ppermute | solution.py:33
  35.6 3.7 %shard_map.109 = (bf16[512,2560]{1,0:T(8,128)(2,1)}, f32[8,128]{1,0:T(8,128)S(1)}) custom-call(bf16[512,1024]{1,0:T(8,128)(2,1)S(1)} %shard_map.106.refs_0_, bf16[2560,512]{1,0:T(8,128)(2,1)S(1)} %copy-done.1, bf16[2560,512]{1,0:T(8,128)(2,1)S(1)} %collective-permute-done.1.refs_1_.refs_2_, ...), custom_call_target="tpu_custom_call", output_to_operand_aliasing={{0}: (5, {})} | custom-call | flops 2281701376 | bytes 11931648 | tf_op jit(solution)/shard_map/pallas_call | solution.py:55
  39.4 1.4 %collective-permute-done.16.refs_1_ = bf16[32,2560]{1,0:T(8,128)(2,1)S(1)} collective-permute-done((bf16[32,2560]{1,0:T(8,128)(2,1)S(1)}, bf16[32,2560]{1,0:T(8,128)(2,1)S(1)}, u32[]{:S(2)}, u32[]{:S(2)}) %collective-permute-start.16) | collective-permute-done | bytes 163872 | tf_op jit(solution)/shard_map/ppermute | solution.py:26
  40.8 0.9 %shard_map.111 = f32[64,2560]{1,0:T(8,128)} custom-call(bf16[32,2560]{1,0:T(8,128)(2,1)S(1)} %shard_map.110.refs_0_.refs_2_, bf16[32,2560]{1,0:T(8,128)(2,1)S(1)} %collective-permute-done.16.refs_1_, bf16[32,2560]{1,0:T(8,128)(2,1)S(1)} %shard_map.110.refs_0_.refs_2_), custom_call_target="tpu_custom_call" | custom-call | bytes 983040 | tf_op jit(solution)/shard_map/pallas_call | solution.py:55
  (36 shorter events, 3.4 us)
Async XLA Ops:
  0.6 9.4 %copy-start = (bf16[512,2560]{1,0:T(8,128)(2,1)S(1)}, bf16[512,2560]{1,0:T(8,128)(2,1)}, u32[]{:S(2)}) copy-start(bf16[512,2560]{1,0:T(8,128)(2,1)} %refs_3_.3) | copy-start | bytes 7864324
  0.6 9.4 %copy-start.2 = (bf16[2560,64]{0,1:T(8,128)(2,1)S(1)}, bf16[2560,64]{0,1:T(8,128)(2,1)}, u32[]{:S(2)}) copy-start(bf16[2560,64]{0,1:T(8,128)(2,1)} %param.10) | copy-start | bytes 983044
  0.7 10.3 %collective-permute-start.1 = (bf16[2560,512]{1,0:T(8,128)(2,1)}, bf16[2560,512]{1,0:T(8,128)(2,1)S(1)}, u32[]{:S(2)}, u32[]{:S(2)}) collective-permute-start(bf16[2560,512]{1,0:T(8,128)(2,1)} %refs_1_.7), channel_id=1, source_target_pairs={{0,1},{1,0},{2,3},{3,2},{4,5},{5,4},{6,7},{7,6},{8,9},{9,8},{10,11... | collective-permute-start | bytes 7864328 | tf_op jit(solution)/shard_map/ppermute | solution.py:26
  2.7 8.8 %collective-permute-start.3 = (bf16[64,512]{1,0:T(8,128)(2,1)S(1)}, bf16[64,512]{1,0:T(8,128)(2,1)S(1)}, u32[]{:S(2)}, u32[]{:S(2)}) collective-permute-start(bf16[64,512]{1,0:T(8,128)(2,1)S(1)} %get-tuple-element.27), channel_id=1, source_target_pairs={{0,8},{1,9},{4,12},{5,13},{8,0},{9,1},{12,4},{13,5},{2,10},{3,11},... | collective-permute-start | bytes 196616 | tf_op jit(solution)/shard_map/ppermute | solution.py:33
  6.3 6.7 %collective-permute-start.4 = (bf16[64,512]{1,0:T(8,128)(2,1)S(1)}, bf16[64,512]{1,0:T(8,128)(2,1)S(1)}, u32[]{:S(2)}, u32[]{:S(2)}) collective-permute-start(bf16[64,512]{1,0:T(8,128)(2,1)S(1)} %get-tuple-element.28), channel_id=1, source_target_pairs={{0,12},{1,13},{4,8},{5,9},{8,4},{9,5},{12,0},{13,1},{2,14},{3,15},... | collective-permute-start | bytes 196616 | tf_op jit(solution)/shard_map/ppermute | solution.py:33
  7.6 5.6 %collective-permute-start.5 = (bf16[64,512]{1,0:T(8,128)(2,1)S(1)}, bf16[64,512]{1,0:T(8,128)(2,1)S(1)}, u32[]{:S(2)}, u32[]{:S(2)}) collective-permute-start(bf16[64,512]{1,0:T(8,128)(2,1)S(1)} %get-tuple-element.29), channel_id=1, source_target_pairs={{0,4},{1,5},{4,0},{5,1},{8,12},{9,13},{12,8},{13,9},{2,6},{3,7},{6... | collective-permute-start | bytes 196616 | tf_op jit(solution)/shard_map/ppermute | solution.py:33
  7.8 7.2 %collective-permute-start = (bf16[128,512]{1,0:T(8,128)(2,1)S(1)}, bf16[128,512]{1,0:T(8,128)(2,1)S(1)}, u32[]{:S(2)}, u32[]{:S(2)}) collective-permute-start(bf16[128,512]{1,0:T(8,128)(2,1)S(1)} %get-tuple-element.24), channel_id=1, source_target_pairs={{0,2},{2,0},{1,3},{3,1},{4,6},{6,4},{5,7},{7,5},{8,10},{10,8},{9,1... | collective-permute-start | bytes 393224 | tf_op jit(solution)/shard_map/ppermute | solution.py:26
  10.0 3.2 %copy-start.3 = (bf16[512,512]{1,0:T(8,128)(2,1)S(1)}, bf16[512,512]{1,0:T(8,128)(2,1)}, u32[]{:S(2)}) copy-start(bf16[512,512]{1,0:T(8,128)(2,1)} %refs_1_.5) | copy-start | bytes 1572868
  11.0 4.4 %collective-permute-start.2 = (bf16[64,512]{1,0:T(8,128)(2,1)S(1)}, bf16[64,512]{1,0:T(8,128)(2,1)S(1)}, u32[]{:S(2)}, u32[]{:S(2)}) collective-permute-start(bf16[64,512]{1,0:T(8,128)(2,1)S(1)} %shard_map.96), channel_id=1, source_target_pairs={{0,2},{2,0},{1,3},{3,1},{4,6},{6,4},{5,7},{7,5},{8,10},{10,8},{9,1... | collective-permute-start | bytes 196616 | tf_op jit(solution)/shard_map/ppermute | solution.py:26
  13.5 7.4 %collective-permute-start.10 = (f32[64,512]{1,0:T(8,128)S(1)}, f32[64,512]{1,0:T(8,128)S(1)}, u32[]{:S(2)}, u32[]{:S(2)}) collective-permute-start(f32[64,512]{1,0:T(8,128)S(1)} %shard_map.97.refs_4_.refs_1_), channel_id=1, source_target_pairs={{0,2},{2,0},{1,3},{3,1},{4,6},{6,4},{5,7},{7,5},{8,10},{10,8},{9,1... | collective-permute-start | bytes 393224 | tf_op jit(solution)/shard_map/ppermute | solution.py:26
  15.7 5.8 %collective-permute-start.8 = (bf16[1,64,512]{2,1,0:T(8,128)(2,1)S(1)}, bf16[1,64,512]{2,1,0:T(8,128)(2,1)S(1)}, u32[]{:S(2)}, u32[]{:S(2)}) collective-permute-start(bf16[1,64,512]{2,1,0:T(8,128)(2,1)S(1)} %get-tuple-element.31.refs_4_.refs_0_), channel_id=1, source_target_pairs={{0,8},{1,9},{4,12},{5,13},{8,0},{9,1},{12,4},{13,5},{2,10},{3,11},... | collective-permute-start | bytes 196616 | tf_op jit(solution)/shard_map/ppermute | solution.py:33
  18.5 4.3 %collective-permute-start.7 = (bf16[1,64,512]{2,1,0:T(8,128)(2,1)S(1)}, bf16[1,64,512]{2,1,0:T(8,128)(2,1)S(1)}, u32[]{:S(2)}, u32[]{:S(2)}) collective-permute-start(bf16[1,64,512]{2,1,0:T(8,128)(2,1)S(1)} %get-tuple-element.31.refs_4_.refs_0_), channel_id=1, source_target_pairs={{0,4},{1,5},{4,0},{5,1},{8,12},{9,13},{12,8},{13,9},{2,6},{3,7},{6... | collective-permute-start | bytes 196616 | tf_op jit(solution)/shard_map/ppermute | solution.py:33
  19.3 6.3 %collective-permute-start.9 = (bf16[1,64,512]{2,1,0:T(8,128)(2,1)S(1)}, bf16[1,64,512]{2,1,0:T(8,128)(2,1)S(1)}, u32[]{:S(2)}, u32[]{:S(2)}) collective-permute-start(bf16[1,64,512]{2,1,0:T(8,128)(2,1)S(1)} %get-tuple-element.31.refs_4_.refs_0_), channel_id=1, source_target_pairs={{0,12},{1,13},{4,8},{5,9},{8,4},{9,5},{12,0},{13,1},{2,14},{3,15},... | collective-permute-start | bytes 196616 | tf_op jit(solution)/shard_map/ppermute | solution.py:33
  20.1 11.4 %collective-permute-start.6 = (bf16[384,512]{1,0:T(8,128)(2,1)S(1)}, bf16[384,512]{1,0:T(8,128)(2,1)S(1)}, u32[]{:S(2)}, u32[]{:S(2)}) collective-permute-start(bf16[384,512]{1,0:T(8,128)(2,1)S(1)} %get-tuple-element.30), channel_id=1, source_target_pairs={{0,2},{2,0},{1,3},{3,1},{4,6},{6,4},{5,7},{7,5},{8,10},{10,8},{9,1... | collective-permute-start | bytes 1179656 | tf_op jit(solution)/shard_map/ppermute | solution.py:26
  21.4 1.7 %collective-permute-start.11 = (f32[32,2560]{1,0:T(8,128)S(1)}, f32[32,2560]{1,0:T(8,128)S(1)}, u32[]{:S(2)}, u32[]{:S(2)}) collective-permute-start(f32[32,2560]{1,0:T(8,128)S(1)} %get-tuple-element.33), channel_id=1, source_target_pairs={{0,1},{1,0},{2,3},{3,2},{4,5},{5,4},{6,7},{7,6},{8,9},{9,8},{10,11... | collective-permute-start | bytes 983048 | tf_op jit(solution)/shard_map/ppermute | solution.py:26
  23.2 4.6 %collective-permute-start.13 = (bf16[16,2560]{1,0:T(8,128)(2,1)S(1)}, bf16[16,2560]{1,0:T(8,128)(2,1)S(1)}, u32[]{:S(2)}, u32[]{:S(2)}) collective-permute-start(bf16[16,2560]{1,0:T(8,128)(2,1)S(1)} %get-tuple-element.34.refs_0_), channel_id=1, source_target_pairs={{0,4},{1,5},{4,0},{5,1},{8,12},{9,13},{12,8},{13,9},{2,6},{3,7},{6... | collective-permute-start | bytes 245768 | tf_op jit(solution)/shard_map/ppermute | solution.py:33
  25.7 4.2 %collective-permute-start.12 = (bf16[4,64,512]{2,1,0:T(8,128)(2,1)S(1)}, bf16[4,64,512]{2,1,0:T(8,128)(2,1)S(1)}, u32[]{:S(2)}, u32[]{:S(2)}) collective-permute-start(bf16[4,64,512]{2,1,0:T(8,128)(2,1)S(1)} %shard_map.103.refs_2_.refs_1_), channel_id=1, source_target_pairs={{0,1},{1,0},{2,3},{3,2},{4,5},{5,4},{6,7},{7,6},{8,9},{9,8},{10,11... | collective-permute-start | bytes 786440 | tf_op jit(solution)/shard_map/ppermute | solution.py:26
  27.8 3.9 %copy-start.1 = (bf16[2560,512]{1,0:T(8,128)(2,1)S(1)}, bf16[2560,512]{1,0:T(8,128)(2,1)}, u32[]{:S(2)}) copy-start(bf16[2560,512]{1,0:T(8,128)(2,1)} %refs_1_.7) | copy-start | bytes 7864324
  27.8 6.4 %collective-permute-start.14 = (bf16[16,2560]{1,0:T(8,128)(2,1)S(1)}, bf16[16,2560]{1,0:T(8,128)(2,1)S(1)}, u32[]{:S(2)}, u32[]{:S(2)}) collective-permute-start(bf16[16,2560]{1,0:T(8,128)(2,1)S(1)} %shard_map.104.refs_4_.refs_0_), channel_id=1, source_target_pairs={{0,8},{1,9},{4,12},{5,13},{8,0},{9,1},{12,4},{13,5},{2,10},{3,11},... | collective-permute-start | bytes 245768 | tf_op jit(solution)/shard_map/ppermute | solution.py:33
  34.2 5.1 %collective-permute-start.15 = (bf16[16,2560]{1,0:T(8,128)(2,1)S(1)}, bf16[16,2560]{1,0:T(8,128)(2,1)S(1)}, u32[]{:S(2)}, u32[]{:S(2)}) collective-permute-start(bf16[16,2560]{1,0:T(8,128)(2,1)S(1)} %shard_map.108.refs_6_.refs_0_), channel_id=1, source_target_pairs={{0,4},{1,5},{4,0},{5,1},{8,12},{9,13},{12,8},{13,9},{2,6},{3,7},{6... | collective-permute-start | bytes 245768 | tf_op jit(solution)/shard_map/ppermute | solution.py:33
  39.4 1.5 %collective-permute-start.16 = (bf16[32,2560]{1,0:T(8,128)(2,1)S(1)}, bf16[32,2560]{1,0:T(8,128)(2,1)S(1)}, u32[]{:S(2)}, u32[]{:S(2)}) collective-permute-start(bf16[32,2560]{1,0:T(8,128)(2,1)S(1)} %shard_map.110.refs_0_.refs_2_), channel_id=1, source_target_pairs={{0,1},{1,0},{2,3},{3,2},{4,5},{5,4},{6,7},{7,6},{8,9},{9,8},{10,11... | collective-permute-start | bytes 491528 | tf_op jit(solution)/shard_map/ppermute | solution.py:26

commit v11 on v10

--- a/solution.py
+++ b/solution.py
@@ -11,9 +11,8 @@
 
 early_part = 4
 
-(busy, first_cost, middling, filling, brief, slight) = (
-    10**10, 5 * 10**9, 5 * 10**9, 10**10, 3 * 10**9, 15 * 10**8
-)
+busy, filling, first_cost, brief = 10**10, 10**10, 5 * 10**9, 3 * 10**9
+little, slight, middling = 15 * 10**8, 15 * 10**8, 5 * 10**8
 
 anywhere = pl.BlockSpec(memory_space=pl.ANY)
 in_hbm = pl.BlockSpec(memory_space=pltpu.HBM)
@@ -188,7 +187,7 @@
     share = rank // 2
 
     def body(lengths, *refs):
-        parts, (tokens, back, keep, send, total) = refs[:count], refs[count:]
+        parts, (tokens, back, keep, send, send_too, total) = refs[:count], refs[count:]
         sub = lax.axis_index("sub")
         both = parts[0][...]
         for part in parts[1:]:
@@ -196,27 +195,47 @@
         live = lax.broadcasted_iota(jnp.int32, both.shape, 1) < lengths[0]
         back[...] = jnp.where(live, both, 0.0).astype(bf16)
         total[...] = scale * jnp.dot(back[...], tokens[...], preferred_element_type=f32)
+        half = share // 2
+        there = pl.multiple_of((1 - sub) * share, share)
         keep[...] = total[pl.ds(pl.multiple_of(sub * share, share), share), :]
-        send[...] = total[pl.ds(pl.multiple_of((1 - sub) * share, share), share), :]
+        send[...] = total[pl.ds(there, half), :]
+        send_too[...] = total[pl.ds(there + half, half), :]
 
     count = len(parts)
     return call(
         body,
         [lengths, *parts, tokens],
         [in_smem] + [in_vmem] * (count + 1),
-        [shape_of((rank, rows), bf16)] + [shape_of((share, features), f32)] * 2,
+        [shape_of((rank, rows), bf16), shape_of((share, features), f32)]
+        + [shape_of((share // 2, features), f32)] * 2,
         after=after,
         scratch_shapes=[pltpu.VMEM((rank, features), f32)],
         flops=2 * rows * rank * features,
     )
 
 
+def marked(after, flops):
+    def body(out):
+        out[...] = jnp.zeros(out.shape, f32)
+
+    return call(body, [], [], [shape_of((8, 128), f32)], after=after, flops=flops)[0]
+
+
+def sum_of(refs):
+    total = refs[0][...].astype(f32)
+    rows = total.shape[0]
+    waiting = []
+    for ref in refs[1:]:
+        waiting.append(ref[...].astype(f32))
+        if sum(piece.shape[0] for piece in waiting) == rows:
+            total = total + (waiting[0] if len(waiting) == 1 else jnp.concatenate(waiting, axis=0))
+            waiting = []
+    return total
+
+
 def add_up(pieces, after=(), flops=0):
     def body(*refs):
-        total = refs[0][...].astype(f32)
-        for piece in refs[1:-1]:
-            total = total + piece[...].astype(f32)
-        refs[-1][...] = total.astype(bf16)
+        refs[-1][...] = sum_of(refs[:-1]).astype(bf16)
 
     return call(
         body,
@@ -233,9 +252,7 @@
     half = rows // 2
 
     def body(*refs):
-        total = refs[0][...].astype(f32)
-        for piece in refs[1:-2]:
-            total = total + piece[...].astype(f32)
+        total = sum_of(refs[:-2])
         upper = lax.rem(lax.div(lax.axis_index("own"), bit), 2) == 1
         low, high = total[:half], total[half:]
         refs[-2][...] = jnp.where(upper, high, low)
@@ -269,20 +286,30 @@
     )[0]
 
 
-def join_shares(mine, other, after):
-    share, features = mine.shape
-
-    def body(mine, other, out):
+def lay_share(share, other, before, after):
+    rows, features = share.shape
+    held_in = [] if before is None else [before]
+
+    def body(share, *refs):
+        out, wide, sem = refs[len(held_in) :]
         sub = lax.axis_index("sub")
-        for side, piece in ((sub, mine), (1 - sub, other)):
-            out[pl.ds(pl.multiple_of(side * share, share), share), :] = piece[...].astype(f32)
-
-    return call(
-        body,
-        [mine, other],
-        [in_vmem] * 2,
-        [shape_of((2 * share, features), f32)],
-        after=after,
+        side = 1 - sub if other else sub
+        wide[...] = share[...].astype(f32)
+        copy = pltpu.make_async_copy(
+            wide, out.at[pl.ds(pl.multiple_of(side * rows, rows), rows)], sem
+        )
+        copy.start()
+        copy.wait()
+
+    return call(
+        body,
+        [share, *held_in],
+        [in_vmem] + [in_hbm] * len(held_in),
+        [shape_of((2 * rows, features), f32)],
+        out_specs=[in_hbm],
+        after=after,
+        input_output_aliases={1: 0} if held_in else {},
+        scratch_shapes=[pltpu.VMEM((rows, features), f32), pltpu.SemaphoreType.DMA],
     )[0]
 
 
@@ -483,9 +510,12 @@
     near, late = head_term(lengths, lows, grad_output, scale, [part, *early_grads])
     late_grads = [shift(late, "tp", step) for step in tp_steps]
     terms = [near] + [swap(near, step, 0) for step in own_steps]
-    back, keep, send = shared_terms(lengths, parts, tokens, scale, [near])
-    pieces = [keep, shift(send, "sub", 1)]
-    met = stack(terms[1:3], flops=middling) if own_count > 1 else near
+    back, keep, *sends = shared_terms(lengths, parts, tokens, scale, [near])
+    pieces = [keep, *[shift(send, "sub", 1) for send in sends]]
+    pause = marked([back], flops=middling)
+    met = pause
+    if own_count > 1:
+        met = stack(terms[1:2], [pause], flops=little)
 
     bits = [1 << i for i in range(own_count.bit_length() - 1)]
     mark = met
@@ -503,17 +533,19 @@
     kept = arrange(lengths, grad_output, list(zip(early_grads, late_grads)), [mark])
     sides = (frozen_value, frozen_other, back, down)
     blocks = features // width_of(features)
-    input_gradient, mark = input_side(kept, *sides, 0, 1, None, [mark])
+    cut = max(1, blocks // 5)
+    input_gradient, mark = input_side(kept, *sides, 0, cut, None, [mark])
     if bits:
         total = add_up([total, swap(total, bits[-1], 0)], [mark])
-    if blocks > 1:
+    if blocks > cut:
         input_gradient, mark = input_side(
-            kept, *sides, 1, blocks - 1, input_gradient, [total]
+            kept, *sides, cut, blocks - cut, input_gradient, [total]
         )
     for bit in reversed(bits[:-1]):
         total = rejoin(total, swap(total, bit, 0), bit, [mark])
         mark = total
-    shared_down_gradient = join_shares(total, shift(total, "sub", 1), [mark]).T
+    laid = lay_share(total, False, None, [mark])
+    shared_down_gradient = lay_share(shift(total, "sub", 1), True, laid, []).T
     return (input_gradient, shared_down_gradient, grad_heads)
 
 

time: 41.8 us -> 42.4 us (1.014)
  waiting for transfers between devices: 7.67 us -> 5.18 us
  starting transfers between devices: 19.3 us -> 21.6 us
  Pallas kernels: 13.2 us -> 13.9 us
    ppermute x9, waiting for transfers between devices: 5.63 us -> 3.17 us  [swap(): lax.ppermute(x, ('own', 'sub'), [(i, i ^ other) for i in range(whole)])]
    ppermute x9, starting transfers between devices: 14.2 us -> 16.1 us  [swap(): lax.ppermute(x, ('own', 'sub'), [(i, i ^ other) for i in range(whole)])]
    pallas_call x18 -> x20, Pallas kernels: 13.2 us -> 13.9 us  [call(): pl.pallas_call(kernel, out_shape=outs, in_specs=list(specs) + [anywhere]...]
    ppermute x8 -> x9, starting transfers between devices: 5.11 us -> 5.46 us  [shift(): lax.ppermute(x, axis, [(i, (i + step) % count) for i in range(count)])]
    ppermute x8 -> x9, waiting for transfers between devices: 2.04 us -> 2.01 us  [shift(): lax.ppermute(x, axis, [(i, (i + step) % count) for i in range(count)])]
  transfers between devices with their start and end apart: 17 -> 18, of which waited for: 8 -> 9; matrix products, arithmetic and copies ran while one was open for 0% -> 0% of each run, Pallas kernels for 29% -> 31%
where the time goes in v11:
time: 42.4 us; the launch traced here: 42.2 us
  starting transfers between devices  21.6 us (51%)
  Pallas kernels  13.9 us (33%)
  waiting for transfers between devices  5.18 us (12%)
  between operations  1.51 us (4%)
    ppermute x9, starting transfers between devices, swap(): lax.ppermute(x, ('own', 'sub'), [(i, i ^ other) for i in range(whole)])  16.1 us
    pallas_call x20, Pallas kernels, call(): pl.pallas_call(kernel, out_shape=outs, in_specs=list(specs) + [anywhere]...  13.9 us
    ppermute x9, starting transfers between devices, shift(): lax.ppermute(x, axis, [(i, (i + step) % count) for i in range(count)])  5.46 us
    ppermute x9, waiting for transfers between devices, swap(): lax.ppermute(x, ('own', 'sub'), [(i, i ^ other) for i in range(whole)])  3.17 us
    ppermute x9, waiting for transfers between devices, shift(): lax.ppermute(x, axis, [(i, (i + step) % count) for i in range(count)])  2.01 us
  transfers between devices with their start and end apart: 18, of which 9 were waited for; matrix products, arithmetic and copies ran while one was open for 0% of the time, Pallas kernels for 31%

profile of v11, /device:TPU:0, one launch (start us, length us, event | category | flops | bytes accessed | tf_op | source)
XLA Modules:
  0.0 42.2 jit_solution(6690487870756342237)
XLA Ops:
  1.2 1.5 %shard_map.94 = (bf16[64,512]{1,0:T(8,128)(2,1)S(1)}, bf16[64,512]{1,0:T(8,128)(2,1)S(1)}, bf16[64,512]{1,0:T(8,128)(2,1)S(1)}, bf16[64,512]{1,0:T(8,128)(2,1)S(...) custom-call(s32[8]{0:T(128)} %refs_0_.8, bf16[16,64,512]{2,1,0:T(8,128)(2,1)} %refs_1_.4, bf16[512,512]{1,0:T(8,128)(2,1)} %refs_1_.5), custom_call_target="tpu_custom_call" | custom-call | flops 5000000000 | bytes 1970208 | tf_op jit(solution)/shard_map/pallas_call | solution.py:54
  2.7 3.6 %collective-permute-start.3 = (bf16[64,512]{1,0:T(8,128)(2,1)S(1)}, bf16[64,512]{1,0:T(8,128)(2,1)S(1)}, u32[]{:S(2)}, u32[]{:S(2)}) collective-permute-start(bf16[64,512]{1,0:T(8,128)(2,1)S(1)} %get-tuple-element.28), channel_id=1, source_target_pairs={{0,8},{1,9},{4,12},{5,13},{8,0},{9,1},{12,4},{13,5},{2,10},{3,11},... | collective-permute-start | bytes 196616 | tf_op jit(solution)/shard_map/ppermute | solution.py:32
  6.3 1.3 %collective-permute-start.4 = (bf16[64,512]{1,0:T(8,128)(2,1)S(1)}, bf16[64,512]{1,0:T(8,128)(2,1)S(1)}, u32[]{:S(2)}, u32[]{:S(2)}) collective-permute-start(bf16[64,512]{1,0:T(8,128)(2,1)S(1)} %get-tuple-element.29), channel_id=1, source_target_pairs={{0,12},{1,13},{4,8},{5,9},{8,4},{9,5},{12,0},{13,1},{2,14},{3,15},... | collective-permute-start | bytes 196616 | tf_op jit(solution)/shard_map/ppermute | solution.py:32
  7.8 1.5 %collective-permute-start = (bf16[128,512]{1,0:T(8,128)(2,1)S(1)}, bf16[128,512]{1,0:T(8,128)(2,1)S(1)}, u32[]{:S(2)}, u32[]{:S(2)}) collective-permute-start(bf16[128,512]{1,0:T(8,128)(2,1)S(1)} %get-tuple-element.25), channel_id=1, source_target_pairs={{0,2},{2,0},{1,3},{3,1},{4,6},{6,4},{5,7},{7,5},{8,10},{10,8},{9,1... | collective-permute-start | bytes 393224 | tf_op jit(solution)/shard_map/ppermute | solution.py:25
  10.0 0.9 %shard_map.95.refs_0_.refs_6_.refs_1_ = f32[64,512]{1,0:T(8,128)S(1)} custom-call(bf16[512,2560]{1,0:T(8,128)(2,1)S(1)} %copy-done, bf16[64,2560]{1,0:T(8,128)(2,1)S(1)} %bitcast.2, bf16[64,512]{1,0:T(8,128)(2,1)S(1)} %get-tuple-element.26.refs_2_.refs_1_), custom_call_target="tpu_custom_call" | custom-call | flops 167772160 | bytes 3080192 | tf_op jit(solution)/shard_map/pallas_call | solution.py:54
  11.0 0.6 %collective-permute-start.2 = (bf16[64,512]{1,0:T(8,128)(2,1)S(1)}, bf16[64,512]{1,0:T(8,128)(2,1)S(1)}, u32[]{:S(2)}, u32[]{:S(2)}) collective-permute-start(bf16[64,512]{1,0:T(8,128)(2,1)S(1)} %shard_map.96), channel_id=1, source_target_pairs={{0,2},{2,0},{1,3},{3,1},{4,6},{6,4},{5,7},{7,5},{8,10},{10,8},{9,1... | collective-permute-start | bytes 196616 | tf_op jit(solution)/shard_map/ppermute | solution.py:25
  11.6 1.4 %collective-permute-done.4.refs_3_ = bf16[64,512]{1,0:T(8,128)(2,1)S(1)} collective-permute-done((bf16[64,512]{1,0:T(8,128)(2,1)S(1)}, bf16[64,512]{1,0:T(8,128)(2,1)S(1)}, u32[]{:S(2)}, u32[]{:S(2)}) %collective-permute-start.4) | collective-permute-done | bytes 65568 | tf_op jit(solution)/shard_map/ppermute | solution.py:32
  13.5 1.6 %collective-permute-start.10 = (f32[64,512]{1,0:T(8,128)S(1)}, f32[64,512]{1,0:T(8,128)S(1)}, u32[]{:S(2)}, u32[]{:S(2)}) collective-permute-start(f32[64,512]{1,0:T(8,128)S(1)} %shard_map.97.refs_4_.refs_1_), channel_id=1, source_target_pairs={{0,2},{2,0},{1,3},{3,1},{4,6},{6,4},{5,7},{7,5},{8,10},{10,8},{9,1... | collective-permute-start | bytes 393224 | tf_op jit(solution)/shard_map/ppermute | solution.py:25
  15.7 1.9 %collective-permute-start.7 = (bf16[1,64,512]{2,1,0:T(8,128)(2,1)S(1)}, bf16[1,64,512]{2,1,0:T(8,128)(2,1)S(1)}, u32[]{:S(2)}, u32[]{:S(2)}) collective-permute-start(bf16[1,64,512]{2,1,0:T(8,128)(2,1)S(1)} %get-tuple-element.32.refs_4_.refs_0_), channel_id=1, source_target_pairs={{0,4},{1,5},{4,0},{5,1},{8,12},{9,13},{12,8},{13,9},{2,6},{3,7},{6... | collective-permute-start | bytes 196616 | tf_op jit(solution)/shard_map/ppermute | solution.py:32
  17.6 2.3 %collective-permute-start.9 = (bf16[1,64,512]{2,1,0:T(8,128)(2,1)S(1)}, bf16[1,64,512]{2,1,0:T(8,128)(2,1)S(1)}, u32[]{:S(2)}, u32[]{:S(2)}) collective-permute-start(bf16[1,64,512]{2,1,0:T(8,128)(2,1)S(1)} %get-tuple-element.32.refs_4_.refs_0_), channel_id=1, source_target_pairs={{0,12},{1,13},{4,8},{5,9},{8,4},{9,5},{12,0},{13,1},{2,14},{3,15},... | collective-permute-start | bytes 196616 | tf_op jit(solution)/shard_map/ppermute | solution.py:32
  19.9 0.6 %shard_map.99 = (bf16[64,512]{1,0:T(8,128)(2,1)S(1)}, f32[32,2560]{1,0:T(8,128)S(1)}, f32[16,2560]{1,0:T(8,128)S(1)}, f32[16,2560]{1,0:T(8,128)S(1)}) custom-call(s32[1]{0:T(128)S(6)} %copy.16.refs_0_, f32[64,512]{1,0:T(8,128)S(1)} %shard_map.97.refs_4_.refs_1_, f32[64,512]{1,0:T(8,128)S(1)} %collective-permute-done.10.refs_2_, ...), custom_call_target="tpu_custom_call" | custom-call | flops 167772160 | bytes 3604484 | tf_op jit(solution)/shard_map/pallas_call | solution.py:54
  21.1 0.5 %collective-permute-start.6 = (bf16[384,512]{1,0:T(8,128)(2,1)S(1)}, bf16[384,512]{1,0:T(8,128)(2,1)S(1)}, u32[]{:S(2)}, u32[]{:S(2)}) collective-permute-start(bf16[384,512]{1,0:T(8,128)(2,1)S(1)} %get-tuple-element.31), channel_id=1, source_target_pairs={{0,2},{2,0},{1,3},{3,1},{4,6},{6,4},{5,7},{7,5},{8,10},{10,8},{9,1... | collective-permute-start | bytes 1179656 | tf_op jit(solution)/shard_map/ppermute | solution.py:25
  22.3 2.1 %collective-permute-start.14 = (bf16[16,2560]{1,0:T(8,128)(2,1)S(1)}, bf16[16,2560]{1,0:T(8,128)(2,1)S(1)}, u32[]{:S(2)}, u32[]{:S(2)}) collective-permute-start(bf16[16,2560]{1,0:T(8,128)(2,1)S(1)} %get-tuple-element.37.refs_0_), channel_id=1, source_target_pairs={{0,4},{1,5},{4,0},{5,1},{8,12},{9,13},{12,8},{13,9},{2,6},{3,7},{6... | collective-permute-start | bytes 245768 | tf_op jit(solution)/shard_map/ppermute | solution.py:32
  24.4 1.4 %shard_map.103 = (f32[16,64,512]{2,1,0:T(8,128)}, f32[8,128]{1,0:T(8,128)S(1)}) custom-call(bf16[16,2560]{1,0:T(8,128)(2,1)S(1)} %get-tuple-element.37.refs_0_), custom_call_target="tpu_custom_call" | custom-call | flops 10000000000 | bytes 2101248 | tf_op jit(solution)/shard_map/pallas_call | solution.py:54
  26.0 1.3 %collective-permute-done.14.refs_1_ = bf16[16,2560]{1,0:T(8,128)(2,1)S(1)} collective-permute-done((bf16[16,2560]{1,0:T(8,128)(2,1)S(1)}, bf16[16,2560]{1,0:T(8,128)(2,1)S(1)}, u32[]{:S(2)}, u32[]{:S(2)}) %collective-permute-start.14) | collective-permute-done | bytes 81952 | tf_op jit(solution)/shard_map/ppermute | solution.py:32
  27.4 2.7 %collective-permute-start.15 = (bf16[16,2560]{1,0:T(8,128)(2,1)S(1)}, bf16[16,2560]{1,0:T(8,128)(2,1)S(1)}, u32[]{:S(2)}, u32[]{:S(2)}) collective-permute-start(bf16[16,2560]{1,0:T(8,128)(2,1)S(1)} %shard_map.105.refs_4_.refs_0_), channel_id=1, source_target_pairs={{0,8},{1,9},{4,12},{5,13},{8,0},{9,1},{12,4},{13,5},{2,10},{3,11},... | collective-permute-start | bytes 245768 | tf_op jit(solution)/shard_map/ppermute | solution.py:32
  30.0 1.7 %shard_map.106 = (f32[16,64,512]{2,1,0:T(8,128)}, f32[8,128]{1,0:T(8,128)S(1)}) custom-call(s32[8]{0:T(128)} %refs_0_.8, bf16[4,64,512]{2,1,0:T(8,128)(2,1)S(1)} %shard_map.104.refs_2_.refs_1_, bf16[4,64,512]{2,1,0:T(8,128)(2,1)S(1)} %collective-permute-done.13.refs_2_, f32[16,64,512]{2,1,0:T(8,128)} %get-tuple-element.39.refs_3_, ...), custom_call_target="tpu_custom_call", output_to_operand_aliasing={{0}: (3, {})} | custom-call | bytes 4722720 | tf_op jit(solution)/shard_map/pallas_call | solution.py:54
  31.7 0.5 %collective-permute-done.6.refs_3_ = bf16[384,512]{1,0:T(8,128)(2,1)S(1)} collective-permute-done((bf16[384,512]{1,0:T(8,128)(2,1)S(1)}, bf16[384,512]{1,0:T(8,128)(2,1)S(1)}, u32[]{:S(2)}, u32[]{:S(2)}) %collective-permute-start.6) | collective-permute-done | bytes 393248 | tf_op jit(solution)/shard_map/ppermute | solution.py:25
  32.3 1.7 %shard_map.108 = (bf16[512,2560]{1,0:T(8,128)(2,1)}, f32[8,128]{1,0:T(8,128)S(1)}) custom-call(bf16[512,1024]{1,0:T(8,128)(2,1)S(1)} %shard_map.107.refs_0_, bf16[2560,512]{1,0:T(8,128)(2,1)S(1)} %copy-done.1, bf16[2560,512]{1,0:T(8,128)(2,1)S(1)} %collective-permute-done.1.refs_1_.refs_2_, bf16[64,512]{1,0:T(8,128)(2,1)S(1)} %get-tuple-element.36.refs_0_.refs_3_, ...), custom_call_target="tpu_custom_call" | custom-call | flops 570425344 | bytes 9310208 | tf_op jit(solution)/shard_map/pallas_call | solution.py:54
  34.2 1.9 %collective-permute-start.16 = (bf16[16,2560]{1,0:T(8,128)(2,1)S(1)}, bf16[16,2560]{1,0:T(8,128)(2,1)S(1)}, u32[]{:S(2)}, u32[]{:S(2)}) collective-permute-start(bf16[16,2560]{1,0:T(8,128)(2,1)S(1)} %shard_map.109.refs_6_.refs_0_), channel_id=1, source_target_pairs={{0,4},{1,5},{4,0},{5,1},{8,12},{9,13},{12,8},{13,9},{2,6},{3,7},{6... | collective-permute-start | bytes 245768 | tf_op jit(solution)/shard_map/ppermute | solution.py:32
  36.2 3.7 %shard_map.110 = (bf16[512,2560]{1,0:T(8,128)(2,1)}, f32[8,128]{1,0:T(8,128)S(1)}) custom-call(bf16[512,1024]{1,0:T(8,128)(2,1)S(1)} %shard_map.107.refs_0_, bf16[2560,512]{1,0:T(8,128)(2,1)S(1)} %copy-done.1, bf16[2560,512]{1,0:T(8,128)(2,1)S(1)} %collective-permute-done.1.refs_1_.refs_2_, ...), custom_call_target="tpu_custom_call", output_to_operand_aliasing={{0}: (5, {})} | custom-call | flops 2281701376 | bytes 11931648 | tf_op jit(solution)/shard_map/pallas_call | solution.py:54
  40.1 0.8 %shard_map.112.refs_1_ = f32[64,2560]{1,0:T(8,128)} custom-call(bf16[32,2560]{1,0:T(8,128)(2,1)S(1)} %shard_map.111.refs_0_.refs_1_, bf16[32,2560]{1,0:T(8,128)(2,1)S(1)} %shard_map.111.refs_0_.refs_1_), custom_call_target="tpu_custom_call" | custom-call | bytes 819200 | tf_op jit(solution)/shard_map/pallas_call | solution.py:54
  40.8 0.6 %collective-permute-done.17.refs_0_ = bf16[32,2560]{1,0:T(8,128)(2,1)S(1)} collective-permute-done((bf16[32,2560]{1,0:T(8,128)(2,1)S(1)}, bf16[32,2560]{1,0:T(8,128)(2,1)S(1)}, u32[]{:S(2)}, u32[]{:S(2)}) %collective-permute-start.17) | collective-permute-done | bytes 163872 | tf_op jit(solution)/shard_map/ppermute | solution.py:25
  41.5 0.8 %shard_map.113 = f32[64,2560]{1,0:T(8,128)} custom-call(bf16[32,2560]{1,0:T(8,128)(2,1)S(1)} %collective-permute-done.17.refs_0_, f32[64,2560]{1,0:T(8,128)} %shard_map.112.refs_1_), custom_call_target="tpu_custom_call", output_to_operand_aliasing={{}: (1, {})} | custom-call | bytes 1474560 | tf_op jit(solution)/shard_map/pallas_call | solution.py:54
  (40 shorter events, 3.7 us)
Async XLA Ops:
  0.6 9.4 %copy-start = (bf16[512,2560]{1,0:T(8,128)(2,1)S(1)}, bf16[512,2560]{1,0:T(8,128)(2,1)}, u32[]{:S(2)}) copy-start(bf16[512,2560]{1,0:T(8,128)(2,1)} %refs_3_.3) | copy-start | bytes 7864324
  0.6 9.4 %copy-start.2 = (bf16[2560,64]{0,1:T(8,128)(2,1)S(1)}, bf16[2560,64]{0,1:T(8,128)(2,1)}, u32[]{:S(2)}) copy-start(bf16[2560,64]{0,1:T(8,128)(2,1)} %param.10) | copy-start | bytes 983044
  0.7 10.3 %collective-permute-start.1 = (bf16[2560,512]{1,0:T(8,128)(2,1)}, bf16[2560,512]{1,0:T(8,128)(2,1)S(1)}, u32[]{:S(2)}, u32[]{:S(2)}) collective-permute-start(bf16[2560,512]{1,0:T(8,128)(2,1)} %refs_1_.7), channel_id=1, source_target_pairs={{0,1},{1,0},{2,3},{3,2},{4,5},{5,4},{6,7},{7,6},{8,9},{9,8},{10,11... | collective-permute-start | bytes 7864328 | tf_op jit(solution)/shard_map/ppermute | solution.py:25
  2.7 8.8 %collective-permute-start.3 = (bf16[64,512]{1,0:T(8,128)(2,1)S(1)}, bf16[64,512]{1,0:T(8,128)(2,1)S(1)}, u32[]{:S(2)}, u32[]{:S(2)}) collective-permute-start(bf16[64,512]{1,0:T(8,128)(2,1)S(1)} %get-tuple-element.28), channel_id=1, source_target_pairs={{0,8},{1,9},{4,12},{5,13},{8,0},{9,1},{12,4},{13,5},{2,10},{3,11},... | collective-permute-start | bytes 196616 | tf_op jit(solution)/shard_map/ppermute | solution.py:32
  6.3 6.7 %collective-permute-start.4 = (bf16[64,512]{1,0:T(8,128)(2,1)S(1)}, bf16[64,512]{1,0:T(8,128)(2,1)S(1)}, u32[]{:S(2)}, u32[]{:S(2)}) collective-permute-start(bf16[64,512]{1,0:T(8,128)(2,1)S(1)} %get-tuple-element.29), channel_id=1, source_target_pairs={{0,12},{1,13},{4,8},{5,9},{8,4},{9,5},{12,0},{13,1},{2,14},{3,15},... | collective-permute-start | bytes 196616 | tf_op jit(solution)/shard_map/ppermute | solution.py:32
  7.6 5.6 %collective-permute-start.5 = (bf16[64,512]{1,0:T(8,128)(2,1)S(1)}, bf16[64,512]{1,0:T(8,128)(2,1)S(1)}, u32[]{:S(2)}, u32[]{:S(2)}) collective-permute-start(bf16[64,512]{1,0:T(8,128)(2,1)S(1)} %get-tuple-element.30), channel_id=1, source_target_pairs={{0,4},{1,5},{4,0},{5,1},{8,12},{9,13},{12,8},{13,9},{2,6},{3,7},{6... | collective-permute-start | bytes 196616 | tf_op jit(solution)/shard_map/ppermute | solution.py:32
  7.8 7.2 %collective-permute-start = (bf16[128,512]{1,0:T(8,128)(2,1)S(1)}, bf16[128,512]{1,0:T(8,128)(2,1)S(1)}, u32[]{:S(2)}, u32[]{:S(2)}) collective-permute-start(bf16[128,512]{1,0:T(8,128)(2,1)S(1)} %get-tuple-element.25), channel_id=1, source_target_pairs={{0,2},{2,0},{1,3},{3,1},{4,6},{6,4},{5,7},{7,5},{8,10},{10,8},{9,1... | collective-permute-start | bytes 393224 | tf_op jit(solution)/shard_map/ppermute | solution.py:25
  10.0 3.2 %copy-start.3 = (bf16[512,512]{1,0:T(8,128)(2,1)S(1)}, bf16[512,512]{1,0:T(8,128)(2,1)}, u32[]{:S(2)}) copy-start(bf16[512,512]{1,0:T(8,128)(2,1)} %refs_1_.5) | copy-start | bytes 1572868
  11.0 4.4 %collective-permute-start.2 = (bf16[64,512]{1,0:T(8,128)(2,1)S(1)}, bf16[64,512]{1,0:T(8,128)(2,1)S(1)}, u32[]{:S(2)}, u32[]{:S(2)}) collective-permute-start(bf16[64,512]{1,0:T(8,128)(2,1)S(1)} %shard_map.96), channel_id=1, source_target_pairs={{0,2},{2,0},{1,3},{3,1},{4,6},{6,4},{5,7},{7,5},{8,10},{10,8},{9,1... | collective-permute-start | bytes 196616 | tf_op jit(solution)/shard_map/ppermute | solution.py:25
  13.5 6.5 %collective-permute-start.10 = (f32[64,512]{1,0:T(8,128)S(1)}, f32[64,512]{1,0:T(8,128)S(1)}, u32[]{:S(2)}, u32[]{:S(2)}) collective-permute-start(f32[64,512]{1,0:T(8,128)S(1)} %shard_map.97.refs_4_.refs_1_), channel_id=1, source_target_pairs={{0,2},{2,0},{1,3},{3,1},{4,6},{6,4},{5,7},{7,5},{8,10},{10,8},{9,1... | collective-permute-start | bytes 393224 | tf_op jit(solution)/shard_map/ppermute | solution.py:25
  15.7 5.4 %collective-permute-start.7 = (bf16[1,64,512]{2,1,0:T(8,128)(2,1)S(1)}, bf16[1,64,512]{2,1,0:T(8,128)(2,1)S(1)}, u32[]{:S(2)}, u32[]{:S(2)}) collective-permute-start(bf16[1,64,512]{2,1,0:T(8,128)(2,1)S(1)} %get-tuple-element.32.refs_4_.refs_0_), channel_id=1, source_target_pairs={{0,4},{1,5},{4,0},{5,1},{8,12},{9,13},{12,8},{13,9},{2,6},{3,7},{6... | collective-permute-start | bytes 196616 | tf_op jit(solution)/shard_map/ppermute | solution.py:32
  17.6 8.3 %collective-permute-start.9 = (bf16[1,64,512]{2,1,0:T(8,128)(2,1)S(1)}, bf16[1,64,512]{2,1,0:T(8,128)(2,1)S(1)}, u32[]{:S(2)}, u32[]{:S(2)}) collective-permute-start(bf16[1,64,512]{2,1,0:T(8,128)(2,1)S(1)} %get-tuple-element.32.refs_4_.refs_0_), channel_id=1, source_target_pairs={{0,12},{1,13},{4,8},{5,9},{8,4},{9,5},{12,0},{13,1},{2,14},{3,15},... | collective-permute-start | bytes 196616 | tf_op jit(solution)/shard_map/ppermute | solution.py:32
  19.9 5.9 %collective-permute-start.8 = (bf16[1,64,512]{2,1,0:T(8,128)(2,1)S(1)}, bf16[1,64,512]{2,1,0:T(8,128)(2,1)S(1)}, u32[]{:S(2)}, u32[]{:S(2)}) collective-permute-start(bf16[1,64,512]{2,1,0:T(8,128)(2,1)S(1)} %get-tuple-element.32.refs_4_.refs_0_), channel_id=1, source_target_pairs={{0,8},{1,9},{4,12},{5,13},{8,0},{9,1},{12,4},{13,5},{2,10},{3,11},... | collective-permute-start | bytes 196616 | tf_op jit(solution)/shard_map/ppermute | solution.py:32
  20.5 1.5 %collective-permute-start.11 = (f32[16,2560]{1,0:T(8,128)S(1)}, f32[16,2560]{1,0:T(8,128)S(1)}, u32[]{:S(2)}, u32[]{:S(2)}) collective-permute-start(f32[16,2560]{1,0:T(8,128)S(1)} %get-tuple-element.34), channel_id=1, source_target_pairs={{0,1},{1,0},{2,3},{3,2},{4,5},{5,4},{6,7},{7,6},{8,9},{9,8},{10,11... | collective-permute-start | bytes 491528 | tf_op jit(solution)/shard_map/ppermute | solution.py:25
  20.6 1.6 %collective-permute-start.12 = (f32[16,2560]{1,0:T(8,128)S(1)}, f32[16,2560]{1,0:T(8,128)S(1)}, u32[]{:S(2)}, u32[]{:S(2)}) collective-permute-start(f32[16,2560]{1,0:T(8,128)S(1)} %get-tuple-element.35), channel_id=1, source_target_pairs={{0,1},{1,0},{2,3},{3,2},{4,5},{5,4},{6,7},{7,6},{8,9},{9,8},{10,11... | collective-permute-start | bytes 491528 | tf_op jit(solution)/shard_map/ppermute | solution.py:25
  21.1 11.1 %collective-permute-start.6 = (bf16[384,512]{1,0:T(8,128)(2,1)S(1)}, bf16[384,512]{1,0:T(8,128)(2,1)S(1)}, u32[]{:S(2)}, u32[]{:S(2)}) collective-permute-start(bf16[384,512]{1,0:T(8,128)(2,1)S(1)} %get-tuple-element.31), channel_id=1, source_target_pairs={{0,2},{2,0},{1,3},{3,1},{4,6},{6,4},{5,7},{7,5},{8,10},{10,8},{9,1... | collective-permute-start | bytes 1179656 | tf_op jit(solution)/shard_map/ppermute | solution.py:25
  22.3 5.0 %collective-permute-start.14 = (bf16[16,2560]{1,0:T(8,128)(2,1)S(1)}, bf16[16,2560]{1,0:T(8,128)(2,1)S(1)}, u32[]{:S(2)}, u32[]{:S(2)}) collective-permute-start(bf16[16,2560]{1,0:T(8,128)(2,1)S(1)} %get-tuple-element.37.refs_0_), channel_id=1, source_target_pairs={{0,4},{1,5},{4,0},{5,1},{8,12},{9,13},{12,8},{13,9},{2,6},{3,7},{6... | collective-permute-start | bytes 245768 | tf_op jit(solution)/shard_map/ppermute | solution.py:32
  25.9 4.1 %collective-permute-start.13 = (bf16[4,64,512]{2,1,0:T(8,128)(2,1)S(1)}, bf16[4,64,512]{2,1,0:T(8,128)(2,1)S(1)}, u32[]{:S(2)}, u32[]{:S(2)}) collective-permute-start(bf16[4,64,512]{2,1,0:T(8,128)(2,1)S(1)} %shard_map.104.refs_2_.refs_1_), channel_id=1, source_target_pairs={{0,1},{1,0},{2,3},{3,2},{4,5},{5,4},{6,7},{7,6},{8,9},{9,8},{10,11... | collective-permute-start | bytes 786440 | tf_op jit(solution)/shard_map/ppermute | solution.py:25
  27.3 5.0 %copy-start.1 = (bf16[2560,512]{1,0:T(8,128)(2,1)S(1)}, bf16[2560,512]{1,0:T(8,128)(2,1)}, u32[]{:S(2)}) copy-start(bf16[2560,512]{1,0:T(8,128)(2,1)} %refs_1_.7) | copy-start | bytes 7864324
  27.4 6.9 %collective-permute-start.15 = (bf16[16,2560]{1,0:T(8,128)(2,1)S(1)}, bf16[16,2560]{1,0:T(8,128)(2,1)S(1)}, u32[]{:S(2)}, u32[]{:S(2)}) collective-permute-start(bf16[16,2560]{1,0:T(8,128)(2,1)S(1)} %shard_map.105.refs_4_.refs_0_), channel_id=1, source_target_pairs={{0,8},{1,9},{4,12},{5,13},{8,0},{9,1},{12,4},{13,5},{2,10},{3,11},... | collective-permute-start | bytes 245768 | tf_op jit(solution)/shard_map/ppermute | solution.py:32
  34.2 5.7 %collective-permute-start.16 = (bf16[16,2560]{1,0:T(8,128)(2,1)S(1)}, bf16[16,2560]{1,0:T(8,128)(2,1)S(1)}, u32[]{:S(2)}, u32[]{:S(2)}) collective-permute-start(bf16[16,2560]{1,0:T(8,128)(2,1)S(1)} %shard_map.109.refs_6_.refs_0_), channel_id=1, source_target_pairs={{0,4},{1,5},{4,0},{5,1},{8,12},{9,13},{12,8},{13,9},{2,6},{3,7},{6... | collective-permute-start | bytes 245768 | tf_op jit(solution)/shard_map/ppermute | solution.py:32
  40.0 1.5 %collective-permute-start.17 = (bf16[32,2560]{1,0:T(8,128)(2,1)S(1)}, bf16[32,2560]{1,0:T(8,128)(2,1)S(1)}, u32[]{:S(2)}, u32[]{:S(2)}) collective-permute-start(bf16[32,2560]{1,0:T(8,128)(2,1)S(1)} %shard_map.111.refs_0_.refs_1_), channel_id=1, source_target_pairs={{0,1},{1,0},{2,3},{3,2},{4,5},{5,4},{6,7},{7,6},{8,9},{9,8},{10,11... | collective-permute-start | bytes 491528 | tf_op jit(solution)/shard_map/ppermute | solution.py:25

commit v12 on v10

--- a/solution.py
+++ b/solution.py
@@ -482,34 +482,44 @@
 
     near, late = head_term(lengths, lows, grad_output, scale, [part, *early_grads])
     late_grads = [shift(late, "tp", step) for step in tp_steps]
-    terms = [near] + [swap(near, step, 0) for step in own_steps]
+    bits = [1 << i for i in range(own_count.bit_length() - 1)]
+    terms, pattern = [near], [0]
+    for bit in reversed(bits[1:]):
+        terms = terms + [swap(term, bit, 0) for term in terms]
+        pattern = pattern + [step ^ bit for step in pattern]
+    nearby = [swap(near, 1, 0)] if bits else []
+
     back, keep, send = shared_terms(lengths, parts, tokens, scale, [near])
     pieces = [keep, shift(send, "sub", 1)]
-    met = stack(terms[1:3], flops=middling) if own_count > 1 else near
-
-    bits = [1 << i for i in range(own_count.bit_length() - 1)]
+    met = stack(terms[1:]) if terms[1:] else near
+    met = stack(nearby, [met], flops=middling) if nearby else met
+
     mark = met
     for bit in bits[:-1]:
         stays, leaves = halve(pieces, bit, [mark])
         pieces = [stays, swap(leaves, bit, 0)]
         mark = leaves
     cleaned, mark = clean((per_owner,) + near.shape[1:], [mark])
+    total = add_up(pieces, [mark], flops=busy)
+    relays = [total]
+    if bits:
+        relays = [stack([term], [total]) for term in terms[1:]]
+        terms = terms + nearby + [swap(relay, 1, 0) for relay in relays]
+        pattern = pattern + [step ^ 1 for step in pattern]
+    kept = arrange(lengths, grad_output, list(zip(early_grads, late_grads)), relays)
+    sides = (frozen_value, frozen_other, back, down)
+    blocks = features // width_of(features)
+    cut = max(1, blocks * 2 // 5)
+    input_gradient, mark = input_side(kept, *sides, 0, cut, None, relays)
     near = stack(terms, [mark])
     far = shift(near, "sub", 1)
-    total = add_up(pieces, [near], flops=busy)
-    grad_heads, mark = place_terms(
-        adapter_ids, near, far, range(own_count), cleaned, [total]
-    )
-    kept = arrange(lengths, grad_output, list(zip(early_grads, late_grads)), [mark])
-    sides = (frozen_value, frozen_other, back, down)
-    blocks = features // width_of(features)
-    input_gradient, mark = input_side(kept, *sides, 0, 1, None, [mark])
     if bits:
-        total = add_up([total, swap(total, bits[-1], 0)], [mark])
-    if blocks > 1:
+        total = add_up([total, swap(total, bits[-1], 0)], [near], flops=busy)
+    if blocks > cut:
         input_gradient, mark = input_side(
-            kept, *sides, 1, blocks - 1, input_gradient, [total]
+            kept, *sides, cut, blocks - cut, input_gradient, [total]
         )
+    grad_heads, mark = place_terms(adapter_ids, near, far, pattern, cleaned, [mark])
     for bit in reversed(bits[:-1]):
         total = rejoin(total, swap(total, bit, 0), bit, [mark])
         mark = total

time: 41.8 us -> 41.8 us (level)
  starting transfers between devices: 19.3 us -> 17.9 us
  waiting for transfers between devices: 7.67 us -> 8.85 us
    ppermute x9, waiting for transfers between devices: 5.63 us -> 7.36 us  [swap(): lax.ppermute(x, ('own', 'sub'), [(i, i ^ other) for i in range(whole)])]
    ppermute x9, starting transfers between devices: 14.2 us -> 12.8 us  [swap(): lax.ppermute(x, ('own', 'sub'), [(i, i ^ other) for i in range(whole)])]
    ppermute x8, waiting for transfers between devices: 2.04 us -> 1.49 us  [shift(): lax.ppermute(x, axis, [(i, (i + step) % count) for i in range(count)])]
    pallas_call x18 -> x20, Pallas kernels: 13.2 us -> 13.4 us  [call(): pl.pallas_call(kernel, out_shape=outs, in_specs=list(specs) + [anywhere]...]
  transfers between devices with their start and end apart: 17 -> 17, of which waited for: 8 -> 8; matrix products, arithmetic and copies ran while one was open for 0% -> 0% of each run, Pallas kernels for 29% -> 30%
where the time goes in v12:
time: 41.8 us; the launch traced here: 41.7 us
  starting transfers between devices  17.9 us (43%)
  Pallas kernels  13.4 us (32%)
  waiting for transfers between devices  8.85 us (21%)
  between operations  1.5 us (4%)
    pallas_call x20, Pallas kernels, call(): pl.pallas_call(kernel, out_shape=outs, in_specs=list(specs) + [anywhere]...  13.4 us
    ppermute x9, starting transfers between devices, swap(): lax.ppermute(x, ('own', 'sub'), [(i, i ^ other) for i in range(whole)])  12.8 us
    ppermute x9, waiting for transfers between devices, swap(): lax.ppermute(x, ('own', 'sub'), [(i, i ^ other) for i in range(whole)])  7.36 us
    ppermute x8, starting transfers between devices, shift(): lax.ppermute(x, axis, [(i, (i + step) % count) for i in range(count)])  5.16 us
    ppermute x8, waiting for transfers between devices, shift(): lax.ppermute(x, axis, [(i, (i + step) % count) for i in range(count)])  1.49 us
  transfers between devices with their start and end apart: 17, of which 8 were waited for; matrix products, arithmetic and copies ran while one was open for 0% of the time, Pallas kernels for 30%

profile of v12, /device:TPU:0, one launch (start us, length us, event | category | flops | bytes accessed | tf_op | source)
XLA Modules:
  0.0 41.7 jit_solution(13950405938457839267)
XLA Ops:
  1.2 1.5 %shard_map.94 = (bf16[64,512]{1,0:T(8,128)(2,1)S(1)}, bf16[64,512]{1,0:T(8,128)(2,1)S(1)}, bf16[64,512]{1,0:T(8,128)(2,1)S(1)}, bf16[64,512]{1,0:T(8,128)(2,1)S(...) custom-call(s32[8]{0:T(128)} %refs_0_.8, bf16[16,64,512]{2,1,0:T(8,128)(2,1)} %refs_1_.4, bf16[512,512]{1,0:T(8,128)(2,1)} %refs_1_.5), custom_call_target="tpu_custom_call" | custom-call | flops 5000000000 | bytes 1970208 | tf_op jit(solution)/shard_map/pallas_call | solution.py:55
  2.7 3.6 %collective-permute-start.3 = (bf16[64,512]{1,0:T(8,128)(2,1)S(1)}, bf16[64,512]{1,0:T(8,128)(2,1)S(1)}, u32[]{:S(2)}, u32[]{:S(2)}) collective-permute-start(bf16[64,512]{1,0:T(8,128)(2,1)S(1)} %get-tuple-element.27), channel_id=1, source_target_pairs={{0,8},{1,9},{4,12},{5,13},{8,0},{9,1},{12,4},{13,5},{2,10},{3,11},... | collective-permute-start | bytes 196616 | tf_op jit(solution)/shard_map/ppermute | solution.py:33
  6.3 1.3 %collective-permute-start.4 = (bf16[64,512]{1,0:T(8,128)(2,1)S(1)}, bf16[64,512]{1,0:T(8,128)(2,1)S(1)}, u32[]{:S(2)}, u32[]{:S(2)}) collective-permute-start(bf16[64,512]{1,0:T(8,128)(2,1)S(1)} %get-tuple-element.28), channel_id=1, source_target_pairs={{0,12},{1,13},{4,8},{5,9},{8,4},{9,5},{12,0},{13,1},{2,14},{3,15},... | collective-permute-start | bytes 196616 | tf_op jit(solution)/shard_map/ppermute | solution.py:33
  7.8 1.5 %collective-permute-start = (bf16[128,512]{1,0:T(8,128)(2,1)S(1)}, bf16[128,512]{1,0:T(8,128)(2,1)S(1)}, u32[]{:S(2)}, u32[]{:S(2)}) collective-permute-start(bf16[128,512]{1,0:T(8,128)(2,1)S(1)} %get-tuple-element.24), channel_id=1, source_target_pairs={{0,2},{2,0},{1,3},{3,1},{4,6},{6,4},{5,7},{7,5},{8,10},{10,8},{9,1... | collective-permute-start | bytes 393224 | tf_op jit(solution)/shard_map/ppermute | solution.py:26
  10.0 0.9 %shard_map.95.refs_0_.refs_6_.refs_1_ = f32[64,512]{1,0:T(8,128)S(1)} custom-call(bf16[512,2560]{1,0:T(8,128)(2,1)S(1)} %copy-done, bf16[64,2560]{1,0:T(8,128)(2,1)S(1)} %bitcast.2, bf16[64,512]{1,0:T(8,128)(2,1)S(1)} %get-tuple-element.25.refs_2_.refs_1_), custom_call_target="tpu_custom_call" | custom-call | flops 167772160 | bytes 3080192 | tf_op jit(solution)/shard_map/pallas_call | solution.py:55
  11.0 0.6 %collective-permute-start.2 = (bf16[64,512]{1,0:T(8,128)(2,1)S(1)}, bf16[64,512]{1,0:T(8,128)(2,1)S(1)}, u32[]{:S(2)}, u32[]{:S(2)}) collective-permute-start(bf16[64,512]{1,0:T(8,128)(2,1)S(1)} %shard_map.96), channel_id=1, source_target_pairs={{0,2},{2,0},{1,3},{3,1},{4,6},{6,4},{5,7},{7,5},{8,10},{10,8},{9,1... | collective-permute-start | bytes 196616 | tf_op jit(solution)/shard_map/ppermute | solution.py:26
  11.6 1.4 %collective-permute-done.4.refs_3_ = bf16[64,512]{1,0:T(8,128)(2,1)S(1)} collective-permute-done((bf16[64,512]{1,0:T(8,128)(2,1)S(1)}, bf16[64,512]{1,0:T(8,128)(2,1)S(1)}, u32[]{:S(2)}, u32[]{:S(2)}) %collective-permute-start.4) | collective-permute-done | bytes 65568 | tf_op jit(solution)/shard_map/ppermute | solution.py:33
  13.5 1.6 %collective-permute-start.8 = (f32[64,512]{1,0:T(8,128)S(1)}, f32[64,512]{1,0:T(8,128)S(1)}, u32[]{:S(2)}, u32[]{:S(2)}) collective-permute-start(f32[64,512]{1,0:T(8,128)S(1)} %shard_map.97.refs_4_.refs_1_), channel_id=1, source_target_pairs={{0,2},{2,0},{1,3},{3,1},{4,6},{6,4},{5,7},{7,5},{8,10},{10,8},{9,1... | collective-permute-start | bytes 393224 | tf_op jit(solution)/shard_map/ppermute | solution.py:26
  15.7 2.8 %collective-permute-start.7 = (bf16[1,64,512]{2,1,0:T(8,128)(2,1)S(1)}, bf16[1,64,512]{2,1,0:T(8,128)(2,1)S(1)}, u32[]{:S(2)}, u32[]{:S(2)}) collective-permute-start(bf16[1,64,512]{2,1,0:T(8,128)(2,1)S(1)} %get-tuple-element.31.refs_4_.refs_0_), channel_id=1, source_target_pairs={{0,8},{1,9},{4,12},{5,13},{8,0},{9,1},{12,4},{13,5},{2,10},{3,11},... | collective-permute-start | bytes 196616 | tf_op jit(solution)/shard_map/ppermute | solution.py:33
  18.5 0.9 %collective-permute-start.10 = (bf16[1,64,512]{2,1,0:T(8,128)(2,1)S(1)}, bf16[1,64,512]{2,1,0:T(8,128)(2,1)S(1)}, u32[]{:S(2)}, u32[]{:S(2)}) collective-permute-start(bf16[1,64,512]{2,1,0:T(8,128)(2,1)S(1)} %get-tuple-element.31.refs_4_.refs_0_), channel_id=1, source_target_pairs={{0,4},{1,5},{4,0},{5,1},{8,12},{9,13},{12,8},{13,9},{2,6},{3,7},{6... | collective-permute-start | bytes 196616 | tf_op jit(solution)/shard_map/ppermute | solution.py:33
  19.3 0.5 %collective-permute-start.6 = (bf16[384,512]{1,0:T(8,128)(2,1)S(1)}, bf16[384,512]{1,0:T(8,128)(2,1)S(1)}, u32[]{:S(2)}, u32[]{:S(2)}) collective-permute-start(bf16[384,512]{1,0:T(8,128)(2,1)S(1)} %get-tuple-element.30), channel_id=1, source_target_pairs={{0,2},{2,0},{1,3},{3,1},{4,6},{6,4},{5,7},{7,5},{8,10},{10,8},{9,1... | collective-permute-start | bytes 1179656 | tf_op jit(solution)/shard_map/ppermute | solution.py:26
  19.9 0.6 %shard_map.99 = (bf16[64,512]{1,0:T(8,128)(2,1)S(1)}, f32[32,2560]{1,0:T(8,128)S(1)}, f32[32,2560]{1,0:T(8,128)S(1)}) custom-call(s32[1]{0:T(128)S(6)} %copy.14.refs_0_, f32[64,512]{1,0:T(8,128)S(1)} %shard_map.97.refs_4_.refs_1_, f32[64,512]{1,0:T(8,128)S(1)} %collective-permute-done.8.refs_2_, bf16[512,2560]{1,0:T(8,128)(2,1)S(1)} %copy-done, ...), custom_call_target="tpu_custom_call" | custom-call | flops 167772160 | bytes 3604484 | tf_op jit(solution)/shard_map/pallas_call | solution.py:55
  21.0 1.7 %collective-permute-done.10.refs_0_.refs_2_ = bf16[1,64,512]{2,1,0:T(8,128)(2,1)S(1)} collective-permute-done((bf16[1,64,512]{2,1,0:T(8,128)(2,1)S(1)}, bf16[1,64,512]{2,1,0:T(8,128)(2,1)S(1)}, u32[]{:S(2)}, u32[]{:S(2)}) %collective-permute-start.10) | collective-permute-done | bytes 65568 | tf_op jit(solution)/shard_map/ppermute | solution.py:33
  22.8 0.9 %collective-permute-start.11 = (bf16[16,2560]{1,0:T(8,128)(2,1)S(1)}, bf16[16,2560]{1,0:T(8,128)(2,1)S(1)}, u32[]{:S(2)}, u32[]{:S(2)}) collective-permute-start(bf16[16,2560]{1,0:T(8,128)(2,1)S(1)} %get-tuple-element.35.refs_0_), channel_id=1, source_target_pairs={{0,4},{1,5},{4,0},{5,1},{8,12},{9,13},{12,8},{13,9},{2,6},{3,7},{6... | collective-permute-start | bytes 245768 | tf_op jit(solution)/shard_map/ppermute | solution.py:33
  23.7 1.4 %shard_map.103 = (f32[16,64,512]{2,1,0:T(8,128)}, f32[8,128]{1,0:T(8,128)S(1)}) custom-call(bf16[16,2560]{1,0:T(8,128)(2,1)S(1)} %get-tuple-element.35.refs_0_), custom_call_target="tpu_custom_call" | custom-call | flops 10000000000 | bytes 2101248 | tf_op jit(solution)/shard_map/pallas_call | solution.py:55
  25.2 2.1 %collective-permute-done.11.refs_1_ = bf16[16,2560]{1,0:T(8,128)(2,1)S(1)} collective-permute-done((bf16[16,2560]{1,0:T(8,128)(2,1)S(1)}, bf16[16,2560]{1,0:T(8,128)(2,1)S(1)}, u32[]{:S(2)}, u32[]{:S(2)}) %collective-permute-start.11) | collective-permute-done | bytes 81952 | tf_op jit(solution)/shard_map/ppermute | solution.py:33
  27.3 1.8 %collective-permute-start.12 = (bf16[16,2560]{1,0:T(8,128)(2,1)S(1)}, bf16[16,2560]{1,0:T(8,128)(2,1)S(1)}, u32[]{:S(2)}, u32[]{:S(2)}) collective-permute-start(bf16[16,2560]{1,0:T(8,128)(2,1)S(1)} %shard_map.104.refs_1_.refs_0_), channel_id=1, source_target_pairs={{0,8},{1,9},{4,12},{5,13},{8,0},{9,1},{12,4},{13,5},{2,10},{3,11},... | collective-permute-start | bytes 245768 | tf_op jit(solution)/shard_map/ppermute | solution.py:33
  29.1 0.8 %collective-permute-start.13 = (bf16[1,64,512]{2,1,0:T(8,128)(2,1)S(1)}, bf16[1,64,512]{2,1,0:T(8,128)(2,1)S(1)}, u32[]{:S(2)}, u32[]{:S(2)}) collective-permute-start(bf16[1,64,512]{2,1,0:T(8,128)(2,1)S(1)} %shard_map.105.refs_4_.refs_5_), channel_id=1, source_target_pairs={{0,4},{1,5},{4,0},{5,1},{8,12},{9,13},{12,8},{13,9},{2,6},{3,7},{6... | collective-permute-start | bytes 196616 | tf_op jit(solution)/shard_map/ppermute | solution.py:33
  30.0 2.4 %shard_map.107 = (bf16[512,2560]{1,0:T(8,128)(2,1)}, f32[8,128]{1,0:T(8,128)S(1)}) custom-call(bf16[512,1024]{1,0:T(8,128)(2,1)S(1)} %shard_map.106.refs_0_, bf16[2560,512]{1,0:T(8,128)(2,1)S(1)} %copy-done.1, bf16[2560,512]{1,0:T(8,128)(2,1)S(1)} %collective-permute-done.1.refs_1_.refs_2_, bf16[64,512]{1,0:T(8,128)(2,1)S(1)} %get-tuple-element.37.refs_3_, ...), custom_call_target="tpu_custom_call" | custom-call | flops 1140850688 | bytes 9310208 | tf_op jit(solution)/shard_map/pallas_call | solution.py:55
  32.4 1.4 %collective-permute-done.13.refs_3_ = bf16[1,64,512]{2,1,0:T(8,128)(2,1)S(1)} collective-permute-done((bf16[1,64,512]{2,1,0:T(8,128)(2,1)S(1)}, bf16[1,64,512]{2,1,0:T(8,128)(2,1)S(1)}, u32[]{:S(2)}, u32[]{:S(2)}) %collective-permute-start.13) | collective-permute-done | bytes 65568 | tf_op jit(solution)/shard_map/ppermute | solution.py:33
  34.4 3.1 %shard_map.110 = (bf16[512,2560]{1,0:T(8,128)(2,1)}, f32[8,128]{1,0:T(8,128)S(1)}) custom-call(bf16[512,1024]{1,0:T(8,128)(2,1)S(1)} %shard_map.106.refs_0_, bf16[2560,512]{1,0:T(8,128)(2,1)S(1)} %copy-done.1, bf16[2560,512]{1,0:T(8,128)(2,1)S(1)} %collective-permute-done.1.refs_1_.refs_2_, ...), custom_call_target="tpu_custom_call", output_to_operand_aliasing={{0}: (5, {})} | custom-call | flops 1711276032 | bytes 11931648 | tf_op jit(solution)/shard_map/pallas_call | solution.py:55
  37.5 1.8 %shard_map.111 = (f32[16,64,512]{2,1,0:T(8,128)}, f32[8,128]{1,0:T(8,128)S(1)}) custom-call(s32[8]{0:T(128)} %refs_0_.8, bf16[4,64,512]{2,1,0:T(8,128)(2,1)S(1)} %shard_map.108.refs_2_.refs_1_, bf16[4,64,512]{2,1,0:T(8,128)(2,1)S(1)} %collective-permute-done.15.refs_2_, f32[16,64,512]{2,1,0:T(8,128)} %get-tuple-element.41.refs_3_, ...), custom_call_target="tpu_custom_call", output_to_operand_aliasing={{0}: (3, {})} | custom-call | bytes 4722720 | tf_op jit(solution)/shard_map/pallas_call | solution.py:55
  39.6 1.2 %collective-permute-done.16.refs_1_ = bf16[32,2560]{1,0:T(8,128)(2,1)S(1)} collective-permute-done((bf16[32,2560]{1,0:T(8,128)(2,1)S(1)}, bf16[32,2560]{1,0:T(8,128)(2,1)S(1)}, u32[]{:S(2)}, u32[]{:S(2)}) %collective-permute-start.16) | collective-permute-done | bytes 163872 | tf_op jit(solution)/shard_map/ppermute | solution.py:26
  40.8 0.9 %shard_map.113 = f32[64,2560]{1,0:T(8,128)} custom-call(bf16[32,2560]{1,0:T(8,128)(2,1)S(1)} %shard_map.112.refs_0_.refs_2_, bf16[32,2560]{1,0:T(8,128)(2,1)S(1)} %collective-permute-done.16.refs_1_, bf16[32,2560]{1,0:T(8,128)(2,1)S(1)} %shard_map.112.refs_0_.refs_2_), custom_call_target="tpu_custom_call" | custom-call | bytes 983040 | tf_op jit(solution)/shard_map/pallas_call | solution.py:55
  (38 shorter events, 3.5 us)
Async XLA Ops:
  0.6 9.4 %copy-start = (bf16[512,2560]{1,0:T(8,128)(2,1)S(1)}, bf16[512,2560]{1,0:T(8,128)(2,1)}, u32[]{:S(2)}) copy-start(bf16[512,2560]{1,0:T(8,128)(2,1)} %refs_3_.3) | copy-start | bytes 7864324
  0.6 9.4 %copy-start.2 = (bf16[2560,64]{0,1:T(8,128)(2,1)S(1)}, bf16[2560,64]{0,1:T(8,128)(2,1)}, u32[]{:S(2)}) copy-start(bf16[2560,64]{0,1:T(8,128)(2,1)} %param.10) | copy-start | bytes 983044
  0.7 10.3 %collective-permute-start.1 = (bf16[2560,512]{1,0:T(8,128)(2,1)}, bf16[2560,512]{1,0:T(8,128)(2,1)S(1)}, u32[]{:S(2)}, u32[]{:S(2)}) collective-permute-start(bf16[2560,512]{1,0:T(8,128)(2,1)} %refs_1_.7), channel_id=1, source_target_pairs={{0,1},{1,0},{2,3},{3,2},{4,5},{5,4},{6,7},{7,6},{8,9},{9,8},{10,11... | collective-permute-start | bytes 7864328 | tf_op jit(solution)/shard_map/ppermute | solution.py:26
  2.7 8.8 %collective-permute-start.3 = (bf16[64,512]{1,0:T(8,128)(2,1)S(1)}, bf16[64,512]{1,0:T(8,128)(2,1)S(1)}, u32[]{:S(2)}, u32[]{:S(2)}) collective-permute-start(bf16[64,512]{1,0:T(8,128)(2,1)S(1)} %get-tuple-element.27), channel_id=1, source_target_pairs={{0,8},{1,9},{4,12},{5,13},{8,0},{9,1},{12,4},{13,5},{2,10},{3,11},... | collective-permute-start | bytes 196616 | tf_op jit(solution)/shard_map/ppermute | solution.py:33
  6.3 6.7 %collective-permute-start.4 = (bf16[64,512]{1,0:T(8,128)(2,1)S(1)}, bf16[64,512]{1,0:T(8,128)(2,1)S(1)}, u32[]{:S(2)}, u32[]{:S(2)}) collective-permute-start(bf16[64,512]{1,0:T(8,128)(2,1)S(1)} %get-tuple-element.28), channel_id=1, source_target_pairs={{0,12},{1,13},{4,8},{5,9},{8,4},{9,5},{12,0},{13,1},{2,14},{3,15},... | collective-permute-start | bytes 196616 | tf_op jit(solution)/shard_map/ppermute | solution.py:33
  7.6 5.6 %collective-permute-start.5 = (bf16[64,512]{1,0:T(8,128)(2,1)S(1)}, bf16[64,512]{1,0:T(8,128)(2,1)S(1)}, u32[]{:S(2)}, u32[]{:S(2)}) collective-permute-start(bf16[64,512]{1,0:T(8,128)(2,1)S(1)} %get-tuple-element.29), channel_id=1, source_target_pairs={{0,4},{1,5},{4,0},{5,1},{8,12},{9,13},{12,8},{13,9},{2,6},{3,7},{6... | collective-permute-start | bytes 196616 | tf_op jit(solution)/shard_map/ppermute | solution.py:33
  7.8 7.2 %collective-permute-start = (bf16[128,512]{1,0:T(8,128)(2,1)S(1)}, bf16[128,512]{1,0:T(8,128)(2,1)S(1)}, u32[]{:S(2)}, u32[]{:S(2)}) collective-permute-start(bf16[128,512]{1,0:T(8,128)(2,1)S(1)} %get-tuple-element.24), channel_id=1, source_target_pairs={{0,2},{2,0},{1,3},{3,1},{4,6},{6,4},{5,7},{7,5},{8,10},{10,8},{9,1... | collective-permute-start | bytes 393224 | tf_op jit(solution)/shard_map/ppermute | solution.py:26
  10.0 3.2 %copy-start.3 = (bf16[512,512]{1,0:T(8,128)(2,1)S(1)}, bf16[512,512]{1,0:T(8,128)(2,1)}, u32[]{:S(2)}) copy-start(bf16[512,512]{1,0:T(8,128)(2,1)} %refs_1_.5) | copy-start | bytes 1572868
  11.0 4.4 %collective-permute-start.2 = (bf16[64,512]{1,0:T(8,128)(2,1)S(1)}, bf16[64,512]{1,0:T(8,128)(2,1)S(1)}, u32[]{:S(2)}, u32[]{:S(2)}) collective-permute-start(bf16[64,512]{1,0:T(8,128)(2,1)S(1)} %shard_map.96), channel_id=1, source_target_pairs={{0,2},{2,0},{1,3},{3,1},{4,6},{6,4},{5,7},{7,5},{8,10},{10,8},{9,1... | collective-permute-start | bytes 196616 | tf_op jit(solution)/shard_map/ppermute | solution.py:26
  13.5 6.4 %collective-permute-start.8 = (f32[64,512]{1,0:T(8,128)S(1)}, f32[64,512]{1,0:T(8,128)S(1)}, u32[]{:S(2)}, u32[]{:S(2)}) collective-permute-start(f32[64,512]{1,0:T(8,128)S(1)} %shard_map.97.refs_4_.refs_1_), channel_id=1, source_target_pairs={{0,2},{2,0},{1,3},{3,1},{4,6},{6,4},{5,7},{7,5},{8,10},{10,8},{9,1... | collective-permute-start | bytes 393224 | tf_op jit(solution)/shard_map/ppermute | solution.py:26
  15.7 5.3 %collective-permute-start.7 = (bf16[1,64,512]{2,1,0:T(8,128)(2,1)S(1)}, bf16[1,64,512]{2,1,0:T(8,128)(2,1)S(1)}, u32[]{:S(2)}, u32[]{:S(2)}) collective-permute-start(bf16[1,64,512]{2,1,0:T(8,128)(2,1)S(1)} %get-tuple-element.31.refs_4_.refs_0_), channel_id=1, source_target_pairs={{0,8},{1,9},{4,12},{5,13},{8,0},{9,1},{12,4},{13,5},{2,10},{3,11},... | collective-permute-start | bytes 196616 | tf_op jit(solution)/shard_map/ppermute | solution.py:33
  18.5 4.3 %collective-permute-start.10 = (bf16[1,64,512]{2,1,0:T(8,128)(2,1)S(1)}, bf16[1,64,512]{2,1,0:T(8,128)(2,1)S(1)}, u32[]{:S(2)}, u32[]{:S(2)}) collective-permute-start(bf16[1,64,512]{2,1,0:T(8,128)(2,1)S(1)} %get-tuple-element.31.refs_4_.refs_0_), channel_id=1, source_target_pairs={{0,4},{1,5},{4,0},{5,1},{8,12},{9,13},{12,8},{13,9},{2,6},{3,7},{6... | collective-permute-start | bytes 196616 | tf_op jit(solution)/shard_map/ppermute | solution.py:33
  19.3 10.6 %collective-permute-start.6 = (bf16[384,512]{1,0:T(8,128)(2,1)S(1)}, bf16[384,512]{1,0:T(8,128)(2,1)S(1)}, u32[]{:S(2)}, u32[]{:S(2)}) collective-permute-start(bf16[384,512]{1,0:T(8,128)(2,1)S(1)} %get-tuple-element.30), channel_id=1, source_target_pairs={{0,2},{2,0},{1,3},{3,1},{4,6},{6,4},{5,7},{7,5},{8,10},{10,8},{9,1... | collective-permute-start | bytes 1179656 | tf_op jit(solution)/shard_map/ppermute | solution.py:26
  20.5 2.3 %collective-permute-start.9 = (f32[32,2560]{1,0:T(8,128)S(1)}, f32[32,2560]{1,0:T(8,128)S(1)}, u32[]{:S(2)}, u32[]{:S(2)}) collective-permute-start(f32[32,2560]{1,0:T(8,128)S(1)} %get-tuple-element.33), channel_id=1, source_target_pairs={{0,1},{1,0},{2,3},{3,2},{4,5},{5,4},{6,7},{7,6},{8,9},{9,8},{10,11... | collective-permute-start | bytes 983048 | tf_op jit(solution)/shard_map/ppermute | solution.py:26
  22.8 4.5 %collective-permute-start.11 = (bf16[16,2560]{1,0:T(8,128)(2,1)S(1)}, bf16[16,2560]{1,0:T(8,128)(2,1)S(1)}, u32[]{:S(2)}, u32[]{:S(2)}) collective-permute-start(bf16[16,2560]{1,0:T(8,128)(2,1)S(1)} %get-tuple-element.35.refs_0_), channel_id=1, source_target_pairs={{0,4},{1,5},{4,0},{5,1},{8,12},{9,13},{12,8},{13,9},{2,6},{3,7},{6... | collective-permute-start | bytes 245768 | tf_op jit(solution)/shard_map/ppermute | solution.py:33
  27.3 2.7 %copy-start.1 = (bf16[2560,512]{1,0:T(8,128)(2,1)S(1)}, bf16[2560,512]{1,0:T(8,128)(2,1)}, u32[]{:S(2)}) copy-start(bf16[2560,512]{1,0:T(8,128)(2,1)} %refs_1_.7) | copy-start | bytes 7864324
  27.3 6.6 %collective-permute-start.12 = (bf16[16,2560]{1,0:T(8,128)(2,1)S(1)}, bf16[16,2560]{1,0:T(8,128)(2,1)S(1)}, u32[]{:S(2)}, u32[]{:S(2)}) collective-permute-start(bf16[16,2560]{1,0:T(8,128)(2,1)S(1)} %shard_map.104.refs_1_.refs_0_), channel_id=1, source_target_pairs={{0,8},{1,9},{4,12},{5,13},{8,0},{9,1},{12,4},{13,5},{2,10},{3,11},... | collective-permute-start | bytes 245768 | tf_op jit(solution)/shard_map/ppermute | solution.py:33
  29.1 4.7 %collective-permute-start.13 = (bf16[1,64,512]{2,1,0:T(8,128)(2,1)S(1)}, bf16[1,64,512]{2,1,0:T(8,128)(2,1)S(1)}, u32[]{:S(2)}, u32[]{:S(2)}) collective-permute-start(bf16[1,64,512]{2,1,0:T(8,128)(2,1)S(1)} %shard_map.105.refs_4_.refs_5_), channel_id=1, source_target_pairs={{0,4},{1,5},{4,0},{5,1},{8,12},{9,13},{12,8},{13,9},{2,6},{3,7},{6... | collective-permute-start | bytes 196616 | tf_op jit(solution)/shard_map/ppermute | solution.py:33
  33.9 3.6 %collective-permute-start.15 = (bf16[4,64,512]{2,1,0:T(8,128)(2,1)S(1)}, bf16[4,64,512]{2,1,0:T(8,128)(2,1)S(1)}, u32[]{:S(2)}, u32[]{:S(2)}) collective-permute-start(bf16[4,64,512]{2,1,0:T(8,128)(2,1)S(1)} %shard_map.108.refs_2_.refs_1_), channel_id=1, source_target_pairs={{0,1},{1,0},{2,3},{3,2},{4,5},{5,4},{6,7},{7,6},{8,9},{9,8},{10,11... | collective-permute-start | bytes 786440 | tf_op jit(solution)/shard_map/ppermute | solution.py:26
  34.0 5.3 %collective-permute-start.14 = (bf16[16,2560]{1,0:T(8,128)(2,1)S(1)}, bf16[16,2560]{1,0:T(8,128)(2,1)S(1)}, u32[]{:S(2)}, u32[]{:S(2)}) collective-permute-start(bf16[16,2560]{1,0:T(8,128)(2,1)S(1)} %shard_map.109.refs_6_.refs_0_), channel_id=1, source_target_pairs={{0,4},{1,5},{4,0},{5,1},{8,12},{9,13},{12,8},{13,9},{2,6},{3,7},{6... | collective-permute-start | bytes 245768 | tf_op jit(solution)/shard_map/ppermute | solution.py:33
  39.4 1.5 %collective-permute-start.16 = (bf16[32,2560]{1,0:T(8,128)(2,1)S(1)}, bf16[32,2560]{1,0:T(8,128)(2,1)S(1)}, u32[]{:S(2)}, u32[]{:S(2)}) collective-permute-start(bf16[32,2560]{1,0:T(8,128)(2,1)S(1)} %shard_map.112.refs_0_.refs_2_), channel_id=1, source_target_pairs={{0,1},{1,0},{2,3},{3,2},{4,5},{5,4},{6,7},{7,6},{8,9},{9,8},{10,11... | collective-permute-start | bytes 491528 | tf_op jit(solution)/shard_map/ppermute | solution.py:26

commit v13 on v10

--- a/solution.py
+++ b/solution.py
@@ -503,12 +503,13 @@
     kept = arrange(lengths, grad_output, list(zip(early_grads, late_grads)), [mark])
     sides = (frozen_value, frozen_other, back, down)
     blocks = features // width_of(features)
-    input_gradient, mark = input_side(kept, *sides, 0, 1, None, [mark])
+    cut = max(1, blocks * 2 // 5)
+    input_gradient, mark = input_side(kept, *sides, 0, cut, None, [mark])
     if bits:
         total = add_up([total, swap(total, bits[-1], 0)], [mark])
-    if blocks > 1:
+    if blocks > cut:
         input_gradient, mark = input_side(
-            kept, *sides, 1, blocks - 1, input_gradient, [total]
+            kept, *sides, cut, blocks - cut, input_gradient, [total]
         )
     for bit in reversed(bits[:-1]):
         total = rejoin(total, swap(total, bit, 0), bit, [mark])

time: 41.8 us -> 41.9 us (level)
  waiting for transfers between devices: 7.67 us -> 6.91 us
  starting transfers between devices: 19.3 us -> 20 us
    ppermute x9, waiting for transfers between devices: 5.63 us -> 4.87 us  [swap(): lax.ppermute(x, ('own', 'sub'), [(i, i ^ other) for i in range(whole)])]
    ppermute x9, starting transfers between devices: 14.2 us -> 14.8 us  [swap(): lax.ppermute(x, ('own', 'sub'), [(i, i ^ other) for i in range(whole)])]
  transfers between devices with their start and end apart: 17 -> 17, of which waited for: 8 -> 7; matrix products, arithmetic and copies ran while one was open for 0% -> 0% of each run, Pallas kernels for 29% -> 30%
where the time goes in v13:
time: 41.9 us; the launch traced here: 41.7 us
  starting transfers between devices  20 us (48%)
  Pallas kernels  13.3 us (32%)
  waiting for transfers between devices  6.91 us (16%)
  between operations  1.52 us (4%)
    ppermute x9, starting transfers between devices, swap(): lax.ppermute(x, ('own', 'sub'), [(i, i ^ other) for i in range(whole)])  14.8 us
    pallas_call x18, Pallas kernels, call(): pl.pallas_call(kernel, out_shape=outs, in_specs=list(specs) + [anywhere]...  13.3 us
    ppermute x8, starting transfers between devices, shift(): lax.ppermute(x, axis, [(i, (i + step) % count) for i in range(count)])  5.11 us
    ppermute x9, waiting for transfers between devices, swap(): lax.ppermute(x, ('own', 'sub'), [(i, i ^ other) for i in range(whole)])  4.87 us
    ppermute x8, waiting for transfers between devices, shift(): lax.ppermute(x, axis, [(i, (i + step) % count) for i in range(count)])  2.04 us
  transfers between devices with their start and end apart: 17, of which 7 were waited for; matrix products, arithmetic and copies ran while one was open for 0% of the time, Pallas kernels for 30%

profile of v13, /device:TPU:0, one launch (start us, length us, event | category | flops | bytes accessed | tf_op | source)
XLA Modules:
  0.0 41.7 jit_solution(5358771634763489100)
XLA Ops:
  1.2 1.5 %shard_map.94 = (bf16[64,512]{1,0:T(8,128)(2,1)S(1)}, bf16[64,512]{1,0:T(8,128)(2,1)S(1)}, bf16[64,512]{1,0:T(8,128)(2,1)S(1)}, bf16[64,512]{1,0:T(8,128)(2,1)S(...) custom-call(s32[8]{0:T(128)} %refs_0_.8, bf16[16,64,512]{2,1,0:T(8,128)(2,1)} %refs_1_.4, bf16[512,512]{1,0:T(8,128)(2,1)} %refs_1_.5), custom_call_target="tpu_custom_call" | custom-call | flops 5000000000 | bytes 1970208 | tf_op jit(solution)/shard_map/pallas_call | solution.py:55
  2.7 3.6 %collective-permute-start.3 = (bf16[64,512]{1,0:T(8,128)(2,1)S(1)}, bf16[64,512]{1,0:T(8,128)(2,1)S(1)}, u32[]{:S(2)}, u32[]{:S(2)}) collective-permute-start(bf16[64,512]{1,0:T(8,128)(2,1)S(1)} %get-tuple-element.27), channel_id=1, source_target_pairs={{0,8},{1,9},{4,12},{5,13},{8,0},{9,1},{12,4},{13,5},{2,10},{3,11},... | collective-permute-start | bytes 196616 | tf_op jit(solution)/shard_map/ppermute | solution.py:33
  6.3 1.3 %collective-permute-start.4 = (bf16[64,512]{1,0:T(8,128)(2,1)S(1)}, bf16[64,512]{1,0:T(8,128)(2,1)S(1)}, u32[]{:S(2)}, u32[]{:S(2)}) collective-permute-start(bf16[64,512]{1,0:T(8,128)(2,1)S(1)} %get-tuple-element.28), channel_id=1, source_target_pairs={{0,12},{1,13},{4,8},{5,9},{8,4},{9,5},{12,0},{13,1},{2,14},{3,15},... | collective-permute-start | bytes 196616 | tf_op jit(solution)/shard_map/ppermute | solution.py:33
  7.8 1.5 %collective-permute-start = (bf16[128,512]{1,0:T(8,128)(2,1)S(1)}, bf16[128,512]{1,0:T(8,128)(2,1)S(1)}, u32[]{:S(2)}, u32[]{:S(2)}) collective-permute-start(bf16[128,512]{1,0:T(8,128)(2,1)S(1)} %get-tuple-element.24), channel_id=1, source_target_pairs={{0,2},{2,0},{1,3},{3,1},{4,6},{6,4},{5,7},{7,5},{8,10},{10,8},{9,1... | collective-permute-start | bytes 393224 | tf_op jit(solution)/shard_map/ppermute | solution.py:26
  10.0 0.9 %shard_map.95.refs_0_.refs_6_.refs_1_ = f32[64,512]{1,0:T(8,128)S(1)} custom-call(bf16[512,2560]{1,0:T(8,128)(2,1)S(1)} %copy-done, bf16[64,2560]{1,0:T(8,128)(2,1)S(1)} %bitcast.2, bf16[64,512]{1,0:T(8,128)(2,1)S(1)} %get-tuple-element.25.refs_2_.refs_1_), custom_call_target="tpu_custom_call" | custom-call | flops 167772160 | bytes 3080192 | tf_op jit(solution)/shard_map/pallas_call | solution.py:55
  11.0 0.6 %collective-permute-start.2 = (bf16[64,512]{1,0:T(8,128)(2,1)S(1)}, bf16[64,512]{1,0:T(8,128)(2,1)S(1)}, u32[]{:S(2)}, u32[]{:S(2)}) collective-permute-start(bf16[64,512]{1,0:T(8,128)(2,1)S(1)} %shard_map.96), channel_id=1, source_target_pairs={{0,2},{2,0},{1,3},{3,1},{4,6},{6,4},{5,7},{7,5},{8,10},{10,8},{9,1... | collective-permute-start | bytes 196616 | tf_op jit(solution)/shard_map/ppermute | solution.py:26
  11.6 1.4 %collective-permute-done.4.refs_3_ = bf16[64,512]{1,0:T(8,128)(2,1)S(1)} collective-permute-done((bf16[64,512]{1,0:T(8,128)(2,1)S(1)}, bf16[64,512]{1,0:T(8,128)(2,1)S(1)}, u32[]{:S(2)}, u32[]{:S(2)}) %collective-permute-start.4) | collective-permute-done | bytes 65568 | tf_op jit(solution)/shard_map/ppermute | solution.py:33
  13.5 1.6 %collective-permute-start.10 = (f32[64,512]{1,0:T(8,128)S(1)}, f32[64,512]{1,0:T(8,128)S(1)}, u32[]{:S(2)}, u32[]{:S(2)}) collective-permute-start(f32[64,512]{1,0:T(8,128)S(1)} %shard_map.97.refs_4_.refs_1_), channel_id=1, source_target_pairs={{0,2},{2,0},{1,3},{3,1},{4,6},{6,4},{5,7},{7,5},{8,10},{10,8},{9,1... | collective-permute-start | bytes 393224 | tf_op jit(solution)/shard_map/ppermute | solution.py:26
  15.7 2.8 %collective-permute-start.8 = (bf16[1,64,512]{2,1,0:T(8,128)(2,1)S(1)}, bf16[1,64,512]{2,1,0:T(8,128)(2,1)S(1)}, u32[]{:S(2)}, u32[]{:S(2)}) collective-permute-start(bf16[1,64,512]{2,1,0:T(8,128)(2,1)S(1)} %get-tuple-element.31.refs_4_.refs_0_), channel_id=1, source_target_pairs={{0,8},{1,9},{4,12},{5,13},{8,0},{9,1},{12,4},{13,5},{2,10},{3,11},... | collective-permute-start | bytes 196616 | tf_op jit(solution)/shard_map/ppermute | solution.py:33
  18.5 0.9 %collective-permute-start.7 = (bf16[1,64,512]{2,1,0:T(8,128)(2,1)S(1)}, bf16[1,64,512]{2,1,0:T(8,128)(2,1)S(1)}, u32[]{:S(2)}, u32[]{:S(2)}) collective-permute-start(bf16[1,64,512]{2,1,0:T(8,128)(2,1)S(1)} %get-tuple-element.31.refs_4_.refs_0_), channel_id=1, source_target_pairs={{0,4},{1,5},{4,0},{5,1},{8,12},{9,13},{12,8},{13,9},{2,6},{3,7},{6... | collective-permute-start | bytes 196616 | tf_op jit(solution)/shard_map/ppermute | solution.py:33
  19.3 0.8 %collective-permute-start.9 = (bf16[1,64,512]{2,1,0:T(8,128)(2,1)S(1)}, bf16[1,64,512]{2,1,0:T(8,128)(2,1)S(1)}, u32[]{:S(2)}, u32[]{:S(2)}) collective-permute-start(bf16[1,64,512]{2,1,0:T(8,128)(2,1)S(1)} %get-tuple-element.31.refs_4_.refs_0_), channel_id=1, source_target_pairs={{0,12},{1,13},{4,8},{5,9},{8,4},{9,5},{12,0},{13,1},{2,14},{3,15},... | collective-permute-start | bytes 196616 | tf_op jit(solution)/shard_map/ppermute | solution.py:33
  20.1 0.7 %collective-permute-start.6 = (bf16[384,512]{1,0:T(8,128)(2,1)S(1)}, bf16[384,512]{1,0:T(8,128)(2,1)S(1)}, u32[]{:S(2)}, u32[]{:S(2)}) collective-permute-start(bf16[384,512]{1,0:T(8,128)(2,1)S(1)} %get-tuple-element.30), channel_id=1, source_target_pairs={{0,2},{2,0},{1,3},{3,1},{4,6},{6,4},{5,7},{7,5},{8,10},{10,8},{9,1... | collective-permute-start | bytes 1179656 | tf_op jit(solution)/shard_map/ppermute | solution.py:26
  20.8 0.6 %shard_map.99 = (bf16[64,512]{1,0:T(8,128)(2,1)S(1)}, f32[32,2560]{1,0:T(8,128)S(1)}, f32[32,2560]{1,0:T(8,128)S(1)}) custom-call(s32[1]{0:T(128)S(6)} %copy.14.refs_0_, f32[64,512]{1,0:T(8,128)S(1)} %shard_map.97.refs_4_.refs_1_, f32[64,512]{1,0:T(8,128)S(1)} %collective-permute-done.10.refs_2_, bf16[512,2560]{1,0:T(8,128)(2,1)S(1)} %copy-done, ...), custom_call_target="tpu_custom_call" | custom-call | flops 167772160 | bytes 3604484 | tf_op jit(solution)/shard_map/pallas_call | solution.py:55
  21.5 1.2 %collective-permute-done.7.refs_0_.refs_1_ = bf16[1,64,512]{2,1,0:T(8,128)(2,1)S(1)} collective-permute-done((bf16[1,64,512]{2,1,0:T(8,128)(2,1)S(1)}, bf16[1,64,512]{2,1,0:T(8,128)(2,1)S(1)}, u32[]{:S(2)}, u32[]{:S(2)}) %collective-permute-start.7) | collective-permute-done | bytes 65568 | tf_op jit(solution)/shard_map/ppermute | solution.py:33
  23.2 1.0 %collective-permute-start.13 = (bf16[16,2560]{1,0:T(8,128)(2,1)S(1)}, bf16[16,2560]{1,0:T(8,128)(2,1)S(1)}, u32[]{:S(2)}, u32[]{:S(2)}) collective-permute-start(bf16[16,2560]{1,0:T(8,128)(2,1)S(1)} %get-tuple-element.34.refs_0_), channel_id=1, source_target_pairs={{0,4},{1,5},{4,0},{5,1},{8,12},{9,13},{12,8},{13,9},{2,6},{3,7},{6... | collective-permute-start | bytes 245768 | tf_op jit(solution)/shard_map/ppermute | solution.py:33
  24.2 1.4 %shard_map.102 = (f32[16,64,512]{2,1,0:T(8,128)}, f32[8,128]{1,0:T(8,128)S(1)}) custom-call(bf16[16,2560]{1,0:T(8,128)(2,1)S(1)} %get-tuple-element.34.refs_0_), custom_call_target="tpu_custom_call" | custom-call | flops 10000000000 | bytes 2101248 | tf_op jit(solution)/shard_map/pallas_call | solution.py:55
  25.8 2.0 %collective-permute-done.13.refs_1_ = bf16[16,2560]{1,0:T(8,128)(2,1)S(1)} collective-permute-done((bf16[16,2560]{1,0:T(8,128)(2,1)S(1)}, bf16[16,2560]{1,0:T(8,128)(2,1)S(1)}, u32[]{:S(2)}, u32[]{:S(2)}) %collective-permute-start.13) | collective-permute-done | bytes 81952 | tf_op jit(solution)/shard_map/ppermute | solution.py:33
  27.8 2.2 %collective-permute-start.14 = (bf16[16,2560]{1,0:T(8,128)(2,1)S(1)}, bf16[16,2560]{1,0:T(8,128)(2,1)S(1)}, u32[]{:S(2)}, u32[]{:S(2)}) collective-permute-start(bf16[16,2560]{1,0:T(8,128)(2,1)S(1)} %shard_map.104.refs_4_.refs_0_), channel_id=1, source_target_pairs={{0,8},{1,9},{4,12},{5,13},{8,0},{9,1},{12,4},{13,5},{2,10},{3,11},... | collective-permute-start | bytes 245768 | tf_op jit(solution)/shard_map/ppermute | solution.py:33
  29.9 1.6 %shard_map.105 = (f32[16,64,512]{2,1,0:T(8,128)}, f32[8,128]{1,0:T(8,128)S(1)}) custom-call(s32[8]{0:T(128)} %refs_0_.8, bf16[4,64,512]{2,1,0:T(8,128)(2,1)S(1)} %shard_map.103.refs_2_.refs_1_, bf16[4,64,512]{2,1,0:T(8,128)(2,1)S(1)} %collective-permute-done.12.refs_2_, f32[16,64,512]{2,1,0:T(8,128)} %get-tuple-element.36.refs_3_, ...), custom_call_target="tpu_custom_call", output_to_operand_aliasing={{0}: (3, {})} | custom-call | bytes 4722720 | tf_op jit(solution)/shard_map/pallas_call | solution.py:55
  31.7 2.4 %shard_map.107 = (bf16[512,2560]{1,0:T(8,128)(2,1)}, f32[8,128]{1,0:T(8,128)S(1)}) custom-call(bf16[512,1024]{1,0:T(8,128)(2,1)S(1)} %shard_map.106.refs_0_, bf16[2560,512]{1,0:T(8,128)(2,1)S(1)} %copy-done.1, bf16[2560,512]{1,0:T(8,128)(2,1)S(1)} %collective-permute-done.1.refs_1_.refs_2_, bf16[64,512]{1,0:T(8,128)(2,1)S(1)} %get-tuple-element.39.refs_3_, ...), custom_call_target="tpu_custom_call" | custom-call | flops 1140850688 | bytes 9310208 | tf_op jit(solution)/shard_map/pallas_call | solution.py:55
  34.2 2.1 %collective-permute-start.15 = (bf16[16,2560]{1,0:T(8,128)(2,1)S(1)}, bf16[16,2560]{1,0:T(8,128)(2,1)S(1)}, u32[]{:S(2)}, u32[]{:S(2)}) collective-permute-start(bf16[16,2560]{1,0:T(8,128)(2,1)S(1)} %shard_map.108.refs_6_.refs_0_), channel_id=1, source_target_pairs={{0,4},{1,5},{4,0},{5,1},{8,12},{9,13},{12,8},{13,9},{2,6},{3,7},{6... | collective-permute-start | bytes 245768 | tf_op jit(solution)/shard_map/ppermute | solution.py:33
  36.2 3.1 %shard_map.109 = (bf16[512,2560]{1,0:T(8,128)(2,1)}, f32[8,128]{1,0:T(8,128)S(1)}) custom-call(bf16[512,1024]{1,0:T(8,128)(2,1)S(1)} %shard_map.106.refs_0_, bf16[2560,512]{1,0:T(8,128)(2,1)S(1)} %copy-done.1, bf16[2560,512]{1,0:T(8,128)(2,1)S(1)} %collective-permute-done.1.refs_1_.refs_2_, ...), custom_call_target="tpu_custom_call", output_to_operand_aliasing={{0}: (5, {})} | custom-call | flops 1711276032 | bytes 11931648 | tf_op jit(solution)/shard_map/pallas_call | solution.py:55
  39.4 1.4 %collective-permute-done.16.refs_1_ = bf16[32,2560]{1,0:T(8,128)(2,1)S(1)} collective-permute-done((bf16[32,2560]{1,0:T(8,128)(2,1)S(1)}, bf16[32,2560]{1,0:T(8,128)(2,1)S(1)}, u32[]{:S(2)}, u32[]{:S(2)}) %collective-permute-start.16) | collective-permute-done | bytes 163872 | tf_op jit(solution)/shard_map/ppermute | solution.py:26
  40.8 0.9 %shard_map.111 = f32[64,2560]{1,0:T(8,128)} custom-call(bf16[32,2560]{1,0:T(8,128)(2,1)S(1)} %shard_map.110.refs_0_.refs_2_, bf16[32,2560]{1,0:T(8,128)(2,1)S(1)} %collective-permute-done.16.refs_1_, bf16[32,2560]{1,0:T(8,128)(2,1)S(1)} %shard_map.110.refs_0_.refs_2_), custom_call_target="tpu_custom_call" | custom-call | bytes 983040 | tf_op jit(solution)/shard_map/pallas_call | solution.py:55
  (36 shorter events, 2.8 us)
Async XLA Ops:
  0.6 9.4 %copy-start = (bf16[512,2560]{1,0:T(8,128)(2,1)S(1)}, bf16[512,2560]{1,0:T(8,128)(2,1)}, u32[]{:S(2)}) copy-start(bf16[512,2560]{1,0:T(8,128)(2,1)} %refs_3_.3) | copy-start | bytes 7864324
  0.6 9.4 %copy-start.2 = (bf16[2560,64]{0,1:T(8,128)(2,1)S(1)}, bf16[2560,64]{0,1:T(8,128)(2,1)}, u32[]{:S(2)}) copy-start(bf16[2560,64]{0,1:T(8,128)(2,1)} %param.10) | copy-start | bytes 983044
  0.7 10.3 %collective-permute-start.1 = (bf16[2560,512]{1,0:T(8,128)(2,1)}, bf16[2560,512]{1,0:T(8,128)(2,1)S(1)}, u32[]{:S(2)}, u32[]{:S(2)}) collective-permute-start(bf16[2560,512]{1,0:T(8,128)(2,1)} %refs_1_.7), channel_id=1, source_target_pairs={{0,1},{1,0},{2,3},{3,2},{4,5},{5,4},{6,7},{7,6},{8,9},{9,8},{10,11... | collective-permute-start | bytes 7864328 | tf_op jit(solution)/shard_map/ppermute | solution.py:26
  2.7 8.8 %collective-permute-start.3 = (bf16[64,512]{1,0:T(8,128)(2,1)S(1)}, bf16[64,512]{1,0:T(8,128)(2,1)S(1)}, u32[]{:S(2)}, u32[]{:S(2)}) collective-permute-start(bf16[64,512]{1,0:T(8,128)(2,1)S(1)} %get-tuple-element.27), channel_id=1, source_target_pairs={{0,8},{1,9},{4,12},{5,13},{8,0},{9,1},{12,4},{13,5},{2,10},{3,11},... | collective-permute-start | bytes 196616 | tf_op jit(solution)/shard_map/ppermute | solution.py:33
  6.3 6.7 %collective-permute-start.4 = (bf16[64,512]{1,0:T(8,128)(2,1)S(1)}, bf16[64,512]{1,0:T(8,128)(2,1)S(1)}, u32[]{:S(2)}, u32[]{:S(2)}) collective-permute-start(bf16[64,512]{1,0:T(8,128)(2,1)S(1)} %get-tuple-element.28), channel_id=1, source_target_pairs={{0,12},{1,13},{4,8},{5,9},{8,4},{9,5},{12,0},{13,1},{2,14},{3,15},... | collective-permute-start | bytes 196616 | tf_op jit(solution)/shard_map/ppermute | solution.py:33
  7.6 5.6 %collective-permute-start.5 = (bf16[64,512]{1,0:T(8,128)(2,1)S(1)}, bf16[64,512]{1,0:T(8,128)(2,1)S(1)}, u32[]{:S(2)}, u32[]{:S(2)}) collective-permute-start(bf16[64,512]{1,0:T(8,128)(2,1)S(1)} %get-tuple-element.29), channel_id=1, source_target_pairs={{0,4},{1,5},{4,0},{5,1},{8,12},{9,13},{12,8},{13,9},{2,6},{3,7},{6... | collective-permute-start | bytes 196616 | tf_op jit(solution)/shard_map/ppermute | solution.py:33
  7.8 7.2 %collective-permute-start = (bf16[128,512]{1,0:T(8,128)(2,1)S(1)}, bf16[128,512]{1,0:T(8,128)(2,1)S(1)}, u32[]{:S(2)}, u32[]{:S(2)}) collective-permute-start(bf16[128,512]{1,0:T(8,128)(2,1)S(1)} %get-tuple-element.24), channel_id=1, source_target_pairs={{0,2},{2,0},{1,3},{3,1},{4,6},{6,4},{5,7},{7,5},{8,10},{10,8},{9,1... | collective-permute-start | bytes 393224 | tf_op jit(solution)/shard_map/ppermute | solution.py:26
  10.0 3.2 %copy-start.3 = (bf16[512,512]{1,0:T(8,128)(2,1)S(1)}, bf16[512,512]{1,0:T(8,128)(2,1)}, u32[]{:S(2)}) copy-start(bf16[512,512]{1,0:T(8,128)(2,1)} %refs_1_.5) | copy-start | bytes 1572868
  11.0 4.4 %collective-permute-start.2 = (bf16[64,512]{1,0:T(8,128)(2,1)S(1)}, bf16[64,512]{1,0:T(8,128)(2,1)S(1)}, u32[]{:S(2)}, u32[]{:S(2)}) collective-permute-start(bf16[64,512]{1,0:T(8,128)(2,1)S(1)} %shard_map.96), channel_id=1, source_target_pairs={{0,2},{2,0},{1,3},{3,1},{4,6},{6,4},{5,7},{7,5},{8,10},{10,8},{9,1... | collective-permute-start | bytes 196616 | tf_op jit(solution)/shard_map/ppermute | solution.py:26
  13.5 7.4 %collective-permute-start.10 = (f32[64,512]{1,0:T(8,128)S(1)}, f32[64,512]{1,0:T(8,128)S(1)}, u32[]{:S(2)}, u32[]{:S(2)}) collective-permute-start(f32[64,512]{1,0:T(8,128)S(1)} %shard_map.97.refs_4_.refs_1_), channel_id=1, source_target_pairs={{0,2},{2,0},{1,3},{3,1},{4,6},{6,4},{5,7},{7,5},{8,10},{10,8},{9,1... | collective-permute-start | bytes 393224 | tf_op jit(solution)/shard_map/ppermute | solution.py:26
  15.7 5.8 %collective-permute-start.8 = (bf16[1,64,512]{2,1,0:T(8,128)(2,1)S(1)}, bf16[1,64,512]{2,1,0:T(8,128)(2,1)S(1)}, u32[]{:S(2)}, u32[]{:S(2)}) collective-permute-start(bf16[1,64,512]{2,1,0:T(8,128)(2,1)S(1)} %get-tuple-element.31.refs_4_.refs_0_), channel_id=1, source_target_pairs={{0,8},{1,9},{4,12},{5,13},{8,0},{9,1},{12,4},{13,5},{2,10},{3,11},... | collective-permute-start | bytes 196616 | tf_op jit(solution)/shard_map/ppermute | solution.py:33
  18.5 4.3 %collective-permute-start.7 = (bf16[1,64,512]{2,1,0:T(8,128)(2,1)S(1)}, bf16[1,64,512]{2,1,0:T(8,128)(2,1)S(1)}, u32[]{:S(2)}, u32[]{:S(2)}) collective-permute-start(bf16[1,64,512]{2,1,0:T(8,128)(2,1)S(1)} %get-tuple-element.31.refs_4_.refs_0_), channel_id=1, source_target_pairs={{0,4},{1,5},{4,0},{5,1},{8,12},{9,13},{12,8},{13,9},{2,6},{3,7},{6... | collective-permute-start | bytes 196616 | tf_op jit(solution)/shard_map/ppermute | solution.py:33
  19.3 6.3 %collective-permute-start.9 = (bf16[1,64,512]{2,1,0:T(8,128)(2,1)S(1)}, bf16[1,64,512]{2,1,0:T(8,128)(2,1)S(1)}, u32[]{:S(2)}, u32[]{:S(2)}) collective-permute-start(bf16[1,64,512]{2,1,0:T(8,128)(2,1)S(1)} %get-tuple-element.31.refs_4_.refs_0_), channel_id=1, source_target_pairs={{0,12},{1,13},{4,8},{5,9},{8,4},{9,5},{12,0},{13,1},{2,14},{3,15},... | collective-permute-start | bytes 196616 | tf_op jit(solution)/shard_map/ppermute | solution.py:33
  20.1 11.5 %collective-permute-start.6 = (bf16[384,512]{1,0:T(8,128)(2,1)S(1)}, bf16[384,512]{1,0:T(8,128)(2,1)S(1)}, u32[]{:S(2)}, u32[]{:S(2)}) collective-permute-start(bf16[384,512]{1,0:T(8,128)(2,1)S(1)} %get-tuple-element.30), channel_id=1, source_target_pairs={{0,2},{2,0},{1,3},{3,1},{4,6},{6,4},{5,7},{7,5},{8,10},{10,8},{9,1... | collective-permute-start | bytes 1179656 | tf_op jit(solution)/shard_map/ppermute | solution.py:26
  21.4 1.7 %collective-permute-start.11 = (f32[32,2560]{1,0:T(8,128)S(1)}, f32[32,2560]{1,0:T(8,128)S(1)}, u32[]{:S(2)}, u32[]{:S(2)}) collective-permute-start(f32[32,2560]{1,0:T(8,128)S(1)} %get-tuple-element.33), channel_id=1, source_target_pairs={{0,1},{1,0},{2,3},{3,2},{4,5},{5,4},{6,7},{7,6},{8,9},{9,8},{10,11... | collective-permute-start | bytes 983048 | tf_op jit(solution)/shard_map/ppermute | solution.py:26
  23.2 4.6 %collective-permute-start.13 = (bf16[16,2560]{1,0:T(8,128)(2,1)S(1)}, bf16[16,2560]{1,0:T(8,128)(2,1)S(1)}, u32[]{:S(2)}, u32[]{:S(2)}) collective-permute-start(bf16[16,2560]{1,0:T(8,128)(2,1)S(1)} %get-tuple-element.34.refs_0_), channel_id=1, source_target_pairs={{0,4},{1,5},{4,0},{5,1},{8,12},{9,13},{12,8},{13,9},{2,6},{3,7},{6... | collective-permute-start | bytes 245768 | tf_op jit(solution)/shard_map/ppermute | solution.py:33
  25.7 4.2 %collective-permute-start.12 = (bf16[4,64,512]{2,1,0:T(8,128)(2,1)S(1)}, bf16[4,64,512]{2,1,0:T(8,128)(2,1)S(1)}, u32[]{:S(2)}, u32[]{:S(2)}) collective-permute-start(bf16[4,64,512]{2,1,0:T(8,128)(2,1)S(1)} %shard_map.103.refs_2_.refs_1_), channel_id=1, source_target_pairs={{0,1},{1,0},{2,3},{3,2},{4,5},{5,4},{6,7},{7,6},{8,9},{9,8},{10,11... | collective-permute-start | bytes 786440 | tf_op jit(solution)/shard_map/ppermute | solution.py:26
  27.8 4.0 %copy-start.1 = (bf16[2560,512]{1,0:T(8,128)(2,1)S(1)}, bf16[2560,512]{1,0:T(8,128)(2,1)}, u32[]{:S(2)}) copy-start(bf16[2560,512]{1,0:T(8,128)(2,1)} %refs_1_.7) | copy-start | bytes 7864324
  27.8 6.4 %collective-permute-start.14 = (bf16[16,2560]{1,0:T(8,128)(2,1)S(1)}, bf16[16,2560]{1,0:T(8,128)(2,1)S(1)}, u32[]{:S(2)}, u32[]{:S(2)}) collective-permute-start(bf16[16,2560]{1,0:T(8,128)(2,1)S(1)} %shard_map.104.refs_4_.refs_0_), channel_id=1, source_target_pairs={{0,8},{1,9},{4,12},{5,13},{8,0},{9,1},{12,4},{13,5},{2,10},{3,11},... | collective-permute-start | bytes 245768 | tf_op jit(solution)/shard_map/ppermute | solution.py:33
  34.2 5.1 %collective-permute-start.15 = (bf16[16,2560]{1,0:T(8,128)(2,1)S(1)}, bf16[16,2560]{1,0:T(8,128)(2,1)S(1)}, u32[]{:S(2)}, u32[]{:S(2)}) collective-permute-start(bf16[16,2560]{1,0:T(8,128)(2,1)S(1)} %shard_map.108.refs_6_.refs_0_), channel_id=1, source_target_pairs={{0,4},{1,5},{4,0},{5,1},{8,12},{9,13},{12,8},{13,9},{2,6},{3,7},{6... | collective-permute-start | bytes 245768 | tf_op jit(solution)/shard_map/ppermute | solution.py:33
  39.4 1.5 %collective-permute-start.16 = (bf16[32,2560]{1,0:T(8,128)(2,1)S(1)}, bf16[32,2560]{1,0:T(8,128)(2,1)S(1)}, u32[]{:S(2)}, u32[]{:S(2)}) collective-permute-start(bf16[32,2560]{1,0:T(8,128)(2,1)S(1)} %shard_map.110.refs_0_.refs_2_), channel_id=1, source_target_pairs={{0,1},{1,0},{2,3},{3,2},{4,5},{5,4},{6,7},{7,6},{8,9},{9,8},{10,11... | collective-permute-start | bytes 491528 | tf_op jit(solution)/shard_map/ppermute | solution.py:26

commit v14 on v13

--- a/solution.py
+++ b/solution.py
@@ -209,6 +209,13 @@
         scratch_shapes=[pltpu.VMEM((rank, features), f32)],
         flops=2 * rows * rank * features,
     )
+
+
+def marked(after, flops):
+    def body(out):
+        out[...] = jnp.zeros(out.shape, f32)
+
+    return call(body, [], [], [shape_of((8, 128), f32)], after=after, flops=flops)[0]
 
 
 def add_up(pieces, after=(), flops=0):
@@ -482,10 +489,10 @@
 
     near, late = head_term(lengths, lows, grad_output, scale, [part, *early_grads])
     late_grads = [shift(late, "tp", step) for step in tp_steps]
-    terms = [near] + [swap(near, step, 0) for step in own_steps]
+    terms = [near] + [swap(near, step, 0) for step in steps[::-1]]
     back, keep, send = shared_terms(lengths, parts, tokens, scale, [near])
     pieces = [keep, shift(send, "sub", 1)]
-    met = stack(terms[1:3], flops=middling) if own_count > 1 else near
+    met = marked([back], flops=middling)
 
     bits = [1 << i for i in range(own_count.bit_length() - 1)]
     mark = met
@@ -498,7 +505,7 @@
     far = shift(near, "sub", 1)
     total = add_up(pieces, [near], flops=busy)
     grad_heads, mark = place_terms(
-        adapter_ids, near, far, range(own_count), cleaned, [total]
+        adapter_ids, near, far, [0] + steps[::-1], cleaned, [total]
     )
     kept = arrange(lengths, grad_output, list(zip(early_grads, late_grads)), [mark])
     sides = (frozen_value, frozen_other, back, down)

time: 41.9 us -> 41.7 us (level)
    ppermute x8, waiting for transfers between devices: 2.04 us -> 3.29 us  [shift(): lax.ppermute(x, axis, [(i, (i + step) % count) for i in range(count)])]
    ppermute x9, waiting for transfers between devices: 4.87 us -> 3.73 us  [swap(): lax.ppermute(x, ('own', 'sub'), [(i, i ^ other) for i in range(whole)])]
where the time goes in v14:
time: 41.7 us; the launch traced here: 41.4 us
  starting transfers between devices  19.7 us (47%)
  Pallas kernels  13.2 us (32%)
  waiting for transfers between devices  7.02 us (17%)
  between operations  1.53 us (4%)
    ppermute x9, starting transfers between devices, swap(): lax.ppermute(x, ('own', 'sub'), [(i, i ^ other) for i in range(whole)])  14.8 us
    pallas_call x18, Pallas kernels, call(): pl.pallas_call(kernel, out_shape=outs, in_specs=list(specs) + [anywhere]...  13.2 us
    ppermute x8, starting transfers between devices, shift(): lax.ppermute(x, axis, [(i, (i + step) % count) for i in range(count)])  4.81 us
    ppermute x9, waiting for transfers between devices, swap(): lax.ppermute(x, ('own', 'sub'), [(i, i ^ other) for i in range(whole)])  3.73 us
    ppermute x8, waiting for transfers between devices, shift(): lax.ppermute(x, axis, [(i, (i + step) % count) for i in range(count)])  3.29 us
  transfers between devices with their start and end apart: 17, of which 7 were waited for; matrix products, arithmetic and copies ran while one was open for 0% of the time, Pallas kernels for 30%

profile of v14, /device:TPU:0, one launch (start us, length us, event | category | flops | bytes accessed | tf_op | source)
XLA Modules:
  0.0 41.4 jit_solution(15384242909585559751)
XLA Ops:
  0.7 0.5 %collective-permute-start.1 = (bf16[2560,512]{1,0:T(8,128)(2,1)}, bf16[2560,512]{1,0:T(8,128)(2,1)S(1)}, u32[]{:S(2)}, u32[]{:S(2)}) collective-permute-start(bf16[2560,512]{1,0:T(8,128)(2,1)} %refs_1_.7), channel_id=1, source_target_pairs={{0,1},{1,0},{2,3},{3,2},{4,5},{5,4},{6,7},{7,6},{8,9},{9,8},{10,11... | collective-permute-start | bytes 7864328 | tf_op jit(solution)/shard_map/ppermute | solution.py:26
  1.2 1.5 %shard_map.94 = (bf16[64,512]{1,0:T(8,128)(2,1)S(1)}, bf16[64,512]{1,0:T(8,128)(2,1)S(1)}, bf16[64,512]{1,0:T(8,128)(2,1)S(1)}, bf16[64,512]{1,0:T(8,128)(2,1)S(...) custom-call(s32[8]{0:T(128)} %refs_0_.8, bf16[16,64,512]{2,1,0:T(8,128)(2,1)} %refs_1_.4, bf16[512,512]{1,0:T(8,128)(2,1)} %refs_1_.5), custom_call_target="tpu_custom_call" | custom-call | flops 5000000000 | bytes 1970208 | tf_op jit(solution)/shard_map/pallas_call | solution.py:55
  2.7 3.6 %collective-permute-start.3 = (bf16[64,512]{1,0:T(8,128)(2,1)S(1)}, bf16[64,512]{1,0:T(8,128)(2,1)S(1)}, u32[]{:S(2)}, u32[]{:S(2)}) collective-permute-start(bf16[64,512]{1,0:T(8,128)(2,1)S(1)} %get-tuple-element.27), channel_id=1, source_target_pairs={{0,8},{1,9},{4,12},{5,13},{8,0},{9,1},{12,4},{13,5},{2,10},{3,11},... | collective-permute-start | bytes 196616 | tf_op jit(solution)/shard_map/ppermute | solution.py:33
  6.3 1.3 %collective-permute-start.4 = (bf16[64,512]{1,0:T(8,128)(2,1)S(1)}, bf16[64,512]{1,0:T(8,128)(2,1)S(1)}, u32[]{:S(2)}, u32[]{:S(2)}) collective-permute-start(bf16[64,512]{1,0:T(8,128)(2,1)S(1)} %get-tuple-element.28), channel_id=1, source_target_pairs={{0,12},{1,13},{4,8},{5,9},{8,4},{9,5},{12,0},{13,1},{2,14},{3,15},... | collective-permute-start | bytes 196616 | tf_op jit(solution)/shard_map/ppermute | solution.py:33
  7.8 1.5 %collective-permute-start = (bf16[128,512]{1,0:T(8,128)(2,1)S(1)}, bf16[128,512]{1,0:T(8,128)(2,1)S(1)}, u32[]{:S(2)}, u32[]{:S(2)}) collective-permute-start(bf16[128,512]{1,0:T(8,128)(2,1)S(1)} %get-tuple-element.24), channel_id=1, source_target_pairs={{0,2},{2,0},{1,3},{3,1},{4,6},{6,4},{5,7},{7,5},{8,10},{10,8},{9,1... | collective-permute-start | bytes 393224 | tf_op jit(solution)/shard_map/ppermute | solution.py:26
  10.0 0.9 %shard_map.95.refs_0_.refs_6_.refs_1_ = f32[64,512]{1,0:T(8,128)S(1)} custom-call(bf16[512,2560]{1,0:T(8,128)(2,1)S(1)} %copy-done, bf16[64,2560]{1,0:T(8,128)(2,1)S(1)} %bitcast.2, bf16[64,512]{1,0:T(8,128)(2,1)S(1)} %get-tuple-element.25.refs_2_.refs_1_), custom_call_target="tpu_custom_call" | custom-call | flops 167772160 | bytes 3080192 | tf_op jit(solution)/shard_map/pallas_call | solution.py:55
  11.0 0.6 %collective-permute-start.2 = (bf16[64,512]{1,0:T(8,128)(2,1)S(1)}, bf16[64,512]{1,0:T(8,128)(2,1)S(1)}, u32[]{:S(2)}, u32[]{:S(2)}) collective-permute-start(bf16[64,512]{1,0:T(8,128)(2,1)S(1)} %shard_map.96), channel_id=1, source_target_pairs={{0,2},{2,0},{1,3},{3,1},{4,6},{6,4},{5,7},{7,5},{8,10},{10,8},{9,1... | collective-permute-start | bytes 196616 | tf_op jit(solution)/shard_map/ppermute | solution.py:26
  11.6 1.4 %collective-permute-done.4.refs_3_ = bf16[64,512]{1,0:T(8,128)(2,1)S(1)} collective-permute-done((bf16[64,512]{1,0:T(8,128)(2,1)S(1)}, bf16[64,512]{1,0:T(8,128)(2,1)S(1)}, u32[]{:S(2)}, u32[]{:S(2)}) %collective-permute-start.4) | collective-permute-done | bytes 65568 | tf_op jit(solution)/shard_map/ppermute | solution.py:33
  13.5 1.6 %collective-permute-start.10 = (f32[64,512]{1,0:T(8,128)S(1)}, f32[64,512]{1,0:T(8,128)S(1)}, u32[]{:S(2)}, u32[]{:S(2)}) collective-permute-start(f32[64,512]{1,0:T(8,128)S(1)} %shard_map.97.refs_4_.refs_1_), channel_id=1, source_target_pairs={{0,2},{2,0},{1,3},{3,1},{4,6},{6,4},{5,7},{7,5},{8,10},{10,8},{9,1... | collective-permute-start | bytes 393224 | tf_op jit(solution)/shard_map/ppermute | solution.py:26
  15.7 2.8 %collective-permute-start.9 = (bf16[1,64,512]{2,1,0:T(8,128)(2,1)S(1)}, bf16[1,64,512]{2,1,0:T(8,128)(2,1)S(1)}, u32[]{:S(2)}, u32[]{:S(2)}) collective-permute-start(bf16[1,64,512]{2,1,0:T(8,128)(2,1)S(1)} %get-tuple-element.31.refs_4_.refs_0_), channel_id=1, source_target_pairs={{0,8},{1,9},{4,12},{5,13},{8,0},{9,1},{12,4},{13,5},{2,10},{3,11},... | collective-permute-start | bytes 196616 | tf_op jit(solution)/shard_map/ppermute | solution.py:33
  18.5 1.5 %collective-permute-start.8 = (bf16[1,64,512]{2,1,0:T(8,128)(2,1)S(1)}, bf16[1,64,512]{2,1,0:T(8,128)(2,1)S(1)}, u32[]{:S(2)}, u32[]{:S(2)}) collective-permute-start(bf16[1,64,512]{2,1,0:T(8,128)(2,1)S(1)} %get-tuple-element.31.refs_4_.refs_0_), channel_id=1, source_target_pairs={{0,12},{1,13},{4,8},{5,9},{8,4},{9,5},{12,0},{13,1},{2,14},{3,15},... | collective-permute-start | bytes 196616 | tf_op jit(solution)/shard_map/ppermute | solution.py:33
  20.4 0.6 %shard_map.99 = (bf16[64,512]{1,0:T(8,128)(2,1)S(1)}, f32[32,2560]{1,0:T(8,128)S(1)}, f32[32,2560]{1,0:T(8,128)S(1)}) custom-call(s32[1]{0:T(128)S(6)} %copy.14.refs_0_, f32[64,512]{1,0:T(8,128)S(1)} %shard_map.97.refs_4_.refs_1_, f32[64,512]{1,0:T(8,128)S(1)} %collective-permute-done.10.refs_2_, bf16[512,2560]{1,0:T(8,128)(2,1)S(1)} %copy-done, ...), custom_call_target="tpu_custom_call" | custom-call | flops 167772160 | bytes 3604484 | tf_op jit(solution)/shard_map/pallas_call | solution.py:55
  21.0 1.6 %collective-permute-done.11.refs_1_ = f32[32,2560]{1,0:T(8,128)S(1)} collective-permute-done((f32[32,2560]{1,0:T(8,128)S(1)}, f32[32,2560]{1,0:T(8,128)S(1)}, u32[]{:S(2)}, u32[]{:S(2)}) %collective-permute-start.11) | collective-permute-done | bytes 327712 | tf_op jit(solution)/shard_map/ppermute | solution.py:26
  22.7 2.1 %collective-permute-start.13 = (bf16[16,2560]{1,0:T(8,128)(2,1)S(1)}, bf16[16,2560]{1,0:T(8,128)(2,1)S(1)}, u32[]{:S(2)}, u32[]{:S(2)}) collective-permute-start(bf16[16,2560]{1,0:T(8,128)(2,1)S(1)} %get-tuple-element.35.refs_0_), channel_id=1, source_target_pairs={{0,4},{1,5},{4,0},{5,1},{8,12},{9,13},{12,8},{13,9},{2,6},{3,7},{6... | collective-permute-start | bytes 245768 | tf_op jit(solution)/shard_map/ppermute | solution.py:33
  24.8 1.4 %shard_map.102 = (f32[16,64,512]{2,1,0:T(8,128)}, f32[8,128]{1,0:T(8,128)S(1)}) custom-call(bf16[16,2560]{1,0:T(8,128)(2,1)S(1)} %get-tuple-element.35.refs_0_), custom_call_target="tpu_custom_call" | custom-call | flops 10000000000 | bytes 2101248 | tf_op jit(solution)/shard_map/pallas_call | solution.py:55
  26.4 1.2 %collective-permute-done.13.refs_1_ = bf16[16,2560]{1,0:T(8,128)(2,1)S(1)} collective-permute-done((bf16[16,2560]{1,0:T(8,128)(2,1)S(1)}, bf16[16,2560]{1,0:T(8,128)(2,1)S(1)}, u32[]{:S(2)}, u32[]{:S(2)}) %collective-permute-start.13) | collective-permute-done | bytes 81952 | tf_op jit(solution)/shard_map/ppermute | solution.py:33
  27.6 2.8 %collective-permute-start.14 = (bf16[16,2560]{1,0:T(8,128)(2,1)S(1)}, bf16[16,2560]{1,0:T(8,128)(2,1)S(1)}, u32[]{:S(2)}, u32[]{:S(2)}) collective-permute-start(bf16[16,2560]{1,0:T(8,128)(2,1)S(1)} %shard_map.104.refs_4_.refs_0_), channel_id=1, source_target_pairs={{0,8},{1,9},{4,12},{5,13},{8,0},{9,1},{12,4},{13,5},{2,10},{3,11},... | collective-permute-start | bytes 245768 | tf_op jit(solution)/shard_map/ppermute | solution.py:33
  30.4 1.6 %shard_map.105 = (f32[16,64,512]{2,1,0:T(8,128)}, f32[8,128]{1,0:T(8,128)S(1)}) custom-call(s32[8]{0:T(128)} %refs_0_.8, bf16[4,64,512]{2,1,0:T(8,128)(2,1)S(1)} %shard_map.103.refs_2_.refs_1_, bf16[4,64,512]{2,1,0:T(8,128)(2,1)S(1)} %collective-permute-done.12.refs_2_, f32[16,64,512]{2,1,0:T(8,128)} %get-tuple-element.37.refs_3_, ...), custom_call_target="tpu_custom_call", output_to_operand_aliasing={{0}: (3, {})} | custom-call | bytes 4722720 | tf_op jit(solution)/shard_map/pallas_call | solution.py:55
  32.1 2.4 %shard_map.107 = (bf16[512,2560]{1,0:T(8,128)(2,1)}, f32[8,128]{1,0:T(8,128)S(1)}) custom-call(bf16[512,1024]{1,0:T(8,128)(2,1)S(1)} %shard_map.106.refs_0_, bf16[2560,512]{1,0:T(8,128)(2,1)S(1)} %copy-done.1, bf16[2560,512]{1,0:T(8,128)(2,1)S(1)} %collective-permute-done.1.refs_1_.refs_2_, bf16[64,512]{1,0:T(8,128)(2,1)S(1)} %get-tuple-element.34.refs_0_.refs_3_, ...), custom_call_target="tpu_custom_call" | custom-call | flops 1140850688 | bytes 9310208 | tf_op jit(solution)/shard_map/pallas_call | solution.py:55
  34.5 0.5 %collective-permute-start.15 = (bf16[16,2560]{1,0:T(8,128)(2,1)S(1)}, bf16[16,2560]{1,0:T(8,128)(2,1)S(1)}, u32[]{:S(2)}, u32[]{:S(2)}) collective-permute-start(bf16[16,2560]{1,0:T(8,128)(2,1)S(1)} %shard_map.108.refs_6_.refs_0_), channel_id=1, source_target_pairs={{0,4},{1,5},{4,0},{5,1},{8,12},{9,13},{12,8},{13,9},{2,6},{3,7},{6... | collective-permute-start | bytes 245768 | tf_op jit(solution)/shard_map/ppermute | solution.py:33
  35.0 3.0 %shard_map.109 = (bf16[512,2560]{1,0:T(8,128)(2,1)}, f32[8,128]{1,0:T(8,128)S(1)}) custom-call(bf16[512,1024]{1,0:T(8,128)(2,1)S(1)} %shard_map.106.refs_0_, bf16[2560,512]{1,0:T(8,128)(2,1)S(1)} %copy-done.1, bf16[2560,512]{1,0:T(8,128)(2,1)S(1)} %collective-permute-done.1.refs_1_.refs_2_, ...), custom_call_target="tpu_custom_call", output_to_operand_aliasing={{0}: (5, {})} | custom-call | flops 1711276032 | bytes 11931648 | tf_op jit(solution)/shard_map/pallas_call | solution.py:55
  38.1 0.9 %collective-permute-done.15.refs_1_ = bf16[16,2560]{1,0:T(8,128)(2,1)S(1)} collective-permute-done((bf16[16,2560]{1,0:T(8,128)(2,1)S(1)}, bf16[16,2560]{1,0:T(8,128)(2,1)S(1)}, u32[]{:S(2)}, u32[]{:S(2)}) %collective-permute-start.15) | collective-permute-done | bytes 81952 | tf_op jit(solution)/shard_map/ppermute | solution.py:33
  39.2 1.4 %collective-permute-done.16.refs_1_ = bf16[32,2560]{1,0:T(8,128)(2,1)S(1)} collective-permute-done((bf16[32,2560]{1,0:T(8,128)(2,1)S(1)}, bf16[32,2560]{1,0:T(8,128)(2,1)S(1)}, u32[]{:S(2)}, u32[]{:S(2)}) %collective-permute-start.16) | collective-permute-done | bytes 163872 | tf_op jit(solution)/shard_map/ppermute | solution.py:26
  40.6 0.9 %shard_map.111 = f32[64,2560]{1,0:T(8,128)} custom-call(bf16[32,2560]{1,0:T(8,128)(2,1)S(1)} %shard_map.110.refs_0_.refs_2_, bf16[32,2560]{1,0:T(8,128)(2,1)S(1)} %collective-permute-done.16.refs_1_, bf16[32,2560]{1,0:T(8,128)(2,1)S(1)} %shard_map.110.refs_0_.refs_2_), custom_call_target="tpu_custom_call" | custom-call | bytes 983040 | tf_op jit(solution)/shard_map/pallas_call | solution.py:55
  (36 shorter events, 2.3 us)
Async XLA Ops:
  0.6 9.4 %copy-start = (bf16[512,2560]{1,0:T(8,128)(2,1)S(1)}, bf16[512,2560]{1,0:T(8,128)(2,1)}, u32[]{:S(2)}) copy-start(bf16[512,2560]{1,0:T(8,128)(2,1)} %refs_3_.3) | copy-start | bytes 7864324
  0.6 9.4 %copy-start.2 = (bf16[2560,64]{0,1:T(8,128)(2,1)S(1)}, bf16[2560,64]{0,1:T(8,128)(2,1)}, u32[]{:S(2)}) copy-start(bf16[2560,64]{0,1:T(8,128)(2,1)} %param.10) | copy-start | bytes 983044
  0.7 10.3 %collective-permute-start.1 = (bf16[2560,512]{1,0:T(8,128)(2,1)}, bf16[2560,512]{1,0:T(8,128)(2,1)S(1)}, u32[]{:S(2)}, u32[]{:S(2)}) collective-permute-start(bf16[2560,512]{1,0:T(8,128)(2,1)} %refs_1_.7), channel_id=1, source_target_pairs={{0,1},{1,0},{2,3},{3,2},{4,5},{5,4},{6,7},{7,6},{8,9},{9,8},{10,11... | collective-permute-start | bytes 7864328 | tf_op jit(solution)/shard_map/ppermute | solution.py:26
  2.7 8.8 %collective-permute-start.3 = (bf16[64,512]{1,0:T(8,128)(2,1)S(1)}, bf16[64,512]{1,0:T(8,128)(2,1)S(1)}, u32[]{:S(2)}, u32[]{:S(2)}) collective-permute-start(bf16[64,512]{1,0:T(8,128)(2,1)S(1)} %get-tuple-element.27), channel_id=1, source_target_pairs={{0,8},{1,9},{4,12},{5,13},{8,0},{9,1},{12,4},{13,5},{2,10},{3,11},... | collective-permute-start | bytes 196616 | tf_op jit(solution)/shard_map/ppermute | solution.py:33
  6.3 6.7 %collective-permute-start.4 = (bf16[64,512]{1,0:T(8,128)(2,1)S(1)}, bf16[64,512]{1,0:T(8,128)(2,1)S(1)}, u32[]{:S(2)}, u32[]{:S(2)}) collective-permute-start(bf16[64,512]{1,0:T(8,128)(2,1)S(1)} %get-tuple-element.28), channel_id=1, source_target_pairs={{0,12},{1,13},{4,8},{5,9},{8,4},{9,5},{12,0},{13,1},{2,14},{3,15},... | collective-permute-start | bytes 196616 | tf_op jit(solution)/shard_map/ppermute | solution.py:33
  7.6 5.6 %collective-permute-start.5 = (bf16[64,512]{1,0:T(8,128)(2,1)S(1)}, bf16[64,512]{1,0:T(8,128)(2,1)S(1)}, u32[]{:S(2)}, u32[]{:S(2)}) collective-permute-start(bf16[64,512]{1,0:T(8,128)(2,1)S(1)} %get-tuple-element.29), channel_id=1, source_target_pairs={{0,4},{1,5},{4,0},{5,1},{8,12},{9,13},{12,8},{13,9},{2,6},{3,7},{6... | collective-permute-start | bytes 196616 | tf_op jit(solution)/shard_map/ppermute | solution.py:33
  7.8 7.2 %collective-permute-start = (bf16[128,512]{1,0:T(8,128)(2,1)S(1)}, bf16[128,512]{1,0:T(8,128)(2,1)S(1)}, u32[]{:S(2)}, u32[]{:S(2)}) collective-permute-start(bf16[128,512]{1,0:T(8,128)(2,1)S(1)} %get-tuple-element.24), channel_id=1, source_target_pairs={{0,2},{2,0},{1,3},{3,1},{4,6},{6,4},{5,7},{7,5},{8,10},{10,8},{9,1... | collective-permute-start | bytes 393224 | tf_op jit(solution)/shard_map/ppermute | solution.py:26
  10.0 3.2 %copy-start.3 = (bf16[512,512]{1,0:T(8,128)(2,1)S(1)}, bf16[512,512]{1,0:T(8,128)(2,1)}, u32[]{:S(2)}) copy-start(bf16[512,512]{1,0:T(8,128)(2,1)} %refs_1_.5) | copy-start | bytes 1572868
  11.0 4.4 %collective-permute-start.2 = (bf16[64,512]{1,0:T(8,128)(2,1)S(1)}, bf16[64,512]{1,0:T(8,128)(2,1)S(1)}, u32[]{:S(2)}, u32[]{:S(2)}) collective-permute-start(bf16[64,512]{1,0:T(8,128)(2,1)S(1)} %shard_map.96), channel_id=1, source_target_pairs={{0,2},{2,0},{1,3},{3,1},{4,6},{6,4},{5,7},{7,5},{8,10},{10,8},{9,1... | collective-permute-start | bytes 196616 | tf_op jit(solution)/shard_map/ppermute | solution.py:26
  13.5 6.9 %collective-permute-start.10 = (f32[64,512]{1,0:T(8,128)S(1)}, f32[64,512]{1,0:T(8,128)S(1)}, u32[]{:S(2)}, u32[]{:S(2)}) collective-permute-start(f32[64,512]{1,0:T(8,128)S(1)} %shard_map.97.refs_4_.refs_1_), channel_id=1, source_target_pairs={{0,2},{2,0},{1,3},{3,1},{4,6},{6,4},{5,7},{7,5},{8,10},{10,8},{9,1... | collective-permute-start | bytes 393224 | tf_op jit(solution)/shard_map/ppermute | solution.py:26
  15.7 10.6 %collective-permute-start.9 = (bf16[1,64,512]{2,1,0:T(8,128)(2,1)S(1)}, bf16[1,64,512]{2,1,0:T(8,128)(2,1)S(1)}, u32[]{:S(2)}, u32[]{:S(2)}) collective-permute-start(bf16[1,64,512]{2,1,0:T(8,128)(2,1)S(1)} %get-tuple-element.31.refs_4_.refs_0_), channel_id=1, source_target_pairs={{0,8},{1,9},{4,12},{5,13},{8,0},{9,1},{12,4},{13,5},{2,10},{3,11},... | collective-permute-start | bytes 196616 | tf_op jit(solution)/shard_map/ppermute | solution.py:33
  18.5 7.8 %collective-permute-start.8 = (bf16[1,64,512]{2,1,0:T(8,128)(2,1)S(1)}, bf16[1,64,512]{2,1,0:T(8,128)(2,1)S(1)}, u32[]{:S(2)}, u32[]{:S(2)}) collective-permute-start(bf16[1,64,512]{2,1,0:T(8,128)(2,1)S(1)} %get-tuple-element.31.refs_4_.refs_0_), channel_id=1, source_target_pairs={{0,12},{1,13},{4,8},{5,9},{8,4},{9,5},{12,0},{13,1},{2,14},{3,15},... | collective-permute-start | bytes 196616 | tf_op jit(solution)/shard_map/ppermute | solution.py:33
  20.0 6.3 %collective-permute-start.7 = (bf16[1,64,512]{2,1,0:T(8,128)(2,1)S(1)}, bf16[1,64,512]{2,1,0:T(8,128)(2,1)S(1)}, u32[]{:S(2)}, u32[]{:S(2)}) collective-permute-start(bf16[1,64,512]{2,1,0:T(8,128)(2,1)S(1)} %get-tuple-element.31.refs_4_.refs_0_), channel_id=1, source_target_pairs={{0,4},{1,5},{4,0},{5,1},{8,12},{9,13},{12,8},{13,9},{2,6},{3,7},{6... | collective-permute-start | bytes 196616 | tf_op jit(solution)/shard_map/ppermute | solution.py:33
  20.0 12.0 %collective-permute-start.6 = (bf16[384,512]{1,0:T(8,128)(2,1)S(1)}, bf16[384,512]{1,0:T(8,128)(2,1)S(1)}, u32[]{:S(2)}, u32[]{:S(2)}) collective-permute-start(bf16[384,512]{1,0:T(8,128)(2,1)S(1)} %get-tuple-element.30), channel_id=1, source_target_pairs={{0,2},{2,0},{1,3},{3,1},{4,6},{6,4},{5,7},{7,5},{8,10},{10,8},{9,1... | collective-permute-start | bytes 1179656 | tf_op jit(solution)/shard_map/ppermute | solution.py:26
  21.0 1.7 %collective-permute-start.11 = (f32[32,2560]{1,0:T(8,128)S(1)}, f32[32,2560]{1,0:T(8,128)S(1)}, u32[]{:S(2)}, u32[]{:S(2)}) collective-permute-start(f32[32,2560]{1,0:T(8,128)S(1)} %get-tuple-element.33), channel_id=1, source_target_pairs={{0,1},{1,0},{2,3},{3,2},{4,5},{5,4},{6,7},{7,6},{8,9},{9,8},{10,11... | collective-permute-start | bytes 983048 | tf_op jit(solution)/shard_map/ppermute | solution.py:26
  22.7 4.8 %collective-permute-start.13 = (bf16[16,2560]{1,0:T(8,128)(2,1)S(1)}, bf16[16,2560]{1,0:T(8,128)(2,1)S(1)}, u32[]{:S(2)}, u32[]{:S(2)}) collective-permute-start(bf16[16,2560]{1,0:T(8,128)(2,1)S(1)} %get-tuple-element.35.refs_0_), channel_id=1, source_target_pairs={{0,4},{1,5},{4,0},{5,1},{8,12},{9,13},{12,8},{13,9},{2,6},{3,7},{6... | collective-permute-start | bytes 245768 | tf_op jit(solution)/shard_map/ppermute | solution.py:33
  26.3 4.1 %collective-permute-start.12 = (bf16[4,64,512]{2,1,0:T(8,128)(2,1)S(1)}, bf16[4,64,512]{2,1,0:T(8,128)(2,1)S(1)}, u32[]{:S(2)}, u32[]{:S(2)}) collective-permute-start(bf16[4,64,512]{2,1,0:T(8,128)(2,1)S(1)} %shard_map.103.refs_2_.refs_1_), channel_id=1, source_target_pairs={{0,1},{1,0},{2,3},{3,2},{4,5},{5,4},{6,7},{7,6},{8,9},{9,8},{10,11... | collective-permute-start | bytes 786440 | tf_op jit(solution)/shard_map/ppermute | solution.py:26
  27.6 4.5 %copy-start.1 = (bf16[2560,512]{1,0:T(8,128)(2,1)S(1)}, bf16[2560,512]{1,0:T(8,128)(2,1)}, u32[]{:S(2)}) copy-start(bf16[2560,512]{1,0:T(8,128)(2,1)} %refs_1_.7) | copy-start | bytes 7864324
  27.6 6.9 %collective-permute-start.14 = (bf16[16,2560]{1,0:T(8,128)(2,1)S(1)}, bf16[16,2560]{1,0:T(8,128)(2,1)S(1)}, u32[]{:S(2)}, u32[]{:S(2)}) collective-permute-start(bf16[16,2560]{1,0:T(8,128)(2,1)S(1)} %shard_map.104.refs_4_.refs_0_), channel_id=1, source_target_pairs={{0,8},{1,9},{4,12},{5,13},{8,0},{9,1},{12,4},{13,5},{2,10},{3,11},... | collective-permute-start | bytes 245768 | tf_op jit(solution)/shard_map/ppermute | solution.py:33
  34.5 4.5 %collective-permute-start.15 = (bf16[16,2560]{1,0:T(8,128)(2,1)S(1)}, bf16[16,2560]{1,0:T(8,128)(2,1)S(1)}, u32[]{:S(2)}, u32[]{:S(2)}) collective-permute-start(bf16[16,2560]{1,0:T(8,128)(2,1)S(1)} %shard_map.108.refs_6_.refs_0_), channel_id=1, source_target_pairs={{0,4},{1,5},{4,0},{5,1},{8,12},{9,13},{12,8},{13,9},{2,6},{3,7},{6... | collective-permute-start | bytes 245768 | tf_op jit(solution)/shard_map/ppermute | solution.py:33
  39.1 1.5 %collective-permute-start.16 = (bf16[32,2560]{1,0:T(8,128)(2,1)S(1)}, bf16[32,2560]{1,0:T(8,128)(2,1)S(1)}, u32[]{:S(2)}, u32[]{:S(2)}) collective-permute-start(bf16[32,2560]{1,0:T(8,128)(2,1)S(1)} %shard_map.110.refs_0_.refs_2_), channel_id=1, source_target_pairs={{0,1},{1,0},{2,3},{3,2},{4,5},{5,4},{6,7},{7,6},{8,9},{9,8},{10,11... | collective-permute-start | bytes 491528 | tf_op jit(solution)/shard_map/ppermute | solution.py:26

commit v15 on v13

--- a/solution.py
+++ b/solution.py
@@ -482,13 +482,13 @@
 
     near, late = head_term(lengths, lows, grad_output, scale, [part, *early_grads])
     late_grads = [shift(late, "tp", step) for step in tp_steps]
-    terms = [near] + [swap(near, step, 0) for step in own_steps]
     back, keep, send = shared_terms(lengths, parts, tokens, scale, [near])
     pieces = [keep, shift(send, "sub", 1)]
-    met = stack(terms[1:3], flops=middling) if own_count > 1 else near
+    met = stack([near], [back], flops=middling)
+    terms = [near] + [swap(met if step == 1 else near, step, 0) for step in steps[::-1]]
 
     bits = [1 << i for i in range(own_count.bit_length() - 1)]
-    mark = met
+    mark = back
     for bit in bits[:-1]:
         stays, leaves = halve(pieces, bit, [mark])
         pieces = [stays, swap(leaves, bit, 0)]
@@ -498,7 +498,7 @@
     far = shift(near, "sub", 1)
     total = add_up(pieces, [near], flops=busy)
     grad_heads, mark = place_terms(
-        adapter_ids, near, far, range(own_count), cleaned, [total]
+        adapter_ids, near, far, [0] + steps[::-1], cleaned, [total]
     )
     kept = arrange(lengths, grad_output, list(zip(early_grads, late_grads)), [mark])
     sides = (frozen_value, frozen_other, back, down)

time: 41.9 us -> 40.7 us (0.971)
  starting transfers between devices: 20 us -> 17 us
  waiting for transfers between devices: 6.91 us -> 8.74 us
    ppermute x9, starting transfers between devices: 14.8 us -> 12.2 us  [swap(): lax.ppermute(x, ('own', 'sub'), [(i, i ^ other) for i in range(whole)])]
    ppermute x8, waiting for transfers between devices: 2.04 us -> 3.2 us  [shift(): lax.ppermute(x, axis, [(i, (i + step) % count) for i in range(count)])]
    ppermute x9, waiting for transfers between devices: 4.87 us -> 5.54 us  [swap(): lax.ppermute(x, ('own', 'sub'), [(i, i ^ other) for i in range(whole)])]
  transfers between devices with their start and end apart: 17 -> 17, of which waited for: 7 -> 9; matrix products, arithmetic and copies ran while one was open for 0% -> 0% of each run, Pallas kernels for 30% -> 30%
where the time goes in v15:
time: 40.7 us; the launch traced here: 40.6 us
  starting transfers between devices  17 us (42%)
  Pallas kernels  13.3 us (33%)
  waiting for transfers between devices  8.74 us (21%)
  between operations  1.51 us (4%)
    pallas_call x18, Pallas kernels, call(): pl.pallas_call(kernel, out_shape=outs, in_specs=list(specs) + [anywhere]...  13.3 us
    ppermute x9, starting transfers between devices, swap(): lax.ppermute(x, ('own', 'sub'), [(i, i ^ other) for i in range(whole)])  12.2 us
    ppermute x9, waiting for transfers between devices, swap(): lax.ppermute(x, ('own', 'sub'), [(i, i ^ other) for i in range(whole)])  5.54 us
    ppermute x8, starting transfers between devices, shift(): lax.ppermute(x, axis, [(i, (i + step) % count) for i in range(count)])  4.81 us
    ppermute x8, waiting for transfers between devices, shift(): lax.ppermute(x, axis, [(i, (i + step) % count) for i in range(count)])  3.2 us
  transfers between devices with their start and end apart: 17, of which 9 were waited for; matrix products, arithmetic and copies ran while one was open for 0% of the time, Pallas kernels for 30%

profile of v15, /device:TPU:0, one launch (start us, length us, event | category | flops | bytes accessed | tf_op | source)
XLA Modules:
  0.0 40.6 jit_solution(12245335087649478580)
XLA Ops:
  1.2 1.5 %shard_map.94 = (bf16[64,512]{1,0:T(8,128)(2,1)S(1)}, bf16[64,512]{1,0:T(8,128)(2,1)S(1)}, bf16[64,512]{1,0:T(8,128)(2,1)S(1)}, bf16[64,512]{1,0:T(8,128)(2,1)S(...) custom-call(s32[8]{0:T(128)} %refs_0_.8, bf16[16,64,512]{2,1,0:T(8,128)(2,1)} %refs_1_.4, bf16[512,512]{1,0:T(8,128)(2,1)} %refs_1_.5), custom_call_target="tpu_custom_call" | custom-call | flops 5000000000 | bytes 1970208 | tf_op jit(solution)/shard_map/pallas_call | solution.py:55
  2.7 3.6 %collective-permute-start.3 = (bf16[64,512]{1,0:T(8,128)(2,1)S(1)}, bf16[64,512]{1,0:T(8,128)(2,1)S(1)}, u32[]{:S(2)}, u32[]{:S(2)}) collective-permute-start(bf16[64,512]{1,0:T(8,128)(2,1)S(1)} %get-tuple-element.27), channel_id=1, source_target_pairs={{0,8},{1,9},{4,12},{5,13},{8,0},{9,1},{12,4},{13,5},{2,10},{3,11},... | collective-permute-start | bytes 196616 | tf_op jit(solution)/shard_map/ppermute | solution.py:33
  6.3 1.3 %collective-permute-start.4 = (bf16[64,512]{1,0:T(8,128)(2,1)S(1)}, bf16[64,512]{1,0:T(8,128)(2,1)S(1)}, u32[]{:S(2)}, u32[]{:S(2)}) collective-permute-start(bf16[64,512]{1,0:T(8,128)(2,1)S(1)} %get-tuple-element.28), channel_id=1, source_target_pairs={{0,12},{1,13},{4,8},{5,9},{8,4},{9,5},{12,0},{13,1},{2,14},{3,15},... | collective-permute-start | bytes 196616 | tf_op jit(solution)/shard_map/ppermute | solution.py:33
  7.8 1.5 %collective-permute-start = (bf16[128,512]{1,0:T(8,128)(2,1)S(1)}, bf16[128,512]{1,0:T(8,128)(2,1)S(1)}, u32[]{:S(2)}, u32[]{:S(2)}) collective-permute-start(bf16[128,512]{1,0:T(8,128)(2,1)S(1)} %get-tuple-element.24), channel_id=1, source_target_pairs={{0,2},{2,0},{1,3},{3,1},{4,6},{6,4},{5,7},{7,5},{8,10},{10,8},{9,1... | collective-permute-start | bytes 393224 | tf_op jit(solution)/shard_map/ppermute | solution.py:26
  10.0 0.9 %shard_map.95.refs_0_.refs_6_.refs_1_ = f32[64,512]{1,0:T(8,128)S(1)} custom-call(bf16[512,2560]{1,0:T(8,128)(2,1)S(1)} %copy-done, bf16[64,2560]{1,0:T(8,128)(2,1)S(1)} %bitcast.2, bf16[64,512]{1,0:T(8,128)(2,1)S(1)} %get-tuple-element.25.refs_2_.refs_1_), custom_call_target="tpu_custom_call" | custom-call | flops 167772160 | bytes 3080192 | tf_op jit(solution)/shard_map/pallas_call | solution.py:55
  11.0 0.6 %collective-permute-start.2 = (bf16[64,512]{1,0:T(8,128)(2,1)S(1)}, bf16[64,512]{1,0:T(8,128)(2,1)S(1)}, u32[]{:S(2)}, u32[]{:S(2)}) collective-permute-start(bf16[64,512]{1,0:T(8,128)(2,1)S(1)} %shard_map.96), channel_id=1, source_target_pairs={{0,2},{2,0},{1,3},{3,1},{4,6},{6,4},{5,7},{7,5},{8,10},{10,8},{9,1... | collective-permute-start | bytes 196616 | tf_op jit(solution)/shard_map/ppermute | solution.py:26
  11.6 1.4 %collective-permute-done.4.refs_3_ = bf16[64,512]{1,0:T(8,128)(2,1)S(1)} collective-permute-done((bf16[64,512]{1,0:T(8,128)(2,1)S(1)}, bf16[64,512]{1,0:T(8,128)(2,1)S(1)}, u32[]{:S(2)}, u32[]{:S(2)}) %collective-permute-start.4) | collective-permute-done | bytes 65568 | tf_op jit(solution)/shard_map/ppermute | solution.py:33
  13.5 1.6 %collective-permute-start.7 = (f32[64,512]{1,0:T(8,128)S(1)}, f32[64,512]{1,0:T(8,128)S(1)}, u32[]{:S(2)}, u32[]{:S(2)}) collective-permute-start(f32[64,512]{1,0:T(8,128)S(1)} %shard_map.97.refs_4_.refs_1_), channel_id=1, source_target_pairs={{0,2},{2,0},{1,3},{3,1},{4,6},{6,4},{5,7},{7,5},{8,10},{10,8},{9,1... | collective-permute-start | bytes 393224 | tf_op jit(solution)/shard_map/ppermute | solution.py:26
  15.7 2.8 %collective-permute-start.10 = (bf16[1,64,512]{2,1,0:T(8,128)(2,1)S(1)}, bf16[1,64,512]{2,1,0:T(8,128)(2,1)S(1)}, u32[]{:S(2)}, u32[]{:S(2)}) collective-permute-start(bf16[1,64,512]{2,1,0:T(8,128)(2,1)S(1)} %get-tuple-element.31.refs_4_.refs_0_), channel_id=1, source_target_pairs={{0,8},{1,9},{4,12},{5,13},{8,0},{9,1},{12,4},{13,5},{2,10},{3,11},... | collective-permute-start | bytes 196616 | tf_op jit(solution)/shard_map/ppermute | solution.py:33
  18.5 1.5 %collective-permute-start.9 = (bf16[1,64,512]{2,1,0:T(8,128)(2,1)S(1)}, bf16[1,64,512]{2,1,0:T(8,128)(2,1)S(1)}, u32[]{:S(2)}, u32[]{:S(2)}) collective-permute-start(bf16[1,64,512]{2,1,0:T(8,128)(2,1)S(1)} %get-tuple-element.31.refs_4_.refs_0_), channel_id=1, source_target_pairs={{0,12},{1,13},{4,8},{5,9},{8,4},{9,5},{12,0},{13,1},{2,14},{3,15},... | collective-permute-start | bytes 196616 | tf_op jit(solution)/shard_map/ppermute | solution.py:33
  20.4 0.6 %shard_map.99 = (bf16[64,512]{1,0:T(8,128)(2,1)S(1)}, f32[32,2560]{1,0:T(8,128)S(1)}, f32[32,2560]{1,0:T(8,128)S(1)}) custom-call(s32[1]{0:T(128)S(6)} %copy.14.refs_0_, f32[64,512]{1,0:T(8,128)S(1)} %shard_map.97.refs_4_.refs_1_, f32[64,512]{1,0:T(8,128)S(1)} %collective-permute-done.7.refs_2_, bf16[512,2560]{1,0:T(8,128)(2,1)S(1)} %copy-done, ...), custom_call_target="tpu_custom_call" | custom-call | flops 167772160 | bytes 3604484 | tf_op jit(solution)/shard_map/pallas_call | solution.py:55
  21.1 1.5 %collective-permute-done.11.refs_1_ = f32[32,2560]{1,0:T(8,128)S(1)} collective-permute-done((f32[32,2560]{1,0:T(8,128)S(1)}, f32[32,2560]{1,0:T(8,128)S(1)}, u32[]{:S(2)}, u32[]{:S(2)}) %collective-permute-start.11) | collective-permute-done | bytes 327712 | tf_op jit(solution)/shard_map/ppermute | solution.py:26
  22.7 0.6 %collective-permute-start.13 = (bf16[16,2560]{1,0:T(8,128)(2,1)S(1)}, bf16[16,2560]{1,0:T(8,128)(2,1)S(1)}, u32[]{:S(2)}, u32[]{:S(2)}) collective-permute-start(bf16[16,2560]{1,0:T(8,128)(2,1)S(1)} %get-tuple-element.35.refs_0_), channel_id=1, source_target_pairs={{0,4},{1,5},{4,0},{5,1},{8,12},{9,13},{12,8},{13,9},{2,6},{3,7},{6... | collective-permute-start | bytes 245768 | tf_op jit(solution)/shard_map/ppermute | solution.py:33
  23.3 1.4 %shard_map.102 = (f32[16,64,512]{2,1,0:T(8,128)}, f32[8,128]{1,0:T(8,128)S(1)}) custom-call(bf16[16,2560]{1,0:T(8,128)(2,1)S(1)} %get-tuple-element.35.refs_0_), custom_call_target="tpu_custom_call" | custom-call | flops 10000000000 | bytes 2101248 | tf_op jit(solution)/shard_map/pallas_call | solution.py:55
  24.7 1.3 %collective-permute-done.8.refs_1_ = bf16[1,64,512]{2,1,0:T(8,128)(2,1)S(1)} collective-permute-done((bf16[1,64,512]{2,1,0:T(8,128)(2,1)S(1)}, bf16[1,64,512]{2,1,0:T(8,128)(2,1)S(1)}, u32[]{:S(2)}, u32[]{:S(2)}) %collective-permute-start.8) | collective-permute-done | bytes 65568 | tf_op jit(solution)/shard_map/ppermute | solution.py:33
  26.2 1.5 %collective-permute-done.13.refs_1_ = bf16[16,2560]{1,0:T(8,128)(2,1)S(1)} collective-permute-done((bf16[16,2560]{1,0:T(8,128)(2,1)S(1)}, bf16[16,2560]{1,0:T(8,128)(2,1)S(1)}, u32[]{:S(2)}, u32[]{:S(2)}) %collective-permute-start.13) | collective-permute-done | bytes 81952 | tf_op jit(solution)/shard_map/ppermute | solution.py:33
  27.7 1.2 %collective-permute-start.14 = (bf16[16,2560]{1,0:T(8,128)(2,1)S(1)}, bf16[16,2560]{1,0:T(8,128)(2,1)S(1)}, u32[]{:S(2)}, u32[]{:S(2)}) collective-permute-start(bf16[16,2560]{1,0:T(8,128)(2,1)S(1)} %shard_map.104.refs_4_.refs_0_), channel_id=1, source_target_pairs={{0,8},{1,9},{4,12},{5,13},{8,0},{9,1},{12,4},{13,5},{2,10},{3,11},... | collective-permute-start | bytes 245768 | tf_op jit(solution)/shard_map/ppermute | solution.py:33
  28.9 1.6 %shard_map.105 = (f32[16,64,512]{2,1,0:T(8,128)}, f32[8,128]{1,0:T(8,128)S(1)}) custom-call(s32[8]{0:T(128)} %refs_0_.8, bf16[4,64,512]{2,1,0:T(8,128)(2,1)S(1)} %shard_map.103.refs_2_.refs_1_, bf16[4,64,512]{2,1,0:T(8,128)(2,1)S(1)} %collective-permute-done.12.refs_2_, f32[16,64,512]{2,1,0:T(8,128)} %get-tuple-element.37.refs_3_, ...), custom_call_target="tpu_custom_call", output_to_operand_aliasing={{0}: (3, {})} | custom-call | bytes 4722720 | tf_op jit(solution)/shard_map/pallas_call | solution.py:55
  30.7 2.4 %shard_map.107 = (bf16[512,2560]{1,0:T(8,128)(2,1)}, f32[8,128]{1,0:T(8,128)S(1)}) custom-call(bf16[512,1024]{1,0:T(8,128)(2,1)S(1)} %shard_map.106.refs_0_, bf16[2560,512]{1,0:T(8,128)(2,1)S(1)} %copy-done.1, bf16[2560,512]{1,0:T(8,128)(2,1)S(1)} %collective-permute-done.1.refs_1_.refs_2_, bf16[64,512]{1,0:T(8,128)(2,1)S(1)} %get-tuple-element.32.refs_1_.refs_2_.refs_3_, ...), custom_call_target="tpu_custom_call" | custom-call | flops 1140850688 | bytes 9310208 | tf_op jit(solution)/shard_map/pallas_call | solution.py:55
  33.1 0.6 %collective-permute-done.14.refs_1_ = bf16[16,2560]{1,0:T(8,128)(2,1)S(1)} collective-permute-done((bf16[16,2560]{1,0:T(8,128)(2,1)S(1)}, bf16[16,2560]{1,0:T(8,128)(2,1)S(1)}, u32[]{:S(2)}, u32[]{:S(2)}) %collective-permute-start.14) | collective-permute-done | bytes 81952 | tf_op jit(solution)/shard_map/ppermute | solution.py:33
  33.7 1.0 %collective-permute-start.15 = (bf16[16,2560]{1,0:T(8,128)(2,1)S(1)}, bf16[16,2560]{1,0:T(8,128)(2,1)S(1)}, u32[]{:S(2)}, u32[]{:S(2)}) collective-permute-start(bf16[16,2560]{1,0:T(8,128)(2,1)S(1)} %shard_map.108.refs_6_.refs_0_), channel_id=1, source_target_pairs={{0,4},{1,5},{4,0},{5,1},{8,12},{9,13},{12,8},{13,9},{2,6},{3,7},{6... | collective-permute-start | bytes 245768 | tf_op jit(solution)/shard_map/ppermute | solution.py:33
  34.7 3.1 %shard_map.109 = (bf16[512,2560]{1,0:T(8,128)(2,1)}, f32[8,128]{1,0:T(8,128)S(1)}) custom-call(bf16[512,1024]{1,0:T(8,128)(2,1)S(1)} %shard_map.106.refs_0_, bf16[2560,512]{1,0:T(8,128)(2,1)S(1)} %copy-done.1, bf16[2560,512]{1,0:T(8,128)(2,1)S(1)} %collective-permute-done.1.refs_1_.refs_2_, ...), custom_call_target="tpu_custom_call", output_to_operand_aliasing={{0}: (5, {})} | custom-call | flops 1711276032 | bytes 11931648 | tf_op jit(solution)/shard_map/pallas_call | solution.py:55
  38.3 1.4 %collective-permute-done.16.refs_1_ = bf16[32,2560]{1,0:T(8,128)(2,1)S(1)} collective-permute-done((bf16[32,2560]{1,0:T(8,128)(2,1)S(1)}, bf16[32,2560]{1,0:T(8,128)(2,1)S(1)}, u32[]{:S(2)}, u32[]{:S(2)}) %collective-permute-start.16) | collective-permute-done | bytes 163872 | tf_op jit(solution)/shard_map/ppermute | solution.py:26
  39.7 0.9 %shard_map.111 = f32[64,2560]{1,0:T(8,128)} custom-call(bf16[32,2560]{1,0:T(8,128)(2,1)S(1)} %shard_map.110.refs_0_.refs_2_, bf16[32,2560]{1,0:T(8,128)(2,1)S(1)} %collective-permute-done.16.refs_1_, bf16[32,2560]{1,0:T(8,128)(2,1)S(1)} %shard_map.110.refs_0_.refs_2_), custom_call_target="tpu_custom_call" | custom-call | bytes 983040 | tf_op jit(solution)/shard_map/pallas_call | solution.py:55
  (36 shorter events, 3.3 us)
Async XLA Ops:
  0.6 9.4 %copy-start = (bf16[512,2560]{1,0:T(8,128)(2,1)S(1)}, bf16[512,2560]{1,0:T(8,128)(2,1)}, u32[]{:S(2)}) copy-start(bf16[512,2560]{1,0:T(8,128)(2,1)} %refs_3_.3) | copy-start | bytes 7864324
  0.6 9.4 %copy-start.2 = (bf16[2560,64]{0,1:T(8,128)(2,1)S(1)}, bf16[2560,64]{0,1:T(8,128)(2,1)}, u32[]{:S(2)}) copy-start(bf16[2560,64]{0,1:T(8,128)(2,1)} %param.10) | copy-start | bytes 983044
  0.7 10.3 %collective-permute-start.1 = (bf16[2560,512]{1,0:T(8,128)(2,1)}, bf16[2560,512]{1,0:T(8,128)(2,1)S(1)}, u32[]{:S(2)}, u32[]{:S(2)}) collective-permute-start(bf16[2560,512]{1,0:T(8,128)(2,1)} %refs_1_.7), channel_id=1, source_target_pairs={{0,1},{1,0},{2,3},{3,2},{4,5},{5,4},{6,7},{7,6},{8,9},{9,8},{10,11... | collective-permute-start | bytes 7864328 | tf_op jit(solution)/shard_map/ppermute | solution.py:26
  2.7 8.8 %collective-permute-start.3 = (bf16[64,512]{1,0:T(8,128)(2,1)S(1)}, bf16[64,512]{1,0:T(8,128)(2,1)S(1)}, u32[]{:S(2)}, u32[]{:S(2)}) collective-permute-start(bf16[64,512]{1,0:T(8,128)(2,1)S(1)} %get-tuple-element.27), channel_id=1, source_target_pairs={{0,8},{1,9},{4,12},{5,13},{8,0},{9,1},{12,4},{13,5},{2,10},{3,11},... | collective-permute-start | bytes 196616 | tf_op jit(solution)/shard_map/ppermute | solution.py:33
  6.3 6.7 %collective-permute-start.4 = (bf16[64,512]{1,0:T(8,128)(2,1)S(1)}, bf16[64,512]{1,0:T(8,128)(2,1)S(1)}, u32[]{:S(2)}, u32[]{:S(2)}) collective-permute-start(bf16[64,512]{1,0:T(8,128)(2,1)S(1)} %get-tuple-element.28), channel_id=1, source_target_pairs={{0,12},{1,13},{4,8},{5,9},{8,4},{9,5},{12,0},{13,1},{2,14},{3,15},... | collective-permute-start | bytes 196616 | tf_op jit(solution)/shard_map/ppermute | solution.py:33
  7.6 5.6 %collective-permute-start.5 = (bf16[64,512]{1,0:T(8,128)(2,1)S(1)}, bf16[64,512]{1,0:T(8,128)(2,1)S(1)}, u32[]{:S(2)}, u32[]{:S(2)}) collective-permute-start(bf16[64,512]{1,0:T(8,128)(2,1)S(1)} %get-tuple-element.29), channel_id=1, source_target_pairs={{0,4},{1,5},{4,0},{5,1},{8,12},{9,13},{12,8},{13,9},{2,6},{3,7},{6... | collective-permute-start | bytes 196616 | tf_op jit(solution)/shard_map/ppermute | solution.py:33
  7.8 7.2 %collective-permute-start = (bf16[128,512]{1,0:T(8,128)(2,1)S(1)}, bf16[128,512]{1,0:T(8,128)(2,1)S(1)}, u32[]{:S(2)}, u32[]{:S(2)}) collective-permute-start(bf16[128,512]{1,0:T(8,128)(2,1)S(1)} %get-tuple-element.24), channel_id=1, source_target_pairs={{0,2},{2,0},{1,3},{3,1},{4,6},{6,4},{5,7},{7,5},{8,10},{10,8},{9,1... | collective-permute-start | bytes 393224 | tf_op jit(solution)/shard_map/ppermute | solution.py:26
  10.0 3.2 %copy-start.3 = (bf16[512,512]{1,0:T(8,128)(2,1)S(1)}, bf16[512,512]{1,0:T(8,128)(2,1)}, u32[]{:S(2)}) copy-start(bf16[512,512]{1,0:T(8,128)(2,1)} %refs_1_.5) | copy-start | bytes 1572868
  11.0 4.4 %collective-permute-start.2 = (bf16[64,512]{1,0:T(8,128)(2,1)S(1)}, bf16[64,512]{1,0:T(8,128)(2,1)S(1)}, u32[]{:S(2)}, u32[]{:S(2)}) collective-permute-start(bf16[64,512]{1,0:T(8,128)(2,1)S(1)} %shard_map.96), channel_id=1, source_target_pairs={{0,2},{2,0},{1,3},{3,1},{4,6},{6,4},{5,7},{7,5},{8,10},{10,8},{9,1... | collective-permute-start | bytes 196616 | tf_op jit(solution)/shard_map/ppermute | solution.py:26
  13.5 6.9 %collective-permute-start.7 = (f32[64,512]{1,0:T(8,128)S(1)}, f32[64,512]{1,0:T(8,128)S(1)}, u32[]{:S(2)}, u32[]{:S(2)}) collective-permute-start(f32[64,512]{1,0:T(8,128)S(1)} %shard_map.97.refs_4_.refs_1_), channel_id=1, source_target_pairs={{0,2},{2,0},{1,3},{3,1},{4,6},{6,4},{5,7},{7,5},{8,10},{10,8},{9,1... | collective-permute-start | bytes 393224 | tf_op jit(solution)/shard_map/ppermute | solution.py:26
  15.7 9.0 %collective-permute-start.10 = (bf16[1,64,512]{2,1,0:T(8,128)(2,1)S(1)}, bf16[1,64,512]{2,1,0:T(8,128)(2,1)S(1)}, u32[]{:S(2)}, u32[]{:S(2)}) collective-permute-start(bf16[1,64,512]{2,1,0:T(8,128)(2,1)S(1)} %get-tuple-element.31.refs_4_.refs_0_), channel_id=1, source_target_pairs={{0,8},{1,9},{4,12},{5,13},{8,0},{9,1},{12,4},{13,5},{2,10},{3,11},... | collective-permute-start | bytes 196616 | tf_op jit(solution)/shard_map/ppermute | solution.py:33
  18.5 6.3 %collective-permute-start.9 = (bf16[1,64,512]{2,1,0:T(8,128)(2,1)S(1)}, bf16[1,64,512]{2,1,0:T(8,128)(2,1)S(1)}, u32[]{:S(2)}, u32[]{:S(2)}) collective-permute-start(bf16[1,64,512]{2,1,0:T(8,128)(2,1)S(1)} %get-tuple-element.31.refs_4_.refs_0_), channel_id=1, source_target_pairs={{0,12},{1,13},{4,8},{5,9},{8,4},{9,5},{12,0},{13,1},{2,14},{3,15},... | collective-permute-start | bytes 196616 | tf_op jit(solution)/shard_map/ppermute | solution.py:33
  20.0 10.6 %collective-permute-start.6 = (bf16[384,512]{1,0:T(8,128)(2,1)S(1)}, bf16[384,512]{1,0:T(8,128)(2,1)S(1)}, u32[]{:S(2)}, u32[]{:S(2)}) collective-permute-start(bf16[384,512]{1,0:T(8,128)(2,1)S(1)} %get-tuple-element.30), channel_id=1, source_target_pairs={{0,2},{2,0},{1,3},{3,1},{4,6},{6,4},{5,7},{7,5},{8,10},{10,8},{9,1... | collective-permute-start | bytes 1179656 | tf_op jit(solution)/shard_map/ppermute | solution.py:26
  21.0 1.7 %collective-permute-start.11 = (f32[32,2560]{1,0:T(8,128)S(1)}, f32[32,2560]{1,0:T(8,128)S(1)}, u32[]{:S(2)}, u32[]{:S(2)}) collective-permute-start(f32[32,2560]{1,0:T(8,128)S(1)} %get-tuple-element.34), channel_id=1, source_target_pairs={{0,1},{1,0},{2,3},{3,2},{4,5},{5,4},{6,7},{7,6},{8,9},{9,8},{10,11... | collective-permute-start | bytes 983048 | tf_op jit(solution)/shard_map/ppermute | solution.py:26
  21.1 5.0 %collective-permute-start.8 = (bf16[1,64,512]{2,1,0:T(8,128)(2,1)S(1)}, bf16[1,64,512]{2,1,0:T(8,128)(2,1)S(1)}, u32[]{:S(2)}, u32[]{:S(2)}) collective-permute-start(bf16[1,64,512]{2,1,0:T(8,128)(2,1)S(1)} %shard_map.100), channel_id=1, source_target_pairs={{0,4},{1,5},{4,0},{5,1},{8,12},{9,13},{12,8},{13,9},{2,6},{3,7},{6... | collective-permute-start | bytes 196616 | tf_op jit(solution)/shard_map/ppermute | solution.py:33
  22.7 5.0 %collective-permute-start.13 = (bf16[16,2560]{1,0:T(8,128)(2,1)S(1)}, bf16[16,2560]{1,0:T(8,128)(2,1)S(1)}, u32[]{:S(2)}, u32[]{:S(2)}) collective-permute-start(bf16[16,2560]{1,0:T(8,128)(2,1)S(1)} %get-tuple-element.35.refs_0_), channel_id=1, source_target_pairs={{0,4},{1,5},{4,0},{5,1},{8,12},{9,13},{12,8},{13,9},{2,6},{3,7},{6... | collective-permute-start | bytes 245768 | tf_op jit(solution)/shard_map/ppermute | solution.py:33
  26.1 2.8 %collective-permute-start.12 = (bf16[4,64,512]{2,1,0:T(8,128)(2,1)S(1)}, bf16[4,64,512]{2,1,0:T(8,128)(2,1)S(1)}, u32[]{:S(2)}, u32[]{:S(2)}) collective-permute-start(bf16[4,64,512]{2,1,0:T(8,128)(2,1)S(1)} %shard_map.103.refs_2_.refs_1_), channel_id=1, source_target_pairs={{0,1},{1,0},{2,3},{3,2},{4,5},{5,4},{6,7},{7,6},{8,9},{9,8},{10,11... | collective-permute-start | bytes 786440 | tf_op jit(solution)/shard_map/ppermute | solution.py:26
  27.7 2.9 %copy-start.1 = (bf16[2560,512]{1,0:T(8,128)(2,1)S(1)}, bf16[2560,512]{1,0:T(8,128)(2,1)}, u32[]{:S(2)}) copy-start(bf16[2560,512]{1,0:T(8,128)(2,1)} %refs_1_.7) | copy-start | bytes 7864324
  27.7 5.9 %collective-permute-start.14 = (bf16[16,2560]{1,0:T(8,128)(2,1)S(1)}, bf16[16,2560]{1,0:T(8,128)(2,1)S(1)}, u32[]{:S(2)}, u32[]{:S(2)}) collective-permute-start(bf16[16,2560]{1,0:T(8,128)(2,1)S(1)} %shard_map.104.refs_4_.refs_0_), channel_id=1, source_target_pairs={{0,8},{1,9},{4,12},{5,13},{8,0},{9,1},{12,4},{13,5},{2,10},{3,11},... | collective-permute-start | bytes 245768 | tf_op jit(solution)/shard_map/ppermute | solution.py:33
  33.7 4.5 %collective-permute-start.15 = (bf16[16,2560]{1,0:T(8,128)(2,1)S(1)}, bf16[16,2560]{1,0:T(8,128)(2,1)S(1)}, u32[]{:S(2)}, u32[]{:S(2)}) collective-permute-start(bf16[16,2560]{1,0:T(8,128)(2,1)S(1)} %shard_map.108.refs_6_.refs_0_), channel_id=1, source_target_pairs={{0,4},{1,5},{4,0},{5,1},{8,12},{9,13},{12,8},{13,9},{2,6},{3,7},{6... | collective-permute-start | bytes 245768 | tf_op jit(solution)/shard_map/ppermute | solution.py:33
  38.3 1.5 %collective-permute-start.16 = (bf16[32,2560]{1,0:T(8,128)(2,1)S(1)}, bf16[32,2560]{1,0:T(8,128)(2,1)S(1)}, u32[]{:S(2)}, u32[]{:S(2)}) collective-permute-start(bf16[32,2560]{1,0:T(8,128)(2,1)S(1)} %shard_map.110.refs_0_.refs_2_), channel_id=1, source_target_pairs={{0,1},{1,0},{2,3},{3,2},{4,5},{5,4},{6,7},{7,6},{8,9},{9,8},{10,11... | collective-permute-start | bytes 491528 | tf_op jit(solution)/shard_map/ppermute | solution.py:26

commit v16 on v15

--- a/solution.py
+++ b/solution.py
@@ -185,30 +185,38 @@
 def shared_terms(lengths, parts, tokens, scale, after):
     rows, features = tokens.shape
     rank = parts[0].shape[0]
-    share = rank // 2
+    share = rank // 4
 
     def body(lengths, *refs):
-        parts, (tokens, back, keep, send, total) = refs[:count], refs[count:]
-        sub = lax.axis_index("sub")
+        parts, (tokens, back, *shares, total) = refs[:count], refs[count:]
+        sub, bit = lax.axis_index("sub"), lax.rem(lax.axis_index("own"), 2)
         both = parts[0][...]
         for part in parts[1:]:
             both = both + part[...]
         live = lax.broadcasted_iota(jnp.int32, both.shape, 1) < lengths[0]
         back[...] = jnp.where(live, both, 0.0).astype(bf16)
         total[...] = scale * jnp.dot(back[...], tokens[...], preferred_element_type=f32)
-        keep[...] = total[pl.ds(pl.multiple_of(sub * share, share), share), :]
-        send[...] = total[pl.ds(pl.multiple_of((1 - sub) * share, share), share), :]
+        places = [(side, half) for side in (sub, 1 - sub) for half in (1 - bit, bit)]
+        for (side, half), out in zip(places, shares):
+            out[...] = total[pl.ds(pl.multiple_of((side * 2 + half) * share, share), share), :]
 
     count = len(parts)
     return call(
         body,
         [lengths, *parts, tokens],
         [in_smem] + [in_vmem] * (count + 1),
-        [shape_of((rank, rows), bf16)] + [shape_of((share, features), f32)] * 2,
+        [shape_of((rank, rows), bf16)] + [shape_of((share, features), f32)] * 4,
         after=after,
         scratch_shapes=[pltpu.VMEM((rank, features), f32)],
         flops=2 * rows * rank * features,
     )
+
+
+def copied(x, after, flops):
+    def body(x, out):
+        out[...] = x[...]
+
+    return call(body, [x], [in_vmem], [shape_of(x.shape, x.dtype)], after=after, flops=flops)[0]
 
 
 def add_up(pieces, after=(), flops=0):
@@ -269,20 +277,30 @@
     )[0]
 
 
-def join_shares(mine, other, after):
-    share, features = mine.shape
-
-    def body(mine, other, out):
+def lay_share(share, other, before, after):
+    rows, features = share.shape
+    held_in = [] if before is None else [before]
+
+    def body(share, *refs):
+        out, wide, sem = refs[len(held_in) :]
         sub = lax.axis_index("sub")
-        for side, piece in ((sub, mine), (1 - sub, other)):
-            out[pl.ds(pl.multiple_of(side * share, share), share), :] = piece[...].astype(f32)
-
-    return call(
-        body,
-        [mine, other],
-        [in_vmem] * 2,
-        [shape_of((2 * share, features), f32)],
-        after=after,
+        side = 1 - sub if other else sub
+        wide[...] = share[...].astype(f32)
+        copy = pltpu.make_async_copy(
+            wide, out.at[pl.ds(pl.multiple_of(side * rows, rows), rows)], sem
+        )
+        copy.start()
+        copy.wait()
+
+    return call(
+        body,
+        [share, *held_in],
+        [in_vmem] + [in_hbm] * len(held_in),
+        [shape_of((2 * rows, features), f32)],
+        out_specs=[in_hbm],
+        after=after,
+        input_output_aliases={1: 0} if held_in else {},
+        scratch_shapes=[pltpu.VMEM((rows, features), f32), pltpu.SemaphoreType.DMA],
     )[0]
 
 
@@ -482,14 +500,16 @@
 
     near, late = head_term(lengths, lows, grad_output, scale, [part, *early_grads])
     late_grads = [shift(late, "tp", step) for step in tp_steps]
-    back, keep, send = shared_terms(lengths, parts, tokens, scale, [near])
-    pieces = [keep, shift(send, "sub", 1)]
+    back, keep, keep_too, send, send_too = shared_terms(lengths, parts, tokens, scale, [near])
     met = stack([near], [back], flops=middling)
     terms = [near] + [swap(met if step == 1 else near, step, 0) for step in steps[::-1]]
 
     bits = [1 << i for i in range(own_count.bit_length() - 1)]
-    mark = back
-    for bit in bits[:-1]:
+    leaves = add_up([keep, shift(send, "sub", 1)])
+    later = copied(send_too, [leaves, terms[-1]], filling)
+    pieces = [keep_too, shift(later, "sub", 1), swap(leaves, 1, 0)]
+    mark = leaves
+    for bit in bits[1:-1]:
         stays, leaves = halve(pieces, bit, [mark])
         pieces = [stays, swap(leaves, bit, 0)]
         mark = leaves
@@ -514,7 +534,8 @@
     for bit in reversed(bits[:-1]):
         total = rejoin(total, swap(total, bit, 0), bit, [mark])
         mark = total
-    shared_down_gradient = join_shares(total, shift(total, "sub", 1), [mark]).T
+    laid = lay_share(total, False, None, [mark])
+    shared_down_gradient = lay_share(shift(total, "sub", 1), True, laid, []).T
     return (input_gradient, shared_down_gradient, grad_heads)
 
 

time: 40.7 us -> 40.9 us (level)
  Pallas kernels: 13.3 us -> 14.1 us
  starting transfers between devices: 17 us -> 16.4 us
    ppermute x8 -> x9, waiting for transfers between devices: 3.2 us -> 2.21 us  [shift(): lax.ppermute(x, axis, [(i, (i + step) % count) for i in range(count)])]
    ppermute x9, waiting for transfers between devices: 5.54 us -> 6.45 us  [swap(): lax.ppermute(x, ('own', 'sub'), [(i, i ^ other) for i in range(whole)])]
    pallas_call x18 -> x20, Pallas kernels: 13.3 us -> 14.1 us  [call(): pl.pallas_call(kernel, out_shape=outs, in_specs=list(specs) + [anywhere]...]
    ppermute x9, starting transfers between devices: 12.2 us -> 11.5 us  [swap(): lax.ppermute(x, ('own', 'sub'), [(i, i ^ other) for i in range(whole)])]
    ppermute x8 -> x9, starting transfers between devices: 4.81 us -> 4.88 us  [shift(): lax.ppermute(x, axis, [(i, (i + step) % count) for i in range(count)])]
  transfers between devices with their start and end apart: 17 -> 18, of which waited for: 9 -> 9; matrix products, arithmetic and copies ran while one was open for 0% -> 0% of each run, Pallas kernels for 30% -> 33%
where the time goes in v16:
time: 40.9 us; the launch traced here: 40.7 us
  starting transfers between devices  16.4 us (40%)
  Pallas kernels  14.1 us (34%)
  waiting for transfers between devices  8.66 us (21%)
  between operations  1.53 us (4%)
    pallas_call x20, Pallas kernels, call(): pl.pallas_call(kernel, out_shape=outs, in_specs=list(specs) + [anywhere]...  14.1 us
    ppermute x9, starting transfers between devices, swap(): lax.ppermute(x, ('own', 'sub'), [(i, i ^ other) for i in range(whole)])  11.5 us
    ppermute x9, waiting for transfers between devices, swap(): lax.ppermute(x, ('own', 'sub'), [(i, i ^ other) for i in range(whole)])  6.45 us
    ppermute x9, starting transfers between devices, shift(): lax.ppermute(x, axis, [(i, (i + step) % count) for i in range(count)])  4.88 us
    ppermute x9, waiting for transfers between devices, shift(): lax.ppermute(x, axis, [(i, (i + step) % count) for i in range(count)])  2.21 us
  transfers between devices with their start and end apart: 18, of which 9 were waited for; matrix products, arithmetic and copies ran while one was open for 0% of the time, Pallas kernels for 33%

profile of v16, /device:TPU:0, one launch (start us, length us, event | category | flops | bytes accessed | tf_op | source)
XLA Modules:
  0.0 40.7 jit_solution(8614095099074741495)
XLA Ops:
  1.2 1.5 %shard_map.94 = (bf16[64,512]{1,0:T(8,128)(2,1)S(1)}, bf16[64,512]{1,0:T(8,128)(2,1)S(1)}, bf16[64,512]{1,0:T(8,128)(2,1)S(1)}, bf16[64,512]{1,0:T(8,128)(2,1)S(...) custom-call(s32[8]{0:T(128)} %refs_0_.8, bf16[16,64,512]{2,1,0:T(8,128)(2,1)} %refs_1_.4, bf16[512,512]{1,0:T(8,128)(2,1)} %refs_1_.5), custom_call_target="tpu_custom_call" | custom-call | flops 5000000000 | bytes 1970208 | tf_op jit(solution)/shard_map/pallas_call | solution.py:55
  2.7 3.6 %collective-permute-start.3 = (bf16[64,512]{1,0:T(8,128)(2,1)S(1)}, bf16[64,512]{1,0:T(8,128)(2,1)S(1)}, u32[]{:S(2)}, u32[]{:S(2)}) collective-permute-start(bf16[64,512]{1,0:T(8,128)(2,1)S(1)} %get-tuple-element.27), channel_id=1, source_target_pairs={{0,8},{1,9},{4,12},{5,13},{8,0},{9,1},{12,4},{13,5},{2,10},{3,11},... | collective-permute-start | bytes 196616 | tf_op jit(solution)/shard_map/ppermute | solution.py:33
  6.3 1.3 %collective-permute-start.4 = (bf16[64,512]{1,0:T(8,128)(2,1)S(1)}, bf16[64,512]{1,0:T(8,128)(2,1)S(1)}, u32[]{:S(2)}, u32[]{:S(2)}) collective-permute-start(bf16[64,512]{1,0:T(8,128)(2,1)S(1)} %get-tuple-element.28), channel_id=1, source_target_pairs={{0,12},{1,13},{4,8},{5,9},{8,4},{9,5},{12,0},{13,1},{2,14},{3,15},... | collective-permute-start | bytes 196616 | tf_op jit(solution)/shard_map/ppermute | solution.py:33
  7.8 1.5 %collective-permute-start = (bf16[128,512]{1,0:T(8,128)(2,1)S(1)}, bf16[128,512]{1,0:T(8,128)(2,1)S(1)}, u32[]{:S(2)}, u32[]{:S(2)}) collective-permute-start(bf16[128,512]{1,0:T(8,128)(2,1)S(1)} %get-tuple-element.24), channel_id=1, source_target_pairs={{0,2},{2,0},{1,3},{3,1},{4,6},{6,4},{5,7},{7,5},{8,10},{10,8},{9,1... | collective-permute-start | bytes 393224 | tf_op jit(solution)/shard_map/ppermute | solution.py:26
  10.0 0.9 %shard_map.95.refs_0_.refs_6_.refs_1_ = f32[64,512]{1,0:T(8,128)S(1)} custom-call(bf16[512,2560]{1,0:T(8,128)(2,1)S(1)} %copy-done, bf16[64,2560]{1,0:T(8,128)(2,1)S(1)} %bitcast.2, bf16[64,512]{1,0:T(8,128)(2,1)S(1)} %get-tuple-element.25.refs_2_.refs_1_), custom_call_target="tpu_custom_call" | custom-call | flops 167772160 | bytes 3080192 | tf_op jit(solution)/shard_map/pallas_call | solution.py:55
  11.0 0.6 %collective-permute-start.2 = (bf16[64,512]{1,0:T(8,128)(2,1)S(1)}, bf16[64,512]{1,0:T(8,128)(2,1)S(1)}, u32[]{:S(2)}, u32[]{:S(2)}) collective-permute-start(bf16[64,512]{1,0:T(8,128)(2,1)S(1)} %shard_map.96), channel_id=1, source_target_pairs={{0,2},{2,0},{1,3},{3,1},{4,6},{6,4},{5,7},{7,5},{8,10},{10,8},{9,1... | collective-permute-start | bytes 196616 | tf_op jit(solution)/shard_map/ppermute | solution.py:26
  11.6 1.4 %collective-permute-done.4.refs_3_ = bf16[64,512]{1,0:T(8,128)(2,1)S(1)} collective-permute-done((bf16[64,512]{1,0:T(8,128)(2,1)S(1)}, bf16[64,512]{1,0:T(8,128)(2,1)S(1)}, u32[]{:S(2)}, u32[]{:S(2)}) %collective-permute-start.4) | collective-permute-done | bytes 65568 | tf_op jit(solution)/shard_map/ppermute | solution.py:33
  13.5 1.6 %collective-permute-start.7 = (f32[64,512]{1,0:T(8,128)S(1)}, f32[64,512]{1,0:T(8,128)S(1)}, u32[]{:S(2)}, u32[]{:S(2)}) collective-permute-start(f32[64,512]{1,0:T(8,128)S(1)} %shard_map.97.refs_4_.refs_1_), channel_id=1, source_target_pairs={{0,2},{2,0},{1,3},{3,1},{4,6},{6,4},{5,7},{7,5},{8,10},{10,8},{9,1... | collective-permute-start | bytes 393224 | tf_op jit(solution)/shard_map/ppermute | solution.py:26
  15.7 2.8 %collective-permute-start.10 = (bf16[1,64,512]{2,1,0:T(8,128)(2,1)S(1)}, bf16[1,64,512]{2,1,0:T(8,128)(2,1)S(1)}, u32[]{:S(2)}, u32[]{:S(2)}) collective-permute-start(bf16[1,64,512]{2,1,0:T(8,128)(2,1)S(1)} %get-tuple-element.31.refs_4_.refs_0_), channel_id=1, source_target_pairs={{0,8},{1,9},{4,12},{5,13},{8,0},{9,1},{12,4},{13,5},{2,10},{3,11},... | collective-permute-start | bytes 196616 | tf_op jit(solution)/shard_map/ppermute | solution.py:33
  18.5 1.5 %collective-permute-start.9 = (bf16[1,64,512]{2,1,0:T(8,128)(2,1)S(1)}, bf16[1,64,512]{2,1,0:T(8,128)(2,1)S(1)}, u32[]{:S(2)}, u32[]{:S(2)}) collective-permute-start(bf16[1,64,512]{2,1,0:T(8,128)(2,1)S(1)} %get-tuple-element.31.refs_4_.refs_0_), channel_id=1, source_target_pairs={{0,12},{1,13},{4,8},{5,9},{8,4},{9,5},{12,0},{13,1},{2,14},{3,15},... | collective-permute-start | bytes 196616 | tf_op jit(solution)/shard_map/ppermute | solution.py:33
  21.1 1.3 %collective-permute-done.11.refs_1_ = f32[16,2560]{1,0:T(8,128)S(1)} collective-permute-done((f32[16,2560]{1,0:T(8,128)S(1)}, f32[16,2560]{1,0:T(8,128)S(1)}, u32[]{:S(2)}, u32[]{:S(2)}) %collective-permute-start.11) | collective-permute-done | bytes 163872 | tf_op jit(solution)/shard_map/ppermute | solution.py:26
  22.4 0.8 %collective-permute-start.14 = (bf16[16,2560]{1,0:T(8,128)(2,1)S(1)}, bf16[16,2560]{1,0:T(8,128)(2,1)S(1)}, u32[]{:S(2)}, u32[]{:S(2)}) collective-permute-start(bf16[16,2560]{1,0:T(8,128)(2,1)S(1)} %shard_map.101.refs_0_.refs_1_), channel_id=1, source_target_pairs={{0,4},{1,5},{4,0},{5,1},{8,12},{9,13},{12,8},{13,9},{2,6},{3,7},{6... | collective-permute-start | bytes 245768 | tf_op jit(solution)/shard_map/ppermute | solution.py:33
  23.3 1.4 %shard_map.102 = (f32[16,64,512]{2,1,0:T(8,128)}, f32[8,128]{1,0:T(8,128)S(1)}) custom-call(bf16[16,2560]{1,0:T(8,128)(2,1)S(1)} %shard_map.101.refs_0_.refs_1_), custom_call_target="tpu_custom_call" | custom-call | flops 10000000000 | bytes 2101248 | tf_op jit(solution)/shard_map/pallas_call | solution.py:55
  24.8 1.3 %collective-permute-done.8.refs_1_ = bf16[1,64,512]{2,1,0:T(8,128)(2,1)S(1)} collective-permute-done((bf16[1,64,512]{2,1,0:T(8,128)(2,1)S(1)}, bf16[1,64,512]{2,1,0:T(8,128)(2,1)S(1)}, u32[]{:S(2)}, u32[]{:S(2)}) %collective-permute-start.8) | collective-permute-done | bytes 65568 | tf_op jit(solution)/shard_map/ppermute | solution.py:33
  26.2 1.5 %collective-permute-done.14.refs_2_ = bf16[16,2560]{1,0:T(8,128)(2,1)S(1)} collective-permute-done((bf16[16,2560]{1,0:T(8,128)(2,1)S(1)}, bf16[16,2560]{1,0:T(8,128)(2,1)S(1)}, u32[]{:S(2)}, u32[]{:S(2)}) %collective-permute-start.14) | collective-permute-done | bytes 81952 | tf_op jit(solution)/shard_map/ppermute | solution.py:33
  27.7 1.1 %collective-permute-start.15 = (bf16[16,2560]{1,0:T(8,128)(2,1)S(1)}, bf16[16,2560]{1,0:T(8,128)(2,1)S(1)}, u32[]{:S(2)}, u32[]{:S(2)}) collective-permute-start(bf16[16,2560]{1,0:T(8,128)(2,1)S(1)} %shard_map.105.refs_4_.refs_0_), channel_id=1, source_target_pairs={{0,8},{1,9},{4,12},{5,13},{8,0},{9,1},{12,4},{13,5},{2,10},{3,11},... | collective-permute-start | bytes 245768 | tf_op jit(solution)/shard_map/ppermute | solution.py:33
  28.9 1.9 %shard_map.106 = (f32[16,64,512]{2,1,0:T(8,128)}, f32[8,128]{1,0:T(8,128)S(1)}) custom-call(s32[8]{0:T(128)} %refs_0_.8, bf16[4,64,512]{2,1,0:T(8,128)(2,1)S(1)} %shard_map.103.refs_3_.refs_1_, bf16[4,64,512]{2,1,0:T(8,128)(2,1)S(1)} %collective-permute-done.12.refs_2_, f32[16,64,512]{2,1,0:T(8,128)} %get-tuple-element.36.refs_3_, ...), custom_call_target="tpu_custom_call", output_to_operand_aliasing={{0}: (3, {})} | custom-call | bytes 4722720 | tf_op jit(solution)/shard_map/pallas_call | solution.py:55
  30.8 2.4 %shard_map.108 = (bf16[512,2560]{1,0:T(8,128)(2,1)}, f32[8,128]{1,0:T(8,128)S(1)}) custom-call(bf16[512,1024]{1,0:T(8,128)(2,1)S(1)} %shard_map.107.refs_0_, bf16[2560,512]{1,0:T(8,128)(2,1)S(1)} %copy-done.1, bf16[2560,512]{1,0:T(8,128)(2,1)S(1)} %collective-permute-done.1.refs_1_.refs_2_, bf16[64,512]{1,0:T(8,128)(2,1)S(1)} %get-tuple-element.32.refs_1_.refs_3_, ...), custom_call_target="tpu_custom_call" | custom-call | flops 1140850688 | bytes 9310208 | tf_op jit(solution)/shard_map/pallas_call | solution.py:55
  33.2 0.7 %collective-permute-done.15.refs_1_ = bf16[16,2560]{1,0:T(8,128)(2,1)S(1)} collective-permute-done((bf16[16,2560]{1,0:T(8,128)(2,1)S(1)}, bf16[16,2560]{1,0:T(8,128)(2,1)S(1)}, u32[]{:S(2)}, u32[]{:S(2)}) %collective-permute-start.15) | collective-permute-done | bytes 81952 | tf_op jit(solution)/shard_map/ppermute | solution.py:33
  34.1 3.1 %shard_map.110 = (bf16[512,2560]{1,0:T(8,128)(2,1)}, f32[8,128]{1,0:T(8,128)S(1)}) custom-call(bf16[512,1024]{1,0:T(8,128)(2,1)S(1)} %shard_map.107.refs_0_, bf16[2560,512]{1,0:T(8,128)(2,1)S(1)} %copy-done.1, bf16[2560,512]{1,0:T(8,128)(2,1)S(1)} %collective-permute-done.1.refs_1_.refs_2_, ...), custom_call_target="tpu_custom_call", output_to_operand_aliasing={{0}: (5, {})} | custom-call | flops 1711276032 | bytes 11931648 | tf_op jit(solution)/shard_map/pallas_call | solution.py:55
  37.2 1.3 %collective-permute-done.16.refs_1_ = bf16[16,2560]{1,0:T(8,128)(2,1)S(1)} collective-permute-done((bf16[16,2560]{1,0:T(8,128)(2,1)S(1)}, bf16[16,2560]{1,0:T(8,128)(2,1)S(1)}, u32[]{:S(2)}, u32[]{:S(2)}) %collective-permute-start.16) | collective-permute-done | bytes 81952 | tf_op jit(solution)/shard_map/ppermute | solution.py:33
  38.6 0.8 %shard_map.112.refs_1_ = f32[64,2560]{1,0:T(8,128)} custom-call(bf16[32,2560]{1,0:T(8,128)(2,1)S(1)} %shard_map.111.refs_0_.refs_1_, bf16[32,2560]{1,0:T(8,128)(2,1)S(1)} %shard_map.111.refs_0_.refs_1_), custom_call_target="tpu_custom_call" | custom-call | bytes 819200 | tf_op jit(solution)/shard_map/pallas_call | solution.py:55
  39.4 0.6 %collective-permute-done.17.refs_0_ = bf16[32,2560]{1,0:T(8,128)(2,1)S(1)} collective-permute-done((bf16[32,2560]{1,0:T(8,128)(2,1)S(1)}, bf16[32,2560]{1,0:T(8,128)(2,1)S(1)}, u32[]{:S(2)}, u32[]{:S(2)}) %collective-permute-start.17) | collective-permute-done | bytes 163872 | tf_op jit(solution)/shard_map/ppermute | solution.py:26
  40.0 0.8 %shard_map.113 = f32[64,2560]{1,0:T(8,128)} custom-call(bf16[32,2560]{1,0:T(8,128)(2,1)S(1)} %collective-permute-done.17.refs_0_, f32[64,2560]{1,0:T(8,128)} %shard_map.112.refs_1_), custom_call_target="tpu_custom_call", output_to_operand_aliasing={{}: (1, {})} | custom-call | bytes 1474560 | tf_op jit(solution)/shard_map/pallas_call | solution.py:55
  (40 shorter events, 3.6 us)
Async XLA Ops:
  0.6 9.4 %copy-start = (bf16[512,2560]{1,0:T(8,128)(2,1)S(1)}, bf16[512,2560]{1,0:T(8,128)(2,1)}, u32[]{:S(2)}) copy-start(bf16[512,2560]{1,0:T(8,128)(2,1)} %refs_3_.3) | copy-start | bytes 7864324
  0.6 9.4 %copy-start.2 = (bf16[2560,64]{0,1:T(8,128)(2,1)S(1)}, bf16[2560,64]{0,1:T(8,128)(2,1)}, u32[]{:S(2)}) copy-start(bf16[2560,64]{0,1:T(8,128)(2,1)} %param.10) | copy-start | bytes 983044
  0.7 10.3 %collective-permute-start.1 = (bf16[2560,512]{1,0:T(8,128)(2,1)}, bf16[2560,512]{1,0:T(8,128)(2,1)S(1)}, u32[]{:S(2)}, u32[]{:S(2)}) collective-permute-start(bf16[2560,512]{1,0:T(8,128)(2,1)} %refs_1_.7), channel_id=1, source_target_pairs={{0,1},{1,0},{2,3},{3,2},{4,5},{5,4},{6,7},{7,6},{8,9},{9,8},{10,11... | collective-permute-start | bytes 7864328 | tf_op jit(solution)/shard_map/ppermute | solution.py:26
  2.7 8.8 %collective-permute-start.3 = (bf16[64,512]{1,0:T(8,128)(2,1)S(1)}, bf16[64,512]{1,0:T(8,128)(2,1)S(1)}, u32[]{:S(2)}, u32[]{:S(2)}) collective-permute-start(bf16[64,512]{1,0:T(8,128)(2,1)S(1)} %get-tuple-element.27), channel_id=1, source_target_pairs={{0,8},{1,9},{4,12},{5,13},{8,0},{9,1},{12,4},{13,5},{2,10},{3,11},... | collective-permute-start | bytes 196616 | tf_op jit(solution)/shard_map/ppermute | solution.py:33
  6.3 6.7 %collective-permute-start.4 = (bf16[64,512]{1,0:T(8,128)(2,1)S(1)}, bf16[64,512]{1,0:T(8,128)(2,1)S(1)}, u32[]{:S(2)}, u32[]{:S(2)}) collective-permute-start(bf16[64,512]{1,0:T(8,128)(2,1)S(1)} %get-tuple-element.28), channel_id=1, source_target_pairs={{0,12},{1,13},{4,8},{5,9},{8,4},{9,5},{12,0},{13,1},{2,14},{3,15},... | collective-permute-start | bytes 196616 | tf_op jit(solution)/shard_map/ppermute | solution.py:33
  7.6 5.6 %collective-permute-start.5 = (bf16[64,512]{1,0:T(8,128)(2,1)S(1)}, bf16[64,512]{1,0:T(8,128)(2,1)S(1)}, u32[]{:S(2)}, u32[]{:S(2)}) collective-permute-start(bf16[64,512]{1,0:T(8,128)(2,1)S(1)} %get-tuple-element.29), channel_id=1, source_target_pairs={{0,4},{1,5},{4,0},{5,1},{8,12},{9,13},{12,8},{13,9},{2,6},{3,7},{6... | collective-permute-start | bytes 196616 | tf_op jit(solution)/shard_map/ppermute | solution.py:33
  7.8 7.2 %collective-permute-start = (bf16[128,512]{1,0:T(8,128)(2,1)S(1)}, bf16[128,512]{1,0:T(8,128)(2,1)S(1)}, u32[]{:S(2)}, u32[]{:S(2)}) collective-permute-start(bf16[128,512]{1,0:T(8,128)(2,1)S(1)} %get-tuple-element.24), channel_id=1, source_target_pairs={{0,2},{2,0},{1,3},{3,1},{4,6},{6,4},{5,7},{7,5},{8,10},{10,8},{9,1... | collective-permute-start | bytes 393224 | tf_op jit(solution)/shard_map/ppermute | solution.py:26
  10.0 3.2 %copy-start.3 = (bf16[512,512]{1,0:T(8,128)(2,1)S(1)}, bf16[512,512]{1,0:T(8,128)(2,1)}, u32[]{:S(2)}) copy-start(bf16[512,512]{1,0:T(8,128)(2,1)} %refs_1_.5) | copy-start | bytes 1572868
  11.0 4.4 %collective-permute-start.2 = (bf16[64,512]{1,0:T(8,128)(2,1)S(1)}, bf16[64,512]{1,0:T(8,128)(2,1)S(1)}, u32[]{:S(2)}, u32[]{:S(2)}) collective-permute-start(bf16[64,512]{1,0:T(8,128)(2,1)S(1)} %shard_map.96), channel_id=1, source_target_pairs={{0,2},{2,0},{1,3},{3,1},{4,6},{6,4},{5,7},{7,5},{8,10},{10,8},{9,1... | collective-permute-start | bytes 196616 | tf_op jit(solution)/shard_map/ppermute | solution.py:26
  13.5 6.9 %collective-permute-start.7 = (f32[64,512]{1,0:T(8,128)S(1)}, f32[64,512]{1,0:T(8,128)S(1)}, u32[]{:S(2)}, u32[]{:S(2)}) collective-permute-start(f32[64,512]{1,0:T(8,128)S(1)} %shard_map.97.refs_4_.refs_1_), channel_id=1, source_target_pairs={{0,2},{2,0},{1,3},{3,1},{4,6},{6,4},{5,7},{7,5},{8,10},{10,8},{9,1... | collective-permute-start | bytes 393224 | tf_op jit(solution)/shard_map/ppermute | solution.py:26
  15.7 7.5 %collective-permute-start.10 = (bf16[1,64,512]{2,1,0:T(8,128)(2,1)S(1)}, bf16[1,64,512]{2,1,0:T(8,128)(2,1)S(1)}, u32[]{:S(2)}, u32[]{:S(2)}) collective-permute-start(bf16[1,64,512]{2,1,0:T(8,128)(2,1)S(1)} %get-tuple-element.31.refs_4_.refs_0_), channel_id=1, source_target_pairs={{0,8},{1,9},{4,12},{5,13},{8,0},{9,1},{12,4},{13,5},{2,10},{3,11},... | collective-permute-start | bytes 196616 | tf_op jit(solution)/shard_map/ppermute | solution.py:33
  18.5 6.3 %collective-permute-start.9 = (bf16[1,64,512]{2,1,0:T(8,128)(2,1)S(1)}, bf16[1,64,512]{2,1,0:T(8,128)(2,1)S(1)}, u32[]{:S(2)}, u32[]{:S(2)}) collective-permute-start(bf16[1,64,512]{2,1,0:T(8,128)(2,1)S(1)} %get-tuple-element.31.refs_4_.refs_0_), channel_id=1, source_target_pairs={{0,12},{1,13},{4,8},{5,9},{8,4},{9,5},{12,0},{13,1},{2,14},{3,15},... | collective-permute-start | bytes 196616 | tf_op jit(solution)/shard_map/ppermute | solution.py:33
  20.0 10.8 %collective-permute-start.6 = (bf16[384,512]{1,0:T(8,128)(2,1)S(1)}, bf16[384,512]{1,0:T(8,128)(2,1)S(1)}, u32[]{:S(2)}, u32[]{:S(2)}) collective-permute-start(bf16[384,512]{1,0:T(8,128)(2,1)S(1)} %get-tuple-element.30), channel_id=1, source_target_pairs={{0,2},{2,0},{1,3},{3,1},{4,6},{6,4},{5,7},{7,5},{8,10},{10,8},{9,1... | collective-permute-start | bytes 1179656 | tf_op jit(solution)/shard_map/ppermute | solution.py:26
  20.9 1.5 %collective-permute-start.11 = (f32[16,2560]{1,0:T(8,128)S(1)}, f32[16,2560]{1,0:T(8,128)S(1)}, u32[]{:S(2)}, u32[]{:S(2)}) collective-permute-start(f32[16,2560]{1,0:T(8,128)S(1)} %get-tuple-element.34), channel_id=1, source_target_pairs={{0,1},{1,0},{2,3},{3,2},{4,5},{5,4},{6,7},{7,6},{8,9},{9,8},{10,11... | collective-permute-start | bytes 491528 | tf_op jit(solution)/shard_map/ppermute | solution.py:26
  21.0 5.0 %collective-permute-start.8 = (bf16[1,64,512]{2,1,0:T(8,128)(2,1)S(1)}, bf16[1,64,512]{2,1,0:T(8,128)(2,1)S(1)}, u32[]{:S(2)}, u32[]{:S(2)}) collective-permute-start(bf16[1,64,512]{2,1,0:T(8,128)(2,1)S(1)} %shard_map.100), channel_id=1, source_target_pairs={{0,4},{1,5},{4,0},{5,1},{8,12},{9,13},{12,8},{13,9},{2,6},{3,7},{6... | collective-permute-start | bytes 196616 | tf_op jit(solution)/shard_map/ppermute | solution.py:33
  22.4 5.3 %collective-permute-start.14 = (bf16[16,2560]{1,0:T(8,128)(2,1)S(1)}, bf16[16,2560]{1,0:T(8,128)(2,1)S(1)}, u32[]{:S(2)}, u32[]{:S(2)}) collective-permute-start(bf16[16,2560]{1,0:T(8,128)(2,1)S(1)} %shard_map.101.refs_0_.refs_1_), channel_id=1, source_target_pairs={{0,4},{1,5},{4,0},{5,1},{8,12},{9,13},{12,8},{13,9},{2,6},{3,7},{6... | collective-permute-start | bytes 245768 | tf_op jit(solution)/shard_map/ppermute | solution.py:33
  23.2 4.5 %collective-permute-start.13 = (f32[16,2560]{1,0:T(8,128)S(1)}, f32[16,2560]{1,0:T(8,128)S(1)}, u32[]{:S(2)}, u32[]{:S(2)}) collective-permute-start(f32[16,2560]{1,0:T(8,128)S(1)} %shard_map.104), channel_id=1, source_target_pairs={{0,1},{1,0},{2,3},{3,2},{4,5},{5,4},{6,7},{7,6},{8,9},{9,8},{10,11... | collective-permute-start | bytes 491528 | tf_op jit(solution)/shard_map/ppermute | solution.py:26
  26.1 2.8 %collective-permute-start.12 = (bf16[4,64,512]{2,1,0:T(8,128)(2,1)S(1)}, bf16[4,64,512]{2,1,0:T(8,128)(2,1)S(1)}, u32[]{:S(2)}, u32[]{:S(2)}) collective-permute-start(bf16[4,64,512]{2,1,0:T(8,128)(2,1)S(1)} %shard_map.103.refs_3_.refs_1_), channel_id=1, source_target_pairs={{0,1},{1,0},{2,3},{3,2},{4,5},{5,4},{6,7},{7,6},{8,9},{9,8},{10,11... | collective-permute-start | bytes 786440 | tf_op jit(solution)/shard_map/ppermute | solution.py:26
  27.7 3.1 %copy-start.1 = (bf16[2560,512]{1,0:T(8,128)(2,1)S(1)}, bf16[2560,512]{1,0:T(8,128)(2,1)}, u32[]{:S(2)}) copy-start(bf16[2560,512]{1,0:T(8,128)(2,1)} %refs_1_.7) | copy-start | bytes 7864324
  27.7 6.2 %collective-permute-start.15 = (bf16[16,2560]{1,0:T(8,128)(2,1)S(1)}, bf16[16,2560]{1,0:T(8,128)(2,1)S(1)}, u32[]{:S(2)}, u32[]{:S(2)}) collective-permute-start(bf16[16,2560]{1,0:T(8,128)(2,1)S(1)} %shard_map.105.refs_4_.refs_0_), channel_id=1, source_target_pairs={{0,8},{1,9},{4,12},{5,13},{8,0},{9,1},{12,4},{13,5},{2,10},{3,11},... | collective-permute-start | bytes 245768 | tf_op jit(solution)/shard_map/ppermute | solution.py:33
  34.0 4.5 %collective-permute-start.16 = (bf16[16,2560]{1,0:T(8,128)(2,1)S(1)}, bf16[16,2560]{1,0:T(8,128)(2,1)S(1)}, u32[]{:S(2)}, u32[]{:S(2)}) collective-permute-start(bf16[16,2560]{1,0:T(8,128)(2,1)S(1)} %shard_map.109.refs_6_.refs_0_), channel_id=1, source_target_pairs={{0,4},{1,5},{4,0},{5,1},{8,12},{9,13},{12,8},{13,9},{2,6},{3,7},{6... | collective-permute-start | bytes 245768 | tf_op jit(solution)/shard_map/ppermute | solution.py:33
  38.5 1.5 %collective-permute-start.17 = (bf16[32,2560]{1,0:T(8,128)(2,1)S(1)}, bf16[32,2560]{1,0:T(8,128)(2,1)S(1)}, u32[]{:S(2)}, u32[]{:S(2)}) collective-permute-start(bf16[32,2560]{1,0:T(8,128)(2,1)S(1)} %shard_map.111.refs_0_.refs_1_), channel_id=1, source_target_pairs={{0,1},{1,0},{2,3},{3,2},{4,5},{5,4},{6,7},{7,6},{8,9},{9,8},{10,11... | collective-permute-start | bytes 491528 | tf_op jit(solution)/shard_map/ppermute | solution.py:26

commit v17 on v15

--- a/solution.py
+++ b/solution.py
@@ -468,7 +468,7 @@
 
     frozen_other = shift(frozen_value, "sub", 1)
     picked, early, away = pick_heads(adapter_ids, head_up, grad_output)
-    steps = sorted(own_steps, key=lambda step: (-step.bit_length(), step))
+    steps = sorted(own_steps, key=lambda step: -step)
     offered = [picked[0]] + [swap(picked[step], step, 0) for step in steps]
     early_grads = [shift(early, "tp", step) for step in tp_steps]
 

time: 40.7 us -> 41.5 us (1.020)
  starting transfers between devices: 17 us -> 18.2 us
    ppermute x9, starting transfers between devices: 12.2 us -> 13.8 us  [swap(): lax.ppermute(x, ('own', 'sub'), [(i, i ^ other) for i in range(whole)])]
    ppermute x8, waiting for transfers between devices: 3.2 us -> 2.39 us  [shift(): lax.ppermute(x, axis, [(i, (i + step) % count) for i in range(count)])]
    ppermute x9, waiting for transfers between devices: 5.54 us -> 6.06 us  [swap(): lax.ppermute(x, ('own', 'sub'), [(i, i ^ other) for i in range(whole)])]
    ppermute x8, starting transfers between devices: 4.81 us -> 4.38 us  [shift(): lax.ppermute(x, axis, [(i, (i + step) % count) for i in range(count)])]
where the time goes in v17:
time: 41.5 us; the launch traced here: 41.4 us
  starting transfers between devices  18.2 us (44%)
  Pallas kernels  13.2 us (32%)
  waiting for transfers between devices  8.45 us (20%)
  between operations  1.5 us (4%)
    ppermute x9, starting transfers between devices, swap(): lax.ppermute(x, ('own', 'sub'), [(i, i ^ other) for i in range(whole)])  13.8 us
    pallas_call x18, Pallas kernels, call(): pl.pallas_call(kernel, out_shape=outs, in_specs=list(specs) + [anywhere]...  13.2 us
    ppermute x9, waiting for transfers between devices, swap(): lax.ppermute(x, ('own', 'sub'), [(i, i ^ other) for i in range(whole)])  6.06 us
    ppermute x8, starting transfers between devices, shift(): lax.ppermute(x, axis, [(i, (i + step) % count) for i in range(count)])  4.38 us
    ppermute x8, waiting for transfers between devices, shift(): lax.ppermute(x, axis, [(i, (i + step) % count) for i in range(count)])  2.39 us
  transfers between devices with their start and end apart: 17, of which 9 were waited for; matrix products, arithmetic and copies ran while one was open for 0% of the time, Pallas kernels for 30%

profile of v17, /device:TPU:0, one launch (start us, length us, event | category | flops | bytes accessed | tf_op | source)
XLA Modules:
  0.0 41.4 jit_solution(14212594093012345191)
XLA Ops:
  0.7 0.5 %collective-permute-start.1 = (bf16[2560,512]{1,0:T(8,128)(2,1)}, bf16[2560,512]{1,0:T(8,128)(2,1)S(1)}, u32[]{:S(2)}, u32[]{:S(2)}) collective-permute-start(bf16[2560,512]{1,0:T(8,128)(2,1)} %refs_1_.7), channel_id=1, source_target_pairs={{0,1},{1,0},{2,3},{3,2},{4,5},{5,4},{6,7},{7,6},{8,9},{9,8},{10,11... | collective-permute-start | bytes 7864328 | tf_op jit(solution)/shard_map/ppermute | solution.py:26
  1.2 1.5 %shard_map.94 = (bf16[64,512]{1,0:T(8,128)(2,1)S(1)}, bf16[64,512]{1,0:T(8,128)(2,1)S(1)}, bf16[64,512]{1,0:T(8,128)(2,1)S(1)}, bf16[64,512]{1,0:T(8,128)(2,1)S(...) custom-call(s32[8]{0:T(128)} %refs_0_.8, bf16[16,64,512]{2,1,0:T(8,128)(2,1)} %refs_1_.4, bf16[512,512]{1,0:T(8,128)(2,1)} %refs_1_.5), custom_call_target="tpu_custom_call" | custom-call | flops 5000000000 | bytes 1970208 | tf_op jit(solution)/shard_map/pallas_call | solution.py:55
  2.7 4.6 %collective-permute-start.3 = (bf16[64,512]{1,0:T(8,128)(2,1)S(1)}, bf16[64,512]{1,0:T(8,128)(2,1)S(1)}, u32[]{:S(2)}, u32[]{:S(2)}) collective-permute-start(bf16[64,512]{1,0:T(8,128)(2,1)S(1)} %get-tuple-element.27), channel_id=1, source_target_pairs={{0,12},{1,13},{4,8},{5,9},{8,4},{9,5},{12,0},{13,1},{2,14},{3,15},... | collective-permute-start | bytes 196616 | tf_op jit(solution)/shard_map/ppermute | solution.py:33
  7.3 0.6 %collective-permute-start.5 = (bf16[64,512]{1,0:T(8,128)(2,1)S(1)}, bf16[64,512]{1,0:T(8,128)(2,1)S(1)}, u32[]{:S(2)}, u32[]{:S(2)}) collective-permute-start(bf16[64,512]{1,0:T(8,128)(2,1)S(1)} %get-tuple-element.29), channel_id=1, source_target_pairs={{0,4},{1,5},{4,0},{5,1},{8,12},{9,13},{12,8},{13,9},{2,6},{3,7},{6... | collective-permute-start | bytes 196616 | tf_op jit(solution)/shard_map/ppermute | solution.py:33
  7.9 1.6 %collective-permute-start = (bf16[128,512]{1,0:T(8,128)(2,1)S(1)}, bf16[128,512]{1,0:T(8,128)(2,1)S(1)}, u32[]{:S(2)}, u32[]{:S(2)}) collective-permute-start(bf16[128,512]{1,0:T(8,128)(2,1)S(1)} %get-tuple-element.24), channel_id=1, source_target_pairs={{0,2},{2,0},{1,3},{3,1},{4,6},{6,4},{5,7},{7,5},{8,10},{10,8},{9,1... | collective-permute-start | bytes 393224 | tf_op jit(solution)/shard_map/ppermute | solution.py:26
  10.2 0.9 %shard_map.95.refs_0_.refs_6_.refs_1_ = f32[64,512]{1,0:T(8,128)S(1)} custom-call(bf16[512,2560]{1,0:T(8,128)(2,1)S(1)} %copy-done, bf16[64,2560]{1,0:T(8,128)(2,1)S(1)} %bitcast.2, bf16[64,512]{1,0:T(8,128)(2,1)S(1)} %get-tuple-element.25.refs_2_.refs_1_), custom_call_target="tpu_custom_call" | custom-call | flops 167772160 | bytes 3080192 | tf_op jit(solution)/shard_map/pallas_call | solution.py:55
  11.6 1.7 %collective-permute-done.4.refs_3_ = bf16[64,512]{1,0:T(8,128)(2,1)S(1)} collective-permute-done((bf16[64,512]{1,0:T(8,128)(2,1)S(1)}, bf16[64,512]{1,0:T(8,128)(2,1)S(1)}, u32[]{:S(2)}, u32[]{:S(2)}) %collective-permute-start.4) | collective-permute-done | bytes 65568 | tf_op jit(solution)/shard_map/ppermute | solution.py:33
  13.7 1.6 %collective-permute-start.7 = (f32[64,512]{1,0:T(8,128)S(1)}, f32[64,512]{1,0:T(8,128)S(1)}, u32[]{:S(2)}, u32[]{:S(2)}) collective-permute-start(f32[64,512]{1,0:T(8,128)S(1)} %shard_map.97.refs_4_.refs_1_), channel_id=1, source_target_pairs={{0,2},{2,0},{1,3},{3,1},{4,6},{6,4},{5,7},{7,5},{8,10},{10,8},{9,1... | collective-permute-start | bytes 393224 | tf_op jit(solution)/shard_map/ppermute | solution.py:26
  15.8 4.2 %collective-permute-start.10 = (bf16[1,64,512]{2,1,0:T(8,128)(2,1)S(1)}, bf16[1,64,512]{2,1,0:T(8,128)(2,1)S(1)}, u32[]{:S(2)}, u32[]{:S(2)}) collective-permute-start(bf16[1,64,512]{2,1,0:T(8,128)(2,1)S(1)} %get-tuple-element.31.refs_4_.refs_0_), channel_id=1, source_target_pairs={{0,12},{1,13},{4,8},{5,9},{8,4},{9,5},{12,0},{13,1},{2,14},{3,15},... | collective-permute-start | bytes 196616 | tf_op jit(solution)/shard_map/ppermute | solution.py:33
  20.1 0.6 %shard_map.99 = (bf16[64,512]{1,0:T(8,128)(2,1)S(1)}, f32[32,2560]{1,0:T(8,128)S(1)}, f32[32,2560]{1,0:T(8,128)S(1)}) custom-call(s32[1]{0:T(128)S(6)} %copy.14.refs_0_, f32[64,512]{1,0:T(8,128)S(1)} %shard_map.97.refs_4_.refs_1_, f32[64,512]{1,0:T(8,128)S(1)} %collective-permute-done.7.refs_2_, bf16[512,2560]{1,0:T(8,128)(2,1)S(1)} %copy-done, ...), custom_call_target="tpu_custom_call" | custom-call | flops 167772160 | bytes 3604484 | tf_op jit(solution)/shard_map/pallas_call | solution.py:55
  20.8 0.9 %collective-permute-start.8 = (bf16[1,64,512]{2,1,0:T(8,128)(2,1)S(1)}, bf16[1,64,512]{2,1,0:T(8,128)(2,1)S(1)}, u32[]{:S(2)}, u32[]{:S(2)}) collective-permute-start(bf16[1,64,512]{2,1,0:T(8,128)(2,1)S(1)} %shard_map.100), channel_id=1, source_target_pairs={{0,4},{1,5},{4,0},{5,1},{8,12},{9,13},{12,8},{13,9},{2,6},{3,7},{6... | collective-permute-start | bytes 196616 | tf_op jit(solution)/shard_map/ppermute | solution.py:33
  21.7 0.7 %collective-permute-done.11.refs_1_ = f32[32,2560]{1,0:T(8,128)S(1)} collective-permute-done((f32[32,2560]{1,0:T(8,128)S(1)}, f32[32,2560]{1,0:T(8,128)S(1)}, u32[]{:S(2)}, u32[]{:S(2)}) %collective-permute-start.11) | collective-permute-done | bytes 327712 | tf_op jit(solution)/shard_map/ppermute | solution.py:26
  22.4 0.9 %collective-permute-start.13 = (bf16[16,2560]{1,0:T(8,128)(2,1)S(1)}, bf16[16,2560]{1,0:T(8,128)(2,1)S(1)}, u32[]{:S(2)}, u32[]{:S(2)}) collective-permute-start(bf16[16,2560]{1,0:T(8,128)(2,1)S(1)} %get-tuple-element.35.refs_0_), channel_id=1, source_target_pairs={{0,4},{1,5},{4,0},{5,1},{8,12},{9,13},{12,8},{13,9},{2,6},{3,7},{6... | collective-permute-start | bytes 245768 | tf_op jit(solution)/shard_map/ppermute | solution.py:33
  23.3 1.4 %shard_map.102 = (f32[16,64,512]{2,1,0:T(8,128)}, f32[8,128]{1,0:T(8,128)S(1)}) custom-call(bf16[16,2560]{1,0:T(8,128)(2,1)S(1)} %get-tuple-element.35.refs_0_), custom_call_target="tpu_custom_call" | custom-call | flops 10000000000 | bytes 2101248 | tf_op jit(solution)/shard_map/pallas_call | solution.py:55
  24.8 0.6 %collective-permute-done.9.refs_2_ = bf16[1,64,512]{2,1,0:T(8,128)(2,1)S(1)} collective-permute-done((bf16[1,64,512]{2,1,0:T(8,128)(2,1)S(1)}, bf16[1,64,512]{2,1,0:T(8,128)(2,1)S(1)}, u32[]{:S(2)}, u32[]{:S(2)}) %collective-permute-start.9) | collective-permute-done | bytes 65568 | tf_op jit(solution)/shard_map/ppermute | solution.py:33
  25.3 1.1 %collective-permute-done.8.refs_1_ = bf16[1,64,512]{2,1,0:T(8,128)(2,1)S(1)} collective-permute-done((bf16[1,64,512]{2,1,0:T(8,128)(2,1)S(1)}, bf16[1,64,512]{2,1,0:T(8,128)(2,1)S(1)}, u32[]{:S(2)}, u32[]{:S(2)}) %collective-permute-start.8) | collective-permute-done | bytes 65568 | tf_op jit(solution)/shard_map/ppermute | solution.py:33
  26.5 1.2 %collective-permute-done.13.refs_1_ = bf16[16,2560]{1,0:T(8,128)(2,1)S(1)} collective-permute-done((bf16[16,2560]{1,0:T(8,128)(2,1)S(1)}, bf16[16,2560]{1,0:T(8,128)(2,1)S(1)}, u32[]{:S(2)}, u32[]{:S(2)}) %collective-permute-start.13) | collective-permute-done | bytes 81952 | tf_op jit(solution)/shard_map/ppermute | solution.py:33
  27.8 2.3 %collective-permute-start.14 = (bf16[16,2560]{1,0:T(8,128)(2,1)S(1)}, bf16[16,2560]{1,0:T(8,128)(2,1)S(1)}, u32[]{:S(2)}, u32[]{:S(2)}) collective-permute-start(bf16[16,2560]{1,0:T(8,128)(2,1)S(1)} %shard_map.104.refs_4_.refs_0_), channel_id=1, source_target_pairs={{0,8},{1,9},{4,12},{5,13},{8,0},{9,1},{12,4},{13,5},{2,10},{3,11},... | collective-permute-start | bytes 245768 | tf_op jit(solution)/shard_map/ppermute | solution.py:33
  30.0 1.6 %shard_map.105 = (f32[16,64,512]{2,1,0:T(8,128)}, f32[8,128]{1,0:T(8,128)S(1)}) custom-call(s32[8]{0:T(128)} %refs_0_.8, bf16[4,64,512]{2,1,0:T(8,128)(2,1)S(1)} %shard_map.103.refs_2_.refs_1_, bf16[4,64,512]{2,1,0:T(8,128)(2,1)S(1)} %collective-permute-done.12.refs_2_, f32[16,64,512]{2,1,0:T(8,128)} %get-tuple-element.37.refs_3_, ...), custom_call_target="tpu_custom_call", output_to_operand_aliasing={{0}: (3, {})} | custom-call | bytes 4722720 | tf_op jit(solution)/shard_map/pallas_call | solution.py:55
  31.8 2.4 %shard_map.107 = (bf16[512,2560]{1,0:T(8,128)(2,1)}, f32[8,128]{1,0:T(8,128)S(1)}) custom-call(bf16[512,1024]{1,0:T(8,128)(2,1)S(1)} %shard_map.106.refs_0_, bf16[2560,512]{1,0:T(8,128)(2,1)S(1)} %copy-done.1, bf16[2560,512]{1,0:T(8,128)(2,1)S(1)} %collective-permute-done.1.refs_1_.refs_2_, bf16[64,512]{1,0:T(8,128)(2,1)S(1)} %get-tuple-element.32.refs_1_.refs_2_.refs_3_, ...), custom_call_target="tpu_custom_call" | custom-call | flops 1140850688 | bytes 9310208 | tf_op jit(solution)/shard_map/pallas_call | solution.py:55
  34.7 3.1 %shard_map.109 = (bf16[512,2560]{1,0:T(8,128)(2,1)}, f32[8,128]{1,0:T(8,128)S(1)}) custom-call(bf16[512,1024]{1,0:T(8,128)(2,1)S(1)} %shard_map.106.refs_0_, bf16[2560,512]{1,0:T(8,128)(2,1)S(1)} %copy-done.1, bf16[2560,512]{1,0:T(8,128)(2,1)S(1)} %collective-permute-done.1.refs_1_.refs_2_, ...), custom_call_target="tpu_custom_call", output_to_operand_aliasing={{0}: (5, {})} | custom-call | flops 1711276032 | bytes 11931648 | tf_op jit(solution)/shard_map/pallas_call | solution.py:55
  37.8 1.2 %collective-permute-done.15.refs_1_ = bf16[16,2560]{1,0:T(8,128)(2,1)S(1)} collective-permute-done((bf16[16,2560]{1,0:T(8,128)(2,1)S(1)}, bf16[16,2560]{1,0:T(8,128)(2,1)S(1)}, u32[]{:S(2)}, u32[]{:S(2)}) %collective-permute-start.15) | collective-permute-done | bytes 81952 | tf_op jit(solution)/shard_map/ppermute | solution.py:33
  39.1 1.4 %collective-permute-done.16.refs_1_ = bf16[32,2560]{1,0:T(8,128)(2,1)S(1)} collective-permute-done((bf16[32,2560]{1,0:T(8,128)(2,1)S(1)}, bf16[32,2560]{1,0:T(8,128)(2,1)S(1)}, u32[]{:S(2)}, u32[]{:S(2)}) %collective-permute-start.16) | collective-permute-done | bytes 163872 | tf_op jit(solution)/shard_map/ppermute | solution.py:26
  40.5 0.9 %shard_map.111 = f32[64,2560]{1,0:T(8,128)} custom-call(bf16[32,2560]{1,0:T(8,128)(2,1)S(1)} %shard_map.110.refs_0_.refs_2_, bf16[32,2560]{1,0:T(8,128)(2,1)S(1)} %collective-permute-done.16.refs_1_, bf16[32,2560]{1,0:T(8,128)(2,1)S(1)} %shard_map.110.refs_0_.refs_2_), custom_call_target="tpu_custom_call" | custom-call | bytes 983040 | tf_op jit(solution)/shard_map/pallas_call | solution.py:55
  (36 shorter events, 2.4 us)
Async XLA Ops:
  0.6 9.6 %copy-start = (bf16[512,2560]{1,0:T(8,128)(2,1)S(1)}, bf16[512,2560]{1,0:T(8,128)(2,1)}, u32[]{:S(2)}) copy-start(bf16[512,2560]{1,0:T(8,128)(2,1)} %refs_3_.3) | copy-start | bytes 7864324
  0.6 9.6 %copy-start.2 = (bf16[2560,64]{0,1:T(8,128)(2,1)S(1)}, bf16[2560,64]{0,1:T(8,128)(2,1)}, u32[]{:S(2)}) copy-start(bf16[2560,64]{0,1:T(8,128)(2,1)} %param.10) | copy-start | bytes 983044
  0.7 10.5 %collective-permute-start.1 = (bf16[2560,512]{1,0:T(8,128)(2,1)}, bf16[2560,512]{1,0:T(8,128)(2,1)S(1)}, u32[]{:S(2)}, u32[]{:S(2)}) collective-permute-start(bf16[2560,512]{1,0:T(8,128)(2,1)} %refs_1_.7), channel_id=1, source_target_pairs={{0,1},{1,0},{2,3},{3,2},{4,5},{5,4},{6,7},{7,6},{8,9},{9,8},{10,11... | collective-permute-start | bytes 7864328 | tf_op jit(solution)/shard_map/ppermute | solution.py:26
  2.7 8.9 %collective-permute-start.3 = (bf16[64,512]{1,0:T(8,128)(2,1)S(1)}, bf16[64,512]{1,0:T(8,128)(2,1)S(1)}, u32[]{:S(2)}, u32[]{:S(2)}) collective-permute-start(bf16[64,512]{1,0:T(8,128)(2,1)S(1)} %get-tuple-element.27), channel_id=1, source_target_pairs={{0,12},{1,13},{4,8},{5,9},{8,4},{9,5},{12,0},{13,1},{2,14},{3,15},... | collective-permute-start | bytes 196616 | tf_op jit(solution)/shard_map/ppermute | solution.py:33
  7.3 6.1 %collective-permute-start.4 = (bf16[64,512]{1,0:T(8,128)(2,1)S(1)}, bf16[64,512]{1,0:T(8,128)(2,1)S(1)}, u32[]{:S(2)}, u32[]{:S(2)}) collective-permute-start(bf16[64,512]{1,0:T(8,128)(2,1)S(1)} %get-tuple-element.28), channel_id=1, source_target_pairs={{0,8},{1,9},{4,12},{5,13},{8,0},{9,1},{12,4},{13,5},{2,10},{3,11},... | collective-permute-start | bytes 196616 | tf_op jit(solution)/shard_map/ppermute | solution.py:33
  7.3 6.1 %collective-permute-start.5 = (bf16[64,512]{1,0:T(8,128)(2,1)S(1)}, bf16[64,512]{1,0:T(8,128)(2,1)S(1)}, u32[]{:S(2)}, u32[]{:S(2)}) collective-permute-start(bf16[64,512]{1,0:T(8,128)(2,1)S(1)} %get-tuple-element.29), channel_id=1, source_target_pairs={{0,4},{1,5},{4,0},{5,1},{8,12},{9,13},{12,8},{13,9},{2,6},{3,7},{6... | collective-permute-start | bytes 196616 | tf_op jit(solution)/shard_map/ppermute | solution.py:33
  7.9 7.3 %collective-permute-start = (bf16[128,512]{1,0:T(8,128)(2,1)S(1)}, bf16[128,512]{1,0:T(8,128)(2,1)S(1)}, u32[]{:S(2)}, u32[]{:S(2)}) collective-permute-start(bf16[128,512]{1,0:T(8,128)(2,1)S(1)} %get-tuple-element.24), channel_id=1, source_target_pairs={{0,2},{2,0},{1,3},{3,1},{4,6},{6,4},{5,7},{7,5},{8,10},{10,8},{9,1... | collective-permute-start | bytes 393224 | tf_op jit(solution)/shard_map/ppermute | solution.py:26
  10.2 3.1 %copy-start.3 = (bf16[512,512]{1,0:T(8,128)(2,1)S(1)}, bf16[512,512]{1,0:T(8,128)(2,1)}, u32[]{:S(2)}) copy-start(bf16[512,512]{1,0:T(8,128)(2,1)} %refs_1_.5) | copy-start | bytes 1572868
  11.2 4.3 %collective-permute-start.2 = (bf16[64,512]{1,0:T(8,128)(2,1)S(1)}, bf16[64,512]{1,0:T(8,128)(2,1)S(1)}, u32[]{:S(2)}, u32[]{:S(2)}) collective-permute-start(bf16[64,512]{1,0:T(8,128)(2,1)S(1)} %shard_map.96), channel_id=1, source_target_pairs={{0,2},{2,0},{1,3},{3,1},{4,6},{6,4},{5,7},{7,5},{8,10},{10,8},{9,1... | collective-permute-start | bytes 196616 | tf_op jit(solution)/shard_map/ppermute | solution.py:26
  13.7 6.4 %collective-permute-start.7 = (f32[64,512]{1,0:T(8,128)S(1)}, f32[64,512]{1,0:T(8,128)S(1)}, u32[]{:S(2)}, u32[]{:S(2)}) collective-permute-start(f32[64,512]{1,0:T(8,128)S(1)} %shard_map.97.refs_4_.refs_1_), channel_id=1, source_target_pairs={{0,2},{2,0},{1,3},{3,1},{4,6},{6,4},{5,7},{7,5},{8,10},{10,8},{9,1... | collective-permute-start | bytes 393224 | tf_op jit(solution)/shard_map/ppermute | solution.py:26
  15.8 9.0 %collective-permute-start.10 = (bf16[1,64,512]{2,1,0:T(8,128)(2,1)S(1)}, bf16[1,64,512]{2,1,0:T(8,128)(2,1)S(1)}, u32[]{:S(2)}, u32[]{:S(2)}) collective-permute-start(bf16[1,64,512]{2,1,0:T(8,128)(2,1)S(1)} %get-tuple-element.31.refs_4_.refs_0_), channel_id=1, source_target_pairs={{0,12},{1,13},{4,8},{5,9},{8,4},{9,5},{12,0},{13,1},{2,14},{3,15},... | collective-permute-start | bytes 196616 | tf_op jit(solution)/shard_map/ppermute | solution.py:33
  20.1 5.3 %collective-permute-start.9 = (bf16[1,64,512]{2,1,0:T(8,128)(2,1)S(1)}, bf16[1,64,512]{2,1,0:T(8,128)(2,1)S(1)}, u32[]{:S(2)}, u32[]{:S(2)}) collective-permute-start(bf16[1,64,512]{2,1,0:T(8,128)(2,1)S(1)} %get-tuple-element.31.refs_4_.refs_0_), channel_id=1, source_target_pairs={{0,8},{1,9},{4,12},{5,13},{8,0},{9,1},{12,4},{13,5},{2,10},{3,11},... | collective-permute-start | bytes 196616 | tf_op jit(solution)/shard_map/ppermute | solution.py:33
  20.1 11.6 %collective-permute-start.6 = (bf16[384,512]{1,0:T(8,128)(2,1)S(1)}, bf16[384,512]{1,0:T(8,128)(2,1)S(1)}, u32[]{:S(2)}, u32[]{:S(2)}) collective-permute-start(bf16[384,512]{1,0:T(8,128)(2,1)S(1)} %get-tuple-element.30), channel_id=1, source_target_pairs={{0,2},{2,0},{1,3},{3,1},{4,6},{6,4},{5,7},{7,5},{8,10},{10,8},{9,1... | collective-permute-start | bytes 1179656 | tf_op jit(solution)/shard_map/ppermute | solution.py:26
  20.7 1.7 %collective-permute-start.11 = (f32[32,2560]{1,0:T(8,128)S(1)}, f32[32,2560]{1,0:T(8,128)S(1)}, u32[]{:S(2)}, u32[]{:S(2)}) collective-permute-start(f32[32,2560]{1,0:T(8,128)S(1)} %get-tuple-element.34), channel_id=1, source_target_pairs={{0,1},{1,0},{2,3},{3,2},{4,5},{5,4},{6,7},{7,6},{8,9},{9,8},{10,11... | collective-permute-start | bytes 983048 | tf_op jit(solution)/shard_map/ppermute | solution.py:26
  20.8 5.7 %collective-permute-start.8 = (bf16[1,64,512]{2,1,0:T(8,128)(2,1)S(1)}, bf16[1,64,512]{2,1,0:T(8,128)(2,1)S(1)}, u32[]{:S(2)}, u32[]{:S(2)}) collective-permute-start(bf16[1,64,512]{2,1,0:T(8,128)(2,1)S(1)} %shard_map.100), channel_id=1, source_target_pairs={{0,4},{1,5},{4,0},{5,1},{8,12},{9,13},{12,8},{13,9},{2,6},{3,7},{6... | collective-permute-start | bytes 196616 | tf_op jit(solution)/shard_map/ppermute | solution.py:33
  22.4 5.3 %collective-permute-start.13 = (bf16[16,2560]{1,0:T(8,128)(2,1)S(1)}, bf16[16,2560]{1,0:T(8,128)(2,1)S(1)}, u32[]{:S(2)}, u32[]{:S(2)}) collective-permute-start(bf16[16,2560]{1,0:T(8,128)(2,1)S(1)} %get-tuple-element.35.refs_0_), channel_id=1, source_target_pairs={{0,4},{1,5},{4,0},{5,1},{8,12},{9,13},{12,8},{13,9},{2,6},{3,7},{6... | collective-permute-start | bytes 245768 | tf_op jit(solution)/shard_map/ppermute | solution.py:33
  26.5 3.6 %collective-permute-start.12 = (bf16[4,64,512]{2,1,0:T(8,128)(2,1)S(1)}, bf16[4,64,512]{2,1,0:T(8,128)(2,1)S(1)}, u32[]{:S(2)}, u32[]{:S(2)}) collective-permute-start(bf16[4,64,512]{2,1,0:T(8,128)(2,1)S(1)} %shard_map.103.refs_2_.refs_1_), channel_id=1, source_target_pairs={{0,1},{1,0},{2,3},{3,2},{4,5},{5,4},{6,7},{7,6},{8,9},{9,8},{10,11... | collective-permute-start | bytes 786440 | tf_op jit(solution)/shard_map/ppermute | solution.py:26
  27.8 4.0 %copy-start.1 = (bf16[2560,512]{1,0:T(8,128)(2,1)S(1)}, bf16[2560,512]{1,0:T(8,128)(2,1)}, u32[]{:S(2)}) copy-start(bf16[2560,512]{1,0:T(8,128)(2,1)} %refs_1_.7) | copy-start | bytes 7864324
  27.8 6.7 %collective-permute-start.14 = (bf16[16,2560]{1,0:T(8,128)(2,1)S(1)}, bf16[16,2560]{1,0:T(8,128)(2,1)S(1)}, u32[]{:S(2)}, u32[]{:S(2)}) collective-permute-start(bf16[16,2560]{1,0:T(8,128)(2,1)S(1)} %shard_map.104.refs_4_.refs_0_), channel_id=1, source_target_pairs={{0,8},{1,9},{4,12},{5,13},{8,0},{9,1},{12,4},{13,5},{2,10},{3,11},... | collective-permute-start | bytes 245768 | tf_op jit(solution)/shard_map/ppermute | solution.py:33
  34.5 4.5 %collective-permute-start.15 = (bf16[16,2560]{1,0:T(8,128)(2,1)S(1)}, bf16[16,2560]{1,0:T(8,128)(2,1)S(1)}, u32[]{:S(2)}, u32[]{:S(2)}) collective-permute-start(bf16[16,2560]{1,0:T(8,128)(2,1)S(1)} %shard_map.108.refs_6_.refs_0_), channel_id=1, source_target_pairs={{0,4},{1,5},{4,0},{5,1},{8,12},{9,13},{12,8},{13,9},{2,6},{3,7},{6... | collective-permute-start | bytes 245768 | tf_op jit(solution)/shard_map/ppermute | solution.py:33
  39.0 1.5 %collective-permute-start.16 = (bf16[32,2560]{1,0:T(8,128)(2,1)S(1)}, bf16[32,2560]{1,0:T(8,128)(2,1)S(1)}, u32[]{:S(2)}, u32[]{:S(2)}) collective-permute-start(bf16[32,2560]{1,0:T(8,128)(2,1)S(1)} %shard_map.110.refs_0_.refs_2_), channel_id=1, source_target_pairs={{0,1},{1,0},{2,3},{3,2},{4,5},{5,4},{6,7},{7,6},{8,9},{9,8},{10,11... | collective-permute-start | bytes 491528 | tf_op jit(solution)/shard_map/ppermute | solution.py:26

commit v18 on v15

--- a/solution.py
+++ b/solution.py
@@ -485,7 +485,7 @@
     back, keep, send = shared_terms(lengths, parts, tokens, scale, [near])
     pieces = [keep, shift(send, "sub", 1)]
     met = stack([near], [back], flops=middling)
-    terms = [near] + [swap(met if step == 1 else near, step, 0) for step in steps[::-1]]
+    terms = [near] + [swap(met if step == own_count - 1 else near, step, 0) for step in steps[::-1]]
 
     bits = [1 << i for i in range(own_count.bit_length() - 1)]
     mark = back

time: 40.7 us -> 42.6 us (1.047)
  waiting for transfers between devices: 8.74 us -> 10.3 us
    ppermute x9, waiting for transfers between devices: 5.54 us -> 8.57 us  [swap(): lax.ppermute(x, ('own', 'sub'), [(i, i ^ other) for i in range(whole)])]
    ppermute x8, waiting for transfers between devices: 3.2 us -> 1.69 us  [shift(): lax.ppermute(x, axis, [(i, (i + step) % count) for i in range(count)])]
  transfers between devices with their start and end apart: 17 -> 17, of which waited for: 9 -> 8; matrix products, arithmetic and copies ran while one was open for 0% -> 0% of each run, Pallas kernels for 30% -> 29%
where the time goes in v18:
time: 42.6 us; the launch traced here: 42.5 us
  starting transfers between devices  17.3 us (41%)
  Pallas kernels  13.4 us (31%)
  waiting for transfers between devices  10.3 us (24%)
  between operations  1.51 us (4%)
    pallas_call x18, Pallas kernels, call(): pl.pallas_call(kernel, out_shape=outs, in_specs=list(specs) + [anywhere]...  13.4 us
    ppermute x9, starting transfers between devices, swap(): lax.ppermute(x, ('own', 'sub'), [(i, i ^ other) for i in range(whole)])  12.4 us
    ppermute x9, waiting for transfers between devices, swap(): lax.ppermute(x, ('own', 'sub'), [(i, i ^ other) for i in range(whole)])  8.57 us
    ppermute x8, starting transfers between devices, shift(): lax.ppermute(x, axis, [(i, (i + step) % count) for i in range(count)])  4.96 us
    ppermute x8, waiting for transfers between devices, shift(): lax.ppermute(x, axis, [(i, (i + step) % count) for i in range(count)])  1.69 us
  transfers between devices with their start and end apart: 17, of which 8 were waited for; matrix products, arithmetic and copies ran while one was open for 0% of the time, Pallas kernels for 29%

profile of v18, /device:TPU:0, one launch (start us, length us, event | category | flops | bytes accessed | tf_op | source)
XLA Modules:
  0.0 42.5 jit_solution(16634800057336641088)
XLA Ops:
  1.2 1.5 %shard_map.94 = (bf16[64,512]{1,0:T(8,128)(2,1)S(1)}, bf16[64,512]{1,0:T(8,128)(2,1)S(1)}, bf16[64,512]{1,0:T(8,128)(2,1)S(1)}, bf16[64,512]{1,0:T(8,128)(2,1)S(...) custom-call(s32[8]{0:T(128)} %refs_0_.8, bf16[16,64,512]{2,1,0:T(8,128)(2,1)} %refs_1_.4, bf16[512,512]{1,0:T(8,128)(2,1)} %refs_1_.5), custom_call_target="tpu_custom_call" | custom-call | flops 5000000000 | bytes 1970208 | tf_op jit(solution)/shard_map/pallas_call | solution.py:55
  2.7 3.6 %collective-permute-start.3 = (bf16[64,512]{1,0:T(8,128)(2,1)S(1)}, bf16[64,512]{1,0:T(8,128)(2,1)S(1)}, u32[]{:S(2)}, u32[]{:S(2)}) collective-permute-start(bf16[64,512]{1,0:T(8,128)(2,1)S(1)} %get-tuple-element.27), channel_id=1, source_target_pairs={{0,8},{1,9},{4,12},{5,13},{8,0},{9,1},{12,4},{13,5},{2,10},{3,11},... | collective-permute-start | bytes 196616 | tf_op jit(solution)/shard_map/ppermute | solution.py:33
  6.3 1.3 %collective-permute-start.4 = (bf16[64,512]{1,0:T(8,128)(2,1)S(1)}, bf16[64,512]{1,0:T(8,128)(2,1)S(1)}, u32[]{:S(2)}, u32[]{:S(2)}) collective-permute-start(bf16[64,512]{1,0:T(8,128)(2,1)S(1)} %get-tuple-element.28), channel_id=1, source_target_pairs={{0,12},{1,13},{4,8},{5,9},{8,4},{9,5},{12,0},{13,1},{2,14},{3,15},... | collective-permute-start | bytes 196616 | tf_op jit(solution)/shard_map/ppermute | solution.py:33
  7.8 1.5 %collective-permute-start = (bf16[128,512]{1,0:T(8,128)(2,1)S(1)}, bf16[128,512]{1,0:T(8,128)(2,1)S(1)}, u32[]{:S(2)}, u32[]{:S(2)}) collective-permute-start(bf16[128,512]{1,0:T(8,128)(2,1)S(1)} %get-tuple-element.24), channel_id=1, source_target_pairs={{0,2},{2,0},{1,3},{3,1},{4,6},{6,4},{5,7},{7,5},{8,10},{10,8},{9,1... | collective-permute-start | bytes 393224 | tf_op jit(solution)/shard_map/ppermute | solution.py:26
  10.0 0.9 %shard_map.95.refs_0_.refs_6_.refs_1_ = f32[64,512]{1,0:T(8,128)S(1)} custom-call(bf16[512,2560]{1,0:T(8,128)(2,1)S(1)} %copy-done, bf16[64,2560]{1,0:T(8,128)(2,1)S(1)} %bitcast.2, bf16[64,512]{1,0:T(8,128)(2,1)S(1)} %get-tuple-element.25.refs_2_.refs_1_), custom_call_target="tpu_custom_call" | custom-call | flops 167772160 | bytes 3080192 | tf_op jit(solution)/shard_map/pallas_call | solution.py:55
  11.0 0.6 %collective-permute-start.2 = (bf16[64,512]{1,0:T(8,128)(2,1)S(1)}, bf16[64,512]{1,0:T(8,128)(2,1)S(1)}, u32[]{:S(2)}, u32[]{:S(2)}) collective-permute-start(bf16[64,512]{1,0:T(8,128)(2,1)S(1)} %shard_map.96), channel_id=1, source_target_pairs={{0,2},{2,0},{1,3},{3,1},{4,6},{6,4},{5,7},{7,5},{8,10},{10,8},{9,1... | collective-permute-start | bytes 196616 | tf_op jit(solution)/shard_map/ppermute | solution.py:26
  11.6 1.4 %collective-permute-done.4.refs_3_ = bf16[64,512]{1,0:T(8,128)(2,1)S(1)} collective-permute-done((bf16[64,512]{1,0:T(8,128)(2,1)S(1)}, bf16[64,512]{1,0:T(8,128)(2,1)S(1)}, u32[]{:S(2)}, u32[]{:S(2)}) %collective-permute-start.4) | collective-permute-done | bytes 65568 | tf_op jit(solution)/shard_map/ppermute | solution.py:33
  13.5 1.6 %collective-permute-start.8 = (f32[64,512]{1,0:T(8,128)S(1)}, f32[64,512]{1,0:T(8,128)S(1)}, u32[]{:S(2)}, u32[]{:S(2)}) collective-permute-start(f32[64,512]{1,0:T(8,128)S(1)} %shard_map.97.refs_4_.refs_1_), channel_id=1, source_target_pairs={{0,2},{2,0},{1,3},{3,1},{4,6},{6,4},{5,7},{7,5},{8,10},{10,8},{9,1... | collective-permute-start | bytes 393224 | tf_op jit(solution)/shard_map/ppermute | solution.py:26
  15.7 2.8 %collective-permute-start.10 = (bf16[1,64,512]{2,1,0:T(8,128)(2,1)S(1)}, bf16[1,64,512]{2,1,0:T(8,128)(2,1)S(1)}, u32[]{:S(2)}, u32[]{:S(2)}) collective-permute-start(bf16[1,64,512]{2,1,0:T(8,128)(2,1)S(1)} %get-tuple-element.31.refs_4_.refs_0_), channel_id=1, source_target_pairs={{0,8},{1,9},{4,12},{5,13},{8,0},{9,1},{12,4},{13,5},{2,10},{3,11},... | collective-permute-start | bytes 196616 | tf_op jit(solution)/shard_map/ppermute | solution.py:33
  18.5 0.9 %collective-permute-start.7 = (bf16[1,64,512]{2,1,0:T(8,128)(2,1)S(1)}, bf16[1,64,512]{2,1,0:T(8,128)(2,1)S(1)}, u32[]{:S(2)}, u32[]{:S(2)}) collective-permute-start(bf16[1,64,512]{2,1,0:T(8,128)(2,1)S(1)} %get-tuple-element.31.refs_4_.refs_0_), channel_id=1, source_target_pairs={{0,4},{1,5},{4,0},{5,1},{8,12},{9,13},{12,8},{13,9},{2,6},{3,7},{6... | collective-permute-start | bytes 196616 | tf_op jit(solution)/shard_map/ppermute | solution.py:33
  19.3 0.5 %collective-permute-start.6 = (bf16[384,512]{1,0:T(8,128)(2,1)S(1)}, bf16[384,512]{1,0:T(8,128)(2,1)S(1)}, u32[]{:S(2)}, u32[]{:S(2)}) collective-permute-start(bf16[384,512]{1,0:T(8,128)(2,1)S(1)} %get-tuple-element.30), channel_id=1, source_target_pairs={{0,2},{2,0},{1,3},{3,1},{4,6},{6,4},{5,7},{7,5},{8,10},{10,8},{9,1... | collective-permute-start | bytes 1179656 | tf_op jit(solution)/shard_map/ppermute | solution.py:26
  19.9 0.6 %shard_map.99 = (bf16[64,512]{1,0:T(8,128)(2,1)S(1)}, f32[32,2560]{1,0:T(8,128)S(1)}, f32[32,2560]{1,0:T(8,128)S(1)}) custom-call(s32[1]{0:T(128)S(6)} %copy.14.refs_0_, f32[64,512]{1,0:T(8,128)S(1)} %shard_map.97.refs_4_.refs_1_, f32[64,512]{1,0:T(8,128)S(1)} %collective-permute-done.8.refs_2_, bf16[512,2560]{1,0:T(8,128)(2,1)S(1)} %copy-done, ...), custom_call_target="tpu_custom_call" | custom-call | flops 167772160 | bytes 3604484 | tf_op jit(solution)/shard_map/pallas_call | solution.py:55
  20.6 2.6 %collective-permute-start.9 = (bf16[1,64,512]{2,1,0:T(8,128)(2,1)S(1)}, bf16[1,64,512]{2,1,0:T(8,128)(2,1)S(1)}, u32[]{:S(2)}, u32[]{:S(2)}) collective-permute-start(bf16[1,64,512]{2,1,0:T(8,128)(2,1)S(1)} %shard_map.100), channel_id=1, source_target_pairs={{0,12},{1,13},{4,8},{5,9},{8,4},{9,5},{12,0},{13,1},{2,14},{3,15},... | collective-permute-start | bytes 196616 | tf_op jit(solution)/shard_map/ppermute | solution.py:33
  23.5 1.4 %shard_map.102 = (f32[16,64,512]{2,1,0:T(8,128)}, f32[8,128]{1,0:T(8,128)S(1)}) custom-call(bf16[16,2560]{1,0:T(8,128)(2,1)S(1)} %get-tuple-element.35.refs_0_), custom_call_target="tpu_custom_call" | custom-call | flops 10000000000 | bytes 2101248 | tf_op jit(solution)/shard_map/pallas_call | solution.py:55
  25.0 2.1 %collective-permute-done.9.refs_2_ = bf16[1,64,512]{2,1,0:T(8,128)(2,1)S(1)} collective-permute-done((bf16[1,64,512]{2,1,0:T(8,128)(2,1)S(1)}, bf16[1,64,512]{2,1,0:T(8,128)(2,1)S(1)}, u32[]{:S(2)}, u32[]{:S(2)}) %collective-permute-start.9) | collective-permute-done | bytes 65568 | tf_op jit(solution)/shard_map/ppermute | solution.py:33
  27.3 1.4 %collective-permute-done.13.refs_1_ = bf16[16,2560]{1,0:T(8,128)(2,1)S(1)} collective-permute-done((bf16[16,2560]{1,0:T(8,128)(2,1)S(1)}, bf16[16,2560]{1,0:T(8,128)(2,1)S(1)}, u32[]{:S(2)}, u32[]{:S(2)}) %collective-permute-start.13) | collective-permute-done | bytes 81952 | tf_op jit(solution)/shard_map/ppermute | solution.py:33
  28.7 0.6 %collective-permute-start.14 = (bf16[16,2560]{1,0:T(8,128)(2,1)S(1)}, bf16[16,2560]{1,0:T(8,128)(2,1)S(1)}, u32[]{:S(2)}, u32[]{:S(2)}) collective-permute-start(bf16[16,2560]{1,0:T(8,128)(2,1)S(1)} %shard_map.104.refs_4_.refs_0_), channel_id=1, source_target_pairs={{0,8},{1,9},{4,12},{5,13},{8,0},{9,1},{12,4},{13,5},{2,10},{3,11},... | collective-permute-start | bytes 245768 | tf_op jit(solution)/shard_map/ppermute | solution.py:33
  29.3 1.7 %shard_map.105 = (f32[16,64,512]{2,1,0:T(8,128)}, f32[8,128]{1,0:T(8,128)S(1)}) custom-call(s32[8]{0:T(128)} %refs_0_.8, bf16[4,64,512]{2,1,0:T(8,128)(2,1)S(1)} %shard_map.103.refs_2_.refs_1_, bf16[4,64,512]{2,1,0:T(8,128)(2,1)S(1)} %collective-permute-done.12.refs_2_, f32[16,64,512]{2,1,0:T(8,128)} %get-tuple-element.37.refs_3_, ...), custom_call_target="tpu_custom_call", output_to_operand_aliasing={{0}: (3, {})} | custom-call | bytes 4722720 | tf_op jit(solution)/shard_map/pallas_call | solution.py:55
  31.2 2.4 %shard_map.107 = (bf16[512,2560]{1,0:T(8,128)(2,1)}, f32[8,128]{1,0:T(8,128)S(1)}) custom-call(bf16[512,1024]{1,0:T(8,128)(2,1)S(1)} %shard_map.106.refs_0_, bf16[2560,512]{1,0:T(8,128)(2,1)S(1)} %copy-done.1, bf16[2560,512]{1,0:T(8,128)(2,1)S(1)} %collective-permute-done.1.refs_1_.refs_2_, bf16[64,512]{1,0:T(8,128)(2,1)S(1)} %get-tuple-element.32.refs_1_.refs_2_.refs_3_, ...), custom_call_target="tpu_custom_call" | custom-call | flops 1140850688 | bytes 9310208 | tf_op jit(solution)/shard_map/pallas_call | solution.py:55
  33.5 2.0 %collective-permute-done.14.refs_1_ = bf16[16,2560]{1,0:T(8,128)(2,1)S(1)} collective-permute-done((bf16[16,2560]{1,0:T(8,128)(2,1)S(1)}, bf16[16,2560]{1,0:T(8,128)(2,1)S(1)}, u32[]{:S(2)}, u32[]{:S(2)}) %collective-permute-start.14) | collective-permute-done | bytes 81952 | tf_op jit(solution)/shard_map/ppermute | solution.py:33
  35.6 3.1 %shard_map.109 = (bf16[512,2560]{1,0:T(8,128)(2,1)}, f32[8,128]{1,0:T(8,128)S(1)}) custom-call(bf16[512,1024]{1,0:T(8,128)(2,1)S(1)} %shard_map.106.refs_0_, bf16[2560,512]{1,0:T(8,128)(2,1)S(1)} %copy-done.1, bf16[2560,512]{1,0:T(8,128)(2,1)S(1)} %collective-permute-done.1.refs_1_.refs_2_, ...), custom_call_target="tpu_custom_call", output_to_operand_aliasing={{0}: (5, {})} | custom-call | flops 1711276032 | bytes 11931648 | tf_op jit(solution)/shard_map/pallas_call | solution.py:55
  38.7 1.4 %collective-permute-done.15.refs_1_ = bf16[16,2560]{1,0:T(8,128)(2,1)S(1)} collective-permute-done((bf16[16,2560]{1,0:T(8,128)(2,1)S(1)}, bf16[16,2560]{1,0:T(8,128)(2,1)S(1)}, u32[]{:S(2)}, u32[]{:S(2)}) %collective-permute-start.15) | collective-permute-done | bytes 81952 | tf_op jit(solution)/shard_map/ppermute | solution.py:33
  40.2 1.4 %collective-permute-done.16.refs_1_ = bf16[32,2560]{1,0:T(8,128)(2,1)S(1)} collective-permute-done((bf16[32,2560]{1,0:T(8,128)(2,1)S(1)}, bf16[32,2560]{1,0:T(8,128)(2,1)S(1)}, u32[]{:S(2)}, u32[]{:S(2)}) %collective-permute-start.16) | collective-permute-done | bytes 163872 | tf_op jit(solution)/shard_map/ppermute | solution.py:26
  41.6 0.9 %shard_map.111 = f32[64,2560]{1,0:T(8,128)} custom-call(bf16[32,2560]{1,0:T(8,128)(2,1)S(1)} %shard_map.110.refs_0_.refs_2_, bf16[32,2560]{1,0:T(8,128)(2,1)S(1)} %collective-permute-done.16.refs_1_, bf16[32,2560]{1,0:T(8,128)(2,1)S(1)} %shard_map.110.refs_0_.refs_2_), custom_call_target="tpu_custom_call" | custom-call | bytes 983040 | tf_op jit(solution)/shard_map/pallas_call | solution.py:55
  (36 shorter events, 2.8 us)
Async XLA Ops:
  0.6 9.4 %copy-start = (bf16[512,2560]{1,0:T(8,128)(2,1)S(1)}, bf16[512,2560]{1,0:T(8,128)(2,1)}, u32[]{:S(2)}) copy-start(bf16[512,2560]{1,0:T(8,128)(2,1)} %refs_3_.3) | copy-start | bytes 7864324
  0.6 9.4 %copy-start.2 = (bf16[2560,64]{0,1:T(8,128)(2,1)S(1)}, bf16[2560,64]{0,1:T(8,128)(2,1)}, u32[]{:S(2)}) copy-start(bf16[2560,64]{0,1:T(8,128)(2,1)} %param.10) | copy-start | bytes 983044
  0.7 10.3 %collective-permute-start.1 = (bf16[2560,512]{1,0:T(8,128)(2,1)}, bf16[2560,512]{1,0:T(8,128)(2,1)S(1)}, u32[]{:S(2)}, u32[]{:S(2)}) collective-permute-start(bf16[2560,512]{1,0:T(8,128)(2,1)} %refs_1_.7), channel_id=1, source_target_pairs={{0,1},{1,0},{2,3},{3,2},{4,5},{5,4},{6,7},{7,6},{8,9},{9,8},{10,11... | collective-permute-start | bytes 7864328 | tf_op jit(solution)/shard_map/ppermute | solution.py:26
  2.7 8.8 %collective-permute-start.3 = (bf16[64,512]{1,0:T(8,128)(2,1)S(1)}, bf16[64,512]{1,0:T(8,128)(2,1)S(1)}, u32[]{:S(2)}, u32[]{:S(2)}) collective-permute-start(bf16[64,512]{1,0:T(8,128)(2,1)S(1)} %get-tuple-element.27), channel_id=1, source_target_pairs={{0,8},{1,9},{4,12},{5,13},{8,0},{9,1},{12,4},{13,5},{2,10},{3,11},... | collective-permute-start | bytes 196616 | tf_op jit(solution)/shard_map/ppermute | solution.py:33
  6.3 6.7 %collective-permute-start.4 = (bf16[64,512]{1,0:T(8,128)(2,1)S(1)}, bf16[64,512]{1,0:T(8,128)(2,1)S(1)}, u32[]{:S(2)}, u32[]{:S(2)}) collective-permute-start(bf16[64,512]{1,0:T(8,128)(2,1)S(1)} %get-tuple-element.28), channel_id=1, source_target_pairs={{0,12},{1,13},{4,8},{5,9},{8,4},{9,5},{12,0},{13,1},{2,14},{3,15},... | collective-permute-start | bytes 196616 | tf_op jit(solution)/shard_map/ppermute | solution.py:33
  7.6 5.6 %collective-permute-start.5 = (bf16[64,512]{1,0:T(8,128)(2,1)S(1)}, bf16[64,512]{1,0:T(8,128)(2,1)S(1)}, u32[]{:S(2)}, u32[]{:S(2)}) collective-permute-start(bf16[64,512]{1,0:T(8,128)(2,1)S(1)} %get-tuple-element.29), channel_id=1, source_target_pairs={{0,4},{1,5},{4,0},{5,1},{8,12},{9,13},{12,8},{13,9},{2,6},{3,7},{6... | collective-permute-start | bytes 196616 | tf_op jit(solution)/shard_map/ppermute | solution.py:33
  7.8 7.2 %collective-permute-start = (bf16[128,512]{1,0:T(8,128)(2,1)S(1)}, bf16[128,512]{1,0:T(8,128)(2,1)S(1)}, u32[]{:S(2)}, u32[]{:S(2)}) collective-permute-start(bf16[128,512]{1,0:T(8,128)(2,1)S(1)} %get-tuple-element.24), channel_id=1, source_target_pairs={{0,2},{2,0},{1,3},{3,1},{4,6},{6,4},{5,7},{7,5},{8,10},{10,8},{9,1... | collective-permute-start | bytes 393224 | tf_op jit(solution)/shard_map/ppermute | solution.py:26
  10.0 3.2 %copy-start.3 = (bf16[512,512]{1,0:T(8,128)(2,1)S(1)}, bf16[512,512]{1,0:T(8,128)(2,1)}, u32[]{:S(2)}) copy-start(bf16[512,512]{1,0:T(8,128)(2,1)} %refs_1_.5) | copy-start | bytes 1572868
  11.0 4.4 %collective-permute-start.2 = (bf16[64,512]{1,0:T(8,128)(2,1)S(1)}, bf16[64,512]{1,0:T(8,128)(2,1)S(1)}, u32[]{:S(2)}, u32[]{:S(2)}) collective-permute-start(bf16[64,512]{1,0:T(8,128)(2,1)S(1)} %shard_map.96), channel_id=1, source_target_pairs={{0,2},{2,0},{1,3},{3,1},{4,6},{6,4},{5,7},{7,5},{8,10},{10,8},{9,1... | collective-permute-start | bytes 196616 | tf_op jit(solution)/shard_map/ppermute | solution.py:26
  13.5 6.4 %collective-permute-start.8 = (f32[64,512]{1,0:T(8,128)S(1)}, f32[64,512]{1,0:T(8,128)S(1)}, u32[]{:S(2)}, u32[]{:S(2)}) collective-permute-start(f32[64,512]{1,0:T(8,128)S(1)} %shard_map.97.refs_4_.refs_1_), channel_id=1, source_target_pairs={{0,2},{2,0},{1,3},{3,1},{4,6},{6,4},{5,7},{7,5},{8,10},{10,8},{9,1... | collective-permute-start | bytes 393224 | tf_op jit(solution)/shard_map/ppermute | solution.py:26
  15.7 9.3 %collective-permute-start.10 = (bf16[1,64,512]{2,1,0:T(8,128)(2,1)S(1)}, bf16[1,64,512]{2,1,0:T(8,128)(2,1)S(1)}, u32[]{:S(2)}, u32[]{:S(2)}) collective-permute-start(bf16[1,64,512]{2,1,0:T(8,128)(2,1)S(1)} %get-tuple-element.31.refs_4_.refs_0_), channel_id=1, source_target_pairs={{0,8},{1,9},{4,12},{5,13},{8,0},{9,1},{12,4},{13,5},{2,10},{3,11},... | collective-permute-start | bytes 196616 | tf_op jit(solution)/shard_map/ppermute | solution.py:33
  18.5 6.5 %collective-permute-start.7 = (bf16[1,64,512]{2,1,0:T(8,128)(2,1)S(1)}, bf16[1,64,512]{2,1,0:T(8,128)(2,1)S(1)}, u32[]{:S(2)}, u32[]{:S(2)}) collective-permute-start(bf16[1,64,512]{2,1,0:T(8,128)(2,1)S(1)} %get-tuple-element.31.refs_4_.refs_0_), channel_id=1, source_target_pairs={{0,4},{1,5},{4,0},{5,1},{8,12},{9,13},{12,8},{13,9},{2,6},{3,7},{6... | collective-permute-start | bytes 196616 | tf_op jit(solution)/shard_map/ppermute | solution.py:33
  19.3 11.7 %collective-permute-start.6 = (bf16[384,512]{1,0:T(8,128)(2,1)S(1)}, bf16[384,512]{1,0:T(8,128)(2,1)S(1)}, u32[]{:S(2)}, u32[]{:S(2)}) collective-permute-start(bf16[384,512]{1,0:T(8,128)(2,1)S(1)} %get-tuple-element.30), channel_id=1, source_target_pairs={{0,2},{2,0},{1,3},{3,1},{4,6},{6,4},{5,7},{7,5},{8,10},{10,8},{9,1... | collective-permute-start | bytes 1179656 | tf_op jit(solution)/shard_map/ppermute | solution.py:26
  20.5 2.7 %collective-permute-start.11 = (f32[32,2560]{1,0:T(8,128)S(1)}, f32[32,2560]{1,0:T(8,128)S(1)}, u32[]{:S(2)}, u32[]{:S(2)}) collective-permute-start(f32[32,2560]{1,0:T(8,128)S(1)} %get-tuple-element.34), channel_id=1, source_target_pairs={{0,1},{1,0},{2,3},{3,2},{4,5},{5,4},{6,7},{7,6},{8,9},{9,8},{10,11... | collective-permute-start | bytes 983048 | tf_op jit(solution)/shard_map/ppermute | solution.py:26
  20.6 6.6 %collective-permute-start.9 = (bf16[1,64,512]{2,1,0:T(8,128)(2,1)S(1)}, bf16[1,64,512]{2,1,0:T(8,128)(2,1)S(1)}, u32[]{:S(2)}, u32[]{:S(2)}) collective-permute-start(bf16[1,64,512]{2,1,0:T(8,128)(2,1)S(1)} %shard_map.100), channel_id=1, source_target_pairs={{0,12},{1,13},{4,8},{5,9},{8,4},{9,5},{12,0},{13,1},{2,14},{3,15},... | collective-permute-start | bytes 196616 | tf_op jit(solution)/shard_map/ppermute | solution.py:33
  23.2 5.5 %collective-permute-start.13 = (bf16[16,2560]{1,0:T(8,128)(2,1)S(1)}, bf16[16,2560]{1,0:T(8,128)(2,1)S(1)}, u32[]{:S(2)}, u32[]{:S(2)}) collective-permute-start(bf16[16,2560]{1,0:T(8,128)(2,1)S(1)} %get-tuple-element.35.refs_0_), channel_id=1, source_target_pairs={{0,4},{1,5},{4,0},{5,1},{8,12},{9,13},{12,8},{13,9},{2,6},{3,7},{6... | collective-permute-start | bytes 245768 | tf_op jit(solution)/shard_map/ppermute | solution.py:33
  27.2 2.1 %collective-permute-start.12 = (bf16[4,64,512]{2,1,0:T(8,128)(2,1)S(1)}, bf16[4,64,512]{2,1,0:T(8,128)(2,1)S(1)}, u32[]{:S(2)}, u32[]{:S(2)}) collective-permute-start(bf16[4,64,512]{2,1,0:T(8,128)(2,1)S(1)} %shard_map.103.refs_2_.refs_1_), channel_id=1, source_target_pairs={{0,1},{1,0},{2,3},{3,2},{4,5},{5,4},{6,7},{7,6},{8,9},{9,8},{10,11... | collective-permute-start | bytes 786440 | tf_op jit(solution)/shard_map/ppermute | solution.py:26
  28.7 2.4 %copy-start.1 = (bf16[2560,512]{1,0:T(8,128)(2,1)S(1)}, bf16[2560,512]{1,0:T(8,128)(2,1)}, u32[]{:S(2)}) copy-start(bf16[2560,512]{1,0:T(8,128)(2,1)} %refs_1_.7) | copy-start | bytes 7864324
  28.7 6.8 %collective-permute-start.14 = (bf16[16,2560]{1,0:T(8,128)(2,1)S(1)}, bf16[16,2560]{1,0:T(8,128)(2,1)S(1)}, u32[]{:S(2)}, u32[]{:S(2)}) collective-permute-start(bf16[16,2560]{1,0:T(8,128)(2,1)S(1)} %shard_map.104.refs_4_.refs_0_), channel_id=1, source_target_pairs={{0,8},{1,9},{4,12},{5,13},{8,0},{9,1},{12,4},{13,5},{2,10},{3,11},... | collective-permute-start | bytes 245768 | tf_op jit(solution)/shard_map/ppermute | solution.py:33
  35.6 4.5 %collective-permute-start.15 = (bf16[16,2560]{1,0:T(8,128)(2,1)S(1)}, bf16[16,2560]{1,0:T(8,128)(2,1)S(1)}, u32[]{:S(2)}, u32[]{:S(2)}) collective-permute-start(bf16[16,2560]{1,0:T(8,128)(2,1)S(1)} %shard_map.108.refs_6_.refs_0_), channel_id=1, source_target_pairs={{0,4},{1,5},{4,0},{5,1},{8,12},{9,13},{12,8},{13,9},{2,6},{3,7},{6... | collective-permute-start | bytes 245768 | tf_op jit(solution)/shard_map/ppermute | solution.py:33
  40.1 1.5 %collective-permute-start.16 = (bf16[32,2560]{1,0:T(8,128)(2,1)S(1)}, bf16[32,2560]{1,0:T(8,128)(2,1)S(1)}, u32[]{:S(2)}, u32[]{:S(2)}) collective-permute-start(bf16[32,2560]{1,0:T(8,128)(2,1)S(1)} %shard_map.110.refs_0_.refs_2_), channel_id=1, source_target_pairs={{0,1},{1,0},{2,3},{3,2},{4,5},{5,4},{6,7},{7,6},{8,9},{9,8},{10,11... | collective-permute-start | bytes 491528 | tf_op jit(solution)/shard_map/ppermute | solution.py:26

commit v19 on v15

--- a/solution.py
+++ b/solution.py
@@ -9,7 +9,7 @@
 f32 = jnp.float32
 bf16 = jnp.bfloat16
 
-early_part = 4
+early_part = 3
 
 (busy, first_cost, middling, filling, brief, slight) = (
     10**10, 5 * 10**9, 5 * 10**9, 10**10, 3 * 10**9, 15 * 10**8
@@ -66,7 +66,7 @@
 def pick_heads(adapter_ids, head_up, grad):
     per_owner, rank, width = head_up.shape
     own_count, sub_count = lax.axis_size("own"), lax.axis_size("sub")
-    first = grad.shape[0] // early_part
+    first = grad.shape[0] * early_part // 16
 
     def body(ids_far, head_up, grad, *refs):
         outs, early, away, ids, maps, sems = refs[:own_count], *refs[own_count:]
@@ -156,7 +156,7 @@
 def head_term(lengths, lows, grad, scale, after):
     rank, rows = lows[0].shape
     columns = grad.shape[1]
-    first = rows // early_part
+    first = rows * early_part // 16
 
     def body(lengths, *refs):
         *lows, grad, term, late = refs
@@ -386,7 +386,7 @@
 def arrange(lengths, grad, pieces, after):
     rows, columns = grad.shape
     count = 1 + len(pieces)
-    first = rows // early_part
+    first = rows * early_part // 16
 
     def body(lengths, grad, *refs):
         pieces, kept = refs[:-1], refs[-1]

time: 40.7 us -> 40.7 us (level)
  transfers between devices with their start and end apart: 17 -> 17, of which waited for: 9 -> 9; matrix products, arithmetic and copies ran while one was open for 0% -> 0% of each run, Pallas kernels for 30% -> 31%
where the time goes in v19:
time: 40.7 us; the launch traced here: 40.6 us
  starting transfers between devices  17 us (42%)
  Pallas kernels  13.4 us (33%)
  waiting for transfers between devices  8.66 us (21%)
  between operations  1.51 us (4%)
    pallas_call x18, Pallas kernels, call(): pl.pallas_call(kernel, out_shape=outs, in_specs=list(specs) + [anywhere]...  13.4 us
    ppermute x9, starting transfers between devices, swap(): lax.ppermute(x, ('own', 'sub'), [(i, i ^ other) for i in range(whole)])  12.2 us
    ppermute x9, waiting for transfers between devices, swap(): lax.ppermute(x, ('own', 'sub'), [(i, i ^ other) for i in range(whole)])  5.45 us
    ppermute x8, starting transfers between devices, shift(): lax.ppermute(x, axis, [(i, (i + step) % count) for i in range(count)])  4.81 us
    ppermute x8, waiting for transfers between devices, shift(): lax.ppermute(x, axis, [(i, (i + step) % count) for i in range(count)])  3.2 us
  transfers between devices with their start and end apart: 17, of which 9 were waited for; matrix products, arithmetic and copies ran while one was open for 0% of the time, Pallas kernels for 31%

profile of v19, /device:TPU:0, one launch (start us, length us, event | category | flops | bytes accessed | tf_op | source)
XLA Modules:
  0.0 40.6 jit_solution(877032854338157076)
XLA Ops:
  1.2 1.5 %shard_map.94 = (bf16[64,512]{1,0:T(8,128)(2,1)S(1)}, bf16[64,512]{1,0:T(8,128)(2,1)S(1)}, bf16[64,512]{1,0:T(8,128)(2,1)S(1)}, bf16[64,512]{1,0:T(8,128)(2,1)S(...) custom-call(s32[8]{0:T(128)} %refs_0_.8, bf16[16,64,512]{2,1,0:T(8,128)(2,1)} %refs_1_.4, bf16[512,512]{1,0:T(8,128)(2,1)} %refs_1_.5), custom_call_target="tpu_custom_call" | custom-call | flops 5000000000 | bytes 1937440 | tf_op jit(solution)/shard_map/pallas_call | solution.py:55
  2.7 3.6 %collective-permute-start.3 = (bf16[64,512]{1,0:T(8,128)(2,1)S(1)}, bf16[64,512]{1,0:T(8,128)(2,1)S(1)}, u32[]{:S(2)}, u32[]{:S(2)}) collective-permute-start(bf16[64,512]{1,0:T(8,128)(2,1)S(1)} %get-tuple-element.27), channel_id=1, source_target_pairs={{0,8},{1,9},{4,12},{5,13},{8,0},{9,1},{12,4},{13,5},{2,10},{3,11},... | collective-permute-start | bytes 196616 | tf_op jit(solution)/shard_map/ppermute | solution.py:33
  6.3 1.3 %collective-permute-start.4 = (bf16[64,512]{1,0:T(8,128)(2,1)S(1)}, bf16[64,512]{1,0:T(8,128)(2,1)S(1)}, u32[]{:S(2)}, u32[]{:S(2)}) collective-permute-start(bf16[64,512]{1,0:T(8,128)(2,1)S(1)} %get-tuple-element.28), channel_id=1, source_target_pairs={{0,12},{1,13},{4,8},{5,9},{8,4},{9,5},{12,0},{13,1},{2,14},{3,15},... | collective-permute-start | bytes 196616 | tf_op jit(solution)/shard_map/ppermute | solution.py:33
  7.8 1.5 %collective-permute-start = (bf16[96,512]{1,0:T(8,128)(2,1)S(1)}, bf16[96,512]{1,0:T(8,128)(2,1)S(1)}, u32[]{:S(2)}, u32[]{:S(2)}) collective-permute-start(bf16[96,512]{1,0:T(8,128)(2,1)S(1)} %get-tuple-element.24), channel_id=1, source_target_pairs={{0,2},{2,0},{1,3},{3,1},{4,6},{6,4},{5,7},{7,5},{8,10},{10,8},{9,1... | collective-permute-start | bytes 294920 | tf_op jit(solution)/shard_map/ppermute | solution.py:26
  10.0 0.9 %shard_map.95.refs_0_.refs_6_.refs_1_ = f32[64,512]{1,0:T(8,128)S(1)} custom-call(bf16[512,2560]{1,0:T(8,128)(2,1)S(1)} %copy-done, bf16[64,2560]{1,0:T(8,128)(2,1)S(1)} %bitcast.2, bf16[64,512]{1,0:T(8,128)(2,1)S(1)} %get-tuple-element.25.refs_2_.refs_1_), custom_call_target="tpu_custom_call" | custom-call | flops 167772160 | bytes 3080192 | tf_op jit(solution)/shard_map/pallas_call | solution.py:55
  11.0 0.6 %collective-permute-start.2 = (bf16[64,512]{1,0:T(8,128)(2,1)S(1)}, bf16[64,512]{1,0:T(8,128)(2,1)S(1)}, u32[]{:S(2)}, u32[]{:S(2)}) collective-permute-start(bf16[64,512]{1,0:T(8,128)(2,1)S(1)} %shard_map.96), channel_id=1, source_target_pairs={{0,2},{2,0},{1,3},{3,1},{4,6},{6,4},{5,7},{7,5},{8,10},{10,8},{9,1... | collective-permute-start | bytes 196616 | tf_op jit(solution)/shard_map/ppermute | solution.py:26
  11.6 1.4 %collective-permute-done.4.refs_3_ = bf16[64,512]{1,0:T(8,128)(2,1)S(1)} collective-permute-done((bf16[64,512]{1,0:T(8,128)(2,1)S(1)}, bf16[64,512]{1,0:T(8,128)(2,1)S(1)}, u32[]{:S(2)}, u32[]{:S(2)}) %collective-permute-start.4) | collective-permute-done | bytes 65568 | tf_op jit(solution)/shard_map/ppermute | solution.py:33
  13.5 1.6 %collective-permute-start.7 = (f32[64,512]{1,0:T(8,128)S(1)}, f32[64,512]{1,0:T(8,128)S(1)}, u32[]{:S(2)}, u32[]{:S(2)}) collective-permute-start(f32[64,512]{1,0:T(8,128)S(1)} %shard_map.97.refs_4_.refs_1_), channel_id=1, source_target_pairs={{0,2},{2,0},{1,3},{3,1},{4,6},{6,4},{5,7},{7,5},{8,10},{10,8},{9,1... | collective-permute-start | bytes 393224 | tf_op jit(solution)/shard_map/ppermute | solution.py:26
  15.7 2.8 %collective-permute-start.10 = (bf16[1,64,512]{2,1,0:T(8,128)(2,1)S(1)}, bf16[1,64,512]{2,1,0:T(8,128)(2,1)S(1)}, u32[]{:S(2)}, u32[]{:S(2)}) collective-permute-start(bf16[1,64,512]{2,1,0:T(8,128)(2,1)S(1)} %get-tuple-element.31.refs_4_.refs_0_), channel_id=1, source_target_pairs={{0,8},{1,9},{4,12},{5,13},{8,0},{9,1},{12,4},{13,5},{2,10},{3,11},... | collective-permute-start | bytes 196616 | tf_op jit(solution)/shard_map/ppermute | solution.py:33
  18.5 1.5 %collective-permute-start.9 = (bf16[1,64,512]{2,1,0:T(8,128)(2,1)S(1)}, bf16[1,64,512]{2,1,0:T(8,128)(2,1)S(1)}, u32[]{:S(2)}, u32[]{:S(2)}) collective-permute-start(bf16[1,64,512]{2,1,0:T(8,128)(2,1)S(1)} %get-tuple-element.31.refs_4_.refs_0_), channel_id=1, source_target_pairs={{0,12},{1,13},{4,8},{5,9},{8,4},{9,5},{12,0},{13,1},{2,14},{3,15},... | collective-permute-start | bytes 196616 | tf_op jit(solution)/shard_map/ppermute | solution.py:33
  20.4 0.6 %shard_map.99 = (bf16[64,512]{1,0:T(8,128)(2,1)S(1)}, f32[32,2560]{1,0:T(8,128)S(1)}, f32[32,2560]{1,0:T(8,128)S(1)}) custom-call(s32[1]{0:T(128)S(6)} %copy.14.refs_0_, f32[64,512]{1,0:T(8,128)S(1)} %shard_map.97.refs_4_.refs_1_, f32[64,512]{1,0:T(8,128)S(1)} %collective-permute-done.7.refs_2_, bf16[512,2560]{1,0:T(8,128)(2,1)S(1)} %copy-done, ...), custom_call_target="tpu_custom_call" | custom-call | flops 167772160 | bytes 3604484 | tf_op jit(solution)/shard_map/pallas_call | solution.py:55
  21.1 1.5 %collective-permute-done.11.refs_1_ = f32[32,2560]{1,0:T(8,128)S(1)} collective-permute-done((f32[32,2560]{1,0:T(8,128)S(1)}, f32[32,2560]{1,0:T(8,128)S(1)}, u32[]{:S(2)}, u32[]{:S(2)}) %collective-permute-start.11) | collective-permute-done | bytes 327712 | tf_op jit(solution)/shard_map/ppermute | solution.py:26
  22.7 0.6 %collective-permute-start.13 = (bf16[16,2560]{1,0:T(8,128)(2,1)S(1)}, bf16[16,2560]{1,0:T(8,128)(2,1)S(1)}, u32[]{:S(2)}, u32[]{:S(2)}) collective-permute-start(bf16[16,2560]{1,0:T(8,128)(2,1)S(1)} %get-tuple-element.35.refs_0_), channel_id=1, source_target_pairs={{0,4},{1,5},{4,0},{5,1},{8,12},{9,13},{12,8},{13,9},{2,6},{3,7},{6... | collective-permute-start | bytes 245768 | tf_op jit(solution)/shard_map/ppermute | solution.py:33
  23.3 1.4 %shard_map.102 = (f32[16,64,512]{2,1,0:T(8,128)}, f32[8,128]{1,0:T(8,128)S(1)}) custom-call(bf16[16,2560]{1,0:T(8,128)(2,1)S(1)} %get-tuple-element.35.refs_0_), custom_call_target="tpu_custom_call" | custom-call | flops 10000000000 | bytes 2101248 | tf_op jit(solution)/shard_map/pallas_call | solution.py:55
  24.8 1.3 %collective-permute-done.8.refs_1_ = bf16[1,64,512]{2,1,0:T(8,128)(2,1)S(1)} collective-permute-done((bf16[1,64,512]{2,1,0:T(8,128)(2,1)S(1)}, bf16[1,64,512]{2,1,0:T(8,128)(2,1)S(1)}, u32[]{:S(2)}, u32[]{:S(2)}) %collective-permute-start.8) | collective-permute-done | bytes 65568 | tf_op jit(solution)/shard_map/ppermute | solution.py:33
  26.2 1.5 %collective-permute-done.13.refs_1_ = bf16[16,2560]{1,0:T(8,128)(2,1)S(1)} collective-permute-done((bf16[16,2560]{1,0:T(8,128)(2,1)S(1)}, bf16[16,2560]{1,0:T(8,128)(2,1)S(1)}, u32[]{:S(2)}, u32[]{:S(2)}) %collective-permute-start.13) | collective-permute-done | bytes 81952 | tf_op jit(solution)/shard_map/ppermute | solution.py:33
  27.7 1.2 %collective-permute-start.14 = (bf16[16,2560]{1,0:T(8,128)(2,1)S(1)}, bf16[16,2560]{1,0:T(8,128)(2,1)S(1)}, u32[]{:S(2)}, u32[]{:S(2)}) collective-permute-start(bf16[16,2560]{1,0:T(8,128)(2,1)S(1)} %shard_map.104.refs_4_.refs_0_), channel_id=1, source_target_pairs={{0,8},{1,9},{4,12},{5,13},{8,0},{9,1},{12,4},{13,5},{2,10},{3,11},... | collective-permute-start | bytes 245768 | tf_op jit(solution)/shard_map/ppermute | solution.py:33
  28.9 1.7 %shard_map.105 = (f32[16,64,512]{2,1,0:T(8,128)}, f32[8,128]{1,0:T(8,128)S(1)}) custom-call(s32[8]{0:T(128)} %refs_0_.8, bf16[4,64,512]{2,1,0:T(8,128)(2,1)S(1)} %shard_map.103.refs_2_.refs_1_, bf16[4,64,512]{2,1,0:T(8,128)(2,1)S(1)} %collective-permute-done.12.refs_2_, f32[16,64,512]{2,1,0:T(8,128)} %get-tuple-element.37.refs_3_, ...), custom_call_target="tpu_custom_call", output_to_operand_aliasing={{0}: (3, {})} | custom-call | bytes 4722720 | tf_op jit(solution)/shard_map/pallas_call | solution.py:55
  30.8 2.4 %shard_map.107 = (bf16[512,2560]{1,0:T(8,128)(2,1)}, f32[8,128]{1,0:T(8,128)S(1)}) custom-call(bf16[512,1024]{1,0:T(8,128)(2,1)S(1)} %shard_map.106.refs_0_, bf16[2560,512]{1,0:T(8,128)(2,1)S(1)} %copy-done.1, bf16[2560,512]{1,0:T(8,128)(2,1)S(1)} %collective-permute-done.1.refs_1_.refs_2_, bf16[64,512]{1,0:T(8,128)(2,1)S(1)} %get-tuple-element.32.refs_1_.refs_2_.refs_3_, ...), custom_call_target="tpu_custom_call" | custom-call | flops 1140850688 | bytes 9310208 | tf_op jit(solution)/shard_map/pallas_call | solution.py:55
  33.1 0.5 %collective-permute-done.14.refs_1_ = bf16[16,2560]{1,0:T(8,128)(2,1)S(1)} collective-permute-done((bf16[16,2560]{1,0:T(8,128)(2,1)S(1)}, bf16[16,2560]{1,0:T(8,128)(2,1)S(1)}, u32[]{:S(2)}, u32[]{:S(2)}) %collective-permute-start.14) | collective-permute-done | bytes 81952 | tf_op jit(solution)/shard_map/ppermute | solution.py:33
  33.7 1.0 %collective-permute-start.15 = (bf16[16,2560]{1,0:T(8,128)(2,1)S(1)}, bf16[16,2560]{1,0:T(8,128)(2,1)S(1)}, u32[]{:S(2)}, u32[]{:S(2)}) collective-permute-start(bf16[16,2560]{1,0:T(8,128)(2,1)S(1)} %shard_map.108.refs_6_.refs_0_), channel_id=1, source_target_pairs={{0,4},{1,5},{4,0},{5,1},{8,12},{9,13},{12,8},{13,9},{2,6},{3,7},{6... | collective-permute-start | bytes 245768 | tf_op jit(solution)/shard_map/ppermute | solution.py:33
  34.7 3.1 %shard_map.109 = (bf16[512,2560]{1,0:T(8,128)(2,1)}, f32[8,128]{1,0:T(8,128)S(1)}) custom-call(bf16[512,1024]{1,0:T(8,128)(2,1)S(1)} %shard_map.106.refs_0_, bf16[2560,512]{1,0:T(8,128)(2,1)S(1)} %copy-done.1, bf16[2560,512]{1,0:T(8,128)(2,1)S(1)} %collective-permute-done.1.refs_1_.refs_2_, ...), custom_call_target="tpu_custom_call", output_to_operand_aliasing={{0}: (5, {})} | custom-call | flops 1711276032 | bytes 11931648 | tf_op jit(solution)/shard_map/pallas_call | solution.py:55
  38.3 1.4 %collective-permute-done.16.refs_1_ = bf16[32,2560]{1,0:T(8,128)(2,1)S(1)} collective-permute-done((bf16[32,2560]{1,0:T(8,128)(2,1)S(1)}, bf16[32,2560]{1,0:T(8,128)(2,1)S(1)}, u32[]{:S(2)}, u32[]{:S(2)}) %collective-permute-start.16) | collective-permute-done | bytes 163872 | tf_op jit(solution)/shard_map/ppermute | solution.py:26
  39.7 0.9 %shard_map.111 = f32[64,2560]{1,0:T(8,128)} custom-call(bf16[32,2560]{1,0:T(8,128)(2,1)S(1)} %shard_map.110.refs_0_.refs_2_, bf16[32,2560]{1,0:T(8,128)(2,1)S(1)} %collective-permute-done.16.refs_1_, bf16[32,2560]{1,0:T(8,128)(2,1)S(1)} %shard_map.110.refs_0_.refs_2_), custom_call_target="tpu_custom_call" | custom-call | bytes 983040 | tf_op jit(solution)/shard_map/pallas_call | solution.py:55
  (36 shorter events, 3.3 us)
Async XLA Ops:
  0.6 9.4 %copy-start = (bf16[512,2560]{1,0:T(8,128)(2,1)S(1)}, bf16[512,2560]{1,0:T(8,128)(2,1)}, u32[]{:S(2)}) copy-start(bf16[512,2560]{1,0:T(8,128)(2,1)} %refs_3_.3) | copy-start | bytes 7864324
  0.6 9.4 %copy-start.2 = (bf16[2560,64]{0,1:T(8,128)(2,1)S(1)}, bf16[2560,64]{0,1:T(8,128)(2,1)}, u32[]{:S(2)}) copy-start(bf16[2560,64]{0,1:T(8,128)(2,1)} %param.10) | copy-start | bytes 983044
  0.7 10.3 %collective-permute-start.1 = (bf16[2560,512]{1,0:T(8,128)(2,1)}, bf16[2560,512]{1,0:T(8,128)(2,1)S(1)}, u32[]{:S(2)}, u32[]{:S(2)}) collective-permute-start(bf16[2560,512]{1,0:T(8,128)(2,1)} %refs_1_.7), channel_id=1, source_target_pairs={{0,1},{1,0},{2,3},{3,2},{4,5},{5,4},{6,7},{7,6},{8,9},{9,8},{10,11... | collective-permute-start | bytes 7864328 | tf_op jit(solution)/shard_map/ppermute | solution.py:26
  2.7 8.8 %collective-permute-start.3 = (bf16[64,512]{1,0:T(8,128)(2,1)S(1)}, bf16[64,512]{1,0:T(8,128)(2,1)S(1)}, u32[]{:S(2)}, u32[]{:S(2)}) collective-permute-start(bf16[64,512]{1,0:T(8,128)(2,1)S(1)} %get-tuple-element.27), channel_id=1, source_target_pairs={{0,8},{1,9},{4,12},{5,13},{8,0},{9,1},{12,4},{13,5},{2,10},{3,11},... | collective-permute-start | bytes 196616 | tf_op jit(solution)/shard_map/ppermute | solution.py:33
  6.3 6.7 %collective-permute-start.4 = (bf16[64,512]{1,0:T(8,128)(2,1)S(1)}, bf16[64,512]{1,0:T(8,128)(2,1)S(1)}, u32[]{:S(2)}, u32[]{:S(2)}) collective-permute-start(bf16[64,512]{1,0:T(8,128)(2,1)S(1)} %get-tuple-element.28), channel_id=1, source_target_pairs={{0,12},{1,13},{4,8},{5,9},{8,4},{9,5},{12,0},{13,1},{2,14},{3,15},... | collective-permute-start | bytes 196616 | tf_op jit(solution)/shard_map/ppermute | solution.py:33
  7.6 5.6 %collective-permute-start.5 = (bf16[64,512]{1,0:T(8,128)(2,1)S(1)}, bf16[64,512]{1,0:T(8,128)(2,1)S(1)}, u32[]{:S(2)}, u32[]{:S(2)}) collective-permute-start(bf16[64,512]{1,0:T(8,128)(2,1)S(1)} %get-tuple-element.29), channel_id=1, source_target_pairs={{0,4},{1,5},{4,0},{5,1},{8,12},{9,13},{12,8},{13,9},{2,6},{3,7},{6... | collective-permute-start | bytes 196616 | tf_op jit(solution)/shard_map/ppermute | solution.py:33
  7.8 7.2 %collective-permute-start = (bf16[96,512]{1,0:T(8,128)(2,1)S(1)}, bf16[96,512]{1,0:T(8,128)(2,1)S(1)}, u32[]{:S(2)}, u32[]{:S(2)}) collective-permute-start(bf16[96,512]{1,0:T(8,128)(2,1)S(1)} %get-tuple-element.24), channel_id=1, source_target_pairs={{0,2},{2,0},{1,3},{3,1},{4,6},{6,4},{5,7},{7,5},{8,10},{10,8},{9,1... | collective-permute-start | bytes 294920 | tf_op jit(solution)/shard_map/ppermute | solution.py:26
  10.0 3.2 %copy-start.3 = (bf16[512,512]{1,0:T(8,128)(2,1)S(1)}, bf16[512,512]{1,0:T(8,128)(2,1)}, u32[]{:S(2)}) copy-start(bf16[512,512]{1,0:T(8,128)(2,1)} %refs_1_.5) | copy-start | bytes 1572868
  11.0 4.4 %collective-permute-start.2 = (bf16[64,512]{1,0:T(8,128)(2,1)S(1)}, bf16[64,512]{1,0:T(8,128)(2,1)S(1)}, u32[]{:S(2)}, u32[]{:S(2)}) collective-permute-start(bf16[64,512]{1,0:T(8,128)(2,1)S(1)} %shard_map.96), channel_id=1, source_target_pairs={{0,2},{2,0},{1,3},{3,1},{4,6},{6,4},{5,7},{7,5},{8,10},{10,8},{9,1... | collective-permute-start | bytes 196616 | tf_op jit(solution)/shard_map/ppermute | solution.py:26
  13.5 6.9 %collective-permute-start.7 = (f32[64,512]{1,0:T(8,128)S(1)}, f32[64,512]{1,0:T(8,128)S(1)}, u32[]{:S(2)}, u32[]{:S(2)}) collective-permute-start(f32[64,512]{1,0:T(8,128)S(1)} %shard_map.97.refs_4_.refs_1_), channel_id=1, source_target_pairs={{0,2},{2,0},{1,3},{3,1},{4,6},{6,4},{5,7},{7,5},{8,10},{10,8},{9,1... | collective-permute-start | bytes 393224 | tf_op jit(solution)/shard_map/ppermute | solution.py:26
  15.7 9.0 %collective-permute-start.10 = (bf16[1,64,512]{2,1,0:T(8,128)(2,1)S(1)}, bf16[1,64,512]{2,1,0:T(8,128)(2,1)S(1)}, u32[]{:S(2)}, u32[]{:S(2)}) collective-permute-start(bf16[1,64,512]{2,1,0:T(8,128)(2,1)S(1)} %get-tuple-element.31.refs_4_.refs_0_), channel_id=1, source_target_pairs={{0,8},{1,9},{4,12},{5,13},{8,0},{9,1},{12,4},{13,5},{2,10},{3,11},... | collective-permute-start | bytes 196616 | tf_op jit(solution)/shard_map/ppermute | solution.py:33
  18.5 6.3 %collective-permute-start.9 = (bf16[1,64,512]{2,1,0:T(8,128)(2,1)S(1)}, bf16[1,64,512]{2,1,0:T(8,128)(2,1)S(1)}, u32[]{:S(2)}, u32[]{:S(2)}) collective-permute-start(bf16[1,64,512]{2,1,0:T(8,128)(2,1)S(1)} %get-tuple-element.31.refs_4_.refs_0_), channel_id=1, source_target_pairs={{0,12},{1,13},{4,8},{5,9},{8,4},{9,5},{12,0},{13,1},{2,14},{3,15},... | collective-permute-start | bytes 196616 | tf_op jit(solution)/shard_map/ppermute | solution.py:33
  20.0 10.7 %collective-permute-start.6 = (bf16[416,512]{1,0:T(8,128)(2,1)S(1)}, bf16[416,512]{1,0:T(8,128)(2,1)S(1)}, u32[]{:S(2)}, u32[]{:S(2)}) collective-permute-start(bf16[416,512]{1,0:T(8,128)(2,1)S(1)} %get-tuple-element.30), channel_id=1, source_target_pairs={{0,2},{2,0},{1,3},{3,1},{4,6},{6,4},{5,7},{7,5},{8,10},{10,8},{9,1... | collective-permute-start | bytes 1277960 | tf_op jit(solution)/shard_map/ppermute | solution.py:26
  21.0 1.7 %collective-permute-start.11 = (f32[32,2560]{1,0:T(8,128)S(1)}, f32[32,2560]{1,0:T(8,128)S(1)}, u32[]{:S(2)}, u32[]{:S(2)}) collective-permute-start(f32[32,2560]{1,0:T(8,128)S(1)} %get-tuple-element.34), channel_id=1, source_target_pairs={{0,1},{1,0},{2,3},{3,2},{4,5},{5,4},{6,7},{7,6},{8,9},{9,8},{10,11... | collective-permute-start | bytes 983048 | tf_op jit(solution)/shard_map/ppermute | solution.py:26
  21.1 5.0 %collective-permute-start.8 = (bf16[1,64,512]{2,1,0:T(8,128)(2,1)S(1)}, bf16[1,64,512]{2,1,0:T(8,128)(2,1)S(1)}, u32[]{:S(2)}, u32[]{:S(2)}) collective-permute-start(bf16[1,64,512]{2,1,0:T(8,128)(2,1)S(1)} %shard_map.100), channel_id=1, source_target_pairs={{0,4},{1,5},{4,0},{5,1},{8,12},{9,13},{12,8},{13,9},{2,6},{3,7},{6... | collective-permute-start | bytes 196616 | tf_op jit(solution)/shard_map/ppermute | solution.py:33
  22.7 5.0 %collective-permute-start.13 = (bf16[16,2560]{1,0:T(8,128)(2,1)S(1)}, bf16[16,2560]{1,0:T(8,128)(2,1)S(1)}, u32[]{:S(2)}, u32[]{:S(2)}) collective-permute-start(bf16[16,2560]{1,0:T(8,128)(2,1)S(1)} %get-tuple-element.35.refs_0_), channel_id=1, source_target_pairs={{0,4},{1,5},{4,0},{5,1},{8,12},{9,13},{12,8},{13,9},{2,6},{3,7},{6... | collective-permute-start | bytes 245768 | tf_op jit(solution)/shard_map/ppermute | solution.py:33
  26.1 2.8 %collective-permute-start.12 = (bf16[4,64,512]{2,1,0:T(8,128)(2,1)S(1)}, bf16[4,64,512]{2,1,0:T(8,128)(2,1)S(1)}, u32[]{:S(2)}, u32[]{:S(2)}) collective-permute-start(bf16[4,64,512]{2,1,0:T(8,128)(2,1)S(1)} %shard_map.103.refs_2_.refs_1_), channel_id=1, source_target_pairs={{0,1},{1,0},{2,3},{3,2},{4,5},{5,4},{6,7},{7,6},{8,9},{9,8},{10,11... | collective-permute-start | bytes 786440 | tf_op jit(solution)/shard_map/ppermute | solution.py:26
  27.7 3.0 %copy-start.1 = (bf16[2560,512]{1,0:T(8,128)(2,1)S(1)}, bf16[2560,512]{1,0:T(8,128)(2,1)}, u32[]{:S(2)}) copy-start(bf16[2560,512]{1,0:T(8,128)(2,1)} %refs_1_.7) | copy-start | bytes 7864324
  27.7 5.9 %collective-permute-start.14 = (bf16[16,2560]{1,0:T(8,128)(2,1)S(1)}, bf16[16,2560]{1,0:T(8,128)(2,1)S(1)}, u32[]{:S(2)}, u32[]{:S(2)}) collective-permute-start(bf16[16,2560]{1,0:T(8,128)(2,1)S(1)} %shard_map.104.refs_4_.refs_0_), channel_id=1, source_target_pairs={{0,8},{1,9},{4,12},{5,13},{8,0},{9,1},{12,4},{13,5},{2,10},{3,11},... | collective-permute-start | bytes 245768 | tf_op jit(solution)/shard_map/ppermute | solution.py:33
  33.7 4.5 %collective-permute-start.15 = (bf16[16,2560]{1,0:T(8,128)(2,1)S(1)}, bf16[16,2560]{1,0:T(8,128)(2,1)S(1)}, u32[]{:S(2)}, u32[]{:S(2)}) collective-permute-start(bf16[16,2560]{1,0:T(8,128)(2,1)S(1)} %shard_map.108.refs_6_.refs_0_), channel_id=1, source_target_pairs={{0,4},{1,5},{4,0},{5,1},{8,12},{9,13},{12,8},{13,9},{2,6},{3,7},{6... | collective-permute-start | bytes 245768 | tf_op jit(solution)/shard_map/ppermute | solution.py:33
  38.2 1.5 %collective-permute-start.16 = (bf16[32,2560]{1,0:T(8,128)(2,1)S(1)}, bf16[32,2560]{1,0:T(8,128)(2,1)S(1)}, u32[]{:S(2)}, u32[]{:S(2)}) collective-permute-start(bf16[32,2560]{1,0:T(8,128)(2,1)S(1)} %shard_map.110.refs_0_.refs_2_), channel_id=1, source_target_pairs={{0,1},{1,0},{2,3},{3,2},{4,5},{5,4},{6,7},{7,6},{8,9},{9,8},{10,11... | collective-permute-start | bytes 491528 | tf_op jit(solution)/shard_map/ppermute | solution.py:26

commit v20 on v19

--- a/solution.py
+++ b/solution.py
@@ -269,20 +269,30 @@
     )[0]
 
 
-def join_shares(mine, other, after):
-    share, features = mine.shape
-
-    def body(mine, other, out):
+def lay_share(share, other, before, after):
+    rows, features = share.shape
+    held_in = [] if before is None else [before]
+
+    def body(share, *refs):
+        out, wide, sem = refs[len(held_in) :]
         sub = lax.axis_index("sub")
-        for side, piece in ((sub, mine), (1 - sub, other)):
-            out[pl.ds(pl.multiple_of(side * share, share), share), :] = piece[...].astype(f32)
-
-    return call(
-        body,
-        [mine, other],
-        [in_vmem] * 2,
-        [shape_of((2 * share, features), f32)],
-        after=after,
+        side = 1 - sub if other else sub
+        wide[...] = share[...].astype(f32)
+        copy = pltpu.make_async_copy(
+            wide, out.at[pl.ds(pl.multiple_of(side * rows, rows), rows)], sem
+        )
+        copy.start()
+        copy.wait()
+
+    return call(
+        body,
+        [share, *held_in],
+        [in_vmem] + [in_hbm] * len(held_in),
+        [shape_of((2 * rows, features), f32)],
+        out_specs=[in_hbm],
+        after=after,
+        input_output_aliases={1: 0} if held_in else {},
+        scratch_shapes=[pltpu.VMEM((rows, features), f32), pltpu.SemaphoreType.DMA],
     )[0]
 
 
@@ -514,7 +524,8 @@
     for bit in reversed(bits[:-1]):
         total = rejoin(total, swap(total, bit, 0), bit, [mark])
         mark = total
-    shared_down_gradient = join_shares(total, shift(total, "sub", 1), [mark]).T
+    laid = lay_share(total, False, None, [mark])
+    shared_down_gradient = lay_share(shift(total, "sub", 1), True, laid, []).T
     return (input_gradient, shared_down_gradient, grad_heads)
 
 

time: 40.7 us -> 40.6 us (level)
  starting transfers between devices: 17 us -> 16.4 us
  Pallas kernels: 13.4 us -> 14 us
    ppermute x8, waiting for transfers between devices: 3.2 us -> 2.44 us  [shift(): lax.ppermute(x, axis, [(i, (i + step) % count) for i in range(count)])]
    pallas_call x18 -> x19, Pallas kernels: 13.4 us -> 14 us  [call(): pl.pallas_call(kernel, out_shape=outs, in_specs=list(specs) + [anywhere]...]
    ppermute x9, waiting for transfers between devices: 5.45 us -> 6.05 us  [swap(): lax.ppermute(x, ('own', 'sub'), [(i, i ^ other) for i in range(whole)])]
    ppermute x9, starting transfers between devices: 12.2 us -> 11.6 us  [swap(): lax.ppermute(x, ('own', 'sub'), [(i, i ^ other) for i in range(whole)])]
  transfers between devices with their start and end apart: 17 -> 17, of which waited for: 9 -> 9; matrix products, arithmetic and copies ran while one was open for 0% -> 0% of each run, Pallas kernels for 31% -> 33%
where the time goes in v20:
time: 40.6 us; the launch traced here: 40.5 us
  starting transfers between devices  16.4 us (40%)
  Pallas kernels  14 us (34%)
  waiting for transfers between devices  8.49 us (21%)
  between operations  1.52 us (4%)
    pallas_call x19, Pallas kernels, call(): pl.pallas_call(kernel, out_shape=outs, in_specs=list(specs) + [anywhere]...  14 us
    ppermute x9, starting transfers between devices, swap(): lax.ppermute(x, ('own', 'sub'), [(i, i ^ other) for i in range(whole)])  11.6 us
    ppermute x9, waiting for transfers between devices, swap(): lax.ppermute(x, ('own', 'sub'), [(i, i ^ other) for i in range(whole)])  6.05 us
    ppermute x8, starting transfers between devices, shift(): lax.ppermute(x, axis, [(i, (i + step) % count) for i in range(count)])  4.81 us
    ppermute x8, waiting for transfers between devices, shift(): lax.ppermute(x, axis, [(i, (i + step) % count) for i in range(count)])  2.44 us
  transfers between devices with their start and end apart: 17, of which 9 were waited for; matrix products, arithmetic and copies ran while one was open for 0% of the time, Pallas kernels for 33%

profile of v20, /device:TPU:0, one launch (start us, length us, event | category | flops | bytes accessed | tf_op | source)
XLA Modules:
  0.0 40.5 jit_solution(15268233506922158084)
XLA Ops:
  1.2 1.5 %shard_map.94 = (bf16[64,512]{1,0:T(8,128)(2,1)S(1)}, bf16[64,512]{1,0:T(8,128)(2,1)S(1)}, bf16[64,512]{1,0:T(8,128)(2,1)S(1)}, bf16[64,512]{1,0:T(8,128)(2,1)S(...) custom-call(s32[8]{0:T(128)} %refs_0_.8, bf16[16,64,512]{2,1,0:T(8,128)(2,1)} %refs_1_.4, bf16[512,512]{1,0:T(8,128)(2,1)} %refs_1_.5), custom_call_target="tpu_custom_call" | custom-call | flops 5000000000 | bytes 1937440 | tf_op jit(solution)/shard_map/pallas_call | solution.py:55
  2.7 3.6 %collective-permute-start.3 = (bf16[64,512]{1,0:T(8,128)(2,1)S(1)}, bf16[64,512]{1,0:T(8,128)(2,1)S(1)}, u32[]{:S(2)}, u32[]{:S(2)}) collective-permute-start(bf16[64,512]{1,0:T(8,128)(2,1)S(1)} %get-tuple-element.27), channel_id=1, source_target_pairs={{0,8},{1,9},{4,12},{5,13},{8,0},{9,1},{12,4},{13,5},{2,10},{3,11},... | collective-permute-start | bytes 196616 | tf_op jit(solution)/shard_map/ppermute | solution.py:33
  6.3 1.3 %collective-permute-start.4 = (bf16[64,512]{1,0:T(8,128)(2,1)S(1)}, bf16[64,512]{1,0:T(8,128)(2,1)S(1)}, u32[]{:S(2)}, u32[]{:S(2)}) collective-permute-start(bf16[64,512]{1,0:T(8,128)(2,1)S(1)} %get-tuple-element.28), channel_id=1, source_target_pairs={{0,12},{1,13},{4,8},{5,9},{8,4},{9,5},{12,0},{13,1},{2,14},{3,15},... | collective-permute-start | bytes 196616 | tf_op jit(solution)/shard_map/ppermute | solution.py:33
  7.8 1.5 %collective-permute-start = (bf16[96,512]{1,0:T(8,128)(2,1)S(1)}, bf16[96,512]{1,0:T(8,128)(2,1)S(1)}, u32[]{:S(2)}, u32[]{:S(2)}) collective-permute-start(bf16[96,512]{1,0:T(8,128)(2,1)S(1)} %get-tuple-element.24), channel_id=1, source_target_pairs={{0,2},{2,0},{1,3},{3,1},{4,6},{6,4},{5,7},{7,5},{8,10},{10,8},{9,1... | collective-permute-start | bytes 294920 | tf_op jit(solution)/shard_map/ppermute | solution.py:26
  10.0 0.9 %shard_map.95.refs_0_.refs_6_.refs_1_ = f32[64,512]{1,0:T(8,128)S(1)} custom-call(bf16[512,2560]{1,0:T(8,128)(2,1)S(1)} %copy-done, bf16[64,2560]{1,0:T(8,128)(2,1)S(1)} %bitcast.2, bf16[64,512]{1,0:T(8,128)(2,1)S(1)} %get-tuple-element.25.refs_2_.refs_1_), custom_call_target="tpu_custom_call" | custom-call | flops 167772160 | bytes 3080192 | tf_op jit(solution)/shard_map/pallas_call | solution.py:55
  11.0 0.6 %collective-permute-start.2 = (bf16[64,512]{1,0:T(8,128)(2,1)S(1)}, bf16[64,512]{1,0:T(8,128)(2,1)S(1)}, u32[]{:S(2)}, u32[]{:S(2)}) collective-permute-start(bf16[64,512]{1,0:T(8,128)(2,1)S(1)} %shard_map.96), channel_id=1, source_target_pairs={{0,2},{2,0},{1,3},{3,1},{4,6},{6,4},{5,7},{7,5},{8,10},{10,8},{9,1... | collective-permute-start | bytes 196616 | tf_op jit(solution)/shard_map/ppermute | solution.py:26
  11.6 1.4 %collective-permute-done.4.refs_3_ = bf16[64,512]{1,0:T(8,128)(2,1)S(1)} collective-permute-done((bf16[64,512]{1,0:T(8,128)(2,1)S(1)}, bf16[64,512]{1,0:T(8,128)(2,1)S(1)}, u32[]{:S(2)}, u32[]{:S(2)}) %collective-permute-start.4) | collective-permute-done | bytes 65568 | tf_op jit(solution)/shard_map/ppermute | solution.py:33
  13.5 1.6 %collective-permute-start.7 = (f32[64,512]{1,0:T(8,128)S(1)}, f32[64,512]{1,0:T(8,128)S(1)}, u32[]{:S(2)}, u32[]{:S(2)}) collective-permute-start(f32[64,512]{1,0:T(8,128)S(1)} %shard_map.97.refs_4_.refs_1_), channel_id=1, source_target_pairs={{0,2},{2,0},{1,3},{3,1},{4,6},{6,4},{5,7},{7,5},{8,10},{10,8},{9,1... | collective-permute-start | bytes 393224 | tf_op jit(solution)/shard_map/ppermute | solution.py:26
  15.7 2.8 %collective-permute-start.10 = (bf16[1,64,512]{2,1,0:T(8,128)(2,1)S(1)}, bf16[1,64,512]{2,1,0:T(8,128)(2,1)S(1)}, u32[]{:S(2)}, u32[]{:S(2)}) collective-permute-start(bf16[1,64,512]{2,1,0:T(8,128)(2,1)S(1)} %get-tuple-element.31.refs_4_.refs_0_), channel_id=1, source_target_pairs={{0,8},{1,9},{4,12},{5,13},{8,0},{9,1},{12,4},{13,5},{2,10},{3,11},... | collective-permute-start | bytes 196616 | tf_op jit(solution)/shard_map/ppermute | solution.py:33
  18.5 1.5 %collective-permute-start.9 = (bf16[1,64,512]{2,1,0:T(8,128)(2,1)S(1)}, bf16[1,64,512]{2,1,0:T(8,128)(2,1)S(1)}, u32[]{:S(2)}, u32[]{:S(2)}) collective-permute-start(bf16[1,64,512]{2,1,0:T(8,128)(2,1)S(1)} %get-tuple-element.31.refs_4_.refs_0_), channel_id=1, source_target_pairs={{0,12},{1,13},{4,8},{5,9},{8,4},{9,5},{12,0},{13,1},{2,14},{3,15},... | collective-permute-start | bytes 196616 | tf_op jit(solution)/shard_map/ppermute | solution.py:33
  20.4 0.6 %shard_map.99 = (bf16[64,512]{1,0:T(8,128)(2,1)S(1)}, f32[32,2560]{1,0:T(8,128)S(1)}, f32[32,2560]{1,0:T(8,128)S(1)}) custom-call(s32[1]{0:T(128)S(6)} %copy.16.refs_0_, f32[64,512]{1,0:T(8,128)S(1)} %shard_map.97.refs_4_.refs_1_, f32[64,512]{1,0:T(8,128)S(1)} %collective-permute-done.7.refs_2_, bf16[512,2560]{1,0:T(8,128)(2,1)S(1)} %copy-done, ...), custom_call_target="tpu_custom_call" | custom-call | flops 167772160 | bytes 3604484 | tf_op jit(solution)/shard_map/pallas_call | solution.py:55
  21.1 1.5 %collective-permute-done.11.refs_1_ = f32[32,2560]{1,0:T(8,128)S(1)} collective-permute-done((f32[32,2560]{1,0:T(8,128)S(1)}, f32[32,2560]{1,0:T(8,128)S(1)}, u32[]{:S(2)}, u32[]{:S(2)}) %collective-permute-start.11) | collective-permute-done | bytes 327712 | tf_op jit(solution)/shard_map/ppermute | solution.py:26
  22.7 0.6 %collective-permute-start.13 = (bf16[16,2560]{1,0:T(8,128)(2,1)S(1)}, bf16[16,2560]{1,0:T(8,128)(2,1)S(1)}, u32[]{:S(2)}, u32[]{:S(2)}) collective-permute-start(bf16[16,2560]{1,0:T(8,128)(2,1)S(1)} %get-tuple-element.35.refs_0_), channel_id=1, source_target_pairs={{0,4},{1,5},{4,0},{5,1},{8,12},{9,13},{12,8},{13,9},{2,6},{3,7},{6... | collective-permute-start | bytes 245768 | tf_op jit(solution)/shard_map/ppermute | solution.py:33
  23.3 1.4 %shard_map.102 = (f32[16,64,512]{2,1,0:T(8,128)}, f32[8,128]{1,0:T(8,128)S(1)}) custom-call(bf16[16,2560]{1,0:T(8,128)(2,1)S(1)} %get-tuple-element.35.refs_0_), custom_call_target="tpu_custom_call" | custom-call | flops 10000000000 | bytes 2101248 | tf_op jit(solution)/shard_map/pallas_call | solution.py:55
  24.8 1.3 %collective-permute-done.8.refs_1_ = bf16[1,64,512]{2,1,0:T(8,128)(2,1)S(1)} collective-permute-done((bf16[1,64,512]{2,1,0:T(8,128)(2,1)S(1)}, bf16[1,64,512]{2,1,0:T(8,128)(2,1)S(1)}, u32[]{:S(2)}, u32[]{:S(2)}) %collective-permute-start.8) | collective-permute-done | bytes 65568 | tf_op jit(solution)/shard_map/ppermute | solution.py:33
  26.2 1.5 %collective-permute-done.13.refs_1_ = bf16[16,2560]{1,0:T(8,128)(2,1)S(1)} collective-permute-done((bf16[16,2560]{1,0:T(8,128)(2,1)S(1)}, bf16[16,2560]{1,0:T(8,128)(2,1)S(1)}, u32[]{:S(2)}, u32[]{:S(2)}) %collective-permute-start.13) | collective-permute-done | bytes 81952 | tf_op jit(solution)/shard_map/ppermute | solution.py:33
  27.7 1.2 %collective-permute-start.14 = (bf16[16,2560]{1,0:T(8,128)(2,1)S(1)}, bf16[16,2560]{1,0:T(8,128)(2,1)S(1)}, u32[]{:S(2)}, u32[]{:S(2)}) collective-permute-start(bf16[16,2560]{1,0:T(8,128)(2,1)S(1)} %shard_map.104.refs_4_.refs_0_), channel_id=1, source_target_pairs={{0,8},{1,9},{4,12},{5,13},{8,0},{9,1},{12,4},{13,5},{2,10},{3,11},... | collective-permute-start | bytes 245768 | tf_op jit(solution)/shard_map/ppermute | solution.py:33
  28.9 1.7 %shard_map.105 = (f32[16,64,512]{2,1,0:T(8,128)}, f32[8,128]{1,0:T(8,128)S(1)}) custom-call(s32[8]{0:T(128)} %refs_0_.8, bf16[4,64,512]{2,1,0:T(8,128)(2,1)S(1)} %shard_map.103.refs_2_.refs_1_, bf16[4,64,512]{2,1,0:T(8,128)(2,1)S(1)} %collective-permute-done.12.refs_2_, f32[16,64,512]{2,1,0:T(8,128)} %get-tuple-element.37.refs_3_, ...), custom_call_target="tpu_custom_call", output_to_operand_aliasing={{0}: (3, {})} | custom-call | bytes 4722720 | tf_op jit(solution)/shard_map/pallas_call | solution.py:55
  30.8 2.4 %shard_map.107 = (bf16[512,2560]{1,0:T(8,128)(2,1)}, f32[8,128]{1,0:T(8,128)S(1)}) custom-call(bf16[512,1024]{1,0:T(8,128)(2,1)S(1)} %shard_map.106.refs_0_, bf16[2560,512]{1,0:T(8,128)(2,1)S(1)} %copy-done.1, bf16[2560,512]{1,0:T(8,128)(2,1)S(1)} %collective-permute-done.1.refs_1_.refs_2_, bf16[64,512]{1,0:T(8,128)(2,1)S(1)} %get-tuple-element.32.refs_1_.refs_2_.refs_3_, ...), custom_call_target="tpu_custom_call" | custom-call | flops 1140850688 | bytes 9310208 | tf_op jit(solution)/shard_map/pallas_call | solution.py:55
  34.1 3.1 %shard_map.109 = (bf16[512,2560]{1,0:T(8,128)(2,1)}, f32[8,128]{1,0:T(8,128)S(1)}) custom-call(bf16[512,1024]{1,0:T(8,128)(2,1)S(1)} %shard_map.106.refs_0_, bf16[2560,512]{1,0:T(8,128)(2,1)S(1)} %copy-done.1, bf16[2560,512]{1,0:T(8,128)(2,1)S(1)} %collective-permute-done.1.refs_1_.refs_2_, ...), custom_call_target="tpu_custom_call", output_to_operand_aliasing={{0}: (5, {})} | custom-call | flops 1711276032 | bytes 11931648 | tf_op jit(solution)/shard_map/pallas_call | solution.py:55
  37.2 1.0 %collective-permute-done.15.refs_1_ = bf16[16,2560]{1,0:T(8,128)(2,1)S(1)} collective-permute-done((bf16[16,2560]{1,0:T(8,128)(2,1)S(1)}, bf16[16,2560]{1,0:T(8,128)(2,1)S(1)}, u32[]{:S(2)}, u32[]{:S(2)}) %collective-permute-start.15) | collective-permute-done | bytes 81952 | tf_op jit(solution)/shard_map/ppermute | solution.py:33
  38.3 0.8 %shard_map.111.refs_1_ = f32[64,2560]{1,0:T(8,128)} custom-call(bf16[32,2560]{1,0:T(8,128)(2,1)S(1)} %shard_map.110.refs_0_.refs_1_, bf16[32,2560]{1,0:T(8,128)(2,1)S(1)} %shard_map.110.refs_0_.refs_1_), custom_call_target="tpu_custom_call" | custom-call | bytes 819200 | tf_op jit(solution)/shard_map/pallas_call | solution.py:55
  39.1 0.6 %collective-permute-done.16.refs_0_ = bf16[32,2560]{1,0:T(8,128)(2,1)S(1)} collective-permute-done((bf16[32,2560]{1,0:T(8,128)(2,1)S(1)}, bf16[32,2560]{1,0:T(8,128)(2,1)S(1)}, u32[]{:S(2)}, u32[]{:S(2)}) %collective-permute-start.16) | collective-permute-done | bytes 163872 | tf_op jit(solution)/shard_map/ppermute | solution.py:26
  39.7 0.8 %shard_map.112 = f32[64,2560]{1,0:T(8,128)} custom-call(bf16[32,2560]{1,0:T(8,128)(2,1)S(1)} %collective-permute-done.16.refs_0_, f32[64,2560]{1,0:T(8,128)} %shard_map.111.refs_1_), custom_call_target="tpu_custom_call", output_to_operand_aliasing={{}: (1, {})} | custom-call | bytes 1474560 | tf_op jit(solution)/shard_map/pallas_call | solution.py:55
  (37 shorter events, 3.8 us)
Async XLA Ops:
  0.6 9.4 %copy-start = (bf16[512,2560]{1,0:T(8,128)(2,1)S(1)}, bf16[512,2560]{1,0:T(8,128)(2,1)}, u32[]{:S(2)}) copy-start(bf16[512,2560]{1,0:T(8,128)(2,1)} %refs_3_.3) | copy-start | bytes 7864324
  0.6 9.4 %copy-start.2 = (bf16[2560,64]{0,1:T(8,128)(2,1)S(1)}, bf16[2560,64]{0,1:T(8,128)(2,1)}, u32[]{:S(2)}) copy-start(bf16[2560,64]{0,1:T(8,128)(2,1)} %param.10) | copy-start | bytes 983044
  0.7 10.3 %collective-permute-start.1 = (bf16[2560,512]{1,0:T(8,128)(2,1)}, bf16[2560,512]{1,0:T(8,128)(2,1)S(1)}, u32[]{:S(2)}, u32[]{:S(2)}) collective-permute-start(bf16[2560,512]{1,0:T(8,128)(2,1)} %refs_1_.7), channel_id=1, source_target_pairs={{0,1},{1,0},{2,3},{3,2},{4,5},{5,4},{6,7},{7,6},{8,9},{9,8},{10,11... | collective-permute-start | bytes 7864328 | tf_op jit(solution)/shard_map/ppermute | solution.py:26
  2.7 8.8 %collective-permute-start.3 = (bf16[64,512]{1,0:T(8,128)(2,1)S(1)}, bf16[64,512]{1,0:T(8,128)(2,1)S(1)}, u32[]{:S(2)}, u32[]{:S(2)}) collective-permute-start(bf16[64,512]{1,0:T(8,128)(2,1)S(1)} %get-tuple-element.27), channel_id=1, source_target_pairs={{0,8},{1,9},{4,12},{5,13},{8,0},{9,1},{12,4},{13,5},{2,10},{3,11},... | collective-permute-start | bytes 196616 | tf_op jit(solution)/shard_map/ppermute | solution.py:33
  6.3 6.7 %collective-permute-start.4 = (bf16[64,512]{1,0:T(8,128)(2,1)S(1)}, bf16[64,512]{1,0:T(8,128)(2,1)S(1)}, u32[]{:S(2)}, u32[]{:S(2)}) collective-permute-start(bf16[64,512]{1,0:T(8,128)(2,1)S(1)} %get-tuple-element.28), channel_id=1, source_target_pairs={{0,12},{1,13},{4,8},{5,9},{8,4},{9,5},{12,0},{13,1},{2,14},{3,15},... | collective-permute-start | bytes 196616 | tf_op jit(solution)/shard_map/ppermute | solution.py:33
  7.6 5.6 %collective-permute-start.5 = (bf16[64,512]{1,0:T(8,128)(2,1)S(1)}, bf16[64,512]{1,0:T(8,128)(2,1)S(1)}, u32[]{:S(2)}, u32[]{:S(2)}) collective-permute-start(bf16[64,512]{1,0:T(8,128)(2,1)S(1)} %get-tuple-element.29), channel_id=1, source_target_pairs={{0,4},{1,5},{4,0},{5,1},{8,12},{9,13},{12,8},{13,9},{2,6},{3,7},{6... | collective-permute-start | bytes 196616 | tf_op jit(solution)/shard_map/ppermute | solution.py:33
  7.8 7.2 %collective-permute-start = (bf16[96,512]{1,0:T(8,128)(2,1)S(1)}, bf16[96,512]{1,0:T(8,128)(2,1)S(1)}, u32[]{:S(2)}, u32[]{:S(2)}) collective-permute-start(bf16[96,512]{1,0:T(8,128)(2,1)S(1)} %get-tuple-element.24), channel_id=1, source_target_pairs={{0,2},{2,0},{1,3},{3,1},{4,6},{6,4},{5,7},{7,5},{8,10},{10,8},{9,1... | collective-permute-start | bytes 294920 | tf_op jit(solution)/shard_map/ppermute | solution.py:26
  10.0 3.2 %copy-start.3 = (bf16[512,512]{1,0:T(8,128)(2,1)S(1)}, bf16[512,512]{1,0:T(8,128)(2,1)}, u32[]{:S(2)}) copy-start(bf16[512,512]{1,0:T(8,128)(2,1)} %refs_1_.5) | copy-start | bytes 1572868
  11.0 4.4 %collective-permute-start.2 = (bf16[64,512]{1,0:T(8,128)(2,1)S(1)}, bf16[64,512]{1,0:T(8,128)(2,1)S(1)}, u32[]{:S(2)}, u32[]{:S(2)}) collective-permute-start(bf16[64,512]{1,0:T(8,128)(2,1)S(1)} %shard_map.96), channel_id=1, source_target_pairs={{0,2},{2,0},{1,3},{3,1},{4,6},{6,4},{5,7},{7,5},{8,10},{10,8},{9,1... | collective-permute-start | bytes 196616 | tf_op jit(solution)/shard_map/ppermute | solution.py:26
  13.5 6.9 %collective-permute-start.7 = (f32[64,512]{1,0:T(8,128)S(1)}, f32[64,512]{1,0:T(8,128)S(1)}, u32[]{:S(2)}, u32[]{:S(2)}) collective-permute-start(f32[64,512]{1,0:T(8,128)S(1)} %shard_map.97.refs_4_.refs_1_), channel_id=1, source_target_pairs={{0,2},{2,0},{1,3},{3,1},{4,6},{6,4},{5,7},{7,5},{8,10},{10,8},{9,1... | collective-permute-start | bytes 393224 | tf_op jit(solution)/shard_map/ppermute | solution.py:26
  15.7 9.0 %collective-permute-start.10 = (bf16[1,64,512]{2,1,0:T(8,128)(2,1)S(1)}, bf16[1,64,512]{2,1,0:T(8,128)(2,1)S(1)}, u32[]{:S(2)}, u32[]{:S(2)}) collective-permute-start(bf16[1,64,512]{2,1,0:T(8,128)(2,1)S(1)} %get-tuple-element.31.refs_4_.refs_0_), channel_id=1, source_target_pairs={{0,8},{1,9},{4,12},{5,13},{8,0},{9,1},{12,4},{13,5},{2,10},{3,11},... | collective-permute-start | bytes 196616 | tf_op jit(solution)/shard_map/ppermute | solution.py:33
  18.5 6.3 %collective-permute-start.9 = (bf16[1,64,512]{2,1,0:T(8,128)(2,1)S(1)}, bf16[1,64,512]{2,1,0:T(8,128)(2,1)S(1)}, u32[]{:S(2)}, u32[]{:S(2)}) collective-permute-start(bf16[1,64,512]{2,1,0:T(8,128)(2,1)S(1)} %get-tuple-element.31.refs_4_.refs_0_), channel_id=1, source_target_pairs={{0,12},{1,13},{4,8},{5,9},{8,4},{9,5},{12,0},{13,1},{2,14},{3,15},... | collective-permute-start | bytes 196616 | tf_op jit(solution)/shard_map/ppermute | solution.py:33
  20.0 10.7 %collective-permute-start.6 = (bf16[416,512]{1,0:T(8,128)(2,1)S(1)}, bf16[416,512]{1,0:T(8,128)(2,1)S(1)}, u32[]{:S(2)}, u32[]{:S(2)}) collective-permute-start(bf16[416,512]{1,0:T(8,128)(2,1)S(1)} %get-tuple-element.30), channel_id=1, source_target_pairs={{0,2},{2,0},{1,3},{3,1},{4,6},{6,4},{5,7},{7,5},{8,10},{10,8},{9,1... | collective-permute-start | bytes 1277960 | tf_op jit(solution)/shard_map/ppermute | solution.py:26
  21.0 1.7 %collective-permute-start.11 = (f32[32,2560]{1,0:T(8,128)S(1)}, f32[32,2560]{1,0:T(8,128)S(1)}, u32[]{:S(2)}, u32[]{:S(2)}) collective-permute-start(f32[32,2560]{1,0:T(8,128)S(1)} %get-tuple-element.34), channel_id=1, source_target_pairs={{0,1},{1,0},{2,3},{3,2},{4,5},{5,4},{6,7},{7,6},{8,9},{9,8},{10,11... | collective-permute-start | bytes 983048 | tf_op jit(solution)/shard_map/ppermute | solution.py:26
  21.1 5.0 %collective-permute-start.8 = (bf16[1,64,512]{2,1,0:T(8,128)(2,1)S(1)}, bf16[1,64,512]{2,1,0:T(8,128)(2,1)S(1)}, u32[]{:S(2)}, u32[]{:S(2)}) collective-permute-start(bf16[1,64,512]{2,1,0:T(8,128)(2,1)S(1)} %shard_map.100), channel_id=1, source_target_pairs={{0,4},{1,5},{4,0},{5,1},{8,12},{9,13},{12,8},{13,9},{2,6},{3,7},{6... | collective-permute-start | bytes 196616 | tf_op jit(solution)/shard_map/ppermute | solution.py:33
  22.7 5.0 %collective-permute-start.13 = (bf16[16,2560]{1,0:T(8,128)(2,1)S(1)}, bf16[16,2560]{1,0:T(8,128)(2,1)S(1)}, u32[]{:S(2)}, u32[]{:S(2)}) collective-permute-start(bf16[16,2560]{1,0:T(8,128)(2,1)S(1)} %get-tuple-element.35.refs_0_), channel_id=1, source_target_pairs={{0,4},{1,5},{4,0},{5,1},{8,12},{9,13},{12,8},{13,9},{2,6},{3,7},{6... | collective-permute-start | bytes 245768 | tf_op jit(solution)/shard_map/ppermute | solution.py:33
  26.1 2.8 %collective-permute-start.12 = (bf16[4,64,512]{2,1,0:T(8,128)(2,1)S(1)}, bf16[4,64,512]{2,1,0:T(8,128)(2,1)S(1)}, u32[]{:S(2)}, u32[]{:S(2)}) collective-permute-start(bf16[4,64,512]{2,1,0:T(8,128)(2,1)S(1)} %shard_map.103.refs_2_.refs_1_), channel_id=1, source_target_pairs={{0,1},{1,0},{2,3},{3,2},{4,5},{5,4},{6,7},{7,6},{8,9},{9,8},{10,11... | collective-permute-start | bytes 786440 | tf_op jit(solution)/shard_map/ppermute | solution.py:26
  27.7 3.0 %copy-start.1 = (bf16[2560,512]{1,0:T(8,128)(2,1)S(1)}, bf16[2560,512]{1,0:T(8,128)(2,1)}, u32[]{:S(2)}) copy-start(bf16[2560,512]{1,0:T(8,128)(2,1)} %refs_1_.7) | copy-start | bytes 7864324
  27.7 5.9 %collective-permute-start.14 = (bf16[16,2560]{1,0:T(8,128)(2,1)S(1)}, bf16[16,2560]{1,0:T(8,128)(2,1)S(1)}, u32[]{:S(2)}, u32[]{:S(2)}) collective-permute-start(bf16[16,2560]{1,0:T(8,128)(2,1)S(1)} %shard_map.104.refs_4_.refs_0_), channel_id=1, source_target_pairs={{0,8},{1,9},{4,12},{5,13},{8,0},{9,1},{12,4},{13,5},{2,10},{3,11},... | collective-permute-start | bytes 245768 | tf_op jit(solution)/shard_map/ppermute | solution.py:33
  33.7 4.5 %collective-permute-start.15 = (bf16[16,2560]{1,0:T(8,128)(2,1)S(1)}, bf16[16,2560]{1,0:T(8,128)(2,1)S(1)}, u32[]{:S(2)}, u32[]{:S(2)}) collective-permute-start(bf16[16,2560]{1,0:T(8,128)(2,1)S(1)} %shard_map.108.refs_6_.refs_0_), channel_id=1, source_target_pairs={{0,4},{1,5},{4,0},{5,1},{8,12},{9,13},{12,8},{13,9},{2,6},{3,7},{6... | collective-permute-start | bytes 245768 | tf_op jit(solution)/shard_map/ppermute | solution.py:33
  38.2 1.5 %collective-permute-start.16 = (bf16[32,2560]{1,0:T(8,128)(2,1)S(1)}, bf16[32,2560]{1,0:T(8,128)(2,1)S(1)}, u32[]{:S(2)}, u32[]{:S(2)}) collective-permute-start(bf16[32,2560]{1,0:T(8,128)(2,1)S(1)} %shard_map.110.refs_0_.refs_1_), channel_id=1, source_target_pairs={{0,1},{1,0},{2,3},{3,2},{4,5},{5,4},{6,7},{7,6},{8,9},{9,8},{10,11... | collective-permute-start | bytes 491528 | tf_op jit(solution)/shard_map/ppermute | solution.py:26

commit v21 on v20

--- a/solution.py
+++ b/solution.py
@@ -9,7 +9,7 @@
 f32 = jnp.float32
 bf16 = jnp.bfloat16
 
-early_part = 3
+early_part = 2
 
 (busy, first_cost, middling, filling, brief, slight) = (
     10**10, 5 * 10**9, 5 * 10**9, 10**10, 3 * 10**9, 15 * 10**8

time: 40.6 us -> 43.4 us (1.069)
  starting transfers between devices: 16.4 us -> 19.8 us
  waiting for transfers between devices: 8.49 us -> 7.98 us
    ppermute x9, starting transfers between devices: 11.6 us -> 14.1 us  [swap(): lax.ppermute(x, ('own', 'sub'), [(i, i ^ other) for i in range(whole)])]
    ppermute x9, waiting for transfers between devices: 6.05 us -> 4.42 us  [swap(): lax.ppermute(x, ('own', 'sub'), [(i, i ^ other) for i in range(whole)])]
    ppermute x8, waiting for transfers between devices: 2.44 us -> 3.57 us  [shift(): lax.ppermute(x, axis, [(i, (i + step) % count) for i in range(count)])]
    ppermute x8, starting transfers between devices: 4.81 us -> 5.73 us  [shift(): lax.ppermute(x, axis, [(i, (i + step) % count) for i in range(count)])]
  transfers between devices with their start and end apart: 17 -> 17, of which waited for: 9 -> 8; matrix products, arithmetic and copies ran while one was open for 0% -> 0% of each run, Pallas kernels for 33% -> 30%
where the time goes in v21:
time: 43.4 us; the launch traced here: 43.3 us
  starting transfers between devices  19.8 us (46%)
  Pallas kernels  13.9 us (32%)
  waiting for transfers between devices  7.98 us (18%)
  between operations  1.53 us (4%)
    ppermute x9, starting transfers between devices, swap(): lax.ppermute(x, ('own', 'sub'), [(i, i ^ other) for i in range(whole)])  14.1 us
    pallas_call x19, Pallas kernels, call(): pl.pallas_call(kernel, out_shape=outs, in_specs=list(specs) + [anywhere]...  13.9 us
    ppermute x8, starting transfers between devices, shift(): lax.ppermute(x, axis, [(i, (i + step) % count) for i in range(count)])  5.73 us
    ppermute x9, waiting for transfers between devices, swap(): lax.ppermute(x, ('own', 'sub'), [(i, i ^ other) for i in range(whole)])  4.42 us
    ppermute x8, waiting for transfers between devices, shift(): lax.ppermute(x, axis, [(i, (i + step) % count) for i in range(count)])  3.57 us
  transfers between devices with their start and end apart: 17, of which 8 were waited for; matrix products, arithmetic and copies ran while one was open for 0% of the time, Pallas kernels for 30%

profile of v21, /device:TPU:0, one launch (start us, length us, event | category | flops | bytes accessed | tf_op | source)
XLA Modules:
  0.0 43.3 jit_solution(11540022259329236380)
XLA Ops:
  1.2 1.5 %shard_map.94 = (bf16[64,512]{1,0:T(8,128)(2,1)S(1)}, bf16[64,512]{1,0:T(8,128)(2,1)S(1)}, bf16[64,512]{1,0:T(8,128)(2,1)S(1)}, bf16[64,512]{1,0:T(8,128)(2,1)S(...) custom-call(s32[8]{0:T(128)} %refs_0_.8, bf16[16,64,512]{2,1,0:T(8,128)(2,1)} %refs_1_.4, bf16[512,512]{1,0:T(8,128)(2,1)} %refs_1_.5), custom_call_target="tpu_custom_call" | custom-call | flops 5000000000 | bytes 1904672 | tf_op jit(solution)/shard_map/pallas_call | solution.py:55
  2.7 3.6 %collective-permute-start.3 = (bf16[64,512]{1,0:T(8,128)(2,1)S(1)}, bf16[64,512]{1,0:T(8,128)(2,1)S(1)}, u32[]{:S(2)}, u32[]{:S(2)}) collective-permute-start(bf16[64,512]{1,0:T(8,128)(2,1)S(1)} %get-tuple-element.27), channel_id=1, source_target_pairs={{0,8},{1,9},{4,12},{5,13},{8,0},{9,1},{12,4},{13,5},{2,10},{3,11},... | collective-permute-start | bytes 196616 | tf_op jit(solution)/shard_map/ppermute | solution.py:33
  6.3 1.3 %collective-permute-start.4 = (bf16[64,512]{1,0:T(8,128)(2,1)S(1)}, bf16[64,512]{1,0:T(8,128)(2,1)S(1)}, u32[]{:S(2)}, u32[]{:S(2)}) collective-permute-start(bf16[64,512]{1,0:T(8,128)(2,1)S(1)} %get-tuple-element.28), channel_id=1, source_target_pairs={{0,12},{1,13},{4,8},{5,9},{8,4},{9,5},{12,0},{13,1},{2,14},{3,15},... | collective-permute-start | bytes 196616 | tf_op jit(solution)/shard_map/ppermute | solution.py:33
  7.8 1.5 %collective-permute-start = (bf16[64,512]{1,0:T(8,128)(2,1)S(1)}, bf16[64,512]{1,0:T(8,128)(2,1)S(1)}, u32[]{:S(2)}, u32[]{:S(2)}) collective-permute-start(bf16[64,512]{1,0:T(8,128)(2,1)S(1)} %get-tuple-element.24), channel_id=1, source_target_pairs={{0,2},{2,0},{1,3},{3,1},{4,6},{6,4},{5,7},{7,5},{8,10},{10,8},{9,1... | collective-permute-start | bytes 196616 | tf_op jit(solution)/shard_map/ppermute | solution.py:26
  10.0 0.9 %shard_map.95.refs_0_.refs_6_.refs_1_ = f32[64,512]{1,0:T(8,128)S(1)} custom-call(bf16[512,2560]{1,0:T(8,128)(2,1)S(1)} %copy-done, bf16[64,2560]{1,0:T(8,128)(2,1)S(1)} %bitcast.2, bf16[64,512]{1,0:T(8,128)(2,1)S(1)} %get-tuple-element.25.refs_2_.refs_1_), custom_call_target="tpu_custom_call" | custom-call | flops 167772160 | bytes 3080192 | tf_op jit(solution)/shard_map/pallas_call | solution.py:55
  11.0 0.6 %collective-permute-start.2 = (bf16[64,512]{1,0:T(8,128)(2,1)S(1)}, bf16[64,512]{1,0:T(8,128)(2,1)S(1)}, u32[]{:S(2)}, u32[]{:S(2)}) collective-permute-start(bf16[64,512]{1,0:T(8,128)(2,1)S(1)} %shard_map.96), channel_id=1, source_target_pairs={{0,2},{2,0},{1,3},{3,1},{4,6},{6,4},{5,7},{7,5},{8,10},{10,8},{9,1... | collective-permute-start | bytes 196616 | tf_op jit(solution)/shard_map/ppermute | solution.py:26
  11.6 1.4 %collective-permute-done.4.refs_3_ = bf16[64,512]{1,0:T(8,128)(2,1)S(1)} collective-permute-done((bf16[64,512]{1,0:T(8,128)(2,1)S(1)}, bf16[64,512]{1,0:T(8,128)(2,1)S(1)}, u32[]{:S(2)}, u32[]{:S(2)}) %collective-permute-start.4) | collective-permute-done | bytes 65568 | tf_op jit(solution)/shard_map/ppermute | solution.py:33
  13.5 1.6 %collective-permute-start.7 = (f32[64,512]{1,0:T(8,128)S(1)}, f32[64,512]{1,0:T(8,128)S(1)}, u32[]{:S(2)}, u32[]{:S(2)}) collective-permute-start(f32[64,512]{1,0:T(8,128)S(1)} %shard_map.97.refs_4_.refs_1_), channel_id=1, source_target_pairs={{0,2},{2,0},{1,3},{3,1},{4,6},{6,4},{5,7},{7,5},{8,10},{10,8},{9,1... | collective-permute-start | bytes 393224 | tf_op jit(solution)/shard_map/ppermute | solution.py:26
  15.7 2.8 %collective-permute-start.10 = (bf16[1,64,512]{2,1,0:T(8,128)(2,1)S(1)}, bf16[1,64,512]{2,1,0:T(8,128)(2,1)S(1)}, u32[]{:S(2)}, u32[]{:S(2)}) collective-permute-start(bf16[1,64,512]{2,1,0:T(8,128)(2,1)S(1)} %get-tuple-element.31.refs_4_.refs_0_), channel_id=1, source_target_pairs={{0,8},{1,9},{4,12},{5,13},{8,0},{9,1},{12,4},{13,5},{2,10},{3,11},... | collective-permute-start | bytes 196616 | tf_op jit(solution)/shard_map/ppermute | solution.py:33
  18.5 1.5 %collective-permute-start.9 = (bf16[1,64,512]{2,1,0:T(8,128)(2,1)S(1)}, bf16[1,64,512]{2,1,0:T(8,128)(2,1)S(1)}, u32[]{:S(2)}, u32[]{:S(2)}) collective-permute-start(bf16[1,64,512]{2,1,0:T(8,128)(2,1)S(1)} %get-tuple-element.31.refs_4_.refs_0_), channel_id=1, source_target_pairs={{0,12},{1,13},{4,8},{5,9},{8,4},{9,5},{12,0},{13,1},{2,14},{3,15},... | collective-permute-start | bytes 196616 | tf_op jit(solution)/shard_map/ppermute | solution.py:33
  20.7 1.3 %collective-permute-start.6 = (bf16[448,512]{1,0:T(8,128)(2,1)S(1)}, bf16[448,512]{1,0:T(8,128)(2,1)S(1)}, u32[]{:S(2)}, u32[]{:S(2)}) collective-permute-start(bf16[448,512]{1,0:T(8,128)(2,1)S(1)} %get-tuple-element.30), channel_id=1, source_target_pairs={{0,2},{2,0},{1,3},{3,1},{4,6},{6,4},{5,7},{7,5},{8,10},{10,8},{9,1... | collective-permute-start | bytes 1376264 | tf_op jit(solution)/shard_map/ppermute | solution.py:26
  22.3 1.0 %collective-permute-start.13 = (bf16[16,2560]{1,0:T(8,128)(2,1)S(1)}, bf16[16,2560]{1,0:T(8,128)(2,1)S(1)}, u32[]{:S(2)}, u32[]{:S(2)}) collective-permute-start(bf16[16,2560]{1,0:T(8,128)(2,1)S(1)} %get-tuple-element.35.refs_0_), channel_id=1, source_target_pairs={{0,4},{1,5},{4,0},{5,1},{8,12},{9,13},{12,8},{13,9},{2,6},{3,7},{6... | collective-permute-start | bytes 245768 | tf_op jit(solution)/shard_map/ppermute | solution.py:33
  23.3 1.4 %shard_map.102 = (f32[16,64,512]{2,1,0:T(8,128)}, f32[8,128]{1,0:T(8,128)S(1)}) custom-call(bf16[16,2560]{1,0:T(8,128)(2,1)S(1)} %get-tuple-element.35.refs_0_), custom_call_target="tpu_custom_call" | custom-call | flops 10000000000 | bytes 2101248 | tf_op jit(solution)/shard_map/pallas_call | solution.py:55
  24.7 1.3 %collective-permute-done.8.refs_1_ = bf16[1,64,512]{2,1,0:T(8,128)(2,1)S(1)} collective-permute-done((bf16[1,64,512]{2,1,0:T(8,128)(2,1)S(1)}, bf16[1,64,512]{2,1,0:T(8,128)(2,1)S(1)}, u32[]{:S(2)}, u32[]{:S(2)}) %collective-permute-start.8) | collective-permute-done | bytes 65568 | tf_op jit(solution)/shard_map/ppermute | solution.py:33
  26.1 1.5 %collective-permute-done.13.refs_1_ = bf16[16,2560]{1,0:T(8,128)(2,1)S(1)} collective-permute-done((bf16[16,2560]{1,0:T(8,128)(2,1)S(1)}, bf16[16,2560]{1,0:T(8,128)(2,1)S(1)}, u32[]{:S(2)}, u32[]{:S(2)}) %collective-permute-start.13) | collective-permute-done | bytes 81952 | tf_op jit(solution)/shard_map/ppermute | solution.py:33
  27.7 1.9 %collective-permute-start.14 = (bf16[16,2560]{1,0:T(8,128)(2,1)S(1)}, bf16[16,2560]{1,0:T(8,128)(2,1)S(1)}, u32[]{:S(2)}, u32[]{:S(2)}) collective-permute-start(bf16[16,2560]{1,0:T(8,128)(2,1)S(1)} %shard_map.104.refs_4_.refs_0_), channel_id=1, source_target_pairs={{0,8},{1,9},{4,12},{5,13},{8,0},{9,1},{12,4},{13,5},{2,10},{3,11},... | collective-permute-start | bytes 245768 | tf_op jit(solution)/shard_map/ppermute | solution.py:33
  29.6 1.6 %shard_map.105 = (f32[16,64,512]{2,1,0:T(8,128)}, f32[8,128]{1,0:T(8,128)S(1)}) custom-call(s32[8]{0:T(128)} %refs_0_.8, bf16[4,64,512]{2,1,0:T(8,128)(2,1)S(1)} %shard_map.103.refs_2_.refs_1_, bf16[4,64,512]{2,1,0:T(8,128)(2,1)S(1)} %collective-permute-done.12.refs_2_, f32[16,64,512]{2,1,0:T(8,128)} %get-tuple-element.37.refs_3_, ...), custom_call_target="tpu_custom_call", output_to_operand_aliasing={{0}: (3, {})} | custom-call | bytes 4722720 | tf_op jit(solution)/shard_map/pallas_call | solution.py:55
  31.2 2.4 %collective-permute-done.6.refs_3_ = bf16[448,512]{1,0:T(8,128)(2,1)S(1)} collective-permute-done((bf16[448,512]{1,0:T(8,128)(2,1)S(1)}, bf16[448,512]{1,0:T(8,128)(2,1)S(1)}, u32[]{:S(2)}, u32[]{:S(2)}) %collective-permute-start.6) | collective-permute-done | bytes 458784 | tf_op jit(solution)/shard_map/ppermute | solution.py:26
  33.8 2.4 %shard_map.107 = (bf16[512,2560]{1,0:T(8,128)(2,1)}, f32[8,128]{1,0:T(8,128)S(1)}) custom-call(bf16[512,1024]{1,0:T(8,128)(2,1)S(1)} %shard_map.106.refs_0_, bf16[2560,512]{1,0:T(8,128)(2,1)S(1)} %copy-done.1, bf16[2560,512]{1,0:T(8,128)(2,1)S(1)} %collective-permute-done.1.refs_1_.refs_2_, bf16[64,512]{1,0:T(8,128)(2,1)S(1)} %get-tuple-element.32.refs_1_.refs_2_.refs_3_, ...), custom_call_target="tpu_custom_call" | custom-call | flops 1140850688 | bytes 9310208 | tf_op jit(solution)/shard_map/pallas_call | solution.py:55
  36.2 1.7 %collective-permute-start.15 = (bf16[16,2560]{1,0:T(8,128)(2,1)S(1)}, bf16[16,2560]{1,0:T(8,128)(2,1)S(1)}, u32[]{:S(2)}, u32[]{:S(2)}) collective-permute-start(bf16[16,2560]{1,0:T(8,128)(2,1)S(1)} %shard_map.108.refs_6_.refs_0_), channel_id=1, source_target_pairs={{0,4},{1,5},{4,0},{5,1},{8,12},{9,13},{12,8},{13,9},{2,6},{3,7},{6... | collective-permute-start | bytes 245768 | tf_op jit(solution)/shard_map/ppermute | solution.py:33
  37.9 3.1 %shard_map.109 = (bf16[512,2560]{1,0:T(8,128)(2,1)}, f32[8,128]{1,0:T(8,128)S(1)}) custom-call(bf16[512,1024]{1,0:T(8,128)(2,1)S(1)} %shard_map.106.refs_0_, bf16[2560,512]{1,0:T(8,128)(2,1)S(1)} %copy-done.1, bf16[2560,512]{1,0:T(8,128)(2,1)S(1)} %collective-permute-done.1.refs_1_.refs_2_, ...), custom_call_target="tpu_custom_call", output_to_operand_aliasing={{0}: (5, {})} | custom-call | flops 1711276032 | bytes 11931648 | tf_op jit(solution)/shard_map/pallas_call | solution.py:55
  41.1 0.8 %shard_map.111.refs_1_ = f32[64,2560]{1,0:T(8,128)} custom-call(bf16[32,2560]{1,0:T(8,128)(2,1)S(1)} %shard_map.110.refs_0_.refs_1_, bf16[32,2560]{1,0:T(8,128)(2,1)S(1)} %shard_map.110.refs_0_.refs_1_), custom_call_target="tpu_custom_call" | custom-call | bytes 819200 | tf_op jit(solution)/shard_map/pallas_call | solution.py:55
  41.9 0.6 %collective-permute-done.16.refs_0_ = bf16[32,2560]{1,0:T(8,128)(2,1)S(1)} collective-permute-done((bf16[32,2560]{1,0:T(8,128)(2,1)S(1)}, bf16[32,2560]{1,0:T(8,128)(2,1)S(1)}, u32[]{:S(2)}, u32[]{:S(2)}) %collective-permute-start.16) | collective-permute-done | bytes 163872 | tf_op jit(solution)/shard_map/ppermute | solution.py:26
  42.5 0.8 %shard_map.112 = f32[64,2560]{1,0:T(8,128)} custom-call(bf16[32,2560]{1,0:T(8,128)(2,1)S(1)} %collective-permute-done.16.refs_0_, f32[64,2560]{1,0:T(8,128)} %shard_map.111.refs_1_), custom_call_target="tpu_custom_call", output_to_operand_aliasing={{}: (1, {})} | custom-call | bytes 1474560 | tf_op jit(solution)/shard_map/pallas_call | solution.py:55
  (37 shorter events, 3.3 us)
Async XLA Ops:
  0.6 9.4 %copy-start = (bf16[512,2560]{1,0:T(8,128)(2,1)S(1)}, bf16[512,2560]{1,0:T(8,128)(2,1)}, u32[]{:S(2)}) copy-start(bf16[512,2560]{1,0:T(8,128)(2,1)} %refs_3_.3) | copy-start | bytes 7864324
  0.6 9.4 %copy-start.2 = (bf16[2560,64]{0,1:T(8,128)(2,1)S(1)}, bf16[2560,64]{0,1:T(8,128)(2,1)}, u32[]{:S(2)}) copy-start(bf16[2560,64]{0,1:T(8,128)(2,1)} %param.10) | copy-start | bytes 983044
  0.7 10.3 %collective-permute-start.1 = (bf16[2560,512]{1,0:T(8,128)(2,1)}, bf16[2560,512]{1,0:T(8,128)(2,1)S(1)}, u32[]{:S(2)}, u32[]{:S(2)}) collective-permute-start(bf16[2560,512]{1,0:T(8,128)(2,1)} %refs_1_.7), channel_id=1, source_target_pairs={{0,1},{1,0},{2,3},{3,2},{4,5},{5,4},{6,7},{7,6},{8,9},{9,8},{10,11... | collective-permute-start | bytes 7864328 | tf_op jit(solution)/shard_map/ppermute | solution.py:26
  2.7 8.8 %collective-permute-start.3 = (bf16[64,512]{1,0:T(8,128)(2,1)S(1)}, bf16[64,512]{1,0:T(8,128)(2,1)S(1)}, u32[]{:S(2)}, u32[]{:S(2)}) collective-permute-start(bf16[64,512]{1,0:T(8,128)(2,1)S(1)} %get-tuple-element.27), channel_id=1, source_target_pairs={{0,8},{1,9},{4,12},{5,13},{8,0},{9,1},{12,4},{13,5},{2,10},{3,11},... | collective-permute-start | bytes 196616 | tf_op jit(solution)/shard_map/ppermute | solution.py:33
  6.3 6.7 %collective-permute-start.4 = (bf16[64,512]{1,0:T(8,128)(2,1)S(1)}, bf16[64,512]{1,0:T(8,128)(2,1)S(1)}, u32[]{:S(2)}, u32[]{:S(2)}) collective-permute-start(bf16[64,512]{1,0:T(8,128)(2,1)S(1)} %get-tuple-element.28), channel_id=1, source_target_pairs={{0,12},{1,13},{4,8},{5,9},{8,4},{9,5},{12,0},{13,1},{2,14},{3,15},... | collective-permute-start | bytes 196616 | tf_op jit(solution)/shard_map/ppermute | solution.py:33
  7.6 5.6 %collective-permute-start.5 = (bf16[64,512]{1,0:T(8,128)(2,1)S(1)}, bf16[64,512]{1,0:T(8,128)(2,1)S(1)}, u32[]{:S(2)}, u32[]{:S(2)}) collective-permute-start(bf16[64,512]{1,0:T(8,128)(2,1)S(1)} %get-tuple-element.29), channel_id=1, source_target_pairs={{0,4},{1,5},{4,0},{5,1},{8,12},{9,13},{12,8},{13,9},{2,6},{3,7},{6... | collective-permute-start | bytes 196616 | tf_op jit(solution)/shard_map/ppermute | solution.py:33
  7.8 7.2 %collective-permute-start = (bf16[64,512]{1,0:T(8,128)(2,1)S(1)}, bf16[64,512]{1,0:T(8,128)(2,1)S(1)}, u32[]{:S(2)}, u32[]{:S(2)}) collective-permute-start(bf16[64,512]{1,0:T(8,128)(2,1)S(1)} %get-tuple-element.24), channel_id=1, source_target_pairs={{0,2},{2,0},{1,3},{3,1},{4,6},{6,4},{5,7},{7,5},{8,10},{10,8},{9,1... | collective-permute-start | bytes 196616 | tf_op jit(solution)/shard_map/ppermute | solution.py:26
  10.0 3.2 %copy-start.3 = (bf16[512,512]{1,0:T(8,128)(2,1)S(1)}, bf16[512,512]{1,0:T(8,128)(2,1)}, u32[]{:S(2)}) copy-start(bf16[512,512]{1,0:T(8,128)(2,1)} %refs_1_.5) | copy-start | bytes 1572868
  11.0 4.4 %collective-permute-start.2 = (bf16[64,512]{1,0:T(8,128)(2,1)S(1)}, bf16[64,512]{1,0:T(8,128)(2,1)S(1)}, u32[]{:S(2)}, u32[]{:S(2)}) collective-permute-start(bf16[64,512]{1,0:T(8,128)(2,1)S(1)} %shard_map.96), channel_id=1, source_target_pairs={{0,2},{2,0},{1,3},{3,1},{4,6},{6,4},{5,7},{7,5},{8,10},{10,8},{9,1... | collective-permute-start | bytes 196616 | tf_op jit(solution)/shard_map/ppermute | solution.py:26
  13.5 6.5 %collective-permute-start.7 = (f32[64,512]{1,0:T(8,128)S(1)}, f32[64,512]{1,0:T(8,128)S(1)}, u32[]{:S(2)}, u32[]{:S(2)}) collective-permute-start(f32[64,512]{1,0:T(8,128)S(1)} %shard_map.97.refs_4_.refs_1_), channel_id=1, source_target_pairs={{0,2},{2,0},{1,3},{3,1},{4,6},{6,4},{5,7},{7,5},{8,10},{10,8},{9,1... | collective-permute-start | bytes 393224 | tf_op jit(solution)/shard_map/ppermute | solution.py:26
  15.7 9.0 %collective-permute-start.10 = (bf16[1,64,512]{2,1,0:T(8,128)(2,1)S(1)}, bf16[1,64,512]{2,1,0:T(8,128)(2,1)S(1)}, u32[]{:S(2)}, u32[]{:S(2)}) collective-permute-start(bf16[1,64,512]{2,1,0:T(8,128)(2,1)S(1)} %get-tuple-element.31.refs_4_.refs_0_), channel_id=1, source_target_pairs={{0,8},{1,9},{4,12},{5,13},{8,0},{9,1},{12,4},{13,5},{2,10},{3,11},... | collective-permute-start | bytes 196616 | tf_op jit(solution)/shard_map/ppermute | solution.py:33
  18.5 6.3 %collective-permute-start.9 = (bf16[1,64,512]{2,1,0:T(8,128)(2,1)S(1)}, bf16[1,64,512]{2,1,0:T(8,128)(2,1)S(1)}, u32[]{:S(2)}, u32[]{:S(2)}) collective-permute-start(bf16[1,64,512]{2,1,0:T(8,128)(2,1)S(1)} %get-tuple-element.31.refs_4_.refs_0_), channel_id=1, source_target_pairs={{0,12},{1,13},{4,8},{5,9},{8,4},{9,5},{12,0},{13,1},{2,14},{3,15},... | collective-permute-start | bytes 196616 | tf_op jit(solution)/shard_map/ppermute | solution.py:33
  20.6 1.7 %collective-permute-start.11 = (f32[32,2560]{1,0:T(8,128)S(1)}, f32[32,2560]{1,0:T(8,128)S(1)}, u32[]{:S(2)}, u32[]{:S(2)}) collective-permute-start(f32[32,2560]{1,0:T(8,128)S(1)} %get-tuple-element.34), channel_id=1, source_target_pairs={{0,1},{1,0},{2,3},{3,2},{4,5},{5,4},{6,7},{7,6},{8,9},{9,8},{10,11... | collective-permute-start | bytes 983048 | tf_op jit(solution)/shard_map/ppermute | solution.py:26
  20.7 5.4 %collective-permute-start.8 = (bf16[1,64,512]{2,1,0:T(8,128)(2,1)S(1)}, bf16[1,64,512]{2,1,0:T(8,128)(2,1)S(1)}, u32[]{:S(2)}, u32[]{:S(2)}) collective-permute-start(bf16[1,64,512]{2,1,0:T(8,128)(2,1)S(1)} %shard_map.100), channel_id=1, source_target_pairs={{0,4},{1,5},{4,0},{5,1},{8,12},{9,13},{12,8},{13,9},{2,6},{3,7},{6... | collective-permute-start | bytes 196616 | tf_op jit(solution)/shard_map/ppermute | solution.py:33
  20.7 12.9 %collective-permute-start.6 = (bf16[448,512]{1,0:T(8,128)(2,1)S(1)}, bf16[448,512]{1,0:T(8,128)(2,1)S(1)}, u32[]{:S(2)}, u32[]{:S(2)}) collective-permute-start(bf16[448,512]{1,0:T(8,128)(2,1)S(1)} %get-tuple-element.30), channel_id=1, source_target_pairs={{0,2},{2,0},{1,3},{3,1},{4,6},{6,4},{5,7},{7,5},{8,10},{10,8},{9,1... | collective-permute-start | bytes 1376264 | tf_op jit(solution)/shard_map/ppermute | solution.py:26
  22.3 5.3 %collective-permute-start.13 = (bf16[16,2560]{1,0:T(8,128)(2,1)S(1)}, bf16[16,2560]{1,0:T(8,128)(2,1)S(1)}, u32[]{:S(2)}, u32[]{:S(2)}) collective-permute-start(bf16[16,2560]{1,0:T(8,128)(2,1)S(1)} %get-tuple-element.35.refs_0_), channel_id=1, source_target_pairs={{0,4},{1,5},{4,0},{5,1},{8,12},{9,13},{12,8},{13,9},{2,6},{3,7},{6... | collective-permute-start | bytes 245768 | tf_op jit(solution)/shard_map/ppermute | solution.py:33
  26.1 3.5 %collective-permute-start.12 = (bf16[4,64,512]{2,1,0:T(8,128)(2,1)S(1)}, bf16[4,64,512]{2,1,0:T(8,128)(2,1)S(1)}, u32[]{:S(2)}, u32[]{:S(2)}) collective-permute-start(bf16[4,64,512]{2,1,0:T(8,128)(2,1)S(1)} %shard_map.103.refs_2_.refs_1_), channel_id=1, source_target_pairs={{0,1},{1,0},{2,3},{3,2},{4,5},{5,4},{6,7},{7,6},{8,9},{9,8},{10,11... | collective-permute-start | bytes 786440 | tf_op jit(solution)/shard_map/ppermute | solution.py:26
  27.6 6.1 %copy-start.1 = (bf16[2560,512]{1,0:T(8,128)(2,1)S(1)}, bf16[2560,512]{1,0:T(8,128)(2,1)}, u32[]{:S(2)}) copy-start(bf16[2560,512]{1,0:T(8,128)(2,1)} %refs_1_.7) | copy-start | bytes 7864324
  27.7 8.5 %collective-permute-start.14 = (bf16[16,2560]{1,0:T(8,128)(2,1)S(1)}, bf16[16,2560]{1,0:T(8,128)(2,1)S(1)}, u32[]{:S(2)}, u32[]{:S(2)}) collective-permute-start(bf16[16,2560]{1,0:T(8,128)(2,1)S(1)} %shard_map.104.refs_4_.refs_0_), channel_id=1, source_target_pairs={{0,8},{1,9},{4,12},{5,13},{8,0},{9,1},{12,4},{13,5},{2,10},{3,11},... | collective-permute-start | bytes 245768 | tf_op jit(solution)/shard_map/ppermute | solution.py:33
  36.2 4.8 %collective-permute-start.15 = (bf16[16,2560]{1,0:T(8,128)(2,1)S(1)}, bf16[16,2560]{1,0:T(8,128)(2,1)S(1)}, u32[]{:S(2)}, u32[]{:S(2)}) collective-permute-start(bf16[16,2560]{1,0:T(8,128)(2,1)S(1)} %shard_map.108.refs_6_.refs_0_), channel_id=1, source_target_pairs={{0,4},{1,5},{4,0},{5,1},{8,12},{9,13},{12,8},{13,9},{2,6},{3,7},{6... | collective-permute-start | bytes 245768 | tf_op jit(solution)/shard_map/ppermute | solution.py:33
  41.1 1.5 %collective-permute-start.16 = (bf16[32,2560]{1,0:T(8,128)(2,1)S(1)}, bf16[32,2560]{1,0:T(8,128)(2,1)S(1)}, u32[]{:S(2)}, u32[]{:S(2)}) collective-permute-start(bf16[32,2560]{1,0:T(8,128)(2,1)S(1)} %shard_map.110.refs_0_.refs_1_), channel_id=1, source_target_pairs={{0,1},{1,0},{2,3},{3,2},{4,5},{5,4},{6,7},{7,6},{8,9},{9,8},{10,11... | collective-permute-start | bytes 491528 | tf_op jit(solution)/shard_map/ppermute | solution.py:26
